TPU v7x, 32 devices: a whole 2x2x4 slice. The times are simulated.
32 devices in a mesh: rows: 8 (over y, x, core), cols: 4 (over z).
Axes of the slice: x: 2, y: 2, z: 4, core: 2. Of those that a mesh axis runs over, the one named last changes fastest.
Arguments:
- coadd_flux: float32 [1024, 4096], P('rows', 'cols'), may hold values from -8 to 8
- inverse_variance: float32 [1024, 4096], P('rows', 'cols'), may hold values from 0.25 to 4
- source_mask: int32 [1024, 4096], P('rows', 'cols'), may hold values 0 or 1
Outputs:
- background: float32 [1024, 4096], P('rows', 'cols')
- rms_map: float32 [1024, 4096], P('rows', 'cols')
All inputs are finite; a program needn't handle non-finite values. No bound on the sum of `source_mask` on one device may be relied on, other than what follows from the above.
Results may differ from a plain program's by a relative error of at most 0.0001.
Values sent between devices are 32-bit elements; how exact they have to be, the bound alone decides.
No kernel may reach another device: no remote copies, remote signals or barrier semaphores. Data moves between devices by JAX's collectives and lax.ppermute only.
A program may use at most 64 MiB of HBM per device.

v0:
```python
import jax
import jax.numpy as jnp
from jax import lax
from jax.sharding import PartitionSpec as P

ITERS = 2
RADIUS = 32


smooth_weight = 2.0
blur_sigma = 10.0


def padded_2(block, sides, width):
    for axis, dim in sides:
        count = lax.axis_size(axis)
        forward = [(i, i + 1) for i in range(count - 1)]
        backward = [(target, source) for source, target in forward]
        low = lax.ppermute(
            lax.slice_in_dim(block, block.shape[dim] - width, None, axis=dim), axis, forward
        )
        high = lax.ppermute(lax.slice_in_dim(block, 0, width, axis=dim), axis, backward)
        block = jnp.concatenate([low, block, high], axis=dim)
    return block


def stencil_local(padded, field, weight):
    beside = padded[2:, 1:-1] + padded[:-2, 1:-1] + padded[1:-1, 2:] + padded[1:-1, :-2]
    return weight * field + smooth_weight * (4.0 * field - beside)


def apply_operator(field, weight):
    padded = padded_2(field, (("rows", 0), ("cols", 1)), 1)
    return stencil_local(padded, field, weight)


def tap_table(out_length):
    offsets = jnp.arange(2 * RADIUS + 1).astype(jnp.float32) - RADIUS
    raw_taps = jnp.exp(-offsets * offsets / (2.0 * blur_sigma * blur_sigma))
    norm_taps = jnp.sum(raw_taps)
    shape = (out_length, out_length + 2 * RADIUS)
    row_index = lax.broadcasted_iota(jnp.int32, shape, 0)
    col_index = lax.broadcasted_iota(jnp.int32, shape, 1)
    spread = col_index - row_index
    inside = (spread >= 0) & (spread <= 2 * RADIUS)
    centred = (spread - RADIUS).astype(jnp.float32)
    values = jnp.exp(-centred * centred / (2.0 * blur_sigma * blur_sigma)) / norm_taps
    return jnp.where(inside, values, 0.0)


def rows_apply(extended, out_length):
    return jnp.dot(tap_table(out_length), extended, precision=lax.Precision.HIGHEST)


def cols_apply(extended, out_length):
    return jnp.dot(extended, tap_table(out_length).T, precision=lax.Precision.HIGHEST)


def pass_rows(field):
    extended = padded_2(field, (("rows", 0),), RADIUS)
    return rows_apply(extended, field.shape[0])


def pass_cols(field):
    extended = padded_2(field, (("cols", 1),), RADIUS)
    return cols_apply(extended, field.shape[1])


def shards(coadd_flux, inverse_variance, source_mask):
    weight = inverse_variance * (1.0 - source_mask.astype(jnp.float32))

    def squares(residual):
        return lax.psum(jnp.sum(residual * residual), ("rows", "cols"))

    background = jnp.zeros_like(coadd_flux)
    residual = weight * coadd_flux
    direction = residual
    norm_now = squares(residual)
    for step in range(ITERS):
        image_term = apply_operator(direction, weight)
        alpha = norm_now / lax.psum(jnp.sum(direction * image_term), ("rows", "cols"))
        background = background + alpha * direction
        residual = residual - alpha * image_term
        if step + 1 < ITERS:
            norm_next = squares(residual)
            direction = residual + norm_next / norm_now * direction
            norm_now = norm_next
    scatter = coadd_flux - background
    smoothed = scatter * scatter
    for repeat in range(2):
        smoothed = pass_rows(smoothed)
        smoothed = pass_cols(smoothed)
    return (background, jnp.sqrt(smoothed + 1e-06))


def solution(mesh):
    return jax.shard_map(
        shards,
        mesh=mesh,
        in_specs=(P("rows", "cols"), P("rows", "cols"), P("rows", "cols")),
        out_specs=(P("rows", "cols"), P("rows", "cols")),
        check_vma=False,
    )
```

profile of v0, /device:TPU:19, one launch (start us, length us, event | category | flops | bytes accessed | tf_op | source)
XLA Modules:
  0.0 213.8 jit_solution(16536778402984142325)
XLA Ops:
  0.6 1.5 fusion.77
  2.2 0.0 copy-start
  2.2 3.8 %collective-permute-start.1 = (f32[1,1024]{1,0:T(1,128)S(1)}, f32[1,1024]{1,0:T(1,128)S(1)}, u32[]{:S(2)}, u32[]{:S(2)}) collective-permute-start(f32[1,1024]{1,0:T(1,128)S(1)} %get-tuple-element.23), channel_id=1, source_target_pairs={{0,4},{4,8},{8,12},{12,16},{16,20},{20,24},{24,28},{1,5},{5,9},{9,... | collective-permute-start | bytes 12296 | tf_op jit(solution)/shard_map/ppermute | solution.py:19
  6.0 1.9 collective-permute-start
  8.0 3.9 %collective-permute-done = f32[1,1024]{1,0:T(1,128)S(1)} collective-permute-done((f32[1,1024]{1,0:T(1,128)S(1)}, f32[1,1024]{1,0:T(1,128)S(1)}, u32[]{:S(2)}, u32[]{:S(2)}) %collective-permute-start) | collective-permute-done | bytes 4128 | tf_op jit(solution)/shard_map/ppermute | solution.py:22
  11.9 0.1 pad_maximum_fusion.21
  11.9 2.1 collective-permute-start.2
  14.0 3.2 %collective-permute-start.3 = (f32[130,1]{1,0:T(8,128)S(1)}, f32[130,1]{1,0:T(8,128)S(1)}, u32[]{:S(2)}, u32[]{:S(2)}) collective-permute-start(f32[130,1]{1,0:T(8,128)S(1)} %get-tuple-element.12), channel_id=1, source_target_pairs={{0,1},{1,2},{2,3},{4,5},{5,6},{6,7},{8,9},{9,10},{10,11},{12,13},{... | collective-permute-start | bytes 1568 | tf_op jit(solution)/shard_map/ppermute | solution.py:19
  17.3 1.8 collective-permute-done.3
  19.1 1.1 multiply_reduce_fusion.1
  20.2 39.6 %all-reduce = (f32[]{:T(128)}, f32[]{:T(128)}) all-reduce(f32[]{:T(128)} %get-tuple-element.3, f32[]{:T(128)} %get-tuple-element.2), channel_id=1, replica_groups=mesh['rows'=8,'cols'=4] {'rows','cols'}, use_global_device_ids=true, to_apply=%region_1.0 | all-reduce | flops 2 | bytes 16 | tf_op jit(solution)/shard_map/psum | solution.py:73
  61.1 0.7 multiply_reduce_fusion
  61.9 39.2 %psum.30 = f32[]{:T(128)} all-reduce(f32[]{:T(128)} %multiply_reduce_fusion), channel_id=1, replica_groups=mesh['rows'=8,'cols'=4] {'rows','cols'}, use_global_device_ids=true, to_apply=%region_5.0 | all-reduce | flops 1 | bytes 8 | tf_op jit(solution)/shard_map/psum | solution.py:73
  102.4 0.1 multiply_add_fusion.1
  102.5 5.5 %collective-permute-start.5 = (f32[1,1024]{1,0:T(1,128)S(1)}, f32[1,1024]{1,0:T(1,128)S(1)}, u32[]{:S(2)}, u32[]{:S(2)}) collective-permute-start(f32[1,1024]{1,0:T(1,128)S(1)} %get-tuple-element.21), channel_id=1, source_target_pairs={{0,4},{4,8},{8,12},{12,16},{16,20},{20,24},{24,28},{1,5},{5,9},{9,... | collective-permute-start | bytes 12296 | tf_op jit(solution)/shard_map/ppermute | solution.py:19
  108.0 1.9 collective-permute-start.4
  110.0 3.9 %collective-permute-done.4 = f32[1,1024]{1,0:T(1,128)S(1)} collective-permute-done((f32[1,1024]{1,0:T(1,128)S(1)}, f32[1,1024]{1,0:T(1,128)S(1)}, u32[]{:S(2)}, u32[]{:S(2)}) %collective-permute-start.4) | collective-permute-done | bytes 4128 | tf_op jit(solution)/shard_map/ppermute | solution.py:22
  113.9 0.1 pad_maximum_fusion.18
  114.0 2.4 %collective-permute-start.6 = (f32[130,1]{1,0:T(8,128)S(1)}, f32[130,1]{1,0:T(8,128)S(1)}, u32[]{:S(2)}, u32[]{:S(2)}) collective-permute-start(f32[130,1]{1,0:T(8,128)S(1)} %get-tuple-element.9), channel_id=1, source_target_pairs={{1,0},{2,1},{3,2},{5,4},{6,5},{7,6},{9,8},{10,9},{11,10},{13,12},{... | collective-permute-start | bytes 1568 | tf_op jit(solution)/shard_map/ppermute | solution.py:22
  116.4 0.0 copy-start.2
  116.4 3.0 %collective-permute-start.7 = (f32[130,1]{1,0:T(8,128)S(1)}, f32[130,1]{1,0:T(8,128)S(1)}, u32[]{:S(2)}, u32[]{:S(2)}) collective-permute-start(f32[130,1]{1,0:T(8,128)S(1)} %get-tuple-element.10), channel_id=1, source_target_pairs={{0,1},{1,2},{2,3},{4,5},{5,6},{6,7},{8,9},{9,10},{10,11},{12,13},{... | collective-permute-start | bytes 1568 | tf_op jit(solution)/shard_map/ppermute | solution.py:19
  119.4 0.0 collective-permute-done.6
  119.4 2.2 %collective-permute-done.7 = f32[130,1]{1,0:T(8,128)S(1)} collective-permute-done((f32[130,1]{1,0:T(8,128)S(1)}, f32[130,1]{1,0:T(8,128)S(1)}, u32[]{:S(2)}, u32[]{:S(2)}) %collective-permute-start.7) | collective-permute-done | bytes 552 | tf_op jit(solution)/shard_map/ppermute | solution.py:19
  121.6 1.1 fusion.34
  122.7 39.1 %psum.31 = f32[]{:T(128)} all-reduce(f32[]{:T(128)} %fusion.34), channel_id=1, replica_groups=mesh['rows'=8,'cols'=4] {'rows','cols'}, use_global_device_ids=true, to_apply=%region_7.0 | all-reduce | flops 1 | bytes 8 | tf_op jit(solution)/shard_map/psum | solution.py:81
  163.1 1.0 subtract_multiply_fusion
  164.1 4.0 %collective-permute-start.8 = (f32[32,1024]{1,0:T(8,128)S(1)}, f32[32,1024]{1,0:T(8,128)S(1)}, u32[]{:S(2)}, u32[]{:S(2)}) collective-permute-start(f32[32,1024]{1,0:T(8,128)S(1)} %get-tuple-element.19), channel_id=1, source_target_pairs={{0,4},{4,8},{8,12},{12,16},{16,20},{20,24},{24,28},{1,5},{5,9},{9,... | collective-permute-start | bytes 393224 | tf_op jit(solution)/shard_map/ppermute | solution.py:19
  168.1 1.9 collective-permute-start.9
  170.1 0.7 fusion.54
  170.8 4.6 %collective-permute-done.9 = f32[32,1024]{1,0:T(8,128)S(1)} collective-permute-done((f32[32,1024]{1,0:T(8,128)S(1)}, f32[32,1024]{1,0:T(8,128)S(1)}, u32[]{:S(2)}, u32[]{:S(2)}) %collective-permute-start.9) | collective-permute-done | bytes 131104 | tf_op jit(solution)/shard_map/ppermute | solution.py:22
  175.3 1.4 fusion.17
  176.7 0.1 fusion.81
  176.8 2.3 %collective-permute-start.11 = (f32[128,32]{1,0:T(8,128)S(1)}, f32[128,32]{1,0:T(8,128)S(1)}, u32[]{:S(2)}, u32[]{:S(2)}) collective-permute-start(f32[128,32]{1,0:T(8,128)S(1)} %get-tuple-element.17), channel_id=1, source_target_pairs={{1,0},{2,1},{3,2},{5,4},{6,5},{7,6},{9,8},{10,9},{11,10},{13,12},{... | collective-permute-start | bytes 49160 | tf_op jit(solution)/shard_map/ppermute | solution.py:22
  179.1 3.0 %collective-permute-start.10 = (f32[128,32]{1,0:T(8,128)S(1)}, f32[128,32]{1,0:T(8,128)S(1)}, u32[]{:S(2)}, u32[]{:S(2)}) collective-permute-start(f32[128,32]{1,0:T(8,128)S(1)} %get-tuple-element.18), channel_id=1, source_target_pairs={{0,1},{1,2},{2,3},{4,5},{5,6},{6,7},{8,9},{9,10},{10,11},{12,13},{... | collective-permute-start | bytes 49160 | tf_op jit(solution)/shard_map/ppermute | solution.py:19
  182.1 2.0 collective-permute-done.10
  184.1 0.3 concatenate.55
  184.4 3.7 %fusion.9 = f32[128,1024]{1,0:T(8,128)S(1)} fusion(f32[128,1088]{1,0:T(8,128)S(1)} %concatenate.55, f32[]{:T(128)} %fusion.54), kind=kOutput, calls=%fused_computation.10 | convolution fusion | flops 1723531264 | bytes 1081348 | tf_op jit(solution)/shard_map/dot_general | solution.py:56
  188.1 3.9 %collective-permute-start.12 = (f32[32,1024]{1,0:T(8,128)S(1)}, f32[32,1024]{1,0:T(8,128)S(1)}, u32[]{:S(2)}, u32[]{:S(2)}) collective-permute-start(f32[32,1024]{1,0:T(8,128)S(1)} %get-tuple-element.15), channel_id=1, source_target_pairs={{0,4},{4,8},{8,12},{12,16},{16,20},{20,24},{24,28},{1,5},{5,9},{9,... | collective-permute-start | bytes 393224 | tf_op jit(solution)/shard_map/ppermute | solution.py:19
  192.1 1.9 collective-permute-start.13
  194.0 0.4 collective-permute-done.12
  194.4 4.9 %collective-permute-done.13 = f32[32,1024]{1,0:T(8,128)S(1)} collective-permute-done((f32[32,1024]{1,0:T(8,128)S(1)}, f32[32,1024]{1,0:T(8,128)S(1)}, u32[]{:S(2)}, u32[]{:S(2)}) %collective-permute-start.13) | collective-permute-done | bytes 131104 | tf_op jit(solution)/shard_map/ppermute | solution.py:22
  199.2 1.4 fusion.23
  200.6 0.1 fusion.79
  200.7 3.2 %collective-permute-start.15 = (f32[128,32]{1,0:T(8,128)S(1)}, f32[128,32]{1,0:T(8,128)S(1)}, u32[]{:S(2)}, u32[]{:S(2)}) collective-permute-start(f32[128,32]{1,0:T(8,128)S(1)} %get-tuple-element.13), channel_id=1, source_target_pairs={{1,0},{2,1},{3,2},{5,4},{6,5},{7,6},{9,8},{10,9},{11,10},{13,12},{... | collective-permute-start | bytes 49160 | tf_op jit(solution)/shard_map/ppermute | solution.py:22
  203.9 2.2 %collective-permute-start.14 = (f32[128,32]{1,0:T(8,128)S(1)}, f32[128,32]{1,0:T(8,128)S(1)}, u32[]{:S(2)}, u32[]{:S(2)}) collective-permute-start(f32[128,32]{1,0:T(8,128)S(1)} %get-tuple-element.14), channel_id=1, source_target_pairs={{0,1},{1,2},{2,3},{4,5},{5,6},{6,7},{8,9},{9,10},{10,11},{12,13},{... | collective-permute-start | bytes 49160 | tf_op jit(solution)/shard_map/ppermute | solution.py:19
  206.2 2.7 %collective-permute-done.14 = f32[128,32]{1,0:T(8,128)S(1)} collective-permute-done((f32[128,32]{1,0:T(8,128)S(1)}, f32[128,32]{1,0:T(8,128)S(1)}, u32[]{:S(2)}, u32[]{:S(2)}) %collective-permute-start.14) | collective-permute-done | bytes 16416 | tf_op jit(solution)/shard_map/ppermute | solution.py:19
  208.9 0.3 concatenate.57
  209.2 4.5 %fusion.14 = f32[128,1024]{1,0:T(8,128)} fusion(f32[128,1088]{1,0:T(8,128)S(1)} %concatenate.57, f32[]{:T(128)} %fusion.54), kind=kOutput, calls=%fused_computation.12 | convolution fusion | flops 1723662336 | bytes 1081348 | tf_op jit(solution)/shard_map/dot_general | solution.py:56
  (14 shorter events, 0.1 us)
Async XLA Ops:
  0.6 18.5 %copy-start.1 = (s32[128,1024]{1,0:T(8,128)S(1)}, s32[128,1024]{1,0:T(8,128)}, u32[]{:S(2)}) copy-start(s32[128,1024]{1,0:T(8,128)} %param.5) | copy-start | bytes 1572868
  2.2 16.9 %copy-start = (f32[128,1024]{1,0:T(8,128)S(1)}, f32[128,1024]{1,0:T(8,128)}, u32[]{:S(2)}) copy-start(f32[128,1024]{1,0:T(8,128)} %param.4) | copy-start | bytes 1572868
  2.2 5.8 %collective-permute-start.1 = (f32[1,1024]{1,0:T(1,128)S(1)}, f32[1,1024]{1,0:T(1,128)S(1)}, u32[]{:S(2)}, u32[]{:S(2)}) collective-permute-start(f32[1,1024]{1,0:T(1,128)S(1)} %get-tuple-element.23), channel_id=1, source_target_pairs={{0,4},{4,8},{8,12},{12,16},{16,20},{20,24},{24,28},{1,5},{5,9},{9,... | collective-permute-start | bytes 12296 | tf_op jit(solution)/shard_map/ppermute | solution.py:19
  6.0 5.8 %collective-permute-start = (f32[1,1024]{1,0:T(1,128)S(1)}, f32[1,1024]{1,0:T(1,128)S(1)}, u32[]{:S(2)}, u32[]{:S(2)}) collective-permute-start(f32[1,1024]{1,0:T(1,128)S(1)} %get-tuple-element.24), channel_id=1, source_target_pairs={{4,0},{8,4},{12,8},{16,12},{20,16},{24,20},{28,24},{5,1},{9,5},{13... | collective-permute-start | bytes 12296 | tf_op jit(solution)/shard_map/ppermute | solution.py:22
  11.9 5.3 %collective-permute-start.2 = (f32[130,1]{1,0:T(8,128)S(1)}, f32[130,1]{1,0:T(8,128)S(1)}, u32[]{:S(2)}, u32[]{:S(2)}) collective-permute-start(f32[130,1]{1,0:T(8,128)S(1)} %get-tuple-element.11), channel_id=1, source_target_pairs={{1,0},{2,1},{3,2},{5,4},{6,5},{7,6},{9,8},{10,9},{11,10},{13,12},{... | collective-permute-start | bytes 1568 | tf_op jit(solution)/shard_map/ppermute | solution.py:22
  14.0 5.1 %collective-permute-start.3 = (f32[130,1]{1,0:T(8,128)S(1)}, f32[130,1]{1,0:T(8,128)S(1)}, u32[]{:S(2)}, u32[]{:S(2)}) collective-permute-start(f32[130,1]{1,0:T(8,128)S(1)} %get-tuple-element.12), channel_id=1, source_target_pairs={{0,1},{1,2},{2,3},{4,5},{5,6},{6,7},{8,9},{9,10},{10,11},{12,13},{... | collective-permute-start | bytes 1568 | tf_op jit(solution)/shard_map/ppermute | solution.py:19
  102.5 7.4 %collective-permute-start.5 = (f32[1,1024]{1,0:T(1,128)S(1)}, f32[1,1024]{1,0:T(1,128)S(1)}, u32[]{:S(2)}, u32[]{:S(2)}) collective-permute-start(f32[1,1024]{1,0:T(1,128)S(1)} %get-tuple-element.21), channel_id=1, source_target_pairs={{0,4},{4,8},{8,12},{12,16},{16,20},{20,24},{24,28},{1,5},{5,9},{9,... | collective-permute-start | bytes 12296 | tf_op jit(solution)/shard_map/ppermute | solution.py:19
  108.0 5.8 %collective-permute-start.4 = (f32[1,1024]{1,0:T(1,128)S(1)}, f32[1,1024]{1,0:T(1,128)S(1)}, u32[]{:S(2)}, u32[]{:S(2)}) collective-permute-start(f32[1,1024]{1,0:T(1,128)S(1)} %get-tuple-element.22), channel_id=1, source_target_pairs={{4,0},{8,4},{12,8},{16,12},{20,16},{24,20},{28,24},{5,1},{9,5},{13... | collective-permute-start | bytes 12296 | tf_op jit(solution)/shard_map/ppermute | solution.py:22
  114.0 5.4 %collective-permute-start.6 = (f32[130,1]{1,0:T(8,128)S(1)}, f32[130,1]{1,0:T(8,128)S(1)}, u32[]{:S(2)}, u32[]{:S(2)}) collective-permute-start(f32[130,1]{1,0:T(8,128)S(1)} %get-tuple-element.9), channel_id=1, source_target_pairs={{1,0},{2,1},{3,2},{5,4},{6,5},{7,6},{9,8},{10,9},{11,10},{13,12},{... | collective-permute-start | bytes 1568 | tf_op jit(solution)/shard_map/ppermute | solution.py:22
  116.4 46.7 %copy-start.2 = (f32[128,1024]{1,0:T(8,128)S(1)}, f32[128,1024]{1,0:T(8,128)}, u32[]{:S(2)}) copy-start(f32[128,1024]{1,0:T(8,128)} %param.3) | copy-start | bytes 1572868
  116.4 5.2 %collective-permute-start.7 = (f32[130,1]{1,0:T(8,128)S(1)}, f32[130,1]{1,0:T(8,128)S(1)}, u32[]{:S(2)}, u32[]{:S(2)}) collective-permute-start(f32[130,1]{1,0:T(8,128)S(1)} %get-tuple-element.10), channel_id=1, source_target_pairs={{0,1},{1,2},{2,3},{4,5},{5,6},{6,7},{8,9},{9,10},{10,11},{12,13},{... | collective-permute-start | bytes 1568 | tf_op jit(solution)/shard_map/ppermute | solution.py:19
  164.1 6.7 %collective-permute-start.8 = (f32[32,1024]{1,0:T(8,128)S(1)}, f32[32,1024]{1,0:T(8,128)S(1)}, u32[]{:S(2)}, u32[]{:S(2)}) collective-permute-start(f32[32,1024]{1,0:T(8,128)S(1)} %get-tuple-element.19), channel_id=1, source_target_pairs={{0,4},{4,8},{8,12},{12,16},{16,20},{20,24},{24,28},{1,5},{5,9},{9,... | collective-permute-start | bytes 393224 | tf_op jit(solution)/shard_map/ppermute | solution.py:19
  168.1 7.2 %collective-permute-start.9 = (f32[32,1024]{1,0:T(8,128)S(1)}, f32[32,1024]{1,0:T(8,128)S(1)}, u32[]{:S(2)}, u32[]{:S(2)}) collective-permute-start(f32[32,1024]{1,0:T(8,128)S(1)} %get-tuple-element.20), channel_id=1, source_target_pairs={{4,0},{8,4},{12,8},{16,12},{20,16},{24,20},{28,24},{5,1},{9,5},{13... | collective-permute-start | bytes 393224 | tf_op jit(solution)/shard_map/ppermute | solution.py:22
  176.8 5.3 %collective-permute-start.11 = (f32[128,32]{1,0:T(8,128)S(1)}, f32[128,32]{1,0:T(8,128)S(1)}, u32[]{:S(2)}, u32[]{:S(2)}) collective-permute-start(f32[128,32]{1,0:T(8,128)S(1)} %get-tuple-element.17), channel_id=1, source_target_pairs={{1,0},{2,1},{3,2},{5,4},{6,5},{7,6},{9,8},{10,9},{11,10},{13,12},{... | collective-permute-start | bytes 49160 | tf_op jit(solution)/shard_map/ppermute | solution.py:22
  179.1 5.0 %collective-permute-start.10 = (f32[128,32]{1,0:T(8,128)S(1)}, f32[128,32]{1,0:T(8,128)S(1)}, u32[]{:S(2)}, u32[]{:S(2)}) collective-permute-start(f32[128,32]{1,0:T(8,128)S(1)} %get-tuple-element.18), channel_id=1, source_target_pairs={{0,1},{1,2},{2,3},{4,5},{5,6},{6,7},{8,9},{9,10},{10,11},{12,13},{... | collective-permute-start | bytes 49160 | tf_op jit(solution)/shard_map/ppermute | solution.py:19
  188.1 6.2 %collective-permute-start.12 = (f32[32,1024]{1,0:T(8,128)S(1)}, f32[32,1024]{1,0:T(8,128)S(1)}, u32[]{:S(2)}, u32[]{:S(2)}) collective-permute-start(f32[32,1024]{1,0:T(8,128)S(1)} %get-tuple-element.15), channel_id=1, source_target_pairs={{0,4},{4,8},{8,12},{12,16},{16,20},{20,24},{24,28},{1,5},{5,9},{9,... | collective-permute-start | bytes 393224 | tf_op jit(solution)/shard_map/ppermute | solution.py:19
  192.1 7.2 %collective-permute-start.13 = (f32[32,1024]{1,0:T(8,128)S(1)}, f32[32,1024]{1,0:T(8,128)S(1)}, u32[]{:S(2)}, u32[]{:S(2)}) collective-permute-start(f32[32,1024]{1,0:T(8,128)S(1)} %get-tuple-element.16), channel_id=1, source_target_pairs={{4,0},{8,4},{12,8},{16,12},{20,16},{24,20},{28,24},{5,1},{9,5},{13... | collective-permute-start | bytes 393224 | tf_op jit(solution)/shard_map/ppermute | solution.py:22
  200.7 5.5 %collective-permute-start.15 = (f32[128,32]{1,0:T(8,128)S(1)}, f32[128,32]{1,0:T(8,128)S(1)}, u32[]{:S(2)}, u32[]{:S(2)}) collective-permute-start(f32[128,32]{1,0:T(8,128)S(1)} %get-tuple-element.13), channel_id=1, source_target_pairs={{1,0},{2,1},{3,2},{5,4},{6,5},{7,6},{9,8},{10,9},{11,10},{13,12},{... | collective-permute-start | bytes 49160 | tf_op jit(solution)/shard_map/ppermute | solution.py:22
  203.9 5.0 %collective-permute-start.14 = (f32[128,32]{1,0:T(8,128)S(1)}, f32[128,32]{1,0:T(8,128)S(1)}, u32[]{:S(2)}, u32[]{:S(2)}) collective-permute-start(f32[128,32]{1,0:T(8,128)S(1)} %get-tuple-element.14), channel_id=1, source_target_pairs={{0,1},{1,2},{2,3},{4,5},{5,6},{6,7},{8,9},{9,10},{10,11},{12,13},{... | collective-permute-start | bytes 49160 | tf_op jit(solution)/shard_map/ppermute | solution.py:19
where the time goes:
time: 215 us; the launch traced here: 214 us
  blocking collectives  118 us (55%)
  starting transfers between devices  46.4 us (22%)
  waiting for transfers between devices  26.3 us (12%)
  matrix products  11 us (5%)
  other arithmetic  6.39 us (3%)
  between operations  4.96 us (2%)
    psum x2, blocking collectives, squares(): return lax.psum(jnp.sum(residual * residual), ('rows', 'cols'))  78.8 us
    psum x1, blocking collectives, shards(): lax.psum(jnp.sum(direction * image_term), ('rows', 'cols'))  39.1 us
    ppermute x8, starting transfers between devices, padded_2(): lax.ppermute(lax.slice_in_dim(block, block.shape[dim] - width, None, axis...  28.7 us
    ppermute x8, starting transfers between devices, padded_2(): lax.ppermute(lax.slice_in_dim(block, 0, width, axis=dim), axis, backward)  17.6 us
    ppermute x8, waiting for transfers between devices, padded_2(): lax.ppermute(lax.slice_in_dim(block, 0, width, axis=dim), axis, backward)  17.2 us
    ppermute x8, waiting for transfers between devices, padded_2(): lax.ppermute(lax.slice_in_dim(block, block.shape[dim] - width, None, axis...  9.11 us
    dot_general x2, matrix products, cols_apply(): jnp.dot(extended, tap_table(out_length).T, precision=lax.Precision.HIGHEST)  8.23 us
  transfers between devices with their start and end apart: 16, of which 9 were waited for; matrix products, arithmetic and copies ran while one was open for 0% of the time, Pallas kernels for 0%

commit v1 on v0

v1 whole, which is shorter than its diff:
```python
import functools

import jax
import jax.numpy as jnp
import ml_dtypes
import numpy as np
from jax import lax
from jax.experimental import pallas as pl
from jax.experimental.pallas import tpu as pltpu
from jax.sharding import PartitionSpec as P

RADIUS = 32
REACH = 2 * RADIUS
LANES = 128
WIDE = REACH + 8
NEAR = 8

smooth_weight = 2.0
blur_sigma = 10.0


def squared_taps(length, first, last):
    offsets = np.arange(2 * RADIUS + 1) - RADIUS
    taps = np.exp(-offsets * offsets / (2.0 * blur_sigma * blur_sigma))
    taps = taps / taps.sum()

    def band(count):
        table = np.zeros((count, count + 2 * RADIUS))
        for k in range(2 * RADIUS + 1):
            table[np.arange(count), np.arange(count) + k] = taps[k]
        return table

    inner = band(length + 2 * RADIUS)
    if first:
        inner[:RADIUS] = 0.0
    if last:
        inner[-RADIUS:] = 0.0
    return band(length) @ inner


def split(table):
    high = table.astype(np.float32).astype(ml_dtypes.bfloat16)
    low = (table - high.astype(np.float64)).astype(np.float32).astype(ml_dtypes.bfloat16)
    return high, low


def row_tables(length):
    tables = []
    for first, last in ((False, False), (True, False), (False, True), (True, True)):
        tables.append(np.concatenate(split(squared_taps(length, first, last)), axis=0))
    return np.stack(tables)


def col_tables():
    tables = []
    for first, last in ((False, False), (True, False), (False, True)):
        tables.append(np.concatenate(split(squared_taps(LANES, first, last).T), axis=1))
    return np.stack(tables)


def split_values(values):
    high = values.astype(jnp.bfloat16)
    return high, (values - high.astype(jnp.float32)).astype(jnp.bfloat16)


def at_edges():
    row, col = lax.axis_index("rows"), lax.axis_index("cols")
    return (
        row == 0,
        row == lax.axis_size("rows") - 1,
        col == 0,
        col == lax.axis_size("cols") - 1,
    )


def beside_columns(field):
    width = field.shape[1]
    return pltpu.roll(field, 1, 1) + pltpu.roll(field, width - 1, 1)


def moments_kernel(f_ref, w_ref, top_ref, bottom_ref, left_ref, right_ref, out_ref, v0_ref, v1_ref):
    rows, cols = f_ref.shape
    width = cols + 2 * LANES
    first_row, last_row, first_col, last_col = at_edges()

    def pair(start):
        if start < NEAR:
            return top_ref[0], top_ref[1]
        if start >= NEAR + rows:
            return bottom_ref[0], bottom_ref[1]
        at = pl.ds(start - NEAR, 8)
        return tuple(
            jnp.concatenate([left_ref[i, at, :], ref[at, :], right_ref[i, at, :]], axis=1)
            for i, ref in enumerate((f_ref, w_ref))
        )

    for start in range(0, rows + 2 * NEAR, 8):
        flux, weight = pair(start)
        v0_ref[pl.ds(start, 8), :] = flux * weight

    zeros = jnp.zeros((8, width), jnp.float32)
    v1_ref[pl.ds(0, 8), :] = zeros
    v1_ref[pl.ds(rows + 2 * NEAR - 8, 8), :] = zeros

    def image(ref, weight, start, count):
        here = ref[pl.ds(start, count), :]
        beside = ref[pl.ds(start - 1, count), :] + ref[pl.ds(start + 1, count), :] + beside_columns(here)
        return here, weight * here + smooth_weight * (4.0 * here - beside)

    for start in range(NEAR, NEAR + rows, 8):
        _, weight = pair(start)
        _, out = image(v0_ref, weight, start, 8)
        v1_ref[pl.ds(start, 8), :] = out

    @pl.when(jnp.logical_not(first_row))
    def _():
        _, out = image(v0_ref, top_ref[1, pl.ds(NEAR - 1, 1), :], NEAR - 1, 1)
        v1_ref[pl.ds(NEAR - 1, 1), :] = out

    @pl.when(jnp.logical_not(last_row))
    def _():
        _, out = image(v0_ref, bottom_ref[1, pl.ds(0, 1), :], NEAR + rows, 1)
        v1_ref[pl.ds(NEAR + rows, 1), :] = out

    @pl.when(first_col)
    def _():
        v1_ref[:, pl.ds(0, LANES)] = jnp.zeros((rows + 2 * NEAR, LANES), jnp.float32)

    @pl.when(last_col)
    def _():
        v1_ref[:, pl.ds(width - LANES, LANES)] = jnp.zeros((rows + 2 * NEAR, LANES), jnp.float32)

    sums = [jnp.zeros((8, cols), jnp.float32) for _ in range(4)]
    for start in range(NEAR, NEAR + rows, 8):
        _, weight = pair(start)
        v1, v2 = image(v1_ref, weight, start, 8)
        v0, v1, v2 = (x[:, LANES : LANES + cols] for x in (v0_ref[pl.ds(start, 8), :], v1, v2))
        sums = [total + term for total, term in zip(sums, (v0 * v0, v0 * v1, v1 * v1, v1 * v2))]
    for i, total in enumerate(sums):
        narrow = sum(total[:, k : k + LANES] for k in range(0, cols, LANES))
        out_ref[pl.ds(i, 1), :] = jnp.sum(narrow, axis=0, keepdims=True)
    out_ref[pl.ds(4, 4), :] = jnp.zeros((4, LANES), jnp.float32)


def coefficients(m0, m1, m2, m3):
    alpha0 = m0 / m1
    norm1 = jnp.maximum(m0 - 2.0 * alpha0 * m1 + alpha0 * alpha0 * m2, 0.0)
    grown = 1.0 + norm1 / m0
    image1 = grown * grown * m1 - 2.0 * grown * alpha0 * m2 + alpha0 * alpha0 * m3
    alpha1 = jnp.where(image1 > 0.0, norm1 / image1, 0.0)
    return alpha0 + alpha1 * grown, -alpha1 * alpha0


def finish_kernel(
    parts_ref, f_ref, w_ref, top_ref, bottom_ref, left_ref, right_ref, rowtaps_ref, coltaps_ref,
    background_ref, rms_ref, v0_ref, high_ref, low_ref,
):
    rows, cols = f_ref.shape
    width = cols + 2 * LANES
    first_row, last_row, first_col, last_col = at_edges()

    totals = jnp.sum(parts_ref[...], axis=0)
    c0, c1 = coefficients(*(jnp.sum(totals[i : i + 1, :], axis=1, keepdims=True) for i in range(4)))

    def pair(start, count):
        if start < WIDE:
            at = pl.ds(start, count)
            return top_ref[0, at, :], top_ref[1, at, :]
        if start >= WIDE + rows:
            at = pl.ds(start - WIDE - rows, count)
            return bottom_ref[0, at, :], bottom_ref[1, at, :]
        at = pl.ds(start - WIDE, count)
        return tuple(
            jnp.concatenate([left_ref[i, at, :], ref[at, :], right_ref[i, at, :]], axis=1)
            for i, ref in enumerate((f_ref, w_ref))
        )

    for start in range(0, rows + 2 * WIDE, 8):
        flux, weight = pair(start, 8)
        v0_ref[pl.ds(start, 8), :] = flux * weight

    step = 16
    for start in range(8, rows + 2 * WIDE - 8, step):
        flux, weight = pair(start, step)
        v0 = v0_ref[pl.ds(start, step), :]
        beside = v0_ref[pl.ds(start - 1, step), :] + v0_ref[pl.ds(start + 1, step), :] + beside_columns(v0)
        v1 = weight * v0 + smooth_weight * (4.0 * v0 - beside)
        background = c0 * v0 + c1 * v1
        if WIDE <= start < WIDE + rows:
            background_ref[pl.ds(start - WIDE, step), :] = background[:, LANES : LANES + cols]
        scatter = flux - background
        high, low = split_values(scatter * scatter)
        high_ref[pl.ds(start - 8, step), :] = high
        low_ref[pl.ds(start - 8, step), :] = low

    def clear(at_rows, at_cols):
        for ref in (high_ref, low_ref):
            ref[at_rows, at_cols] = jnp.zeros((at_rows.size, at_cols.size), jnp.bfloat16)

    everywhere_r, everywhere_c = pl.ds(0, rows + 2 * REACH), pl.ds(0, width)
    pl.when(first_row)(lambda: clear(pl.ds(0, REACH), everywhere_c))
    pl.when(last_row)(lambda: clear(pl.ds(REACH + rows, REACH), everywhere_c))
    pl.when(first_col)(lambda: clear(everywhere_r, pl.ds(0, LANES)))
    pl.when(last_col)(lambda: clear(everywhere_r, pl.ds(width - LANES, LANES)))

    dot = functools.partial(jnp.dot, preferred_element_type=jnp.float32)
    table = rowtaps_ref[first_row.astype(jnp.int32) + 2 * last_row.astype(jnp.int32)]
    high = dot(table, high_ref[...])
    passed = high[:rows] + (high[rows:] + dot(table[:rows], low_ref[...]))
    passed = pltpu.roll(passed, width - (LANES - REACH), 1)
    high, low = split_values(passed)
    blocks = cols // LANES
    for j in range(blocks):
        which = 0
        if j == 0:
            which = first_col.astype(jnp.int32)
        elif j == blocks - 1:
            which = 2 * last_col.astype(jnp.int32)
        table = coltaps_ref[which]
        at = slice(j * LANES, j * LANES + 2 * LANES)
        both = dot(high[:, at], table)
        smoothed = both[:, :LANES] + (both[:, LANES:] + dot(low[:, at], table[:, :LANES]))
        rms_ref[:, pl.ds(j * LANES, LANES)] = jnp.sqrt(smoothed + 1e-06)


def shift(block, axis, step):
    count = lax.axis_size(axis)
    pairs = [(i, i + step) for i in range(count) if 0 <= i + step < count]
    return lax.ppermute(block, axis, pairs)


def shards(coadd_flux, inverse_variance, source_mask):
    rows, cols = coadd_flux.shape
    width = cols + 2 * LANES
    devices = lax.axis_size("rows") * lax.axis_size("cols")
    weight = inverse_variance * (1.0 - source_mask.astype(jnp.float32))
    both = jnp.stack([coadd_flux, weight])
    left = shift(both[:, :, cols - LANES :], "cols", 1)
    right = shift(both[:, :, :LANES], "cols", -1)
    extended = jnp.concatenate([left, both, right], axis=2)
    near_top = shift(extended[:, rows - NEAR :], "rows", 1)
    near_bottom = shift(extended[:, :NEAR], "rows", -1)
    top = shift(extended[:, rows - WIDE :], "rows", 1)
    bottom = shift(extended[:, :WIDE], "rows", -1)

    vmem = pl.BlockSpec(memory_space=pltpu.VMEM)
    field = jax.ShapeDtypeStruct((rows, cols), jnp.float32)
    parts = pl.pallas_call(
        moments_kernel,
        out_shape=jax.ShapeDtypeStruct((8, LANES), jnp.float32),
        in_specs=[vmem] * 6,
        out_specs=vmem,
        scratch_shapes=[pltpu.VMEM((rows + 2 * NEAR, width), jnp.float32)] * 2,
        compiler_params=pltpu.CompilerParams(vmem_limit_bytes=16 << 20),
        name="moments",
    )(coadd_flux, weight, near_top, near_bottom, left, right)

    parts = jnp.broadcast_to(parts[None], (devices, 8, LANES))
    parts = lax.all_to_all(parts, ("rows", "cols"), 0, 0, tiled=True)

    return tuple(
        pl.pallas_call(
            finish_kernel,
            out_shape=(field, field),
            in_specs=[vmem] * 9,
            out_specs=(vmem, vmem),
            scratch_shapes=[
                pltpu.VMEM((rows + 2 * WIDE, width), jnp.float32),
                pltpu.VMEM((rows + 2 * REACH, width), jnp.bfloat16),
                pltpu.VMEM((rows + 2 * REACH, width), jnp.bfloat16),
            ],
            compiler_params=pltpu.CompilerParams(vmem_limit_bytes=32 << 20),
            name="finish",
        )(
            parts, coadd_flux, weight, top, bottom, left, right,
            jnp.asarray(row_tables(rows)), jnp.asarray(col_tables()),
        )
    )


def solution(mesh):
    return jax.shard_map(
        shards,
        mesh=mesh,
        in_specs=(P("rows", "cols"), P("rows", "cols"), P("rows", "cols")),
        out_specs=(P("rows", "cols"), P("rows", "cols")),
        check_vma=False,
    )
```

time: 215 us -> 53.2 us (0.25)
  the two profiles are of different devices: /device:TPU:19 before, /device:TPU:0 now
where the time goes in v1:
time: 53.2 us; the launch traced here: 52.9 us
  blocking collectives  24.3 us (46%)
  starting transfers between devices  15.6 us (29%)
  waiting for transfers between devices  6.46 us (12%)
  Pallas kernels  4.17 us (8%)
  other arithmetic  1.45 us (3%)
  between operations  0.78 us (1%)
    all_to_all x1, blocking collectives, shards(): parts = lax.all_to_all(parts, ('rows', 'cols'), 0, 0, tiled=True)  24.3 us
    ppermute x6, starting transfers between devices, shift(): return lax.ppermute(block, axis, pairs)  15.6 us
    ppermute x6, waiting for transfers between devices, shift(): return lax.ppermute(block, axis, pairs)  6.46 us
    pallas_call x1, Pallas kernels, shards(): pl.pallas_call(finish_kernel, out_shape=(field, field), in_specs=[vmem] *...  3.08 us
    mul x1, other arithmetic, shards(): weight = inverse_variance * (1.0 - source_mask.astype(jnp.float32))  1.33 us
    pallas_call x1, Pallas kernels, shards(): pl.pallas_call(moments_kernel, out_shape=jax.ShapeDtypeStruct((8, LANES),...  1.09 us
  transfers between devices with their start and end apart: 6, of which 3 were waited for; matrix products, arithmetic and copies ran while one was open for 0% of the time, Pallas kernels for 2%

profile of v1, /device:TPU:0, one launch (start us, length us, event | category | flops | bytes accessed | tf_op | source)
XLA Modules:
  0.0 52.9 jit_solution(8173239488679436243)
XLA Ops:
  0.6 0.0 copy-start
  0.6 1.3 %subtract_multiply_fusion.w_ref = f32[128,1024]{1,0:T(8,128)S(1)} fusion(f32[128,1024]{1,0:T(8,128)} %param.6, s32[128,1024]{1,0:T(8,128)} %param.7), kind=kLoop, calls=%fused_computation.1 | loop fusion | flops 393216 | bytes 1572864 | tf_op jit(solution)/shard_map/mul | solution.py:236
  2.0 0.0 copy-done
  2.0 4.9 %collective-permute-start = (f32[2,128,128]{2,1,0:T(8,128)S(1)}, f32[2,128,128]{2,1,0:T(8,128)S(1)}, u32[]{:S(2)}, u32[]{:S(2)}) collective-permute-start(f32[2,128,128]{2,1,0:T(8,128)S(1)} %get-tuple-element.6), channel_id=1, source_target_pairs={{0,1},{1,2},{2,3},{4,5},{5,6},{6,7},{8,9},{9,10},{10,11},{12,13},{... | collective-permute-start | bytes 393224 | tf_op jit(solution)/shard_map/ppermute | solution.py:229
  7.0 1.3 %collective-permute-start.1 = (f32[2,128,128]{2,1,0:T(8,128)S(1)}, f32[2,128,128]{2,1,0:T(8,128)S(1)}, u32[]{:S(2)}, u32[]{:S(2)}) collective-permute-start(f32[2,128,128]{2,1,0:T(8,128)S(1)} %get-tuple-element.7), channel_id=1, source_target_pairs={{1,0},{2,1},{3,2},{5,4},{6,5},{7,6},{9,8},{10,9},{11,10},{13,12},{... | collective-permute-start | bytes 393224 | tf_op jit(solution)/shard_map/ppermute | solution.py:229
  8.3 1.4 %collective-permute-done.left_ref = f32[2,128,128]{2,1,0:T(8,128)S(1)} collective-permute-done((f32[2,128,128]{2,1,0:T(8,128)S(1)}, f32[2,128,128]{2,1,0:T(8,128)S(1)}, u32[]{:S(2)}, u32[]{:S(2)}) %collective-permute-start) | collective-permute-done | bytes 131104 | tf_op jit(solution)/shard_map/ppermute | solution.py:229
  9.7 4.1 %collective-permute-done.1.right_ref = f32[2,128,128]{2,1,0:T(8,128)S(1)} collective-permute-done((f32[2,128,128]{2,1,0:T(8,128)S(1)}, f32[2,128,128]{2,1,0:T(8,128)S(1)}, u32[]{:S(2)}, u32[]{:S(2)}) %collective-permute-start.1) | collective-permute-done | bytes 131104 | tf_op jit(solution)/shard_map/ppermute | solution.py:229
  13.8 0.1 pad_maximum_fusion
  13.9 0.1 fusion
  14.0 1.3 %collective-permute-start.5 = (f32[2,72,1280]{2,1,0:T(8,128)S(1)}, f32[2,72,1280]{2,1,0:T(8,128)S(1)}, u32[]{:S(2)}, u32[]{:S(2)}) collective-permute-start(f32[2,72,1280]{2,1,0:T(8,128)S(1)} %get-tuple-element.2), channel_id=1, source_target_pairs={{4,0},{8,4},{12,8},{16,12},{20,16},{24,20},{28,24},{5,1},{9,5},{13... | collective-permute-start | bytes 2211848 | tf_op jit(solution)/shard_map/ppermute | solution.py:229
  15.3 0.0 copy-start.1
  15.3 0.0 copy-start.2
  15.4 3.2 %collective-permute-start.4 = (f32[2,72,1280]{2,1,0:T(8,128)S(1)}, f32[2,72,1280]{2,1,0:T(8,128)S(1)}, u32[]{:S(2)}, u32[]{:S(2)}) collective-permute-start(f32[2,72,1280]{2,1,0:T(8,128)S(1)} %get-tuple-element.3), channel_id=1, source_target_pairs={{0,4},{4,8},{8,12},{12,16},{16,20},{20,24},{24,28},{1,5},{5,9},{9,... | collective-permute-start | bytes 2211848 | tf_op jit(solution)/shard_map/ppermute | solution.py:229
  18.6 1.3 %collective-permute-start.3 = (f32[2,8,1280]{2,1,0:T(8,128)S(1)}, f32[2,8,1280]{2,1,0:T(8,128)S(1)}, u32[]{:S(2)}, u32[]{:S(2)}) collective-permute-start(f32[2,8,1280]{2,1,0:T(8,128)S(1)} %get-tuple-element.4), channel_id=1, source_target_pairs={{4,0},{8,4},{12,8},{16,12},{20,16},{24,20},{28,24},{5,1},{9,5},{13... | collective-permute-start | bytes 245768 | tf_op jit(solution)/shard_map/ppermute | solution.py:229
  19.9 3.6 %collective-permute-start.2 = (f32[2,8,1280]{2,1,0:T(8,128)S(1)}, f32[2,8,1280]{2,1,0:T(8,128)S(1)}, u32[]{:S(2)}, u32[]{:S(2)}) collective-permute-start(f32[2,8,1280]{2,1,0:T(8,128)S(1)} %get-tuple-element.5), channel_id=1, source_target_pairs={{0,4},{4,8},{8,12},{12,16},{16,20},{20,24},{24,28},{1,5},{5,9},{9,... | collective-permute-start | bytes 245768 | tf_op jit(solution)/shard_map/ppermute | solution.py:229
  23.5 0.0 collective-permute-done.3.bottom_ref
  23.5 0.9 %collective-permute-done.2.top_ref = f32[2,8,1280]{2,1,0:T(8,128)S(1)} collective-permute-done((f32[2,8,1280]{2,1,0:T(8,128)S(1)}, f32[2,8,1280]{2,1,0:T(8,128)S(1)}, u32[]{:S(2)}, u32[]{:S(2)}) %collective-permute-start.2) | collective-permute-done | bytes 81952 | tf_op jit(solution)/shard_map/ppermute | solution.py:229
  24.4 1.1 %moments.1 = f32[8,128]{1,0:T(8,128)S(1)} custom-call(f32[128,1024]{1,0:T(8,128)S(1)} %copy-done, f32[128,1024]{1,0:T(8,128)S(1)} %subtract_multiply_fusion.w_ref, f32[2,8,1280]{2,1,0:T(8,128)S(1)} %collective-permute-done.2.top_ref, f32[2,8,1280]{2,1,0:T(8,128)S(1)} %collective-permute-done.3.bottom_ref, f32[2,128,128]{2,1,0:T(8,128)S(1)} %collective-permute-done.left_ref, ...), custom_call_target="tpu_custom_call" | custom-call | tf_op jit(solution)/shard_map/moments/pallas_call | solution.py:248
  25.5 24.3 %all_to_all.5.parts_ref = f32[32,8,128]{2,1,0:T(8,128)S(1)} all-to-all(f32[32,8,128]{2,1,0:T(8,128)S(1)} %broadcast_in_dim.2), channel_id=1, replica_groups=mesh['rows'=8,'cols'=4] {'rows','cols'}, dimensions={0} | all-to-all | bytes 262144 | tf_op jit(solution)/shard_map/all_to_all | solution.py:259
  49.8 0.0 collective-permute-done.5.bottom_ref
  49.8 0.0 collective-permute-done.4.top_ref
  49.8 0.0 copy-done.1
  49.8 0.0 copy-done.2
  49.8 3.1 %finish.1 = (f32[128,1024]{1,0:T(8,128)}, f32[128,1024]{1,0:T(8,128)}) custom-call(f32[32,8,128]{2,1,0:T(8,128)S(1)} %all_to_all.5.parts_ref, f32[128,1024]{1,0:T(8,128)S(1)} %copy-done, f32[128,1024]{1,0:T(8,128)S(1)} %subtract_multiply_fusion.w_ref, f32[2,72,1280]{2,1,0:T(8,128)S(1)} %collective-permute-done.4.top_ref, ...), custom_call_target="tpu_custom_call" | custom-call | tf_op jit(solution)/shard_map/finish/pallas_call | solution.py:262
  (3 shorter events, 0.0 us)
Async XLA Ops:
  0.6 1.4 %copy-start = (f32[128,1024]{1,0:T(8,128)S(1)}, f32[128,1024]{1,0:T(8,128)}, u32[]{:S(2)}) copy-start(f32[128,1024]{1,0:T(8,128)} %f_ref.3) | copy-start | bytes 1572868
  2.0 7.7 %collective-permute-start = (f32[2,128,128]{2,1,0:T(8,128)S(1)}, f32[2,128,128]{2,1,0:T(8,128)S(1)}, u32[]{:S(2)}, u32[]{:S(2)}) collective-permute-start(f32[2,128,128]{2,1,0:T(8,128)S(1)} %get-tuple-element.6), channel_id=1, source_target_pairs={{0,1},{1,2},{2,3},{4,5},{5,6},{6,7},{8,9},{9,10},{10,11},{12,13},{... | collective-permute-start | bytes 393224 | tf_op jit(solution)/shard_map/ppermute | solution.py:229
  7.0 6.9 %collective-permute-start.1 = (f32[2,128,128]{2,1,0:T(8,128)S(1)}, f32[2,128,128]{2,1,0:T(8,128)S(1)}, u32[]{:S(2)}, u32[]{:S(2)}) collective-permute-start(f32[2,128,128]{2,1,0:T(8,128)S(1)} %get-tuple-element.7), channel_id=1, source_target_pairs={{1,0},{2,1},{3,2},{5,4},{6,5},{7,6},{9,8},{10,9},{11,10},{13,12},{... | collective-permute-start | bytes 393224 | tf_op jit(solution)/shard_map/ppermute | solution.py:229
  14.0 35.8 %collective-permute-start.5 = (f32[2,72,1280]{2,1,0:T(8,128)S(1)}, f32[2,72,1280]{2,1,0:T(8,128)S(1)}, u32[]{:S(2)}, u32[]{:S(2)}) collective-permute-start(f32[2,72,1280]{2,1,0:T(8,128)S(1)} %get-tuple-element.2), channel_id=1, source_target_pairs={{4,0},{8,4},{12,8},{16,12},{20,16},{24,20},{28,24},{5,1},{9,5},{13... | collective-permute-start | bytes 2211848 | tf_op jit(solution)/shard_map/ppermute | solution.py:229
  15.3 34.5 %copy-start.1 = (bf16[4,256,256]{2,1,0:T(8,128)(2,1)S(1)}, bf16[4,256,256]{2,1,0:T(8,128)(2,1)}, u32[]{:S(2)}) copy-start(bf16[4,256,256]{2,1,0:T(8,128)(2,1)} %constant.6.clone.rowtaps_ref) | copy-start | bytes 1572868
  15.3 34.5 %copy-start.2 = (bf16[3,256,256]{2,1,0:T(8,128)(2,1)S(1)}, bf16[3,256,256]{2,1,0:T(8,128)(2,1)}, u32[]{:S(2)}) copy-start(bf16[3,256,256]{2,1,0:T(8,128)(2,1)} %constant.7.clone.coltaps_ref) | copy-start | bytes 1179652
  15.4 34.5 %collective-permute-start.4 = (f32[2,72,1280]{2,1,0:T(8,128)S(1)}, f32[2,72,1280]{2,1,0:T(8,128)S(1)}, u32[]{:S(2)}, u32[]{:S(2)}) collective-permute-start(f32[2,72,1280]{2,1,0:T(8,128)S(1)} %get-tuple-element.3), channel_id=1, source_target_pairs={{0,4},{4,8},{8,12},{12,16},{16,20},{20,24},{24,28},{1,5},{5,9},{9,... | collective-permute-start | bytes 2211848 | tf_op jit(solution)/shard_map/ppermute | solution.py:229
  18.6 4.9 %collective-permute-start.3 = (f32[2,8,1280]{2,1,0:T(8,128)S(1)}, f32[2,8,1280]{2,1,0:T(8,128)S(1)}, u32[]{:S(2)}, u32[]{:S(2)}) collective-permute-start(f32[2,8,1280]{2,1,0:T(8,128)S(1)} %get-tuple-element.4), channel_id=1, source_target_pairs={{4,0},{8,4},{12,8},{16,12},{20,16},{24,20},{28,24},{5,1},{9,5},{13... | collective-permute-start | bytes 245768 | tf_op jit(solution)/shard_map/ppermute | solution.py:229
  19.9 4.5 %collective-permute-start.2 = (f32[2,8,1280]{2,1,0:T(8,128)S(1)}, f32[2,8,1280]{2,1,0:T(8,128)S(1)}, u32[]{:S(2)}, u32[]{:S(2)}) collective-permute-start(f32[2,8,1280]{2,1,0:T(8,128)S(1)} %get-tuple-element.5), channel_id=1, source_target_pairs={{0,4},{4,8},{8,12},{12,16},{16,20},{20,24},{24,28},{1,5},{5,9},{9,... | collective-permute-start | bytes 245768 | tf_op jit(solution)/shard_map/ppermute | solution.py:229

commit v2 on v1

--- a/solution.py
+++ b/solution.py
@@ -78,68 +78,85 @@
     return pltpu.roll(field, 1, 1) + pltpu.roll(field, width - 1, 1)
 
 
-def moments_kernel(f_ref, w_ref, top_ref, bottom_ref, left_ref, right_ref, out_ref, v0_ref, v1_ref):
+def weights(inverse_variance, source_mask):
+    return inverse_variance * (1.0 - source_mask.astype(jnp.float32))
+
+
+def moments_kernel(f_ref, iv_ref, mask_ref, top_ref, bottom_ref, left_ref, right_ref, out_ref, v0_ref, v1_ref):
     rows, cols = f_ref.shape
     width = cols + 2 * LANES
     first_row, last_row, first_col, last_col = at_edges()
-
-    def pair(start):
-        if start < NEAR:
-            return top_ref[0], top_ref[1]
-        if start >= NEAR + rows:
-            return bottom_ref[0], bottom_ref[1]
-        at = pl.ds(start - NEAR, 8)
-        return tuple(
-            jnp.concatenate([left_ref[i, at, :], ref[at, :], right_ref[i, at, :]], axis=1)
-            for i, ref in enumerate((f_ref, w_ref))
-        )
-
-    for start in range(0, rows + 2 * NEAR, 8):
-        flux, weight = pair(start)
-        v0_ref[pl.ds(start, 8), :] = flux * weight
-
-    zeros = jnp.zeros((8, width), jnp.float32)
-    v1_ref[pl.ds(0, 8), :] = zeros
-    v1_ref[pl.ds(rows + 2 * NEAR - 8, 8), :] = zeros
+    centre = pl.ds(LANES, cols)
+
+    def weight_of(start):
+        at = pl.ds(start, 8)
+        own = weights(iv_ref[at, :], mask_ref[at, :])
+        return jnp.concatenate([left_ref[1, at, :], own, right_ref[1, at, :]], axis=1)
+
+    for at, near_ref in ((pl.ds(0, NEAR), top_ref), (pl.ds(NEAR + rows, NEAR), bottom_ref)):
+        v0_ref[at, :] = jnp.zeros((NEAR, width), jnp.float32)
+        v1_ref[at, :] = jnp.zeros((NEAR, width), jnp.float32)
+        v0_ref[at, centre] = near_ref[...]
+    for start in range(0, rows, 8):
+        at = pl.ds(start, 8)
+        flux = jnp.concatenate([left_ref[0, at, :], f_ref[at, :], right_ref[0, at, :]], axis=1)
+        v0_ref[pl.ds(NEAR + start, 8), :] = flux * weight_of(start)
 
     def image(ref, weight, start, count):
         here = ref[pl.ds(start, count), :]
         beside = ref[pl.ds(start - 1, count), :] + ref[pl.ds(start + 1, count), :] + beside_columns(here)
         return here, weight * here + smooth_weight * (4.0 * here - beside)
 
-    for start in range(NEAR, NEAR + rows, 8):
-        _, weight = pair(start)
-        _, out = image(v0_ref, weight, start, 8)
-        v1_ref[pl.ds(start, 8), :] = out
-
-    @pl.when(jnp.logical_not(first_row))
-    def _():
-        _, out = image(v0_ref, top_ref[1, pl.ds(NEAR - 1, 1), :], NEAR - 1, 1)
-        v1_ref[pl.ds(NEAR - 1, 1), :] = out
-
-    @pl.when(jnp.logical_not(last_row))
-    def _():
-        _, out = image(v0_ref, bottom_ref[1, pl.ds(0, 1), :], NEAR + rows, 1)
-        v1_ref[pl.ds(NEAR + rows, 1), :] = out
-
-    @pl.when(first_col)
-    def _():
-        v1_ref[:, pl.ds(0, LANES)] = jnp.zeros((rows + 2 * NEAR, LANES), jnp.float32)
-
-    @pl.when(last_col)
-    def _():
-        v1_ref[:, pl.ds(width - LANES, LANES)] = jnp.zeros((rows + 2 * NEAR, LANES), jnp.float32)
+    for start in range(0, rows, 8):
+        _, out = image(v0_ref, weight_of(start), NEAR + start, 8)
+        v1_ref[pl.ds(NEAR + start, 8), :] = out
+
+    def edge_row(near_ref, row, at):
+        weight = jnp.concatenate([jnp.zeros((1, LANES), jnp.float32), near_ref[pl.ds(row, 1), :], jnp.zeros((1, LANES), jnp.float32)], axis=1)
+        _, out = image(v0_ref, weight, at, 1)
+        v1_ref[pl.ds(at, 1), :] = out
+
+    pl.when(jnp.logical_not(first_row))(lambda: edge_row(top_ref, 5, NEAR - 1))
+    pl.when(jnp.logical_not(last_row))(lambda: edge_row(bottom_ref, 2, NEAR + rows))
+
+    def clear(start):
+        v1_ref[:, pl.ds(start, LANES)] = jnp.zeros((rows + 2 * NEAR, LANES), jnp.float32)
+
+    pl.when(first_col)(lambda: clear(0))
+    pl.when(last_col)(lambda: clear(width - LANES))
 
     sums = [jnp.zeros((8, cols), jnp.float32) for _ in range(4)]
-    for start in range(NEAR, NEAR + rows, 8):
-        _, weight = pair(start)
-        v1, v2 = image(v1_ref, weight, start, 8)
-        v0, v1, v2 = (x[:, LANES : LANES + cols] for x in (v0_ref[pl.ds(start, 8), :], v1, v2))
+    for start in range(0, rows, 8):
+        v1, v2 = image(v1_ref, weight_of(start), NEAR + start, 8)
+        v0 = v0_ref[pl.ds(NEAR + start, 8), centre]
+        v1, v2 = v1[:, LANES : LANES + cols], v2[:, LANES : LANES + cols]
         sums = [total + term for total, term in zip(sums, (v0 * v0, v0 * v1, v1 * v1, v1 * v2))]
     for i, total in enumerate(sums):
         narrow = sum(total[:, k : k + LANES] for k in range(0, cols, LANES))
         out_ref[pl.ds(i, 1), :] = jnp.sum(narrow, axis=0, keepdims=True)
-    out_ref[pl.ds(4, 4), :] = jnp.zeros((4, LANES), jnp.float32)
+    on_left = lax.broadcasted_iota(jnp.int32, (1, LANES), 1) < LANES // 2
+    corners = ((v1_ref, NEAR), (v1_ref, NEAR + rows - 1), (v0_ref, NEAR), (v0_ref, NEAR + rows - 1))
+    for i, (ref, row) in enumerate(corners):
+        at = pl.ds(row, 1)
+        out_ref[pl.ds(4 + i, 1), :] = jnp.where(on_left, ref[at, pl.ds(LANES, LANES)], ref[at, pl.ds(cols, LANES)])
+
+
+def corner_terms(parts):
+    ncols, nrows = parts.shape[:2]
+    flat = parts.reshape(ncols * nrows, 8, LANES)
+    v1_top, v1_bottom, v0_top, v0_bottom = (flat[:, i, :] for i in range(4, 8))
+    index = lax.broadcasted_iota(jnp.int32, (ncols * nrows, LANES), 0)
+    lane = lax.broadcasted_iota(jnp.int32, (ncols * nrows, LANES), 1)
+    col, row = index // nrows, index % nrows
+    total = jnp.zeros((ncols * nrows, LANES), jnp.float32)
+    for mine, theirs, step_row in ((v1_top, v0_bottom, -1), (v1_bottom, v0_top, 1)):
+        for step_col in (-1, 1):
+            shifted = pltpu.roll(theirs, (-(step_col * nrows + step_row)) % (ncols * nrows), 0)
+            shifted = pltpu.roll(shifted, 1 if step_col < 0 else LANES - 1, 1)
+            there = (row + step_row >= 0) & (row + step_row < nrows) & (col + step_col >= 0) & (col + step_col < ncols)
+            there = there & (lane == (0 if step_col < 0 else LANES - 1))
+            total = total + jnp.where(there, mine * shifted, 0.0)
+    return 8.0 * jnp.sum(jnp.sum(total, axis=0, keepdims=True), axis=1, keepdims=True)
 
 
 def coefficients(m0, m1, m2, m3):
@@ -152,30 +169,31 @@
 
 
 def finish_kernel(
-    parts_ref, f_ref, w_ref, top_ref, bottom_ref, left_ref, right_ref, rowtaps_ref, coltaps_ref,
+    parts_ref, f_ref, iv_ref, mask_ref, top_ref, bottom_ref, left_ref, right_ref, rowtaps_ref, coltaps_ref,
     background_ref, rms_ref, v0_ref, high_ref, low_ref,
 ):
     rows, cols = f_ref.shape
     width = cols + 2 * LANES
     first_row, last_row, first_col, last_col = at_edges()
 
-    totals = jnp.sum(parts_ref[...], axis=0)
-    c0, c1 = coefficients(*(jnp.sum(totals[i : i + 1, :], axis=1, keepdims=True) for i in range(4)))
+    parts = parts_ref[...]
+    totals = jnp.sum(parts.reshape(-1, 8, LANES), axis=0)
+    moments = [jnp.sum(totals[i : i + 1, :], axis=1, keepdims=True) for i in range(4)]
+    moments[3] = moments[3] + corner_terms(parts)
+    c0, c1 = coefficients(*moments)
 
     def pair(start, count):
-        if start < WIDE:
-            at = pl.ds(start, count)
-            return top_ref[0, at, :], top_ref[1, at, :]
-        if start >= WIDE + rows:
-            at = pl.ds(start - WIDE - rows, count)
-            return bottom_ref[0, at, :], bottom_ref[1, at, :]
+        for ref, begin in ((top_ref, WIDE - REACH), (bottom_ref, WIDE + rows)):
+            if begin <= start < begin + REACH:
+                return ref[pl.ds(start - begin, count), :], ref[pl.ds(REACH + start - begin, count), :]
         at = pl.ds(start - WIDE, count)
-        return tuple(
-            jnp.concatenate([left_ref[i, at, :], ref[at, :], right_ref[i, at, :]], axis=1)
-            for i, ref in enumerate((f_ref, w_ref))
-        )
-
-    for start in range(0, rows + 2 * WIDE, 8):
+        flux = jnp.concatenate([left_ref[0, at, :], f_ref[at, :], right_ref[0, at, :]], axis=1)
+        own = weights(iv_ref[at, :], mask_ref[at, :])
+        return flux, jnp.concatenate([left_ref[1, at, :], own, right_ref[1, at, :]], axis=1)
+
+    v0_ref[pl.ds(0, 8), :] = top_ref[pl.ds(2 * REACH, 8), :]
+    v0_ref[pl.ds(rows + 2 * WIDE - 8, 8), :] = bottom_ref[pl.ds(2 * REACH, 8), :]
+    for start in range(8, rows + 2 * WIDE - 8, 8):
         flux, weight = pair(start, 8)
         v0_ref[pl.ds(start, 8), :] = flux * weight
 
@@ -232,37 +250,56 @@
 def shards(coadd_flux, inverse_variance, source_mask):
     rows, cols = coadd_flux.shape
     width = cols + 2 * LANES
-    devices = lax.axis_size("rows") * lax.axis_size("cols")
-    weight = inverse_variance * (1.0 - source_mask.astype(jnp.float32))
-    both = jnp.stack([coadd_flux, weight])
-    left = shift(both[:, :, cols - LANES :], "cols", 1)
-    right = shift(both[:, :, :LANES], "cols", -1)
-    extended = jnp.concatenate([left, both, right], axis=2)
-    near_top = shift(extended[:, rows - NEAR :], "rows", 1)
-    near_bottom = shift(extended[:, :NEAR], "rows", -1)
-    top = shift(extended[:, rows - WIDE :], "rows", 1)
-    bottom = shift(extended[:, :WIDE], "rows", -1)
+    nrows, ncols = lax.axis_size("rows"), lax.axis_size("cols")
+
+    def edge(start, stop, dim):
+        flux, variance, mask = (
+            lax.slice_in_dim(x, start, stop, axis=dim) for x in (coadd_flux, inverse_variance, source_mask)
+        )
+        return flux, weights(variance, mask)
+
+    left = shift(jnp.stack(edge(cols - LANES, cols, 1)), "cols", 1)
+    right = shift(jnp.stack(edge(0, LANES, 1)), "cols", -1)
+    flux, weight = edge(rows - NEAR, rows, 0)
+    near_top = jnp.concatenate([flux[:5], weight[7:], (flux * weight)[6:]])
+    flux, weight = edge(0, NEAR, 0)
+    near_bottom = jnp.concatenate([(flux * weight)[:2], weight[:1], flux[3:]])
+    near_top = shift(near_top, "rows", 1)
+    near_bottom = shift(near_bottom, "rows", -1)
+
+    def wide(start, beyond):
+        flux, weight = (
+            jnp.concatenate([left[i, start : start + WIDE], x, right[i, start : start + WIDE]], axis=1)
+            for i, x in enumerate(edge(start, start + WIDE, 0))
+        )
+        at = slice(WIDE - REACH, WIDE) if beyond == 0 else slice(0, REACH)
+        return jnp.concatenate([flux[at], weight[at], (flux * weight)[beyond : beyond + 8]])
+
+    top = shift(wide(rows - WIDE, 0), "rows", 1)
+    bottom = shift(wide(0, REACH), "rows", -1)
 
     vmem = pl.BlockSpec(memory_space=pltpu.VMEM)
     field = jax.ShapeDtypeStruct((rows, cols), jnp.float32)
+    own = (coadd_flux, inverse_variance, source_mask)
     parts = pl.pallas_call(
         moments_kernel,
         out_shape=jax.ShapeDtypeStruct((8, LANES), jnp.float32),
-        in_specs=[vmem] * 6,
+        in_specs=[vmem] * 7,
         out_specs=vmem,
         scratch_shapes=[pltpu.VMEM((rows + 2 * NEAR, width), jnp.float32)] * 2,
         compiler_params=pltpu.CompilerParams(vmem_limit_bytes=16 << 20),
         name="moments",
-    )(coadd_flux, weight, near_top, near_bottom, left, right)
-
-    parts = jnp.broadcast_to(parts[None], (devices, 8, LANES))
-    parts = lax.all_to_all(parts, ("rows", "cols"), 0, 0, tiled=True)
+    )(*own, near_top, near_bottom, left, right)
+
+    for axis in ("rows", "cols"):
+        parts = jnp.broadcast_to(parts[None], (lax.axis_size(axis),) + parts.shape)
+        parts = lax.all_to_all(parts, axis, 0, 0, tiled=True)
 
     return tuple(
         pl.pallas_call(
             finish_kernel,
             out_shape=(field, field),
-            in_specs=[vmem] * 9,
+            in_specs=[vmem] * 10,
             out_specs=(vmem, vmem),
             scratch_shapes=[
                 pltpu.VMEM((rows + 2 * WIDE, width), jnp.float32),
@@ -272,7 +309,7 @@
             compiler_params=pltpu.CompilerParams(vmem_limit_bytes=32 << 20),
             name="finish",
         )(
-            parts, coadd_flux, weight, top, bottom, left, right,
+            parts, *own, top, bottom, left, right,
             jnp.asarray(row_tables(rows)), jnp.asarray(col_tables()),
         )
     )

time: 53.2 us -> 58.1 us (1.092)
  blocking collectives: 24.3 us -> 28 us
  waiting for transfers between devices: 6.46 us -> 4.35 us
  other arithmetic: 1.45 us -> 3.27 us
  local copies, waits for them, and re-layouts: 0.14 us -> 1.11 us
    all_to_all x1 -> x2, blocking collectives: 24.3 us -> 28 us  [shards(): parts = lax.all_to_all(parts, axis, 0, 0, tiled=True)]
    ppermute x6, waiting for transfers between devices: 6.46 us -> 4.35 us  [shift(): return lax.ppermute(block, axis, pairs)]
    another operation x0 -> x3, other arithmetic: none -> 1.06 us  [the longest x2 1.05 us: shards(): right = shift(jnp.stack(edge(0, LANES, 1)), 'cols', -1)]
    another operation x0 -> x1, local copies, waits for them, and re-layouts: none -> 0.88 us  [shards(): right = shift(jnp.stack(edge(0, LANES, 1)), 'cols', -1)]
    mul x1 -> x6, other arithmetic: 1.33 us -> 1.96 us  [the longest x2 1.92 us: weights(): return inverse_variance * (1.0 - source_mask.astype(jnp.float32))]
  transfers between devices with their start and end apart: 6 -> 6, of which waited for: 3 -> 2; matrix products, arithmetic and copies ran while one was open for 0% -> 4% of each run, Pallas kernels for 2% -> 2%
where the time goes in v2:
time: 58.1 us; the launch traced here: 57.6 us
  blocking collectives  28 us (48%)
  starting transfers between devices  15.6 us (27%)
  waiting for transfers between devices  4.35 us (7%)
  Pallas kernels  4.34 us (7%)
  other arithmetic  3.27 us (6%)
  local copies, waits for them, and re-layouts  1.11 us (2%)
  between operations  0.95 us (2%)
    all_to_all x2, blocking collectives, shards(): parts = lax.all_to_all(parts, axis, 0, 0, tiled=True)  28 us
    ppermute x6, starting transfers between devices, shift(): return lax.ppermute(block, axis, pairs)  15.6 us
    ppermute x6, waiting for transfers between devices, shift(): return lax.ppermute(block, axis, pairs)  4.35 us
    pallas_call x1, Pallas kernels, shards(): pl.pallas_call(finish_kernel, out_shape=(field, field), in_specs=[vmem] *...  3.18 us
    mul x2, other arithmetic, weights(): return inverse_variance * (1.0 - source_mask.astype(jnp.float32))  1.92 us
  transfers between devices with their start and end apart: 6, of which 2 were waited for; matrix products, arithmetic and copies ran while one was open for 4% of the time, Pallas kernels for 2%

profile of v2, /device:TPU:0, one launch (start us, length us, event | category | flops | bytes accessed | tf_op | source)
XLA Modules:
  0.0 57.6 jit_solution(13630406153495889928)
XLA Ops:
  0.6 0.9 %slice_bitcast_fusion = (f32[1,128,128]{2,1,0:T(8,128)S(1)}, f32[1,128,128]{2,1,0:T(8,128)S(1)}) fusion(f32[128,1024]{1,0:T(8,128)} %f_ref.3), kind=kLoop, calls=%fused_computation.11 | loop fusion | bytes 262144 | tf_op jit(solution)/shard_map/stack | solution.py:262
  1.5 0.0 copy-start
  1.5 0.0 copy-start.1
  1.5 1.0 %multiply_bitcast_fusion = (f32[1,128,128]{2,1,0:T(8,128)S(1)}, f32[1,128,128]{2,1,0:T(8,128)S(1)}) fusion(s32[128,1024]{1,0:T(8,128)} %mask_ref.3, f32[128,1024]{1,0:T(8,128)} %iv_ref.3), kind=kLoop, calls=%fused_computation.10 | loop fusion | flops 98304 | bytes 393216 | tf_op jit(solution)/shard_map/stack | solution.py:262
  2.6 4.9 %collective-permute-start.2 = (f32[2,128,128]{2,1,0:T(8,128)S(1)}, f32[2,128,128]{2,1,0:T(8,128)S(1)}, u32[]{:S(2)}, u32[]{:S(2)}) collective-permute-start(f32[2,128,128]{2,1,0:T(8,128)S(1)} %pad_maximum_fusion.6), channel_id=1, source_target_pairs={{0,1},{1,2},{2,3},{4,5},{5,6},{6,7},{8,9},{9,10},{10,11},{12,13},{... | collective-permute-start | bytes 393224 | tf_op jit(solution)/shard_map/ppermute | solution.py:247
  7.6 1.3 %collective-permute-start.3 = (f32[2,128,128]{2,1,0:T(8,128)S(1)}, f32[2,128,128]{2,1,0:T(8,128)S(1)}, u32[]{:S(2)}, u32[]{:S(2)}) collective-permute-start(f32[2,128,128]{2,1,0:T(8,128)S(1)} %pad_maximum_fusion.7), channel_id=1, source_target_pairs={{1,0},{2,1},{3,2},{5,4},{6,5},{7,6},{9,8},{10,9},{11,10},{13,12},{... | collective-permute-start | bytes 393224 | tf_op jit(solution)/shard_map/ppermute | solution.py:247
  8.9 0.0 copy-done
  8.9 0.0 copy-done.1
  8.9 0.8 %subtract_multiply_fusion.2 = (f32[8,1024]{1,0:T(8,128)S(1)}, f32[8,1024]{1,0:T(8,128)S(1)}, f32[8,1024]{1,0:T(8,128)S(1)}, f32[8,1024]{1,0:T(8,128)S(1)}) fusion(s32[128,1024]{1,0:T(8,128)} %mask_ref.3, f32[128,1024]{1,0:T(8,128)S(1)} %copy-done.1, f32[128,1024]{1,0:T(8,128)S(1)} %copy-done), kind=kLoop, calls=%fused_computation.26 | loop fusion | flops 49152 | bytes 327680 | tf_op jit(solution)/shard_map/mul | solution.py:82
  9.7 1.1 %subtract_multiply_fusion = (f32[72,1024]{1,0:T(8,128)S(1)}, f32[72,1024]{1,0:T(8,128)S(1)}) fusion(s32[128,1024]{1,0:T(8,128)} %mask_ref.3, f32[128,1024]{1,0:T(8,128)S(1)} %copy-done.1), kind=kLoop, calls=%fused_computation.6 | loop fusion | flops 442368 | bytes 1769472 | tf_op jit(solution)/shard_map/mul | solution.py:82
  10.9 3.5 %collective-permute-done.3.right_ref = f32[2,128,128]{2,1,0:T(8,128)S(1)} collective-permute-done((f32[2,128,128]{2,1,0:T(8,128)S(1)}, f32[2,128,128]{2,1,0:T(8,128)S(1)}, u32[]{:S(2)}, u32[]{:S(2)}) %collective-permute-start.3) | collective-permute-done | bytes 131104 | tf_op jit(solution)/shard_map/ppermute | solution.py:247
  14.4 0.0 collective-permute-done.2.left_ref
  14.5 0.1 pad_maximum_fusion.4
  14.6 0.1 pad_maximum_fusion.2
  14.8 0.1 pad_maximum_fusion
  14.8 0.0 copy-start.2
  14.8 1.5 %collective-permute-start.4 = (f32[136,1280]{1,0:T(8,128)S(1)}, f32[136,1280]{1,0:T(8,128)S(1)}, u32[]{:S(2)}, u32[]{:S(2)}) collective-permute-start(f32[136,1280]{1,0:T(8,128)S(1)} %pad_maximum_fusion), channel_id=1, source_target_pairs={{0,4},{4,8},{8,12},{12,16},{16,20},{20,24},{24,28},{1,5},{5,9},{9,... | collective-permute-start | bytes 2088968 | tf_op jit(solution)/shard_map/ppermute | solution.py:247
  16.3 1.3 %collective-permute-start.5 = (f32[136,1280]{1,0:T(8,128)S(1)}, f32[136,1280]{1,0:T(8,128)S(1)}, u32[]{:S(2)}, u32[]{:S(2)}) collective-permute-start(f32[136,1280]{1,0:T(8,128)S(1)} %pad_maximum_fusion.1), channel_id=1, source_target_pairs={{4,0},{8,4},{12,8},{16,12},{20,16},{24,20},{28,24},{5,1},{9,5},{13... | collective-permute-start | bytes 2088968 | tf_op jit(solution)/shard_map/ppermute | solution.py:247
  17.7 1.3 %collective-permute-start.1 = (f32[8,1024]{1,0:T(8,128)S(1)}, f32[8,1024]{1,0:T(8,128)S(1)}, u32[]{:S(2)}, u32[]{:S(2)}) collective-permute-start(f32[8,1024]{1,0:T(8,128)S(1)} %pad_maximum_fusion.9), channel_id=1, source_target_pairs={{4,0},{8,4},{12,8},{16,12},{20,16},{24,20},{28,24},{5,1},{9,5},{13... | collective-permute-start | bytes 98312 | tf_op jit(solution)/shard_map/ppermute | solution.py:247
  19.0 5.3 %collective-permute-start = (f32[8,1024]{1,0:T(8,128)S(1)}, f32[8,1024]{1,0:T(8,128)S(1)}, u32[]{:S(2)}, u32[]{:S(2)}) collective-permute-start(f32[8,1024]{1,0:T(8,128)S(1)} %pad_maximum_fusion.8), channel_id=1, source_target_pairs={{0,4},{4,8},{8,12},{12,16},{16,20},{20,24},{24,28},{1,5},{5,9},{9,... | collective-permute-start | bytes 98312 | tf_op jit(solution)/shard_map/ppermute | solution.py:247
  24.4 0.0 collective-permute-done.1.bottom_ref
  24.4 0.8 %collective-permute-done.top_ref = f32[8,1024]{1,0:T(8,128)S(1)} collective-permute-done((f32[8,1024]{1,0:T(8,128)S(1)}, f32[8,1024]{1,0:T(8,128)S(1)}, u32[]{:S(2)}, u32[]{:S(2)}) %collective-permute-start) | collective-permute-done | bytes 32800 | tf_op jit(solution)/shard_map/ppermute | solution.py:247
  25.2 0.0 copy-done.2
  25.2 0.0 copy-start.4
  25.2 1.2 %moments.1 = f32[8,128]{1,0:T(8,128)S(1)} custom-call(f32[128,1024]{1,0:T(8,128)S(1)} %copy-done, f32[128,1024]{1,0:T(8,128)S(1)} %copy-done.1, s32[128,1024]{1,0:T(8,128)S(1)} %copy-done.2, f32[8,1024]{1,0:T(8,128)S(1)} %collective-permute-done.top_ref, f32[8,1024]{1,0:T(8,128)S(1)} %collective-permute-done.1.bottom_ref, ...), custom_call_target="tpu_custom_call" | custom-call | tf_op jit(solution)/shard_map/moments/pallas_call | solution.py:284
  26.4 0.0 copy-start.3
  26.4 18.3 %all_to_all.10 = f32[8,8,128]{2,1,0:T(8,128)S(1)} all-to-all(f32[8,8,128]{2,1,0:T(8,128)S(1)} %broadcast_in_dim.4), channel_id=1, replica_groups=mesh['rows'=8,'cols'=4] {'rows'}, dimensions={0} | all-to-all | bytes 65536 | tf_op jit(solution)/shard_map/all_to_all | solution.py:296
  44.7 9.7 %all_to_all.11.parts_ref = f32[4,8,8,128]{3,2,1,0:T(8,128)S(1)} all-to-all(f32[4,8,8,128]{3,2,1,0:T(8,128)S(1)} %broadcast_in_dim.5), channel_id=1, replica_groups=mesh['rows'=8,'cols'=4] {'cols'}, dimensions={0} | all-to-all | bytes 262144 | tf_op jit(solution)/shard_map/all_to_all | solution.py:296
  54.4 0.0 collective-permute-done.4.top_ref
  54.4 0.0 collective-permute-done.5.bottom_ref
  54.4 0.0 copy-done.4
  54.4 0.0 copy-done.3
  54.4 3.2 %finish.1 = (f32[128,1024]{1,0:T(8,128)}, f32[128,1024]{1,0:T(8,128)}) custom-call(f32[4,8,8,128]{3,2,1,0:T(8,128)S(1)} %all_to_all.11.parts_ref, f32[128,1024]{1,0:T(8,128)S(1)} %copy-done, f32[128,1024]{1,0:T(8,128)S(1)} %copy-done.1, s32[128,1024]{1,0:T(8,128)S(1)} %copy-done.2, f32[136,1280]{1,0:T(8,128)S(1)} %collective-permute-done.4.top_ref, ...), custom_call_target="tpu_custom_call" | custom-call | tf_op jit(solution)/shard_map/finish/pallas_call | solution.py:299
  (21 shorter events, 0.3 us)
Async XLA Ops:
  1.5 7.4 %copy-start = (f32[128,1024]{1,0:T(8,128)S(1)}, f32[128,1024]{1,0:T(8,128)}, u32[]{:S(2)}) copy-start(f32[128,1024]{1,0:T(8,128)} %f_ref.3) | copy-start | bytes 1572868
  1.5 7.4 %copy-start.1 = (f32[128,1024]{1,0:T(8,128)S(1)}, f32[128,1024]{1,0:T(8,128)}, u32[]{:S(2)}) copy-start(f32[128,1024]{1,0:T(8,128)} %iv_ref.3) | copy-start | bytes 1572868
  2.6 11.8 %collective-permute-start.2 = (f32[2,128,128]{2,1,0:T(8,128)S(1)}, f32[2,128,128]{2,1,0:T(8,128)S(1)}, u32[]{:S(2)}, u32[]{:S(2)}) collective-permute-start(f32[2,128,128]{2,1,0:T(8,128)S(1)} %pad_maximum_fusion.6), channel_id=1, source_target_pairs={{0,1},{1,2},{2,3},{4,5},{5,6},{6,7},{8,9},{9,10},{10,11},{12,13},{... | collective-permute-start | bytes 393224 | tf_op jit(solution)/shard_map/ppermute | solution.py:247
  7.6 6.9 %collective-permute-start.3 = (f32[2,128,128]{2,1,0:T(8,128)S(1)}, f32[2,128,128]{2,1,0:T(8,128)S(1)}, u32[]{:S(2)}, u32[]{:S(2)}) collective-permute-start(f32[2,128,128]{2,1,0:T(8,128)S(1)} %pad_maximum_fusion.7), channel_id=1, source_target_pairs={{1,0},{2,1},{3,2},{5,4},{6,5},{7,6},{9,8},{10,9},{11,10},{13,12},{... | collective-permute-start | bytes 393224 | tf_op jit(solution)/shard_map/ppermute | solution.py:247
  14.8 10.4 %copy-start.2 = (s32[128,1024]{1,0:T(8,128)S(1)}, s32[128,1024]{1,0:T(8,128)}, u32[]{:S(2)}) copy-start(s32[128,1024]{1,0:T(8,128)} %mask_ref.3) | copy-start | bytes 1572868
  14.8 39.6 %collective-permute-start.4 = (f32[136,1280]{1,0:T(8,128)S(1)}, f32[136,1280]{1,0:T(8,128)S(1)}, u32[]{:S(2)}, u32[]{:S(2)}) collective-permute-start(f32[136,1280]{1,0:T(8,128)S(1)} %pad_maximum_fusion), channel_id=1, source_target_pairs={{0,4},{4,8},{8,12},{12,16},{16,20},{20,24},{24,28},{1,5},{5,9},{9,... | collective-permute-start | bytes 2088968 | tf_op jit(solution)/shard_map/ppermute | solution.py:247
  16.3 38.1 %collective-permute-start.5 = (f32[136,1280]{1,0:T(8,128)S(1)}, f32[136,1280]{1,0:T(8,128)S(1)}, u32[]{:S(2)}, u32[]{:S(2)}) collective-permute-start(f32[136,1280]{1,0:T(8,128)S(1)} %pad_maximum_fusion.1), channel_id=1, source_target_pairs={{4,0},{8,4},{12,8},{16,12},{20,16},{24,20},{28,24},{5,1},{9,5},{13... | collective-permute-start | bytes 2088968 | tf_op jit(solution)/shard_map/ppermute | solution.py:247
  17.7 6.7 %collective-permute-start.1 = (f32[8,1024]{1,0:T(8,128)S(1)}, f32[8,1024]{1,0:T(8,128)S(1)}, u32[]{:S(2)}, u32[]{:S(2)}) collective-permute-start(f32[8,1024]{1,0:T(8,128)S(1)} %pad_maximum_fusion.9), channel_id=1, source_target_pairs={{4,0},{8,4},{12,8},{16,12},{20,16},{24,20},{28,24},{5,1},{9,5},{13... | collective-permute-start | bytes 98312 | tf_op jit(solution)/shard_map/ppermute | solution.py:247
  19.0 6.2 %collective-permute-start = (f32[8,1024]{1,0:T(8,128)S(1)}, f32[8,1024]{1,0:T(8,128)S(1)}, u32[]{:S(2)}, u32[]{:S(2)}) collective-permute-start(f32[8,1024]{1,0:T(8,128)S(1)} %pad_maximum_fusion.8), channel_id=1, source_target_pairs={{0,4},{4,8},{8,12},{12,16},{16,20},{20,24},{24,28},{1,5},{5,9},{9,... | collective-permute-start | bytes 98312 | tf_op jit(solution)/shard_map/ppermute | solution.py:247
  25.2 29.2 %copy-start.4 = (bf16[3,256,256]{2,1,0:T(8,128)(2,1)S(1)}, bf16[3,256,256]{2,1,0:T(8,128)(2,1)}, u32[]{:S(2)}) copy-start(bf16[3,256,256]{2,1,0:T(8,128)(2,1)} %constant.2.clone.coltaps_ref) | copy-start | bytes 1179652
  26.4 28.0 %copy-start.3 = (bf16[4,256,256]{2,1,0:T(8,128)(2,1)S(1)}, bf16[4,256,256]{2,1,0:T(8,128)(2,1)}, u32[]{:S(2)}) copy-start(bf16[4,256,256]{2,1,0:T(8,128)(2,1)} %constant.4.clone.rowtaps_ref) | copy-start | bytes 1572868

commit v3 on v2

--- a/solution.py
+++ b/solution.py
@@ -82,81 +82,90 @@
     return inverse_variance * (1.0 - source_mask.astype(jnp.float32))
 
 
-def moments_kernel(f_ref, iv_ref, mask_ref, top_ref, bottom_ref, left_ref, right_ref, out_ref, v0_ref, v1_ref):
+def extended(f_ref, iv_ref, mask_ref, left_ref, right_ref, at):
+    flux = jnp.concatenate([left_ref[0, at, :], f_ref[at, :], right_ref[0, at, :]], axis=1)
+    weight = weights(iv_ref[at, :], mask_ref[at, :])
+    return flux, jnp.concatenate([left_ref[1, at, :], weight, right_ref[1, at, :]], axis=1)
+
+
+def wide_kernel(f_ref, iv_ref, mask_ref, left_ref, right_ref, down_ref, up_ref):
+    rows = f_ref.shape[0]
+
+    def pair(start, count):
+        at = pl.ds(start, count)
+        return extended(f_ref, iv_ref, mask_ref, left_ref, right_ref, at)
+
+    for out_ref, begin, beyond in ((down_ref, rows - REACH, rows - WIDE), (up_ref, 0, REACH)):
+        for start in range(0, REACH, 8):
+            flux, weight = pair(begin + start, 8)
+            out_ref[pl.ds(start, 8), :] = flux
+            out_ref[pl.ds(REACH + start, 8), :] = weight
+        flux, weight = pair(beyond, 8)
+        out_ref[pl.ds(2 * REACH, 8), :] = flux * weight
+
+
+def moments_kernel(f_ref, iv_ref, mask_ref, top_ref, left_ref, out_ref, v0_ref, v1_ref):
     rows, cols = f_ref.shape
-    width = cols + 2 * LANES
+    width = LANES + cols
     first_row, last_row, first_col, last_col = at_edges()
-    centre = pl.ds(LANES, cols)
+    base = 2 * NEAR
+    lane = lax.broadcasted_iota(jnp.int32, (8, LANES), 1)
+    row = lax.broadcasted_iota(jnp.int32, (8, width), 0)
+    beside_image = lane >= jnp.where(first_col, LANES, LANES - 3)
 
     def weight_of(start):
         at = pl.ds(start, 8)
-        own = weights(iv_ref[at, :], mask_ref[at, :])
-        return jnp.concatenate([left_ref[1, at, :], own, right_ref[1, at, :]], axis=1)
-
-    for at, near_ref in ((pl.ds(0, NEAR), top_ref), (pl.ds(NEAR + rows, NEAR), bottom_ref)):
-        v0_ref[at, :] = jnp.zeros((NEAR, width), jnp.float32)
-        v1_ref[at, :] = jnp.zeros((NEAR, width), jnp.float32)
-        v0_ref[at, centre] = near_ref[...]
+        return jnp.concatenate([left_ref[1, at, :], weights(iv_ref[at, :], mask_ref[at, :])], axis=1)
+
+    def image(ref, weight, start):
+        here = ref[pl.ds(start, 8), :]
+        beside = ref[pl.ds(start - 1, 8), :] + ref[pl.ds(start + 1, 8), :] + beside_columns(here)
+        return here, weight * here + smooth_weight * (4.0 * here - beside)
+
+    def clean(field, keep):
+        return jnp.concatenate([jnp.where(keep, field[:, :LANES], 0.0), field[:, LANES:]], axis=1)
+
+    for ref in (v0_ref, v1_ref):
+        for start in (0, NEAR, base + rows):
+            ref[pl.ds(start, 8), :] = jnp.zeros((8, width), jnp.float32)
+    top = top_ref[...]
+    v0_ref[pl.ds(NEAR, 8), :] = clean(jnp.where(row >= 4, top, 0.0), lane >= LANES - 4)
+    top_weight = pltpu.roll(top, 4, 0)
     for start in range(0, rows, 8):
         at = pl.ds(start, 8)
-        flux = jnp.concatenate([left_ref[0, at, :], f_ref[at, :], right_ref[0, at, :]], axis=1)
-        v0_ref[pl.ds(NEAR + start, 8), :] = flux * weight_of(start)
-
-    def image(ref, weight, start, count):
-        here = ref[pl.ds(start, count), :]
-        beside = ref[pl.ds(start - 1, count), :] + ref[pl.ds(start + 1, count), :] + beside_columns(here)
-        return here, weight * here + smooth_weight * (4.0 * here - beside)
-
+        flux = jnp.concatenate([left_ref[0, at, :], f_ref[at, :]], axis=1)
+        v0_ref[pl.ds(base + start, 8), :] = clean(flux * weight_of(start), lane >= LANES - 4)
+
+    _, out = image(v0_ref, top_weight, NEAR)
+    out = jnp.where(row >= jnp.where(first_row, 8, 5), out, 0.0)
+    v1_ref[pl.ds(NEAR, 8), :] = clean(out, beside_image)
     for start in range(0, rows, 8):
-        _, out = image(v0_ref, weight_of(start), NEAR + start, 8)
-        v1_ref[pl.ds(NEAR + start, 8), :] = out
-
-    def edge_row(near_ref, row, at):
-        weight = jnp.concatenate([jnp.zeros((1, LANES), jnp.float32), near_ref[pl.ds(row, 1), :], jnp.zeros((1, LANES), jnp.float32)], axis=1)
-        _, out = image(v0_ref, weight, at, 1)
-        v1_ref[pl.ds(at, 1), :] = out
-
-    pl.when(jnp.logical_not(first_row))(lambda: edge_row(top_ref, 5, NEAR - 1))
-    pl.when(jnp.logical_not(last_row))(lambda: edge_row(bottom_ref, 2, NEAR + rows))
-
-    def clear(start):
-        v1_ref[:, pl.ds(start, LANES)] = jnp.zeros((rows + 2 * NEAR, LANES), jnp.float32)
-
-    pl.when(first_col)(lambda: clear(0))
-    pl.when(last_col)(lambda: clear(width - LANES))
-
-    sums = [jnp.zeros((8, cols), jnp.float32) for _ in range(4)]
-    for start in range(0, rows, 8):
-        v1, v2 = image(v1_ref, weight_of(start), NEAR + start, 8)
-        v0 = v0_ref[pl.ds(NEAR + start, 8), centre]
-        v1, v2 = v1[:, LANES : LANES + cols], v2[:, LANES : LANES + cols]
-        sums = [total + term for total, term in zip(sums, (v0 * v0, v0 * v1, v1 * v1, v1 * v2))]
+        _, out = image(v0_ref, weight_of(start), base + start)
+        v1_ref[pl.ds(base + start, 8), :] = clean(out, beside_image)
+
+    def terms(start, weight, keep=None):
+        v1, v2 = image(v1_ref, weight, start)
+        v0 = v0_ref[pl.ds(start, 8), :]
+        if keep is not None:
+            v0, v1 = jnp.where(keep, v0, 0.0), jnp.where(keep, v1, 0.0)
+        return v0 * v0, v0 * v1, v1 * v1, v1 * v2
+
+    sums = terms(NEAR, top_weight, row >= 6)
+    for start in range(0, rows - 8, 8):
+        sums = [total + term for total, term in zip(sums, terms(base + start, weight_of(start)))]
+    keep = row < jnp.where(last_row, 8, 6)
+    sums = [total + term for total, term in zip(sums, terms(base + rows - 8, weight_of(rows - 8), keep))]
+
+    out_lane = lax.broadcasted_iota(jnp.int32, (1, LANES), 1)
+    result = jnp.zeros((1, LANES), jnp.float32)
     for i, total in enumerate(sums):
-        narrow = sum(total[:, k : k + LANES] for k in range(0, cols, LANES))
-        out_ref[pl.ds(i, 1), :] = jnp.sum(narrow, axis=0, keepdims=True)
-    on_left = lax.broadcasted_iota(jnp.int32, (1, LANES), 1) < LANES // 2
-    corners = ((v1_ref, NEAR), (v1_ref, NEAR + rows - 1), (v0_ref, NEAR), (v0_ref, NEAR + rows - 1))
-    for i, (ref, row) in enumerate(corners):
-        at = pl.ds(row, 1)
-        out_ref[pl.ds(4 + i, 1), :] = jnp.where(on_left, ref[at, pl.ds(LANES, LANES)], ref[at, pl.ds(cols, LANES)])
-
-
-def corner_terms(parts):
-    ncols, nrows = parts.shape[:2]
-    flat = parts.reshape(ncols * nrows, 8, LANES)
-    v1_top, v1_bottom, v0_top, v0_bottom = (flat[:, i, :] for i in range(4, 8))
-    index = lax.broadcasted_iota(jnp.int32, (ncols * nrows, LANES), 0)
-    lane = lax.broadcasted_iota(jnp.int32, (ncols * nrows, LANES), 1)
-    col, row = index // nrows, index % nrows
-    total = jnp.zeros((ncols * nrows, LANES), jnp.float32)
-    for mine, theirs, step_row in ((v1_top, v0_bottom, -1), (v1_bottom, v0_top, 1)):
-        for step_col in (-1, 1):
-            shifted = pltpu.roll(theirs, (-(step_col * nrows + step_row)) % (ncols * nrows), 0)
-            shifted = pltpu.roll(shifted, 1 if step_col < 0 else LANES - 1, 1)
-            there = (row + step_row >= 0) & (row + step_row < nrows) & (col + step_col >= 0) & (col + step_col < ncols)
-            there = there & (lane == (0 if step_col < 0 else LANES - 1))
-            total = total + jnp.where(there, mine * shifted, 0.0)
-    return 8.0 * jnp.sum(jnp.sum(total, axis=0, keepdims=True), axis=1, keepdims=True)
+        narrow = jnp.where(lane >= LANES - 2, total[:, :LANES], 0.0)
+        for k in range(LANES, width - LANES, LANES):
+            narrow = narrow + total[:, k : k + LANES]
+        ends = jnp.where(lane < jnp.where(last_col, LANES, LANES - 2), total[:, width - LANES :], 0.0)
+        total = jnp.sum(jnp.sum(narrow + ends, axis=0, keepdims=True), axis=1, keepdims=True)
+        result = jnp.where(out_lane == i, total, result)
+    out_ref[...] = result
 
 
 def coefficients(m0, m1, m2, m3):
@@ -176,20 +185,16 @@
     width = cols + 2 * LANES
     first_row, last_row, first_col, last_col = at_edges()
 
-    parts = parts_ref[...]
-    totals = jnp.sum(parts.reshape(-1, 8, LANES), axis=0)
-    moments = [jnp.sum(totals[i : i + 1, :], axis=1, keepdims=True) for i in range(4)]
-    moments[3] = moments[3] + corner_terms(parts)
+    totals = jnp.sum(parts_ref[...].reshape(-1, LANES), axis=0, keepdims=True)
+    lane = lax.broadcasted_iota(jnp.int32, (1, LANES), 1)
+    moments = [jnp.sum(jnp.where(lane == i, totals, 0.0), axis=1, keepdims=True) for i in range(4)]
     c0, c1 = coefficients(*moments)
 
     def pair(start, count):
         for ref, begin in ((top_ref, WIDE - REACH), (bottom_ref, WIDE + rows)):
             if begin <= start < begin + REACH:
                 return ref[pl.ds(start - begin, count), :], ref[pl.ds(REACH + start - begin, count), :]
-        at = pl.ds(start - WIDE, count)
-        flux = jnp.concatenate([left_ref[0, at, :], f_ref[at, :], right_ref[0, at, :]], axis=1)
-        own = weights(iv_ref[at, :], mask_ref[at, :])
-        return flux, jnp.concatenate([left_ref[1, at, :], own, right_ref[1, at, :]], axis=1)
+        return extended(f_ref, iv_ref, mask_ref, left_ref, right_ref, pl.ds(start - WIDE, count))
 
     v0_ref[pl.ds(0, 8), :] = top_ref[pl.ds(2 * REACH, 8), :]
     v0_ref[pl.ds(rows + 2 * WIDE - 8, 8), :] = bottom_ref[pl.ds(2 * REACH, 8), :]
@@ -250,7 +255,7 @@
 def shards(coadd_flux, inverse_variance, source_mask):
     rows, cols = coadd_flux.shape
     width = cols + 2 * LANES
-    nrows, ncols = lax.axis_size("rows"), lax.axis_size("cols")
+    devices = lax.axis_size("rows") * lax.axis_size("cols")
 
     def edge(start, stop, dim):
         flux, variance, mask = (
@@ -260,40 +265,36 @@
 
     left = shift(jnp.stack(edge(cols - LANES, cols, 1)), "cols", 1)
     right = shift(jnp.stack(edge(0, LANES, 1)), "cols", -1)
-    flux, weight = edge(rows - NEAR, rows, 0)
-    near_top = jnp.concatenate([flux[:5], weight[7:], (flux * weight)[6:]])
-    flux, weight = edge(0, NEAR, 0)
-    near_bottom = jnp.concatenate([(flux * weight)[:2], weight[:1], flux[3:]])
-    near_top = shift(near_top, "rows", 1)
-    near_bottom = shift(near_bottom, "rows", -1)
-
-    def wide(start, beyond):
-        flux, weight = (
-            jnp.concatenate([left[i, start : start + WIDE], x, right[i, start : start + WIDE]], axis=1)
-            for i, x in enumerate(edge(start, start + WIDE, 0))
-        )
-        at = slice(WIDE - REACH, WIDE) if beyond == 0 else slice(0, REACH)
-        return jnp.concatenate([flux[at], weight[at], (flux * weight)[beyond : beyond + 8]])
-
-    top = shift(wide(rows - WIDE, 0), "rows", 1)
-    bottom = shift(wide(0, REACH), "rows", -1)
+    flux, weight = (
+        jnp.concatenate([left[i, rows - NEAR :], x], axis=1) for i, x in enumerate(edge(rows - NEAR, rows, 0))
+    )
+    near = shift(jnp.concatenate([weight[4:], (flux * weight)[4:]]), "rows", 1)
 
     vmem = pl.BlockSpec(memory_space=pltpu.VMEM)
     field = jax.ShapeDtypeStruct((rows, cols), jnp.float32)
     own = (coadd_flux, inverse_variance, source_mask)
+    (left_after, right_after), near = lax.optimization_barrier(((left, right), near))
+    down, up = pl.pallas_call(
+        wide_kernel,
+        out_shape=(jax.ShapeDtypeStruct((2 * REACH + 8, width), jnp.float32),) * 2,
+        in_specs=[vmem] * 5,
+        out_specs=(vmem, vmem),
+        compiler_params=pltpu.CompilerParams(vmem_limit_bytes=16 << 20),
+        name="wide",
+    )(*own, left_after, right_after)
+    top = shift(down, "rows", 1)
+    bottom = shift(up, "rows", -1)
     parts = pl.pallas_call(
         moments_kernel,
-        out_shape=jax.ShapeDtypeStruct((8, LANES), jnp.float32),
-        in_specs=[vmem] * 7,
+        out_shape=jax.ShapeDtypeStruct((1, LANES), jnp.float32),
+        in_specs=[vmem] * 5,
         out_specs=vmem,
-        scratch_shapes=[pltpu.VMEM((rows + 2 * NEAR, width), jnp.float32)] * 2,
+        scratch_shapes=[pltpu.VMEM((rows + 3 * NEAR, LANES + cols), jnp.float32)] * 2,
         compiler_params=pltpu.CompilerParams(vmem_limit_bytes=16 << 20),
         name="moments",
-    )(*own, near_top, near_bottom, left, right)
-
-    for axis in ("rows", "cols"):
-        parts = jnp.broadcast_to(parts[None], (lax.axis_size(axis),) + parts.shape)
-        parts = lax.all_to_all(parts, axis, 0, 0, tiled=True)
+    )(*own, near, left)
+    parts = jnp.broadcast_to(parts[None], (devices, 1, LANES))
+    parts = lax.all_to_all(parts, ("rows", "cols"), 0, 0, tiled=True)
 
     return tuple(
         pl.pallas_call(

time: 58.1 us -> 41.4 us (0.71)
  blocking collectives: 28 us -> 17.9 us
  starting transfers between devices: 15.6 us -> 11.5 us
  other arithmetic: 3.27 us -> 1.91 us
  waiting for transfers between devices: 4.35 us -> 3.43 us
    all_to_all x2 -> x1, blocking collectives: 28 us -> 17.9 us  [shards(): parts = lax.all_to_all(parts, ('rows', 'cols'), 0, 0, tiled=True)]
    ppermute x6 -> x5, starting transfers between devices: 15.6 us -> 11.5 us  [shift(): return lax.ppermute(block, axis, pairs)]
    mul x2 -> x1, other arithmetic: 1.92 us -> 0.77 us  [weights(): return inverse_variance * (1.0 - source_mask.astype(jnp.float32))]
    unnamed x10 -> x12, local copies, waits for them, and re-layouts: 0.03 us -> 1.07 us
    ppermute x6 -> x5, waiting for transfers between devices: 4.35 us -> 3.43 us  [shift(): return lax.ppermute(block, axis, pairs)]
    another operation x1 -> x0, local copies, waits for them, and re-layouts: 0.88 us -> none  [shards(): right = shift(jnp.stack(edge(0, LANES, 1)), 'cols', -1)]
    pallas_call x1 -> x2, Pallas kernels: 1.16 us -> 1.31 us  [the longest x1 1.19 us: shards(): pl.pallas_call(moments_kernel, out_shape=jax.ShapeDtypeStruct((1, LANES),...]
  transfers between devices with their start and end apart: 6 -> 5, of which waited for: 2 -> 2; matrix products, arithmetic and copies ran while one was open for 4% -> 2% of each run, Pallas kernels for 2% -> 3%
where the time goes in v3:
time: 41.4 us; the launch traced here: 41 us
  blocking collectives  17.9 us (43%)
  starting transfers between devices  11.5 us (28%)
  Pallas kernels  4.44 us (11%)
  waiting for transfers between devices  3.43 us (8%)
  other arithmetic  1.91 us (5%)
  local copies, waits for them, and re-layouts  1.09 us (3%)
  between operations  0.78 us (2%)
    all_to_all x1, blocking collectives, shards(): parts = lax.all_to_all(parts, ('rows', 'cols'), 0, 0, tiled=True)  17.9 us
    ppermute x5, starting transfers between devices, shift(): return lax.ppermute(block, axis, pairs)  11.5 us
    ppermute x5, waiting for transfers between devices, shift(): return lax.ppermute(block, axis, pairs)  3.43 us
    pallas_call x1, Pallas kernels, shards(): pl.pallas_call(finish_kernel, out_shape=(field, field), in_specs=[vmem] *...  3.13 us
    pallas_call x1, Pallas kernels, shards(): pl.pallas_call(moments_kernel, out_shape=jax.ShapeDtypeStruct((1, LANES),...  1.19 us
    another operation x2, other arithmetic, shards(): right = shift(jnp.stack(edge(0, LANES, 1)), 'cols', -1)  1.1 us
    unnamed x12, local copies, waits for them, and re-layouts  1.07 us
  transfers between devices with their start and end apart: 5, of which 2 were waited for; matrix products, arithmetic and copies ran while one was open for 2% of the time, Pallas kernels for 3%

profile of v3, /device:TPU:0, one launch (start us, length us, event | category | flops | bytes accessed | tf_op | source)
XLA Modules:
  0.0 41.0 jit_solution(4593034488495754361)
XLA Ops:
  0.6 0.0 copy-start.1
  0.6 1.1 %multiply_bitcast_fusion = (f32[1,128,128]{2,1,0:T(8,128)S(1)}, f32[1,128,128]{2,1,0:T(8,128)S(1)}, f32[1,128,128]{2,1,0:T(8,128)S(1)}, f32[1,128,128]{2,1,0:T(8,128)S(1)}) fusion(s32[128,1024]{1,0:T(8,128)} %mask_ref.5, f32[128,1024]{1,0:T(8,128)} %iv_ref.5, f32[128,1024]{1,0:T(8,128)} %f_ref.5), kind=kLoop, calls=%fused_computation.2 | loop fusion | flops 98304 | bytes 655360 | tf_op jit(solution)/shard_map/stack | solution.py:267
  1.7 0.0 copy-start
  1.8 5.1 %collective-permute-start = (f32[2,128,128]{2,1,0:T(8,128)S(1)}, f32[2,128,128]{2,1,0:T(8,128)S(1)}, u32[]{:S(2)}, u32[]{:S(2)}) collective-permute-start(f32[2,128,128]{2,1,0:T(8,128)S(1)} %pad_maximum_fusion), channel_id=1, source_target_pairs={{0,1},{1,2},{2,3},{4,5},{5,6},{6,7},{8,9},{9,10},{10,11},{12,13},{... | collective-permute-start | bytes 393224 | tf_op jit(solution)/shard_map/ppermute | solution.py:252
  6.9 1.3 %collective-permute-start.1 = (f32[2,128,128]{2,1,0:T(8,128)S(1)}, f32[2,128,128]{2,1,0:T(8,128)S(1)}, u32[]{:S(2)}, u32[]{:S(2)}) collective-permute-start(f32[2,128,128]{2,1,0:T(8,128)S(1)} %pad_maximum_fusion.1), channel_id=1, source_target_pairs={{1,0},{2,1},{3,2},{5,4},{6,5},{7,6},{9,8},{10,9},{11,10},{13,12},{... | collective-permute-start | bytes 393224 | tf_op jit(solution)/shard_map/ppermute | solution.py:252
  8.2 0.0 copy-done.1
  8.2 0.0 slice-start
  8.2 0.8 %subtract_multiply_fusion = f32[8,1024]{1,0:T(8,128)S(1)} fusion(s32[128,1024]{1,0:T(8,128)} %mask_ref.5, f32[128,1024]{1,0:T(8,128)S(1)} %copy-done.1), kind=kLoop, calls=%fused_computation.9 | loop fusion | flops 24576 | bytes 98304 | tf_op jit(solution)/shard_map/mul | solution.py:82
  8.9 0.6 %collective-permute-done.left_ref = f32[2,128,128]{2,1,0:T(8,128)S(1)} collective-permute-done((f32[2,128,128]{2,1,0:T(8,128)S(1)}, f32[2,128,128]{2,1,0:T(8,128)S(1)}, u32[]{:S(2)}, u32[]{:S(2)}) %collective-permute-start) | collective-permute-done | bytes 131104 | tf_op jit(solution)/shard_map/ppermute | solution.py:252
  9.6 0.0 slice-done
  9.6 1.3 %collective-permute-start.2 = (f32[8,1152]{1,0:T(8,128)S(1)}, f32[8,1152]{1,0:T(8,128)S(1)}, u32[]{:S(2)}, u32[]{:S(2)}) collective-permute-start(f32[8,1152]{1,0:T(8,128)S(1)} %pad_maximum_fusion.2), channel_id=1, source_target_pairs={{0,4},{4,8},{8,12},{12,16},{16,20},{20,24},{24,28},{1,5},{5,9},{9,... | collective-permute-start | bytes 110600 | tf_op jit(solution)/shard_map/ppermute | solution.py:252
  10.9 2.8 %collective-permute-done.1.right_ref = f32[2,128,128]{2,1,0:T(8,128)S(1)} collective-permute-done((f32[2,128,128]{2,1,0:T(8,128)S(1)}, f32[2,128,128]{2,1,0:T(8,128)S(1)}, u32[]{:S(2)}, u32[]{:S(2)}) %collective-permute-start.1) | collective-permute-done | bytes 131104 | tf_op jit(solution)/shard_map/ppermute | solution.py:252
  13.7 0.0 collective-permute-done.2.top_ref
  13.7 0.0 copy-done
  13.7 0.0 copy-start.2
  13.7 1.0 %copy-done.2 = s32[128,1024]{1,0:T(8,128)S(1)} copy-done((s32[128,1024]{1,0:T(8,128)S(1)}, s32[128,1024]{1,0:T(8,128)}, u32[]{:S(2)}) %copy-start.2) | copy-done | bytes 524312
  14.8 0.1 wide.1
  14.9 2.4 %collective-permute-start.3 = (f32[136,1280]{1,0:T(8,128)S(1)}, f32[136,1280]{1,0:T(8,128)S(1)}, u32[]{:S(2)}, u32[]{:S(2)}) collective-permute-start(f32[136,1280]{1,0:T(8,128)S(1)} %get-tuple-element.10), channel_id=1, source_target_pairs={{0,4},{4,8},{8,12},{12,16},{16,20},{20,24},{24,28},{1,5},{5,9},{9,... | collective-permute-start | bytes 2088968 | tf_op jit(solution)/shard_map/ppermute | solution.py:252
  17.3 0.0 copy-start.3
  17.3 0.0 copy-start.4
  17.3 0.0 copy-start.5
  17.3 1.4 %collective-permute-start.4 = (f32[136,1280]{1,0:T(8,128)S(1)}, f32[136,1280]{1,0:T(8,128)S(1)}, u32[]{:S(2)}, u32[]{:S(2)}) collective-permute-start(f32[136,1280]{1,0:T(8,128)S(1)} %get-tuple-element.11), channel_id=1, source_target_pairs={{4,0},{8,4},{12,8},{16,12},{20,16},{24,20},{28,24},{5,1},{9,5},{13... | collective-permute-start | bytes 2088968 | tf_op jit(solution)/shard_map/ppermute | solution.py:252
  18.8 1.2 %moments.1 = f32[1,128]{1,0:T(1,128)S(1)} custom-call(f32[128,1024]{1,0:T(8,128)S(1)} %copy-done, f32[128,1024]{1,0:T(8,128)S(1)} %copy-done.1, s32[128,1024]{1,0:T(8,128)S(1)} %copy-done.2, f32[8,1152]{1,0:T(8,128)S(1)} %collective-permute-done.2.top_ref, f32[2,128,128]{2,1,0:T(8,128)S(1)} %collective-permute-done.left_ref), custom_call_target="tpu_custom_call" | custom-call | tf_op jit(solution)/shard_map/moments/pallas_call | solution.py:287
  20.0 17.9 %all_to_all.5.parts_ref = f32[32,1,128]{2,1,0:T(1,128)S(1)} all-to-all(f32[32,1,128]{2,1,0:T(1,128)S(1)} %broadcast_in_dim.9), channel_id=1, replica_groups=mesh['rows'=8,'cols'=4] {'rows','cols'}, dimensions={0} | all-to-all | bytes 32768 | tf_op jit(solution)/shard_map/all_to_all | solution.py:297
  37.8 0.0 collective-permute-done.3.top_ref
  37.8 0.0 collective-permute-done.4.bottom_ref
  37.8 0.0 copy-done.3
  37.9 0.0 copy-done.4
  37.9 0.0 copy-done.5
  37.9 3.1 %finish.1 = (f32[128,1024]{1,0:T(8,128)}, f32[128,1024]{1,0:T(8,128)}) custom-call(f32[32,1,128]{2,1,0:T(1,128)S(1)} %all_to_all.5.parts_ref, f32[128,1024]{1,0:T(8,128)S(1)} %copy-done, f32[128,1024]{1,0:T(8,128)S(1)} %copy-done.1, s32[128,1024]{1,0:T(8,128)S(1)} %copy-done.3, f32[136,1280]{1,0:T(8,128)S(1)} %collective-permute-done.3.top_ref, ...), custom_call_target="tpu_custom_call" | custom-call | tf_op jit(solution)/shard_map/finish/pallas_call | solution.py:300
  (6 shorter events, 0.1 us)
Async XLA Ops:
  0.6 7.5 %copy-start.1 = (f32[128,1024]{1,0:T(8,128)S(1)}, f32[128,1024]{1,0:T(8,128)}, u32[]{:S(2)}) copy-start(f32[128,1024]{1,0:T(8,128)} %iv_ref.5) | copy-start | bytes 1572868
  1.7 12.0 %copy-start = (f32[128,1024]{1,0:T(8,128)S(1)}, f32[128,1024]{1,0:T(8,128)}, u32[]{:S(2)}) copy-start(f32[128,1024]{1,0:T(8,128)} %f_ref.5) | copy-start | bytes 1572868
  1.8 7.8 %collective-permute-start = (f32[2,128,128]{2,1,0:T(8,128)S(1)}, f32[2,128,128]{2,1,0:T(8,128)S(1)}, u32[]{:S(2)}, u32[]{:S(2)}) collective-permute-start(f32[2,128,128]{2,1,0:T(8,128)S(1)} %pad_maximum_fusion), channel_id=1, source_target_pairs={{0,1},{1,2},{2,3},{4,5},{5,6},{6,7},{8,9},{9,10},{10,11},{12,13},{... | collective-permute-start | bytes 393224 | tf_op jit(solution)/shard_map/ppermute | solution.py:252
  6.9 6.9 %collective-permute-start.1 = (f32[2,128,128]{2,1,0:T(8,128)S(1)}, f32[2,128,128]{2,1,0:T(8,128)S(1)}, u32[]{:S(2)}, u32[]{:S(2)}) collective-permute-start(f32[2,128,128]{2,1,0:T(8,128)S(1)} %pad_maximum_fusion.1), channel_id=1, source_target_pairs={{1,0},{2,1},{3,2},{5,4},{6,5},{7,6},{9,8},{10,9},{11,10},{13,12},{... | collective-permute-start | bytes 393224 | tf_op jit(solution)/shard_map/ppermute | solution.py:252
  8.2 1.4 %slice-start = ((f32[128,1024]{1,0:T(8,128)}), f32[8,1024]{1,0:T(8,128)S(1)}, s32[]{:S(2)}) async-start(f32[128,1024]{1,0:T(8,128)} %f_ref.5), calls=%async_computation.1 | async-start | bytes 65536 | tf_op jit(solution)/shard_map/slice | solution.py:262
  9.6 4.1 %collective-permute-start.2 = (f32[8,1152]{1,0:T(8,128)S(1)}, f32[8,1152]{1,0:T(8,128)S(1)}, u32[]{:S(2)}, u32[]{:S(2)}) collective-permute-start(f32[8,1152]{1,0:T(8,128)S(1)} %pad_maximum_fusion.2), channel_id=1, source_target_pairs={{0,4},{4,8},{8,12},{12,16},{16,20},{20,24},{24,28},{1,5},{5,9},{9,... | collective-permute-start | bytes 110600 | tf_op jit(solution)/shard_map/ppermute | solution.py:252
  13.7 1.0 %copy-start.2 = (s32[128,1024]{1,0:T(8,128)S(1)}, s32[128,1024]{1,0:T(8,128)}, u32[]{:S(2)}) copy-start(s32[128,1024]{1,0:T(8,128)} %mask_ref.5) | copy-start | bytes 1572868
  14.9 23.0 %collective-permute-start.3 = (f32[136,1280]{1,0:T(8,128)S(1)}, f32[136,1280]{1,0:T(8,128)S(1)}, u32[]{:S(2)}, u32[]{:S(2)}) collective-permute-start(f32[136,1280]{1,0:T(8,128)S(1)} %get-tuple-element.10), channel_id=1, source_target_pairs={{0,4},{4,8},{8,12},{12,16},{16,20},{20,24},{24,28},{1,5},{5,9},{9,... | collective-permute-start | bytes 2088968 | tf_op jit(solution)/shard_map/ppermute | solution.py:252
  17.3 20.6 %copy-start.3 = (s32[128,1024]{1,0:T(8,128)S(1)}, s32[128,1024]{1,0:T(8,128)}, u32[]{:S(2)}) copy-start(s32[128,1024]{1,0:T(8,128)} %mask_ref.5) | copy-start | bytes 1572868
  17.3 20.6 %copy-start.4 = (bf16[4,256,256]{2,1,0:T(8,128)(2,1)S(1)}, bf16[4,256,256]{2,1,0:T(8,128)(2,1)}, u32[]{:S(2)}) copy-start(bf16[4,256,256]{2,1,0:T(8,128)(2,1)} %constant.2.clone.rowtaps_ref) | copy-start | bytes 1572868
  17.3 20.5 %copy-start.5 = (bf16[3,256,256]{2,1,0:T(8,128)(2,1)S(1)}, bf16[3,256,256]{2,1,0:T(8,128)(2,1)}, u32[]{:S(2)}) copy-start(bf16[3,256,256]{2,1,0:T(8,128)(2,1)} %constant.8.clone.coltaps_ref) | copy-start | bytes 1179652
  17.3 20.5 %collective-permute-start.4 = (f32[136,1280]{1,0:T(8,128)S(1)}, f32[136,1280]{1,0:T(8,128)S(1)}, u32[]{:S(2)}, u32[]{:S(2)}) collective-permute-start(f32[136,1280]{1,0:T(8,128)S(1)} %get-tuple-element.11), channel_id=1, source_target_pairs={{4,0},{8,4},{12,8},{16,12},{20,16},{24,20},{28,24},{5,1},{9,5},{13... | collective-permute-start | bytes 2088968 | tf_op jit(solution)/shard_map/ppermute | solution.py:252

commit v4 on v3

--- a/solution.py
+++ b/solution.py
@@ -82,18 +82,18 @@
     return inverse_variance * (1.0 - source_mask.astype(jnp.float32))
 
 
-def extended(f_ref, iv_ref, mask_ref, left_ref, right_ref, at):
+def extended(f_ref, w_ref, left_ref, right_ref, at):
     flux = jnp.concatenate([left_ref[0, at, :], f_ref[at, :], right_ref[0, at, :]], axis=1)
-    weight = weights(iv_ref[at, :], mask_ref[at, :])
+    weight = w_ref[at, :]
     return flux, jnp.concatenate([left_ref[1, at, :], weight, right_ref[1, at, :]], axis=1)
 
 
-def wide_kernel(f_ref, iv_ref, mask_ref, left_ref, right_ref, down_ref, up_ref):
+def wide_kernel(f_ref, w_ref, left_ref, right_ref, down_ref, up_ref):
     rows = f_ref.shape[0]
 
     def pair(start, count):
         at = pl.ds(start, count)
-        return extended(f_ref, iv_ref, mask_ref, left_ref, right_ref, at)
+        return extended(f_ref, w_ref, left_ref, right_ref, at)
 
     for out_ref, begin, beyond in ((down_ref, rows - REACH, rows - WIDE), (up_ref, 0, REACH)):
         for start in range(0, REACH, 8):
@@ -104,7 +104,7 @@
         out_ref[pl.ds(2 * REACH, 8), :] = flux * weight
 
 
-def moments_kernel(f_ref, iv_ref, mask_ref, top_ref, left_ref, out_ref, v0_ref, v1_ref):
+def moments_kernel(f_ref, w_ref, top_ref, left_ref, out_ref, v0_ref, v1_ref):
     rows, cols = f_ref.shape
     width = LANES + cols
     first_row, last_row, first_col, last_col = at_edges()
@@ -115,7 +115,7 @@
 
     def weight_of(start):
         at = pl.ds(start, 8)
-        return jnp.concatenate([left_ref[1, at, :], weights(iv_ref[at, :], mask_ref[at, :])], axis=1)
+        return jnp.concatenate([left_ref[1, at, :], w_ref[at, :]], axis=1)
 
     def image(ref, weight, start):
         here = ref[pl.ds(start, 8), :]
@@ -178,7 +178,7 @@
 
 
 def finish_kernel(
-    parts_ref, f_ref, iv_ref, mask_ref, top_ref, bottom_ref, left_ref, right_ref, rowtaps_ref, coltaps_ref,
+    parts_ref, f_ref, w_ref, top_ref, bottom_ref, left_ref, right_ref, rowtaps_ref, coltaps_ref,
     background_ref, rms_ref, v0_ref, high_ref, low_ref,
 ):
     rows, cols = f_ref.shape
@@ -194,7 +194,7 @@
         for ref, begin in ((top_ref, WIDE - REACH), (bottom_ref, WIDE + rows)):
             if begin <= start < begin + REACH:
                 return ref[pl.ds(start - begin, count), :], ref[pl.ds(REACH + start - begin, count), :]
-        return extended(f_ref, iv_ref, mask_ref, left_ref, right_ref, pl.ds(start - WIDE, count))
+        return extended(f_ref, w_ref, left_ref, right_ref, pl.ds(start - WIDE, count))
 
     v0_ref[pl.ds(0, 8), :] = top_ref[pl.ds(2 * REACH, 8), :]
     v0_ref[pl.ds(rows + 2 * WIDE - 8, 8), :] = bottom_ref[pl.ds(2 * REACH, 8), :]
@@ -255,7 +255,6 @@
 def shards(coadd_flux, inverse_variance, source_mask):
     rows, cols = coadd_flux.shape
     width = cols + 2 * LANES
-    devices = lax.axis_size("rows") * lax.axis_size("cols")
 
     def edge(start, stop, dim):
         flux, variance, mask = (
@@ -272,35 +271,34 @@
 
     vmem = pl.BlockSpec(memory_space=pltpu.VMEM)
     field = jax.ShapeDtypeStruct((rows, cols), jnp.float32)
-    own = (coadd_flux, inverse_variance, source_mask)
-    (left_after, right_after), near = lax.optimization_barrier(((left, right), near))
+    own = (coadd_flux, weights(inverse_variance, source_mask))
+    parts = pl.pallas_call(
+        moments_kernel,
+        out_shape=jax.ShapeDtypeStruct((1, LANES), jnp.float32),
+        in_specs=[vmem] * 4,
+        out_specs=vmem,
+        scratch_shapes=[pltpu.VMEM((rows + 3 * NEAR, LANES + cols), jnp.float32)] * 2,
+        compiler_params=pltpu.CompilerParams(vmem_limit_bytes=16 << 20),
+        name="moments",
+    )(*own, near, left)
+    left_after, right_after, parts = lax.optimization_barrier((left, right, parts))
     down, up = pl.pallas_call(
         wide_kernel,
         out_shape=(jax.ShapeDtypeStruct((2 * REACH + 8, width), jnp.float32),) * 2,
-        in_specs=[vmem] * 5,
+        in_specs=[vmem] * 4,
         out_specs=(vmem, vmem),
         compiler_params=pltpu.CompilerParams(vmem_limit_bytes=16 << 20),
         name="wide",
     )(*own, left_after, right_after)
     top = shift(down, "rows", 1)
     bottom = shift(up, "rows", -1)
-    parts = pl.pallas_call(
-        moments_kernel,
-        out_shape=jax.ShapeDtypeStruct((1, LANES), jnp.float32),
-        in_specs=[vmem] * 5,
-        out_specs=vmem,
-        scratch_shapes=[pltpu.VMEM((rows + 3 * NEAR, LANES + cols), jnp.float32)] * 2,
-        compiler_params=pltpu.CompilerParams(vmem_limit_bytes=16 << 20),
-        name="moments",
-    )(*own, near, left)
-    parts = jnp.broadcast_to(parts[None], (devices, 1, LANES))
-    parts = lax.all_to_all(parts, ("rows", "cols"), 0, 0, tiled=True)
+    parts = lax.all_gather(parts, ("rows", "cols"))
 
     return tuple(
         pl.pallas_call(
             finish_kernel,
             out_shape=(field, field),
-            in_specs=[vmem] * 10,
+            in_specs=[vmem] * 9,
             out_specs=(vmem, vmem),
             scratch_shapes=[
                 pltpu.VMEM((rows + 2 * WIDE, width), jnp.float32),

time: 41.4 us -> 93 us (2.25)
  blocking collectives: 17.9 us -> 70.8 us
  starting transfers between devices: 11.5 us -> 12.8 us
  local copies, waits for them, and re-layouts: 1.09 us -> 0.03 us
    all_gather x0 -> x1, blocking collectives: none -> 70.8 us  [shards(): parts = lax.all_gather(parts, ('rows', 'cols'))]
    all_to_all x1 -> x0, blocking collectives: 17.9 us -> none  [shards(): parts = lax.all_to_all(parts, ('rows', 'cols'), 0, 0, tiled=True)]
    ppermute x5, starting transfers between devices: 11.5 us -> 12.8 us  [shift(): return lax.ppermute(block, axis, pairs)]
    unnamed x12 -> x10, local copies, waits for them, and re-layouts: 1.07 us -> 0.02 us
  transfers between devices with their start and end apart: 5 -> 5, of which waited for: 2 -> 3; matrix products, arithmetic and copies ran while one was open for 2% -> 0% of each run, Pallas kernels for 3% -> 1%
where the time goes in v4:
time: 93 us; the launch traced here: 92.7 us
  blocking collectives  70.8 us (76%)
  starting transfers between devices  12.8 us (14%)
  Pallas kernels  4.28 us (5%)
  waiting for transfers between devices  2.82 us (3%)
  other arithmetic  1.25 us (1%)
    all_gather x1, blocking collectives, shards(): parts = lax.all_gather(parts, ('rows', 'cols'))  70.8 us
    ppermute x5, starting transfers between devices, shift(): return lax.ppermute(block, axis, pairs)  12.8 us
    pallas_call x1, Pallas kernels, shards(): pl.pallas_call(finish_kernel, out_shape=(field, field), in_specs=[vmem] *...  3.07 us
    ppermute x5, waiting for transfers between devices, shift(): return lax.ppermute(block, axis, pairs)  2.82 us
  transfers between devices with their start and end apart: 5, of which 3 were waited for; matrix products, arithmetic and copies ran while one was open for 0% of the time, Pallas kernels for 1%

profile of v4, /device:TPU:0, one launch (start us, length us, event | category | flops | bytes accessed | tf_op | source)
XLA Modules:
  0.0 92.7 jit_solution(4452552356570026231)
XLA Ops:
  0.6 0.0 copy-start.4
  0.6 0.0 copy-start.3
  0.6 1.1 %multiply_bitcast_fusion = (f32[1,128,128]{2,1,0:T(8,128)S(1)}, f32[1,128,128]{2,1,0:T(8,128)S(1)}, f32[1,128,128]{2,1,0:T(8,128)S(1)}, f32[1,128,128]{2,1,0:T(8,128)S(1)}) fusion(s32[128,1024]{1,0:T(8,128)} %param.7, f32[128,1024]{1,0:T(8,128)} %param.6, f32[128,1024]{1,0:T(8,128)} %f_ref.5), kind=kLoop, calls=%fused_computation.3 | loop fusion | flops 98304 | bytes 655360 | tf_op jit(solution)/shard_map/stack | solution.py:266
  1.8 4.9 %collective-permute-start = (f32[2,128,128]{2,1,0:T(8,128)S(1)}, f32[2,128,128]{2,1,0:T(8,128)S(1)}, u32[]{:S(2)}, u32[]{:S(2)}) collective-permute-start(f32[2,128,128]{2,1,0:T(8,128)S(1)} %pad_maximum_fusion), channel_id=1, source_target_pairs={{0,1},{1,2},{2,3},{4,5},{5,6},{6,7},{8,9},{9,10},{10,11},{12,13},{... | collective-permute-start | bytes 393224 | tf_op jit(solution)/shard_map/ppermute | solution.py:252
  6.7 1.3 %collective-permute-start.1 = (f32[2,128,128]{2,1,0:T(8,128)S(1)}, f32[2,128,128]{2,1,0:T(8,128)S(1)}, u32[]{:S(2)}, u32[]{:S(2)}) collective-permute-start(f32[2,128,128]{2,1,0:T(8,128)S(1)} %pad_maximum_fusion.1), channel_id=1, source_target_pairs={{1,0},{2,1},{3,2},{5,4},{6,5},{7,6},{9,8},{10,9},{11,10},{13,12},{... | collective-permute-start | bytes 393224 | tf_op jit(solution)/shard_map/ppermute | solution.py:252
  8.0 0.0 copy-done.4
  8.1 0.0 copy-done.3
  8.1 0.0 slice-start
  8.1 1.4 %collective-permute-done.left_ref = f32[2,128,128]{2,1,0:T(8,128)S(1)} collective-permute-done((f32[2,128,128]{2,1,0:T(8,128)S(1)}, f32[2,128,128]{2,1,0:T(8,128)S(1)}, u32[]{:S(2)}, u32[]{:S(2)}) %collective-permute-start) | collective-permute-done | bytes 131104 | tf_op jit(solution)/shard_map/ppermute | solution.py:252
  9.5 0.0 slice-done
  9.5 0.0 copy-start
  9.5 1.4 %collective-permute-start.2 = (f32[8,1152]{1,0:T(8,128)S(1)}, f32[8,1152]{1,0:T(8,128)S(1)}, u32[]{:S(2)}, u32[]{:S(2)}) collective-permute-start(f32[8,1152]{1,0:T(8,128)S(1)} %pad_maximum_fusion.2), channel_id=1, source_target_pairs={{0,4},{4,8},{8,12},{12,16},{16,20},{20,24},{24,28},{1,5},{5,9},{9,... | collective-permute-start | bytes 110600 | tf_op jit(solution)/shard_map/ppermute | solution.py:252
  10.9 0.1 subtract_multiply_fusion.w_ref
  11.0 0.8 collective-permute-done.2.top_ref
  11.8 0.0 copy-done
  11.8 1.1 %moments.1 = f32[1,128]{1,0:T(1,128)S(1)} custom-call(f32[128,1024]{1,0:T(8,128)S(1)} %copy-done, f32[128,1024]{1,0:T(8,128)S(1)} %subtract_multiply_fusion.w_ref, f32[8,1152]{1,0:T(8,128)S(1)} %collective-permute-done.2.top_ref, f32[2,128,128]{2,1,0:T(8,128)S(1)} %collective-permute-done.left_ref), custom_call_target="tpu_custom_call" | custom-call | tf_op jit(solution)/shard_map/moments/pallas_call | solution.py:275
  12.9 0.0 copy-start.1
  12.9 0.0 copy-start.2
  12.9 0.7 collective-permute-done.1.right_ref
  13.6 0.1 wide.1
  13.7 3.8 %collective-permute-start.3 = (f32[136,1280]{1,0:T(8,128)S(1)}, f32[136,1280]{1,0:T(8,128)S(1)}, u32[]{:S(2)}, u32[]{:S(2)}) collective-permute-start(f32[136,1280]{1,0:T(8,128)S(1)} %get-tuple-element.10), channel_id=1, source_target_pairs={{0,4},{4,8},{8,12},{12,16},{16,20},{20,24},{24,28},{1,5},{5,9},{9,... | collective-permute-start | bytes 2088968 | tf_op jit(solution)/shard_map/ppermute | solution.py:252
  17.5 1.3 %collective-permute-start.4 = (f32[136,1280]{1,0:T(8,128)S(1)}, f32[136,1280]{1,0:T(8,128)S(1)}, u32[]{:S(2)}, u32[]{:S(2)}) collective-permute-start(f32[136,1280]{1,0:T(8,128)S(1)} %get-tuple-element.11), channel_id=1, source_target_pairs={{4,0},{8,4},{12,8},{16,12},{20,16},{24,20},{28,24},{5,1},{9,5},{13... | collective-permute-start | bytes 2088968 | tf_op jit(solution)/shard_map/ppermute | solution.py:252
  18.8 70.8 %all-gather.1.parts_ref = f32[32,1,128]{2,1,0:T(1,128)S(1)} all-gather(f32[1,1,128]{2,1,0:T(1,128)S(1)} %bitcast.13), channel_id=2, replica_groups=mesh['rows'=8,'cols'=4] {'rows','cols'}, dimensions={0}, use_global_device_ids=true | all-gather | bytes 16896 | tf_op jit(solution)/shard_map/all_gather | solution.py:295
  89.6 0.0 collective-permute-done.3.top_ref
  89.6 0.0 collective-permute-done.4.bottom_ref
  89.6 0.0 copy-done.1
  89.6 0.0 copy-done.2
  89.6 3.1 %finish.1 = (f32[128,1024]{1,0:T(8,128)}, f32[128,1024]{1,0:T(8,128)}) custom-call(f32[32,1,128]{2,1,0:T(1,128)S(1)} %all-gather.1.parts_ref, f32[128,1024]{1,0:T(8,128)S(1)} %copy-done, f32[128,1024]{1,0:T(8,128)S(1)} %subtract_multiply_fusion.w_ref, f32[136,1280]{1,0:T(8,128)S(1)} %collective-permute-done.3.top_ref, ...), custom_call_target="tpu_custom_call" | custom-call | tf_op jit(solution)/shard_map/finish/pallas_call | solution.py:298
  (6 shorter events, 0.1 us)
Async XLA Ops:
  0.6 7.4 %copy-start.4 = (s32[128,1024]{1,0:T(8,128)S(1)}, s32[128,1024]{1,0:T(8,128)}, u32[]{:S(2)}) copy-start(s32[128,1024]{1,0:T(8,128)} %param.7) | copy-start | bytes 1572868
  0.6 7.4 %copy-start.3 = (f32[128,1024]{1,0:T(8,128)S(1)}, f32[128,1024]{1,0:T(8,128)}, u32[]{:S(2)}) copy-start(f32[128,1024]{1,0:T(8,128)} %param.6) | copy-start | bytes 1572868
  1.8 7.7 %collective-permute-start = (f32[2,128,128]{2,1,0:T(8,128)S(1)}, f32[2,128,128]{2,1,0:T(8,128)S(1)}, u32[]{:S(2)}, u32[]{:S(2)}) collective-permute-start(f32[2,128,128]{2,1,0:T(8,128)S(1)} %pad_maximum_fusion), channel_id=1, source_target_pairs={{0,1},{1,2},{2,3},{4,5},{5,6},{6,7},{8,9},{9,10},{10,11},{12,13},{... | collective-permute-start | bytes 393224 | tf_op jit(solution)/shard_map/ppermute | solution.py:252
  6.7 6.9 %collective-permute-start.1 = (f32[2,128,128]{2,1,0:T(8,128)S(1)}, f32[2,128,128]{2,1,0:T(8,128)S(1)}, u32[]{:S(2)}, u32[]{:S(2)}) collective-permute-start(f32[2,128,128]{2,1,0:T(8,128)S(1)} %pad_maximum_fusion.1), channel_id=1, source_target_pairs={{1,0},{2,1},{3,2},{5,4},{6,5},{7,6},{9,8},{10,9},{11,10},{13,12},{... | collective-permute-start | bytes 393224 | tf_op jit(solution)/shard_map/ppermute | solution.py:252
  8.1 1.4 %slice-start = ((f32[128,1024]{1,0:T(8,128)}), f32[8,1024]{1,0:T(8,128)S(1)}, s32[]{:S(2)}) async-start(f32[128,1024]{1,0:T(8,128)} %f_ref.5), calls=%async_computation | async-start | bytes 65536 | tf_op jit(solution)/shard_map/slice | solution.py:261
  9.5 2.3 %copy-start = (f32[128,1024]{1,0:T(8,128)S(1)}, f32[128,1024]{1,0:T(8,128)}, u32[]{:S(2)}) copy-start(f32[128,1024]{1,0:T(8,128)} %f_ref.5) | copy-start | bytes 1572868
  9.5 2.3 %collective-permute-start.2 = (f32[8,1152]{1,0:T(8,128)S(1)}, f32[8,1152]{1,0:T(8,128)S(1)}, u32[]{:S(2)}, u32[]{:S(2)}) collective-permute-start(f32[8,1152]{1,0:T(8,128)S(1)} %pad_maximum_fusion.2), channel_id=1, source_target_pairs={{0,4},{4,8},{8,12},{12,16},{16,20},{20,24},{24,28},{1,5},{5,9},{9,... | collective-permute-start | bytes 110600 | tf_op jit(solution)/shard_map/ppermute | solution.py:252
  12.9 76.7 %copy-start.1 = (bf16[4,256,256]{2,1,0:T(8,128)(2,1)S(1)}, bf16[4,256,256]{2,1,0:T(8,128)(2,1)}, u32[]{:S(2)}) copy-start(bf16[4,256,256]{2,1,0:T(8,128)(2,1)} %constant.4.clone.rowtaps_ref) | copy-start | bytes 1572868
  12.9 76.7 %copy-start.2 = (bf16[3,256,256]{2,1,0:T(8,128)(2,1)S(1)}, bf16[3,256,256]{2,1,0:T(8,128)(2,1)}, u32[]{:S(2)}) copy-start(bf16[3,256,256]{2,1,0:T(8,128)(2,1)} %constant.2.clone.coltaps_ref) | copy-start | bytes 1179652
  13.7 75.9 %collective-permute-start.3 = (f32[136,1280]{1,0:T(8,128)S(1)}, f32[136,1280]{1,0:T(8,128)S(1)}, u32[]{:S(2)}, u32[]{:S(2)}) collective-permute-start(f32[136,1280]{1,0:T(8,128)S(1)} %get-tuple-element.10), channel_id=1, source_target_pairs={{0,4},{4,8},{8,12},{12,16},{16,20},{20,24},{24,28},{1,5},{5,9},{9,... | collective-permute-start | bytes 2088968 | tf_op jit(solution)/shard_map/ppermute | solution.py:252
  17.5 72.1 %collective-permute-start.4 = (f32[136,1280]{1,0:T(8,128)S(1)}, f32[136,1280]{1,0:T(8,128)S(1)}, u32[]{:S(2)}, u32[]{:S(2)}) collective-permute-start(f32[136,1280]{1,0:T(8,128)S(1)} %get-tuple-element.11), channel_id=1, source_target_pairs={{4,0},{8,4},{12,8},{16,12},{20,16},{24,20},{28,24},{5,1},{9,5},{13... | collective-permute-start | bytes 2088968 | tf_op jit(solution)/shard_map/ppermute | solution.py:252

commit v5 on v4

--- a/solution.py
+++ b/solution.py
@@ -88,20 +88,27 @@
     return flux, jnp.concatenate([left_ref[1, at, :], weight, right_ref[1, at, :]], axis=1)
 
 
-def wide_kernel(f_ref, w_ref, left_ref, right_ref, down_ref, up_ref):
+def wide_kernel(f_ref, w_ref, left_ref, right_ref, near_ref, far_ref):
     rows = f_ref.shape[0]
-
-    def pair(start, count):
-        at = pl.ds(start, count)
-        return extended(f_ref, w_ref, left_ref, right_ref, at)
-
-    for out_ref, begin, beyond in ((down_ref, rows - REACH, rows - WIDE), (up_ref, 0, REACH)):
+    even = lax.axis_index("rows") % 2 == 0
+
+    def write(out_ref, begin, beyond):
         for start in range(0, REACH, 8):
-            flux, weight = pair(begin + start, 8)
+            flux, weight = extended(f_ref, w_ref, left_ref, right_ref, pl.ds(begin + start, 8))
             out_ref[pl.ds(start, 8), :] = flux
             out_ref[pl.ds(REACH + start, 8), :] = weight
-        flux, weight = pair(beyond, 8)
+        flux, weight = extended(f_ref, w_ref, left_ref, right_ref, pl.ds(beyond, 8))
         out_ref[pl.ds(2 * REACH, 8), :] = flux * weight
+
+    @pl.when(even)
+    def _():
+        write(near_ref, rows - REACH, rows - WIDE)
+        write(far_ref, 0, REACH)
+
+    @pl.when(jnp.logical_not(even))
+    def _():
+        write(near_ref, 0, REACH)
+        write(far_ref, rows - REACH, rows - WIDE)
 
 
 def moments_kernel(f_ref, w_ref, top_ref, left_ref, out_ref, v0_ref, v1_ref):
@@ -178,7 +185,7 @@
 
 
 def finish_kernel(
-    parts_ref, f_ref, w_ref, top_ref, bottom_ref, left_ref, right_ref, rowtaps_ref, coltaps_ref,
+    parts_ref, f_ref, w_ref, near_ref, far_ref, left_ref, right_ref, rowtaps_ref, coltaps_ref,
     background_ref, rms_ref, v0_ref, high_ref, low_ref,
 ):
     rows, cols = f_ref.shape
@@ -190,14 +197,21 @@
     moments = [jnp.sum(jnp.where(lane == i, totals, 0.0), axis=1, keepdims=True) for i in range(4)]
     c0, c1 = coefficients(*moments)
 
+    even = lax.axis_index("rows") % 2 == 0
+
+    def beyond(below, start, count):
+        at = pl.ds(start, count)
+        one, other = (near_ref, far_ref) if below else (far_ref, near_ref)
+        return jnp.where(even, one[at, :], other[at, :])
+
     def pair(start, count):
-        for ref, begin in ((top_ref, WIDE - REACH), (bottom_ref, WIDE + rows)):
+        for below, begin in ((False, WIDE - REACH), (True, WIDE + rows)):
             if begin <= start < begin + REACH:
-                return ref[pl.ds(start - begin, count), :], ref[pl.ds(REACH + start - begin, count), :]
+                return beyond(below, start - begin, count), beyond(below, REACH + start - begin, count)
         return extended(f_ref, w_ref, left_ref, right_ref, pl.ds(start - WIDE, count))
 
-    v0_ref[pl.ds(0, 8), :] = top_ref[pl.ds(2 * REACH, 8), :]
-    v0_ref[pl.ds(rows + 2 * WIDE - 8, 8), :] = bottom_ref[pl.ds(2 * REACH, 8), :]
+    v0_ref[pl.ds(0, 8), :] = beyond(False, 2 * REACH, 8)
+    v0_ref[pl.ds(rows + 2 * WIDE - 8, 8), :] = beyond(True, 2 * REACH, 8)
     for start in range(8, rows + 2 * WIDE - 8, 8):
         flux, weight = pair(start, 8)
         v0_ref[pl.ds(start, 8), :] = flux * weight
@@ -252,6 +266,12 @@
     return lax.ppermute(block, axis, pairs)
 
 
+def swap(block, axis, first):
+    count = lax.axis_size(axis)
+    pairs = [(i, i + 1) for i in range(first, count - 1, 2)]
+    return lax.ppermute(block, axis, pairs + [(j, i) for i, j in pairs])
+
+
 def shards(coadd_flux, inverse_variance, source_mask):
     rows, cols = coadd_flux.shape
     width = cols + 2 * LANES
@@ -272,6 +292,17 @@
     vmem = pl.BlockSpec(memory_space=pltpu.VMEM)
     field = jax.ShapeDtypeStruct((rows, cols), jnp.float32)
     own = (coadd_flux, weights(inverse_variance, source_mask))
+    to_near, to_far = pl.pallas_call(
+        wide_kernel,
+        out_shape=(jax.ShapeDtypeStruct((2 * REACH + 8, width), jnp.float32),) * 2,
+        in_specs=[vmem] * 4,
+        out_specs=(vmem, vmem),
+        compiler_params=pltpu.CompilerParams(vmem_limit_bytes=16 << 20),
+        name="wide",
+    )(*own, left, right)
+    to_near, to_far, near = lax.optimization_barrier((to_near, to_far, near))
+    from_near = swap(to_near, "rows", 0)
+    from_far = swap(to_far, "rows", 1)
     parts = pl.pallas_call(
         moments_kernel,
         out_shape=jax.ShapeDtypeStruct((1, LANES), jnp.float32),
@@ -281,18 +312,9 @@
         compiler_params=pltpu.CompilerParams(vmem_limit_bytes=16 << 20),
         name="moments",
     )(*own, near, left)
-    left_after, right_after, parts = lax.optimization_barrier((left, right, parts))
-    down, up = pl.pallas_call(
-        wide_kernel,
-        out_shape=(jax.ShapeDtypeStruct((2 * REACH + 8, width), jnp.float32),) * 2,
-        in_specs=[vmem] * 4,
-        out_specs=(vmem, vmem),
-        compiler_params=pltpu.CompilerParams(vmem_limit_bytes=16 << 20),
-        name="wide",
-    )(*own, left_after, right_after)
-    top = shift(down, "rows", 1)
-    bottom = shift(up, "rows", -1)
-    parts = lax.all_gather(parts, ("rows", "cols"))
+    devices = lax.axis_size("rows") * lax.axis_size("cols")
+    parts = jnp.broadcast_to(parts[None], (devices, 1, LANES))
+    parts = lax.all_to_all(parts, ("rows", "cols"), 0, 0, tiled=True)
 
     return tuple(
         pl.pallas_call(
@@ -308,7 +330,7 @@
             compiler_params=pltpu.CompilerParams(vmem_limit_bytes=32 << 20),
             name="finish",
         )(
-            parts, *own, top, bottom, left, right,
+            parts, *own, from_near, from_far, left, right,
             jnp.asarray(row_tables(rows)), jnp.asarray(col_tables()),
         )
     )

time: 93 us -> 38.9 us (0.42)
  blocking collectives: 70.8 us -> 19 us
  starting transfers between devices: 12.8 us -> 8.81 us
  waiting for transfers between devices: 2.82 us -> 3.95 us
    all_gather x1 -> x0, blocking collectives: 70.8 us -> none  [shards(): parts = lax.all_gather(parts, ('rows', 'cols'))]
    all_to_all x0 -> x1, blocking collectives: none -> 19 us  [shards(): parts = lax.all_to_all(parts, ('rows', 'cols'), 0, 0, tiled=True)]
    ppermute x5 -> x3, starting transfers between devices: 12.8 us -> 7.65 us  [shift(): return lax.ppermute(block, axis, pairs)]
    ppermute x0 -> x2, starting transfers between devices: none -> 1.15 us  [swap(): return lax.ppermute(block, axis, pairs + [(j, i) for i, j in pairs])]
    ppermute x5 -> x3, waiting for transfers between devices: 2.82 us -> 3.95 us  [shift(): return lax.ppermute(block, axis, pairs)]
  transfers between devices with their start and end apart: 5 -> 5, of which waited for: 3 -> 2; matrix products, arithmetic and copies ran while one was open for 0% -> 0% of each run, Pallas kernels for 1% -> 3%
where the time goes in v5:
time: 38.9 us; the launch traced here: 38.2 us
  blocking collectives  19 us (49%)
  starting transfers between devices  8.81 us (23%)
  Pallas kernels  4.33 us (11%)
  waiting for transfers between devices  3.95 us (10%)
  other arithmetic  1.25 us (3%)
  between operations  0.8 us (2%)
    all_to_all x1, blocking collectives, shards(): parts = lax.all_to_all(parts, ('rows', 'cols'), 0, 0, tiled=True)  19 us
    ppermute x3, starting transfers between devices, shift(): return lax.ppermute(block, axis, pairs)  7.65 us
    ppermute x3, waiting for transfers between devices, shift(): return lax.ppermute(block, axis, pairs)  3.95 us
    pallas_call x1, Pallas kernels, shards(): pl.pallas_call(finish_kernel, out_shape=(field, field), in_specs=[vmem] *...  3.12 us
    ppermute x2, starting transfers between devices, swap(): return lax.ppermute(block, axis, pairs + [(j, i) for i, j in pairs])  1.15 us
    another operation x2, other arithmetic, shards(): right = shift(jnp.stack(edge(0, LANES, 1)), 'cols', -1)  1.13 us
    pallas_call x1, Pallas kernels, shards(): pl.pallas_call(moments_kernel, out_shape=jax.ShapeDtypeStruct((1, LANES),...  1.12 us
  transfers between devices with their start and end apart: 5, of which 2 were waited for; matrix products, arithmetic and copies ran while one was open for 0% of the time, Pallas kernels for 3%

profile of v5, /device:TPU:0, one launch (start us, length us, event | category | flops | bytes accessed | tf_op | source)
XLA Modules:
  0.0 38.2 jit_solution(12640976752087903195)
XLA Ops:
  0.6 0.0 copy-start.4
  0.6 0.0 copy-start.3
  0.6 1.1 %multiply_bitcast_fusion = (f32[1,128,128]{2,1,0:T(8,128)S(1)}, f32[1,128,128]{2,1,0:T(8,128)S(1)}, f32[1,128,128]{2,1,0:T(8,128)S(1)}, f32[1,128,128]{2,1,0:T(8,128)S(1)}) fusion(s32[128,1024]{1,0:T(8,128)} %param.7, f32[128,1024]{1,0:T(8,128)} %param.6, f32[128,1024]{1,0:T(8,128)} %f_ref.5), kind=kLoop, calls=%fused_computation.3 | loop fusion | flops 98304 | bytes 655360 | tf_op jit(solution)/shard_map/stack | solution.py:286
  1.8 4.9 %collective-permute-start = (f32[2,128,128]{2,1,0:T(8,128)S(1)}, f32[2,128,128]{2,1,0:T(8,128)S(1)}, u32[]{:S(2)}, u32[]{:S(2)}) collective-permute-start(f32[2,128,128]{2,1,0:T(8,128)S(1)} %pad_maximum_fusion), channel_id=1, source_target_pairs={{0,1},{1,2},{2,3},{4,5},{5,6},{6,7},{8,9},{9,10},{10,11},{12,13},{... | collective-permute-start | bytes 393224 | tf_op jit(solution)/shard_map/ppermute | solution.py:266
  6.7 1.3 %collective-permute-start.1 = (f32[2,128,128]{2,1,0:T(8,128)S(1)}, f32[2,128,128]{2,1,0:T(8,128)S(1)}, u32[]{:S(2)}, u32[]{:S(2)}) collective-permute-start(f32[2,128,128]{2,1,0:T(8,128)S(1)} %pad_maximum_fusion.1), channel_id=1, source_target_pairs={{1,0},{2,1},{3,2},{5,4},{6,5},{7,6},{9,8},{10,9},{11,10},{13,12},{... | collective-permute-start | bytes 393224 | tf_op jit(solution)/shard_map/ppermute | solution.py:266
  8.0 0.0 copy-done.4
  8.1 0.0 copy-done.3
  8.1 0.0 slice-start
  8.1 1.4 %collective-permute-done.left_ref = f32[2,128,128]{2,1,0:T(8,128)S(1)} collective-permute-done((f32[2,128,128]{2,1,0:T(8,128)S(1)}, f32[2,128,128]{2,1,0:T(8,128)S(1)}, u32[]{:S(2)}, u32[]{:S(2)}) %collective-permute-start) | collective-permute-done | bytes 131104 | tf_op jit(solution)/shard_map/ppermute | solution.py:266
  9.5 0.0 slice-done
  9.5 0.0 copy-start
  9.5 1.4 %collective-permute-start.2 = (f32[8,1152]{1,0:T(8,128)S(1)}, f32[8,1152]{1,0:T(8,128)S(1)}, u32[]{:S(2)}, u32[]{:S(2)}) collective-permute-start(f32[8,1152]{1,0:T(8,128)S(1)} %pad_maximum_fusion.2), channel_id=1, source_target_pairs={{0,4},{4,8},{8,12},{12,16},{16,20},{20,24},{24,28},{1,5},{5,9},{9,... | collective-permute-start | bytes 110600 | tf_op jit(solution)/shard_map/ppermute | solution.py:266
  10.9 0.1 subtract_multiply_fusion.w_ref
  11.0 2.6 %collective-permute-done.1.right_ref = f32[2,128,128]{2,1,0:T(8,128)S(1)} collective-permute-done((f32[2,128,128]{2,1,0:T(8,128)S(1)}, f32[2,128,128]{2,1,0:T(8,128)S(1)}, u32[]{:S(2)}, u32[]{:S(2)}) %collective-permute-start.1) | collective-permute-done | bytes 131104 | tf_op jit(solution)/shard_map/ppermute | solution.py:266
  13.6 0.0 copy-done
  13.6 0.1 wide.1
  13.7 0.0 collective-permute-done.2.top_ref
  13.7 0.0 copy-start.1
  13.7 0.0 copy-start.2
  13.8 0.5 %collective-permute-start.3 = (f32[136,1280]{1,0:T(8,128)S(1)}, f32[136,1280]{1,0:T(8,128)S(1)}, u32[]{:S(2)}, u32[]{:S(2)}) collective-permute-start(f32[136,1280]{1,0:T(8,128)S(1)} %get-tuple-element.10), channel_id=1, source_target_pairs={{0,4},{8,12},{16,20},{24,28},{4,0},{12,8},{20,16},{28,24},{1,5},{9... | collective-permute-start | bytes 2088968 | tf_op jit(solution)/shard_map/ppermute | solution.py:272
  14.2 0.7 %collective-permute-start.4 = (f32[136,1280]{1,0:T(8,128)S(1)}, f32[136,1280]{1,0:T(8,128)S(1)}, u32[]{:S(2)}, u32[]{:S(2)}) collective-permute-start(f32[136,1280]{1,0:T(8,128)S(1)} %get-tuple-element.11), channel_id=1, source_target_pairs={{4,8},{12,16},{20,24},{8,4},{16,12},{24,20},{5,9},{13,17},{21,25},... | collective-permute-start | bytes 2088968 | tf_op jit(solution)/shard_map/ppermute | solution.py:272
  14.9 1.1 %moments.1 = f32[1,128]{1,0:T(1,128)S(1)} custom-call(f32[128,1024]{1,0:T(8,128)S(1)} %copy-done, f32[128,1024]{1,0:T(8,128)S(1)} %subtract_multiply_fusion.w_ref, f32[8,1152]{1,0:T(8,128)S(1)} %collective-permute-done.2.top_ref, f32[2,128,128]{2,1,0:T(8,128)S(1)} %collective-permute-done.left_ref), custom_call_target="tpu_custom_call" | custom-call | tf_op jit(solution)/shard_map/moments/pallas_call | solution.py:306
  16.0 19.0 %all_to_all.5.parts_ref = f32[32,1,128]{2,1,0:T(1,128)S(1)} all-to-all(f32[32,1,128]{2,1,0:T(1,128)S(1)} %broadcast_in_dim.9), channel_id=1, replica_groups=mesh['rows'=8,'cols'=4] {'rows','cols'}, dimensions={0} | all-to-all | bytes 32768 | tf_op jit(solution)/shard_map/all_to_all | solution.py:317
  35.1 0.0 collective-permute-done.3.near_ref
  35.1 0.0 collective-permute-done.4.far_ref
  35.1 0.0 copy-done.1
  35.1 0.0 copy-done.2
  35.1 3.1 %finish.1 = (f32[128,1024]{1,0:T(8,128)}, f32[128,1024]{1,0:T(8,128)}) custom-call(f32[32,1,128]{2,1,0:T(1,128)S(1)} %all_to_all.5.parts_ref, f32[128,1024]{1,0:T(8,128)S(1)} %copy-done, f32[128,1024]{1,0:T(8,128)S(1)} %subtract_multiply_fusion.w_ref, f32[136,1280]{1,0:T(8,128)S(1)} %collective-permute-done.3.near_ref, ...), custom_call_target="tpu_custom_call" | custom-call | tf_op jit(solution)/shard_map/finish/pallas_call | solution.py:320
  (7 shorter events, 0.1 us)
Async XLA Ops:
  0.6 7.4 %copy-start.4 = (s32[128,1024]{1,0:T(8,128)S(1)}, s32[128,1024]{1,0:T(8,128)}, u32[]{:S(2)}) copy-start(s32[128,1024]{1,0:T(8,128)} %param.7) | copy-start | bytes 1572868
  0.6 7.4 %copy-start.3 = (f32[128,1024]{1,0:T(8,128)S(1)}, f32[128,1024]{1,0:T(8,128)}, u32[]{:S(2)}) copy-start(f32[128,1024]{1,0:T(8,128)} %param.6) | copy-start | bytes 1572868
  1.8 7.7 %collective-permute-start = (f32[2,128,128]{2,1,0:T(8,128)S(1)}, f32[2,128,128]{2,1,0:T(8,128)S(1)}, u32[]{:S(2)}, u32[]{:S(2)}) collective-permute-start(f32[2,128,128]{2,1,0:T(8,128)S(1)} %pad_maximum_fusion), channel_id=1, source_target_pairs={{0,1},{1,2},{2,3},{4,5},{5,6},{6,7},{8,9},{9,10},{10,11},{12,13},{... | collective-permute-start | bytes 393224 | tf_op jit(solution)/shard_map/ppermute | solution.py:266
  6.7 6.9 %collective-permute-start.1 = (f32[2,128,128]{2,1,0:T(8,128)S(1)}, f32[2,128,128]{2,1,0:T(8,128)S(1)}, u32[]{:S(2)}, u32[]{:S(2)}) collective-permute-start(f32[2,128,128]{2,1,0:T(8,128)S(1)} %pad_maximum_fusion.1), channel_id=1, source_target_pairs={{1,0},{2,1},{3,2},{5,4},{6,5},{7,6},{9,8},{10,9},{11,10},{13,12},{... | collective-permute-start | bytes 393224 | tf_op jit(solution)/shard_map/ppermute | solution.py:266
  8.1 1.4 %slice-start = ((f32[128,1024]{1,0:T(8,128)}), f32[8,1024]{1,0:T(8,128)S(1)}, s32[]{:S(2)}) async-start(f32[128,1024]{1,0:T(8,128)} %f_ref.5), calls=%async_computation.1 | async-start | bytes 65536 | tf_op jit(solution)/shard_map/slice | solution.py:281
  9.5 4.1 %copy-start = (f32[128,1024]{1,0:T(8,128)S(1)}, f32[128,1024]{1,0:T(8,128)}, u32[]{:S(2)}) copy-start(f32[128,1024]{1,0:T(8,128)} %f_ref.5) | copy-start | bytes 1572868
  9.5 4.2 %collective-permute-start.2 = (f32[8,1152]{1,0:T(8,128)S(1)}, f32[8,1152]{1,0:T(8,128)S(1)}, u32[]{:S(2)}, u32[]{:S(2)}) collective-permute-start(f32[8,1152]{1,0:T(8,128)S(1)} %pad_maximum_fusion.2), channel_id=1, source_target_pairs={{0,4},{4,8},{8,12},{12,16},{16,20},{20,24},{24,28},{1,5},{5,9},{9,... | collective-permute-start | bytes 110600 | tf_op jit(solution)/shard_map/ppermute | solution.py:266
  13.7 21.3 %copy-start.1 = (bf16[4,256,256]{2,1,0:T(8,128)(2,1)S(1)}, bf16[4,256,256]{2,1,0:T(8,128)(2,1)}, u32[]{:S(2)}) copy-start(bf16[4,256,256]{2,1,0:T(8,128)(2,1)} %constant.4.clone.rowtaps_ref) | copy-start | bytes 1572868
  13.7 21.3 %copy-start.2 = (bf16[3,256,256]{2,1,0:T(8,128)(2,1)S(1)}, bf16[3,256,256]{2,1,0:T(8,128)(2,1)}, u32[]{:S(2)}) copy-start(bf16[3,256,256]{2,1,0:T(8,128)(2,1)} %constant.2.clone.coltaps_ref) | copy-start | bytes 1179652
  13.8 21.3 %collective-permute-start.3 = (f32[136,1280]{1,0:T(8,128)S(1)}, f32[136,1280]{1,0:T(8,128)S(1)}, u32[]{:S(2)}, u32[]{:S(2)}) collective-permute-start(f32[136,1280]{1,0:T(8,128)S(1)} %get-tuple-element.10), channel_id=1, source_target_pairs={{0,4},{8,12},{16,20},{24,28},{4,0},{12,8},{20,16},{28,24},{1,5},{9... | collective-permute-start | bytes 2088968 | tf_op jit(solution)/shard_map/ppermute | solution.py:272
  14.2 20.8 %collective-permute-start.4 = (f32[136,1280]{1,0:T(8,128)S(1)}, f32[136,1280]{1,0:T(8,128)S(1)}, u32[]{:S(2)}, u32[]{:S(2)}) collective-permute-start(f32[136,1280]{1,0:T(8,128)S(1)} %get-tuple-element.11), channel_id=1, source_target_pairs={{4,8},{12,16},{20,24},{8,4},{16,12},{24,20},{5,9},{13,17},{21,25},... | collective-permute-start | bytes 2088968 | tf_op jit(solution)/shard_map/ppermute | solution.py:272

commit v6 on v1

v6 whole, which is shorter than its diff:
```python
import functools

import jax
import jax.numpy as jnp
import ml_dtypes
import numpy as np
from jax import lax
from jax.experimental import pallas as pl
from jax.experimental.pallas import tpu as pltpu
from jax.sharding import PartitionSpec as P

RADIUS = 32
REACH = 2 * RADIUS
LANES = 128
WIDE = REACH + 8
NEAR = 8
VECTORS = 8

smooth_weight = 2.0
blur_sigma = 10.0


def squared_taps(length, first, last):
    offsets = np.arange(2 * RADIUS + 1) - RADIUS
    taps = np.exp(-offsets * offsets / (2.0 * blur_sigma * blur_sigma))
    taps = taps / taps.sum()

    def band(count):
        table = np.zeros((count, count + 2 * RADIUS))
        for k in range(2 * RADIUS + 1):
            table[np.arange(count), np.arange(count) + k] = taps[k]
        return table

    inner = band(length + 2 * RADIUS)
    if first:
        inner[:RADIUS] = 0.0
    if last:
        inner[-RADIUS:] = 0.0
    return band(length) @ inner


def split(table):
    high = table.astype(np.float32).astype(ml_dtypes.bfloat16)
    low = (table - high.astype(np.float64)).astype(np.float32).astype(ml_dtypes.bfloat16)
    return high, low


def row_tables(length):
    tables = []
    for first, last in ((False, False), (True, False), (False, True), (True, True)):
        tables.append(np.concatenate(split(squared_taps(length, first, last)), axis=0))
    return np.stack(tables)


def col_tables():
    tables = []
    for first, last in ((False, False), (True, False), (False, True)):
        tables.append(np.concatenate(split(squared_taps(LANES, first, last).T), axis=1))
    return np.stack(tables)


def split_values(values):
    high = values.astype(jnp.bfloat16)
    return high, (values - high.astype(jnp.float32)).astype(jnp.bfloat16)


def at_edges():
    row, col = lax.axis_index("rows"), lax.axis_index("cols")
    return (
        row == 0,
        row == lax.axis_size("rows") - 1,
        col == 0,
        col == lax.axis_size("cols") - 1,
    )


def is_even():
    return lax.axis_index("rows") % 2 == 0


def beside_columns(field):
    width = field.shape[1]
    return pltpu.roll(field, 1, 1) + pltpu.roll(field, width - 1, 1)


def weights(inverse_variance, source_mask):
    return inverse_variance * (1.0 - source_mask.astype(jnp.float32))


def coefficients(m0, m1, m2, m3):
    alpha0 = m0 / m1
    norm1 = jnp.maximum(m0 - 2.0 * alpha0 * m1 + alpha0 * alpha0 * m2, 0.0)
    grown = 1.0 + norm1 / m0
    image1 = grown * grown * m1 - 2.0 * grown * alpha0 * m2 + alpha0 * alpha0 * m3
    alpha1 = jnp.where(image1 > 0.0, norm1 / image1, 0.0)
    return alpha0 + alpha1 * grown, -alpha1 * alpha0


def wide_kernel(f_ref, w_ref, near_ref, far_ref):
    rows = f_ref.shape[0]

    def write(out_ref, begin, beyond):
        out_ref[pl.ds(0, REACH), :] = f_ref[pl.ds(begin, REACH), :]
        out_ref[pl.ds(REACH, REACH), :] = w_ref[pl.ds(begin, REACH), :]
        out_ref[pl.ds(2 * REACH, 8), :] = f_ref[pl.ds(beyond, 8), :] * w_ref[pl.ds(beyond, 8), :]

    @pl.when(is_even())
    def _():
        write(near_ref, rows - REACH, rows - WIDE)
        write(far_ref, 0, REACH)

    @pl.when(jnp.logical_not(is_even()))
    def _():
        write(near_ref, 0, REACH)
        write(far_ref, rows - REACH, rows - WIDE)


def moments_kernel(f_ref, w_ref, far_ref, near_ref, out_ref, v0_ref, v1_ref, edge_ref):
    rows, cols = f_ref.shape
    width = cols + LANES
    first_row, last_row, _, _ = at_edges()
    even = is_even()
    own, pad = pl.ds(0, cols), pl.ds(cols, LANES)

    far_weight = far_ref[pl.ds(8, 8), :]
    far_v0 = far_ref[pl.ds(0, 8), :] * far_weight
    above, below = near_ref[pl.ds(2 * REACH - 8, 8), :], near_ref[pl.ds(REACH, 8), :]
    top = jnp.where(even, far_v0, near_ref[pl.ds(REACH - 8, 8), :] * above)
    bottom = jnp.where(even, near_ref[pl.ds(0, 8), :] * below, far_v0)
    top_weight = jnp.where(even, far_weight, above)[7:]
    bottom_weight = jnp.where(even, below, far_weight)[:1]

    for ref in (v0_ref, v1_ref):
        ref[:, pad] = jnp.zeros((rows + 2 * NEAR, LANES), jnp.float32)
    for start in (0, NEAR + rows):
        v1_ref[pl.ds(start, 8), own] = jnp.zeros((8, cols), jnp.float32)
    v0_ref[pl.ds(0, 8), own] = top
    v0_ref[pl.ds(NEAR + rows, 8), own] = bottom
    for start in range(0, rows, 8):
        at = pl.ds(start, 8)
        v0_ref[pl.ds(NEAR + start, 8), own] = f_ref[at, :] * w_ref[at, :]

    def image(ref, weight, start, count):
        here = ref[pl.ds(start, count), :]
        beside = ref[pl.ds(start - 1, count), own] + ref[pl.ds(start + 1, count), own] + beside_columns(here)[:, :cols]
        here = here[:, :cols]
        return here, weight * here + smooth_weight * (4.0 * here - beside)

    for start in range(0, rows, 8):
        _, out = image(v0_ref, w_ref[pl.ds(start, 8), :], NEAR + start, 8)
        v1_ref[pl.ds(NEAR + start, 8), own] = out

    def edge_row(weight, at):
        _, out = image(v0_ref, weight, at, 1)
        v1_ref[pl.ds(at, 1), own] = out

    pl.when(jnp.logical_not(first_row))(lambda: edge_row(top_weight, NEAR - 1))
    pl.when(jnp.logical_not(last_row))(lambda: edge_row(bottom_weight, NEAR + rows))

    lane = lax.broadcasted_iota(jnp.int32, (8, LANES), 1)
    sums = [jnp.zeros((8, cols), jnp.float32) for _ in range(4)]
    for start in range(0, rows, 8):
        weight = w_ref[pl.ds(start, 8), :]
        v0 = v0_ref[pl.ds(NEAR + start, 8), own]
        v1, v2 = image(v1_ref, weight, NEAR + start, 8)
        sums = [total + term for total, term in zip(sums, (v0 * v0, v0 * v1, v1 * v1, v1 * v2))]
        edges = jnp.zeros((8, LANES), jnp.float32)
        for k, field in enumerate((v0, v1, v2, weight)):
            edges = jnp.where(lane == k, pltpu.roll(field[:, cols - LANES :], k + 1, 1), edges)
            edges = jnp.where(lane == 4 + k, pltpu.roll(field[:, :LANES], 4 + k, 1), edges)
        edge_ref[pl.ds(start, 8), :] = edges

    result = jnp.zeros((1, LANES), jnp.float32)
    for i, total in enumerate(sums):
        narrow = sum(total[:, k : k + LANES] for k in range(0, cols, LANES))
        total = jnp.sum(jnp.sum(narrow, axis=0, keepdims=True), axis=1, keepdims=True)
        result = jnp.where(lane[:1] == i, total, result)
    out_ref[:, pl.ds(0, LANES)] = result
    vectors = edge_ref[...].T
    for k in range(VECTORS):
        out_ref[:, pl.ds((k + 1) * LANES, LANES)] = vectors[k : k + 1, :]


def coupled(parts_ref, nrows, ncols):
    count = nrows * ncols
    lam = smooth_weight

    def part(k):
        return parts_ref[:, :, pl.ds(k * LANES, LANES)].reshape(count, LANES)

    device = lax.broadcasted_iota(jnp.int32, (count, LANES), 0)
    lane = lax.broadcasted_iota(jnp.int32, (count, LANES), 1)
    joined = device % ncols < ncols - 1
    a0, a1, ua, wa = (jnp.where(joined, part(1 + k), 0.0) for k in range(4))
    b0, b1, ub, wb = (jnp.where(joined, pltpu.roll(part(5 + k), count - 1, 0), 0.0) for k in range(4))

    def next_row(field):
        inside = pltpu.roll(field, LANES - 1, 1)
        beyond = jnp.where(device < count - ncols, pltpu.roll(inside, count - ncols, 0), 0.0)
        return jnp.where(lane == LANES - 1, beyond, inside)

    def total(field):
        return jnp.sum(jnp.sum(field, axis=0, keepdims=True), axis=1, keepdims=True)

    scalars = jnp.sum(part(0), axis=0, keepdims=True)
    m0, m1, m2, m3 = (total(jnp.where(lane[:1] == i, scalars, 0.0)) for i in range(4))
    m1 = m1 - 2.0 * lam * total(a0 * b0)
    m2 = m2 + total(lam * lam * (a0 * a0 + b0 * b0) - 2.0 * lam * (a1 * b0 + b1 * a0))
    m3 = m3 + total(
        lam * lam * ((wa + 4.0 * lam) * b0 * b0 + (wb + 4.0 * lam) * a0 * a0)
        - 2.0 * lam * (b0 * ua + a0 * ub + (a1 - lam * b0) * (b1 - lam * a0))
        - 2.0 * lam * lam * lam * (a0 * next_row(a0) + b0 * next_row(b0))
    )
    return m0, m1, m2, m3


def neighbours(parts_ref, nrows, ncols):
    row, col = lax.axis_index("rows"), lax.axis_index("cols")
    lane = lax.broadcasted_iota(jnp.int32, (LANES, LANES), 1)
    vectors = []
    for vector, step_col in ((1, -1), (5, 1)):
        for step_row in (-1, 0, 1):
            r, c = row + step_row, col + step_col
            there = (r >= 0) & (r < nrows) & (c >= 0) & (c < ncols)
            index = jnp.where(there, r * ncols + c, 0)
            found = parts_ref[index, :, pl.ds(vector * LANES, LANES)]
            vectors.append(jnp.where(there, found, 0.0))
    vectors.append(jnp.zeros((LANES - len(vectors), LANES), jnp.float32))
    columns = jnp.concatenate(vectors, axis=0).T
    sides = []
    for begin, target in ((0, 0), (3, LANES - 1)):
        moved = [jnp.where(lane == target, pltpu.roll(columns, (target - begin - k) % LANES, 1), 0.0) for k in range(3)]
        sides.append(jnp.concatenate([moved[0][LANES - REACH :], moved[1], moved[2][:REACH]], axis=0))
    return sides


def halo(near_ref, far_ref, below, start, count, at_cols):
    at = pl.ds(start, count)
    one, other = (near_ref, far_ref) if below else (far_ref, near_ref)
    return jnp.where(is_even(), one[at, at_cols], other[at, at_cols])


def pair(f_ref, w_ref, near_ref, far_ref, start, count, at_cols):
    rows = f_ref.shape[0]
    for below, begin in ((False, WIDE - REACH), (True, WIDE + rows)):
        if begin <= start < begin + REACH:
            return tuple(halo(near_ref, far_ref, below, start - begin + k, count, at_cols) for k in (0, REACH))
    at = pl.ds(start - WIDE, count)
    return f_ref[at, at_cols], w_ref[at, at_cols]


def product(refs, v0_ref, at_cols, target):
    rows = refs[0].shape[0]
    v0_ref[pl.ds(0, 8), target] = halo(refs[2], refs[3], False, 2 * REACH, 8, at_cols)
    v0_ref[pl.ds(rows + 2 * WIDE - 8, 8), target] = halo(refs[2], refs[3], True, 2 * REACH, 8, at_cols)
    for start in range(8, rows + 2 * WIDE - 8, 8):
        flux, weight = pair(*refs, start, 8, at_cols)
        v0_ref[pl.ds(start, 8), target] = flux * weight


def clear_outside(refs, rows):
    first_row, last_row, _, _ = at_edges()

    def clear(start):
        for ref in refs:
            ref[pl.ds(start, REACH), :] = jnp.zeros((REACH, ref.shape[1]), jnp.bfloat16)

    pl.when(first_row)(lambda: clear(0))
    pl.when(last_row)(lambda: clear(REACH + rows))


def dot(left, right):
    return jnp.dot(left, right, preferred_element_type=jnp.float32)


def row_pass(rowtaps_ref, high, low, rows):
    first_row, last_row, _, _ = at_edges()
    table = rowtaps_ref[first_row.astype(jnp.int32) + 2 * last_row.astype(jnp.int32)]
    both = dot(table, high)
    return both[:rows] + (both[rows:] + dot(table[:rows], low))


def edges_kernel(
    nrows, ncols, parts_ref, f_ref, w_ref, near_ref, far_ref, rowtaps_ref,
    coefficients_ref, left_ref, right_ref, first_ref, last_ref, v0_ref, high_ref, low_ref,
):
    rows, cols = f_ref.shape
    refs = (f_ref, w_ref, near_ref, far_ref)
    c0, c1 = coefficients(*coupled(parts_ref, nrows, ncols))
    coefficients_ref[pl.ds(0, 8), :] = jnp.broadcast_to(c0, (8, LANES))
    coefficients_ref[pl.ds(8, 8), :] = jnp.broadcast_to(c1, (8, LANES))
    left_ref[...], right_ref[...] = neighbours(parts_ref, nrows, ncols)

    step = 16
    lane = lax.broadcasted_iota(jnp.int32, (step, 2 * LANES), 1)
    for side, begin in enumerate((0, cols - 2 * LANES)):
        target = pl.ds(side * 2 * LANES, 2 * LANES)
        product(refs, v0_ref, pl.ds(begin, 2 * LANES), target)
        at_cols = pl.ds(side * (cols - LANES), LANES)
        here_at = slice(side * LANES, side * LANES + LANES)
        wrapped = lane == side * (2 * LANES - 1)
        for start in range(8, rows + 2 * WIDE - 8, step):
            flux, weight = pair(*refs, start, step, at_cols)
            field = v0_ref[pl.ds(start, step), target]
            inner = pltpu.roll(field, 2 * LANES - 1 if side == 0 else 1, 1)
            outer = jnp.where(wrapped, 0.0, pltpu.roll(field, 1 if side == 0 else 2 * LANES - 1, 1))
            beside = v0_ref[pl.ds(start - 1, step), target] + v0_ref[pl.ds(start + 1, step), target] + inner + outer
            v0 = field[:, here_at]
            beside = beside[:, here_at] + (left_ref, right_ref)[side][pl.ds(start - 8, step), :]
            v1 = weight * v0 + smooth_weight * (4.0 * v0 - beside)
            scatter = flux - (c0 * v0 + c1 * v1)
            high, low = split_values(scatter * scatter)
            high_ref[pl.ds(start - 8, step), pl.ds(side * LANES, LANES)] = high
            low_ref[pl.ds(start - 8, step), pl.ds(side * LANES, LANES)] = low
    clear_outside((high_ref, low_ref), rows)
    passed = row_pass(rowtaps_ref, high_ref[...], low_ref[...], rows)
    first_ref[...] = passed[:, :LANES]
    last_ref[...] = passed[:, LANES:]


def main_kernel(
    coefficients_ref, left_ref, right_ref, f_ref, w_ref, near_ref, far_ref, rowtaps_ref,
    background_ref, passed_ref, v0_ref, high_ref, low_ref,
):
    rows, cols = f_ref.shape
    refs = (f_ref, w_ref, near_ref, far_ref)
    own = pl.ds(0, cols)
    c0, c1 = coefficients_ref[pl.ds(0, 1), pl.ds(0, 1)], coefficients_ref[pl.ds(8, 1), pl.ds(0, 1)]
    v0_ref[:, pl.ds(cols, LANES)] = jnp.zeros((rows + 2 * WIDE, LANES), jnp.float32)
    product(refs, v0_ref, own, own)
    step = 16
    for start in range(8, rows + 2 * WIDE - 8, step):
        flux, weight = pair(*refs, start, step, own)
        field = v0_ref[pl.ds(start, step), :]
        beside = v0_ref[pl.ds(start - 1, step), own] + v0_ref[pl.ds(start + 1, step), own] + beside_columns(field)[:, :cols]
        at = pl.ds(start - 8, step)
        beside = jnp.concatenate(
            [beside[:, :LANES] + left_ref[at, :], beside[:, LANES : cols - LANES], beside[:, cols - LANES :] + right_ref[at, :]],
            axis=1,
        )
        v0 = field[:, :cols]
        v1 = weight * v0 + smooth_weight * (4.0 * v0 - beside)
        background = c0 * v0 + c1 * v1
        if WIDE <= start < WIDE + rows:
            background_ref[pl.ds(start - WIDE, step), :] = background
        scatter = flux - background
        high_ref[at, :], low_ref[at, :] = split_values(scatter * scatter)
    clear_outside((high_ref, low_ref), rows)
    passed_ref[...] = row_pass(rowtaps_ref, high_ref[...], low_ref[...], rows)


def final_kernel(passed_ref, left_ref, right_ref, coltaps_ref, rms_ref):
    rows, cols = passed_ref.shape
    width = cols + 2 * LANES
    _, _, first_col, last_col = at_edges()
    passed = jnp.concatenate([left_ref[...], passed_ref[...], right_ref[...]], axis=1)
    passed = pltpu.roll(passed, width - (LANES - REACH), 1)
    high, low = split_values(passed)
    blocks = cols // LANES
    for j in range(blocks):
        which = 0
        if j == 0:
            which = first_col.astype(jnp.int32)
        elif j == blocks - 1:
            which = 2 * last_col.astype(jnp.int32)
        table = coltaps_ref[which]
        at = slice(j * LANES, j * LANES + 2 * LANES)
        both = dot(high[:, at], table)
        smoothed = both[:, :LANES] + (both[:, LANES:] + dot(low[:, at], table[:, :LANES]))
        rms_ref[:, pl.ds(j * LANES, LANES)] = jnp.sqrt(smoothed + 1e-06)


def shift(block, axis, step):
    count = lax.axis_size(axis)
    pairs = [(i, i + step) for i in range(count) if 0 <= i + step < count]
    return lax.ppermute(block, axis, pairs)


def swap(block, axis, first):
    count = lax.axis_size(axis)
    pairs = [(i, i + 1) for i in range(first, count - 1, 2)]
    return lax.ppermute(block, axis, pairs + [(j, i) for i, j in pairs])


def call(kernel, name, outs, scratch=(), limit=16):
    vmem = pl.BlockSpec(memory_space=pltpu.VMEM)

    def run(*args):
        return pl.pallas_call(
            kernel,
            out_shape=tuple(jax.ShapeDtypeStruct(shape, jnp.float32) for shape in outs),
            in_specs=[vmem] * len(args),
            out_specs=(vmem,) * len(outs),
            scratch_shapes=[pltpu.VMEM(shape, dtype) for shape, dtype in scratch],
            compiler_params=pltpu.CompilerParams(vmem_limit_bytes=limit << 20),
            name=name,
        )(*args)

    return run


def shards(coadd_flux, inverse_variance, source_mask):
    rows, cols = coadd_flux.shape
    nrows, ncols = lax.axis_size("rows"), lax.axis_size("cols")
    message = (VECTORS + 1) * LANES
    f32, bf16 = jnp.float32, jnp.bfloat16

    begin = jnp.where(is_even(), 0, rows - NEAR)
    flux, variance, mask = (
        lax.dynamic_slice(x, (begin, 0), (NEAR, cols)) for x in (coadd_flux, inverse_variance, source_mask)
    )
    narrow = swap(jnp.concatenate([flux, weights(variance, mask)]), "rows", 1)

    own = (coadd_flux, weights(inverse_variance, source_mask))
    wide = (2 * REACH + 8, cols)
    to_near, to_far = call(wide_kernel, "wide", (wide, wide))(*own)
    to_near, to_far, narrow = lax.optimization_barrier((to_near, to_far, narrow))
    near = swap(to_near, "rows", 0)
    far = swap(to_far, "rows", 1)

    field = ((rows + 2 * NEAR, cols + LANES), f32)
    (parts,) = call(moments_kernel, "moments", ((1, message),), (field, field, ((rows, LANES), f32)))(*own, narrow, near)
    parts = jnp.broadcast_to(parts[None], (nrows * ncols, 1, message))
    parts = lax.all_to_all(parts, ("rows", "cols"), 0, 0, tiled=True)

    row_taps, col_taps = jnp.asarray(row_tables(rows)), jnp.asarray(col_tables())
    column, reached, block = (rows + 2 * REACH, LANES), rows + 2 * REACH, (rows, LANES)
    numbers, left, right, first, last = call(
        functools.partial(edges_kernel, nrows, ncols),
        "edges",
        ((16, LANES), column, column, block, block),
        (((rows + 2 * WIDE, 4 * LANES), f32),) + (((reached, 2 * LANES), bf16),) * 2,
    )(parts, *own, near, far, row_taps)
    from_left = shift(last, "cols", 1)
    from_right = shift(first, "cols", -1)
    background, passed = call(
        main_kernel,
        "main",
        ((rows, cols), (rows, cols)),
        (((rows + 2 * WIDE, cols + LANES), f32),) + (((reached, cols), bf16),) * 2,
        32,
    )(numbers, left, right, *own, near, far, row_taps)
    (rms,) = call(final_kernel, "final", ((rows, cols),))(passed, from_left, from_right, col_taps)
    return background, rms


def solution(mesh):
    return jax.shard_map(
        shards,
        mesh=mesh,
        in_specs=(P("rows", "cols"), P("rows", "cols"), P("rows", "cols")),
        out_specs=(P("rows", "cols"), P("rows", "cols")),
        check_vma=False,
    )
```

time: 53.2 us -> 40.6 us (0.76)
  blocking collectives: 24.3 us -> 0 us
  waiting for transfers between devices: 6.46 us -> 12.4 us
  starting transfers between devices: 15.6 us -> 18.1 us
  Pallas kernels: 4.17 us -> 6.14 us
  other arithmetic: 1.45 us -> 2.11 us
  local copies, waits for them, and re-layouts: 0.14 us -> 0.75 us
    all_to_all x1 -> x0, blocking collectives: 24.3 us -> none  [shards(): parts = lax.all_to_all(parts, ('rows', 'cols'), 0, 0, tiled=True)]
    ppermute x6 -> x2, starting transfers between devices: 15.6 us -> 3.82 us  [shift(): return lax.ppermute(block, axis, pairs)]
    all_to_all x0 -> x1, waiting for transfers between devices: none -> 8.62 us  [shards(): parts = lax.all_to_all(parts, ('rows', 'cols'), 0, 0, tiled=True)]
    all_to_all x0 -> x1, starting transfers between devices: none -> 7.96 us  [shards(): parts = lax.all_to_all(parts, ('rows', 'cols'), 0, 0, tiled=True)]
    ppermute x0 -> x3, starting transfers between devices: none -> 6.32 us  [swap(): return lax.ppermute(block, axis, pairs + [(j, i) for i, j in pairs])]
    ppermute x6 -> x2, waiting for transfers between devices: 6.46 us -> 2.9 us  [shift(): return lax.ppermute(block, axis, pairs)]
    pallas_call x2 -> x5, Pallas kernels: 4.17 us -> 6.14 us  [run(): pl.pallas_call(kernel, out_shape=tuple((jax.ShapeDtypeStruct(shape, jnp.f...]
    ppermute x0 -> x3, waiting for transfers between devices: none -> 0.9 us  [swap(): return lax.ppermute(block, axis, pairs + [(j, i) for i, j in pairs])]
  transfers between devices with their start and end apart: 6 -> 6, of which waited for: 3 -> 3; matrix products, arithmetic and copies ran while one was open for 0% -> 5% of each run, Pallas kernels for 2% -> 10%
where the time goes in v6:
time: 40.6 us; the launch traced here: 40.3 us
  starting transfers between devices  18.1 us (45%)
  waiting for transfers between devices  12.4 us (31%)
  Pallas kernels  6.14 us (15%)
  other arithmetic  2.11 us (5%)
  between operations  0.76 us (2%)
  local copies, waits for them, and re-layouts  0.75 us (2%)
    all_to_all x1, waiting for transfers between devices, shards(): parts = lax.all_to_all(parts, ('rows', 'cols'), 0, 0, tiled=True)  8.62 us
    all_to_all x1, starting transfers between devices, shards(): parts = lax.all_to_all(parts, ('rows', 'cols'), 0, 0, tiled=True)  7.96 us
    ppermute x3, starting transfers between devices, swap(): return lax.ppermute(block, axis, pairs + [(j, i) for i, j in pairs])  6.32 us
    pallas_call x5, Pallas kernels, run(): pl.pallas_call(kernel, out_shape=tuple((jax.ShapeDtypeStruct(shape, jnp.f...  6.14 us
    ppermute x2, starting transfers between devices, shift(): return lax.ppermute(block, axis, pairs)  3.82 us
    ppermute x2, waiting for transfers between devices, shift(): return lax.ppermute(block, axis, pairs)  2.9 us
    mul x2, other arithmetic, weights(): return inverse_variance * (1.0 - source_mask.astype(jnp.float32))  2.07 us
    ppermute x3, waiting for transfers between devices, swap(): return lax.ppermute(block, axis, pairs + [(j, i) for i, j in pairs])  0.9 us
  transfers between devices with their start and end apart: 6, of which 3 were waited for; matrix products, arithmetic and copies ran while one was open for 5% of the time, Pallas kernels for 10%

profile of v6, /device:TPU:0, one launch (start us, length us, event | category | flops | bytes accessed | tf_op | source)
XLA Modules:
  0.0 40.3 jit_solution(11102299645199011894)
XLA Ops:
  0.6 0.8 %subtract_multiply_fusion.1 = (f32[8,1024]{1,0:T(8,128)S(1)}, f32[8,1024]{1,0:T(8,128)S(1)}) fusion(s32[128,1024]{1,0:T(8,128)} %param.7, s32[]{:T(128)S(6)} %select_n.15, f32[128,1024]{1,0:T(8,128)} %param.6, f32[128,1024]{1,0:T(8,128)} %f_ref.7), kind=kLoop, calls=%fused_computation.2 | loop fusion | flops 24576 | bytes 163844 | tf_op jit(solution)/shard_map/mul | solution.py:87
  1.5 0.0 copy-start
  1.5 0.8 %collective-permute-start = (f32[16,1024]{1,0:T(8,128)S(1)}, f32[16,1024]{1,0:T(8,128)S(1)}, u32[]{:S(2)}, u32[]{:S(2)}) collective-permute-start(f32[16,1024]{1,0:T(8,128)S(1)} %pad_maximum_fusion), channel_id=1, source_target_pairs={{4,8},{12,16},{20,24},{8,4},{16,12},{24,20},{5,9},{13,17},{21,25},... | collective-permute-start | bytes 196616 | tf_op jit(solution)/shard_map/ppermute | solution.py:382
  2.3 1.3 %subtract_multiply_fusion.w_ref = f32[128,1024]{1,0:T(8,128)S(1)} fusion(f32[128,1024]{1,0:T(8,128)} %param.6, s32[128,1024]{1,0:T(8,128)} %param.7), kind=kLoop, calls=%fused_computation | loop fusion | flops 393216 | bytes 1572864 | tf_op jit(solution)/shard_map/mul | solution.py:87
  3.5 0.0 copy-done
  3.6 0.1 wide.1
  3.7 0.0 collective-permute-done.far_ref
  3.7 4.8 %collective-permute-start.1 = (f32[136,1024]{1,0:T(8,128)S(1)}, f32[136,1024]{1,0:T(8,128)S(1)}, u32[]{:S(2)}, u32[]{:S(2)}) collective-permute-start(f32[136,1024]{1,0:T(8,128)S(1)} %get-tuple-element.17), channel_id=1, source_target_pairs={{0,4},{8,12},{16,20},{24,28},{4,0},{12,8},{20,16},{28,24},{1,5},{9... | collective-permute-start | bytes 1671176 | tf_op jit(solution)/shard_map/ppermute | solution.py:382
  8.5 0.7 %collective-permute-start.2 = (f32[136,1024]{1,0:T(8,128)S(1)}, f32[136,1024]{1,0:T(8,128)S(1)}, u32[]{:S(2)}, u32[]{:S(2)}) collective-permute-start(f32[136,1024]{1,0:T(8,128)S(1)} %get-tuple-element.18), channel_id=1, source_target_pairs={{4,8},{12,16},{20,24},{8,4},{16,12},{24,20},{5,9},{13,17},{21,25},... | collective-permute-start | bytes 1671176 | tf_op jit(solution)/shard_map/ppermute | solution.py:382
  9.2 0.9 %collective-permute-done.1.near_ref = f32[136,1024]{1,0:T(8,128)S(1)} collective-permute-done((f32[136,1024]{1,0:T(8,128)S(1)}, f32[136,1024]{1,0:T(8,128)S(1)}, u32[]{:S(2)}, u32[]{:S(2)}) %collective-permute-start.1) | collective-permute-done | bytes 557088 | tf_op jit(solution)/shard_map/ppermute | solution.py:382
  10.1 0.0 copy-start.1
  10.1 1.9 %moments.1 = f32[1,1152]{1,0:T(1,128)S(1)} custom-call(f32[128,1024]{1,0:T(8,128)S(1)} %copy-done, f32[128,1024]{1,0:T(8,128)S(1)} %subtract_multiply_fusion.w_ref, f32[16,1024]{1,0:T(8,128)S(1)} %collective-permute-done.far_ref, f32[136,1024]{1,0:T(8,128)S(1)} %collective-permute-done.1.near_ref), custom_call_target="tpu_custom_call" | custom-call | tf_op jit(solution)/shard_map/moments/pallas_call | solution.py:389
  12.0 0.7 %broadcast_in_dim.9 = f32[32,1,1152]{2,1,0:T(1,128)} broadcast(f32[1152]{0:T(1024)S(1)} %reduce), dimensions={2} | broadcast | bytes 152064 | tf_op jit(solution)/shard_map/broadcast_in_dim | solution.py:423
  12.8 8.0 %all-to-all-start = ((f32[32,1,1152]{2,1,0:T(1,128)}), f32[32,1,1152]{2,1,0:T(1,128)S(1)}, u32[]{:S(2)}, u32[]{:S(2)}) async-start(f32[32,1,1152]{2,1,0:T(1,128)} %broadcast_in_dim.9), calls=%async_computation | async-start | bytes 294912 | tf_op jit(solution)/shard_map/all_to_all | solution.py:424
  20.7 0.0 collective-permute-done.2.far_ref
  20.8 8.6 %all-to-all-done.parts_ref = f32[32,1,1152]{2,1,0:T(1,128)S(1)} async-done(((f32[32,1,1152]{2,1,0:T(1,128)}), f32[32,1,1152]{2,1,0:T(1,128)S(1)}, u32[]{:S(2)}, u32[]{:S(2)}) %all-to-all-start) | async-done | bytes 147488 | tf_op jit(solution)/shard_map/all_to_all | solution.py:424
  29.4 0.0 copy-done.1
  29.4 0.9 %edges.1 = (f32[16,128]{1,0:T(8,128)S(1)}, f32[256,128]{1,0:T(8,128)S(1)}, f32[256,128]{1,0:T(8,128)S(1)}, f32[128,128]{1,0:T(8,128)S(1)}, f32[128,128]{1,0:T(8,128)S(1)}) custom-call(f32[32,1,1152]{2,1,0:T(1,128)S(1)} %all-to-all-done.parts_ref, f32[128,1024]{1,0:T(8,128)S(1)} %copy-done, f32[128,1024]{1,0:T(8,128)S(1)} %subtract_multiply_fusion.w_ref, ...), custom_call_target="tpu_custom_call" | custom-call | tf_op jit(solution)/shard_map/edges/pallas_call | solution.py:389
  30.3 2.5 %collective-permute-start.3 = (f32[128,128]{1,0:T(8,128)S(1)}, f32[128,128]{1,0:T(8,128)S(1)}, u32[]{:S(2)}, u32[]{:S(2)}) collective-permute-start(f32[128,128]{1,0:T(8,128)S(1)} %get-tuple-element.24), channel_id=1, source_target_pairs={{0,1},{1,2},{2,3},{4,5},{5,6},{6,7},{8,9},{9,10},{10,11},{12,13},{... | collective-permute-start | bytes 196616 | tf_op jit(solution)/shard_map/ppermute | solution.py:376
  32.8 1.3 %collective-permute-start.4 = (f32[128,128]{1,0:T(8,128)S(1)}, f32[128,128]{1,0:T(8,128)S(1)}, u32[]{:S(2)}, u32[]{:S(2)}) collective-permute-start(f32[128,128]{1,0:T(8,128)S(1)} %get-tuple-element.25), channel_id=1, source_target_pairs={{1,0},{2,1},{3,2},{5,4},{6,5},{7,6},{9,8},{10,9},{11,10},{13,12},{... | collective-permute-start | bytes 196616 | tf_op jit(solution)/shard_map/ppermute | solution.py:376
  34.1 0.0 copy-start.2
  34.1 1.9 %main.1 = (f32[128,1024]{1,0:T(8,128)}, f32[128,1024]{1,0:T(8,128)S(1)}) custom-call(f32[16,128]{1,0:T(8,128)S(1)} %get-tuple-element.19.coefficients_ref, f32[256,128]{1,0:T(8,128)S(1)} %get-tuple-element.20.left_ref, f32[256,128]{1,0:T(8,128)S(1)} %get-tuple-element.21.right_ref, f32[128,1024]{1,0:T(8,128)S(1)} %copy-done, ...), custom_call_target="tpu_custom_call" | custom-call | tf_op jit(solution)/shard_map/main/pallas_call | solution.py:389
  36.1 0.0 collective-permute-done.3.left_ref
  36.1 2.9 %collective-permute-done.4.right_ref = f32[128,128]{1,0:T(8,128)S(1)} collective-permute-done((f32[128,128]{1,0:T(8,128)S(1)}, f32[128,128]{1,0:T(8,128)S(1)}, u32[]{:S(2)}, u32[]{:S(2)}) %collective-permute-start.4) | collective-permute-done | bytes 65568 | tf_op jit(solution)/shard_map/ppermute | solution.py:376
  39.0 0.0 copy-done.2
  39.0 1.3 %final.1 = f32[128,1024]{1,0:T(8,128)} custom-call(f32[128,1024]{1,0:T(8,128)S(1)} %get-tuple-element.23.passed_ref, f32[128,128]{1,0:T(8,128)S(1)} %collective-permute-done.3.left_ref, f32[128,128]{1,0:T(8,128)S(1)} %collective-permute-done.4.right_ref, bf16[3,256,256]{2,1,0:T(8,128)(2,1)S(1)} %copy-done.2), custom_call_target="tpu_custom_call" | custom-call | tf_op jit(solution)/shard_map/final/pallas_call | solution.py:389
  (2 shorter events, 0.0 us)
Async XLA Ops:
  1.5 2.1 %copy-start = (f32[128,1024]{1,0:T(8,128)S(1)}, f32[128,1024]{1,0:T(8,128)}, u32[]{:S(2)}) copy-start(f32[128,1024]{1,0:T(8,128)} %f_ref.7) | copy-start | bytes 1572868
  1.5 2.2 %collective-permute-start = (f32[16,1024]{1,0:T(8,128)S(1)}, f32[16,1024]{1,0:T(8,128)S(1)}, u32[]{:S(2)}, u32[]{:S(2)}) collective-permute-start(f32[16,1024]{1,0:T(8,128)S(1)} %pad_maximum_fusion), channel_id=1, source_target_pairs={{4,8},{12,16},{20,24},{8,4},{16,12},{24,20},{5,9},{13,17},{21,25},... | collective-permute-start | bytes 196616 | tf_op jit(solution)/shard_map/ppermute | solution.py:382
  3.7 6.4 %collective-permute-start.1 = (f32[136,1024]{1,0:T(8,128)S(1)}, f32[136,1024]{1,0:T(8,128)S(1)}, u32[]{:S(2)}, u32[]{:S(2)}) collective-permute-start(f32[136,1024]{1,0:T(8,128)S(1)} %get-tuple-element.17), channel_id=1, source_target_pairs={{0,4},{8,12},{16,20},{24,28},{4,0},{12,8},{20,16},{28,24},{1,5},{9... | collective-permute-start | bytes 1671176 | tf_op jit(solution)/shard_map/ppermute | solution.py:382
  8.5 12.2 %collective-permute-start.2 = (f32[136,1024]{1,0:T(8,128)S(1)}, f32[136,1024]{1,0:T(8,128)S(1)}, u32[]{:S(2)}, u32[]{:S(2)}) collective-permute-start(f32[136,1024]{1,0:T(8,128)S(1)} %get-tuple-element.18), channel_id=1, source_target_pairs={{4,8},{12,16},{20,24},{8,4},{16,12},{24,20},{5,9},{13,17},{21,25},... | collective-permute-start | bytes 1671176 | tf_op jit(solution)/shard_map/ppermute | solution.py:382
  10.1 19.3 %copy-start.1 = (bf16[4,256,256]{2,1,0:T(8,128)(2,1)S(1)}, bf16[4,256,256]{2,1,0:T(8,128)(2,1)}, u32[]{:S(2)}) copy-start(bf16[4,256,256]{2,1,0:T(8,128)(2,1)} %constant.31.clone.rowtaps_ref) | copy-start | bytes 1572868
  12.8 16.6 %all-to-all-start = ((f32[32,1,1152]{2,1,0:T(1,128)}), f32[32,1,1152]{2,1,0:T(1,128)S(1)}, u32[]{:S(2)}, u32[]{:S(2)}) async-start(f32[32,1,1152]{2,1,0:T(1,128)} %broadcast_in_dim.9), calls=%async_computation | async-start | bytes 294912 | tf_op jit(solution)/shard_map/all_to_all | solution.py:424
  30.3 5.8 %collective-permute-start.3 = (f32[128,128]{1,0:T(8,128)S(1)}, f32[128,128]{1,0:T(8,128)S(1)}, u32[]{:S(2)}, u32[]{:S(2)}) collective-permute-start(f32[128,128]{1,0:T(8,128)S(1)} %get-tuple-element.24), channel_id=1, source_target_pairs={{0,1},{1,2},{2,3},{4,5},{5,6},{6,7},{8,9},{9,10},{10,11},{12,13},{... | collective-permute-start | bytes 196616 | tf_op jit(solution)/shard_map/ppermute | solution.py:376
  32.8 6.2 %collective-permute-start.4 = (f32[128,128]{1,0:T(8,128)S(1)}, f32[128,128]{1,0:T(8,128)S(1)}, u32[]{:S(2)}, u32[]{:S(2)}) collective-permute-start(f32[128,128]{1,0:T(8,128)S(1)} %get-tuple-element.25), channel_id=1, source_target_pairs={{1,0},{2,1},{3,2},{5,4},{6,5},{7,6},{9,8},{10,9},{11,10},{13,12},{... | collective-permute-start | bytes 196616 | tf_op jit(solution)/shard_map/ppermute | solution.py:376
  34.1 4.9 %copy-start.2 = (bf16[3,256,256]{2,1,0:T(8,128)(2,1)S(1)}, bf16[3,256,256]{2,1,0:T(8,128)(2,1)}, u32[]{:S(2)}) copy-start(bf16[3,256,256]{2,1,0:T(8,128)(2,1)} %constant.32.clone.coltaps_ref) | copy-start | bytes 1179652

commit v7 on v6

--- a/solution.py
+++ b/solution.py
@@ -96,39 +96,46 @@
     return alpha0 + alpha1 * grown, -alpha1 * alpha0
 
 
-def wide_kernel(f_ref, w_ref, near_ref, far_ref):
+def prepare_kernel(f_ref, iv_ref, mask_ref, w_ref, near_ref, far_ref):
     rows = f_ref.shape[0]
-
-    def write(out_ref, begin, beyond):
+    w_ref[...] = weights(iv_ref[...], mask_ref[...])
+
+    def write(out_ref, begin):
         out_ref[pl.ds(0, REACH), :] = f_ref[pl.ds(begin, REACH), :]
         out_ref[pl.ds(REACH, REACH), :] = w_ref[pl.ds(begin, REACH), :]
-        out_ref[pl.ds(2 * REACH, 8), :] = f_ref[pl.ds(beyond, 8), :] * w_ref[pl.ds(beyond, 8), :]
+
+    def near_product(begin):
+        near_ref[pl.ds(2 * REACH, 8), :] = f_ref[pl.ds(begin, 8), :] * w_ref[pl.ds(begin, 8), :]
 
     @pl.when(is_even())
     def _():
-        write(near_ref, rows - REACH, rows - WIDE)
-        write(far_ref, 0, REACH)
+        write(near_ref, rows - REACH)
+        near_product(rows - WIDE)
+        write(far_ref, 0)
 
     @pl.when(jnp.logical_not(is_even()))
     def _():
-        write(near_ref, 0, REACH)
-        write(far_ref, rows - REACH, rows - WIDE)
-
-
-def moments_kernel(f_ref, w_ref, far_ref, near_ref, out_ref, v0_ref, v1_ref, edge_ref):
+        write(near_ref, 0)
+        near_product(REACH)
+        write(far_ref, rows - REACH)
+
+
+def moments_kernel(f_ref, w_ref, narrow_ref, near_ref, out_ref, v0_ref, v1_ref, edge_ref):
     rows, cols = f_ref.shape
     width = cols + LANES
     first_row, last_row, _, _ = at_edges()
     even = is_even()
     own, pad = pl.ds(0, cols), pl.ds(cols, LANES)
 
-    far_weight = far_ref[pl.ds(8, 8), :]
-    far_v0 = far_ref[pl.ds(0, 8), :] * far_weight
     above, below = near_ref[pl.ds(2 * REACH - 8, 8), :], near_ref[pl.ds(REACH, 8), :]
-    top = jnp.where(even, far_v0, near_ref[pl.ds(REACH - 8, 8), :] * above)
-    bottom = jnp.where(even, near_ref[pl.ds(0, 8), :] * below, far_v0)
-    top_weight = jnp.where(even, far_weight, above)[7:]
-    bottom_weight = jnp.where(even, below, far_weight)[:1]
+    nothing = jnp.zeros((6, cols), jnp.float32)
+    nearest, second, far_weight = (narrow_ref[pl.ds(k, 1), :] for k in range(3))
+    far_above = jnp.concatenate([nothing, second, nearest], axis=0)
+    far_below = jnp.concatenate([nearest, second, nothing], axis=0)
+    top = jnp.where(even, far_above, near_ref[pl.ds(REACH - 8, 8), :] * above)
+    bottom = jnp.where(even, near_ref[pl.ds(0, 8), :] * below, far_below)
+    top_weight = jnp.where(even, far_weight, above[7:])
+    bottom_weight = jnp.where(even, below[:1], far_weight)
 
     for ref in (v0_ref, v1_ref):
         ref[:, pad] = jnp.zeros((rows + 2 * NEAR, LANES), jnp.float32)
@@ -175,10 +182,10 @@
         narrow = sum(total[:, k : k + LANES] for k in range(0, cols, LANES))
         total = jnp.sum(jnp.sum(narrow, axis=0, keepdims=True), axis=1, keepdims=True)
         result = jnp.where(lane[:1] == i, total, result)
-    out_ref[:, pl.ds(0, LANES)] = result
     vectors = edge_ref[...].T
-    for k in range(VECTORS):
-        out_ref[:, pl.ds((k + 1) * LANES, LANES)] = vectors[k : k + 1, :]
+    message = jnp.concatenate([result] + [vectors[k : k + 1, :] for k in range(VECTORS)], axis=1)
+    for k in range(out_ref.shape[0]):
+        out_ref[k] = message
 
 
 def coupled(parts_ref, nrows, ncols):
@@ -240,7 +247,13 @@
     return jnp.where(is_even(), one[at, at_cols], other[at, at_cols])
 
 
-def pair(f_ref, w_ref, near_ref, far_ref, start, count, at_cols):
+def last_row(near_ref, narrow_ref, below, at_cols):
+    near = near_ref[pl.ds(2 * REACH + (0 if below else 7), 1), at_cols]
+    far = narrow_ref[pl.ds(3, 1), at_cols]
+    return jnp.where(is_even(), near, far) if below else jnp.where(is_even(), far, near)
+
+
+def pair(f_ref, w_ref, near_ref, far_ref, narrow_ref, start, count, at_cols):
     rows = f_ref.shape[0]
     for below, begin in ((False, WIDE - REACH), (True, WIDE + rows)):
         if begin <= start < begin + REACH:
@@ -251,8 +264,8 @@
 
 def product(refs, v0_ref, at_cols, target):
     rows = refs[0].shape[0]
-    v0_ref[pl.ds(0, 8), target] = halo(refs[2], refs[3], False, 2 * REACH, 8, at_cols)
-    v0_ref[pl.ds(rows + 2 * WIDE - 8, 8), target] = halo(refs[2], refs[3], True, 2 * REACH, 8, at_cols)
+    v0_ref[pl.ds(7, 1), target] = last_row(refs[2], refs[4], False, at_cols)
+    v0_ref[pl.ds(rows + 2 * WIDE - 8, 1), target] = last_row(refs[2], refs[4], True, at_cols)
     for start in range(8, rows + 2 * WIDE - 8, 8):
         flux, weight = pair(*refs, start, 8, at_cols)
         v0_ref[pl.ds(start, 8), target] = flux * weight
@@ -281,11 +294,11 @@
 
 
 def edges_kernel(
-    nrows, ncols, parts_ref, f_ref, w_ref, near_ref, far_ref, rowtaps_ref,
+    nrows, ncols, parts_ref, f_ref, w_ref, near_ref, far_ref, narrow_ref, rowtaps_ref,
     coefficients_ref, left_ref, right_ref, first_ref, last_ref, v0_ref, high_ref, low_ref,
 ):
     rows, cols = f_ref.shape
-    refs = (f_ref, w_ref, near_ref, far_ref)
+    refs = (f_ref, w_ref, near_ref, far_ref, narrow_ref)
     c0, c1 = coefficients(*coupled(parts_ref, nrows, ncols))
     coefficients_ref[pl.ds(0, 8), :] = jnp.broadcast_to(c0, (8, LANES))
     coefficients_ref[pl.ds(8, 8), :] = jnp.broadcast_to(c1, (8, LANES))
@@ -314,16 +327,19 @@
             low_ref[pl.ds(start - 8, step), pl.ds(side * LANES, LANES)] = low
     clear_outside((high_ref, low_ref), rows)
     passed = row_pass(rowtaps_ref, high_ref[...], low_ref[...], rows)
-    first_ref[...] = passed[:, :LANES]
-    last_ref[...] = passed[:, LANES:]
+    upper, lower = slice(0, rows // 2), slice(rows // 2, rows)
+    first, last = passed[:, :LANES], passed[:, LANES:]
+    on_left = lax.broadcasted_iota(jnp.int32, (rows // 2, LANES), 1) < REACH
+    first_ref[...] = jnp.where(on_left, first[upper], pltpu.roll(first[lower], REACH, 1))
+    last_ref[...] = jnp.where(on_left, pltpu.roll(last[upper], REACH, 1), last[lower])
 
 
 def main_kernel(
-    coefficients_ref, left_ref, right_ref, f_ref, w_ref, near_ref, far_ref, rowtaps_ref,
-    background_ref, passed_ref, v0_ref, high_ref, low_ref,
+    coefficients_ref, left_ref, right_ref, f_ref, w_ref, near_ref, far_ref, narrow_ref, rowtaps_ref, coltaps_ref,
+    background_ref, rms_ref, sides_ref, v0_ref, high_ref, low_ref,
 ):
     rows, cols = f_ref.shape
-    refs = (f_ref, w_ref, near_ref, far_ref)
+    refs = (f_ref, w_ref, near_ref, far_ref, narrow_ref)
     own = pl.ds(0, cols)
     c0, c1 = coefficients_ref[pl.ds(0, 1), pl.ds(0, 1)], coefficients_ref[pl.ds(8, 1), pl.ds(0, 1)]
     v0_ref[:, pl.ds(cols, LANES)] = jnp.zeros((rows + 2 * WIDE, LANES), jnp.float32)
@@ -346,28 +362,42 @@
         scatter = flux - background
         high_ref[at, :], low_ref[at, :] = split_values(scatter * scatter)
     clear_outside((high_ref, low_ref), rows)
-    passed_ref[...] = row_pass(rowtaps_ref, high_ref[...], low_ref[...], rows)
-
-
-def final_kernel(passed_ref, left_ref, right_ref, coltaps_ref, rms_ref):
-    rows, cols = passed_ref.shape
-    width = cols + 2 * LANES
+    passed = row_pass(rowtaps_ref, high_ref[...], low_ref[...], rows)
+    sides_ref[:, pl.ds(0, 2 * LANES)] = passed[:, : 2 * LANES]
+    sides_ref[:, pl.ds(2 * LANES, 2 * LANES)] = passed[:, cols - 2 * LANES :]
+    high, low = split_values(pltpu.roll(passed, REACH, 1))
+    for j in range(1, cols // LANES - 1):
+        at = slice(j * LANES, j * LANES + 2 * LANES)
+        rms_ref[:, pl.ds(j * LANES, LANES)] = column_pass(coltaps_ref[0], high[:, at], low[:, at])
+
+
+def column_pass(table, high, low):
+    both = dot(high, table)
+    smoothed = both[:, :LANES] + (both[:, LANES:] + dot(low, table[:, :LANES]))
+    return jnp.sqrt(smoothed + 1e-06)
+
+
+def final_kernel(rms_in_ref, sides_ref, left_ref, right_ref, coltaps_ref, rms_ref, blocks_ref, sems):
+    rows, cols = rms_ref.shape
+    del rms_in_ref
     _, _, first_col, last_col = at_edges()
-    passed = jnp.concatenate([left_ref[...], passed_ref[...], right_ref[...]], axis=1)
-    passed = pltpu.roll(passed, width - (LANES - REACH), 1)
-    high, low = split_values(passed)
-    blocks = cols // LANES
-    for j in range(blocks):
-        which = 0
-        if j == 0:
-            which = first_col.astype(jnp.int32)
-        elif j == blocks - 1:
-            which = 2 * last_col.astype(jnp.int32)
-        table = coltaps_ref[which]
-        at = slice(j * LANES, j * LANES + 2 * LANES)
-        both = dot(high[:, at], table)
-        smoothed = both[:, :LANES] + (both[:, LANES:] + dot(low[:, at], table[:, :LANES]))
-        rms_ref[:, pl.ds(j * LANES, LANES)] = jnp.sqrt(smoothed + 1e-06)
+    left, right = left_ref[...], right_ref[...]
+    left = jnp.concatenate([pltpu.roll(left, REACH, 1), left], axis=0)
+    right = jnp.concatenate([right, pltpu.roll(right, REACH, 1)], axis=0)
+    sides = sides_ref[...]
+    windows = (
+        pltpu.roll(jnp.concatenate([left, sides[:, : 2 * LANES]], axis=1), 3 * LANES - REACH, 1)[:, : 2 * LANES],
+        pltpu.roll(jnp.concatenate([sides[:, 2 * LANES :], right], axis=1), 3 * LANES - REACH, 1)[:, : 2 * LANES],
+    )
+    copies = []
+    for side, which in enumerate((first_col.astype(jnp.int32), 2 * last_col.astype(jnp.int32))):
+        high, low = split_values(windows[side])
+        blocks_ref[side] = column_pass(coltaps_ref[which], high, low)
+        target = rms_ref.at[:, pl.ds(side * (cols - LANES), LANES)]
+        copies.append(pltpu.make_async_copy(blocks_ref.at[side], target, sems.at[side]))
+        copies[-1].start()
+    for copy in copies:
+        copy.wait()
 
 
 def shift(block, axis, step):
@@ -382,16 +412,18 @@
     return lax.ppermute(block, axis, pairs + [(j, i) for i, j in pairs])
 
 
-def call(kernel, name, outs, scratch=(), limit=16):
+def call(kernel, name, outs, scratch=(), limit=16, in_place=False):
     vmem = pl.BlockSpec(memory_space=pltpu.VMEM)
+    there = pl.BlockSpec(memory_space=pl.ANY)
 
     def run(*args):
         return pl.pallas_call(
             kernel,
             out_shape=tuple(jax.ShapeDtypeStruct(shape, jnp.float32) for shape in outs),
-            in_specs=[vmem] * len(args),
-            out_specs=(vmem,) * len(outs),
-            scratch_shapes=[pltpu.VMEM(shape, dtype) for shape, dtype in scratch],
+            in_specs=[there if in_place and i == 0 else vmem for i in range(len(args))],
+            out_specs=(there if in_place else vmem,) * len(outs),
+            scratch_shapes=list(scratch),
+            input_output_aliases={0: 0} if in_place else {},
             compiler_params=pltpu.CompilerParams(vmem_limit_bytes=limit << 20),
             name=name,
         )(*args)
@@ -403,44 +435,55 @@
     rows, cols = coadd_flux.shape
     nrows, ncols = lax.axis_size("rows"), lax.axis_size("cols")
     message = (VECTORS + 1) * LANES
-    f32, bf16 = jnp.float32, jnp.bfloat16
-
-    begin = jnp.where(is_even(), 0, rows - NEAR)
-    flux, variance, mask = (
-        lax.dynamic_slice(x, (begin, 0), (NEAR, cols)) for x in (coadd_flux, inverse_variance, source_mask)
-    )
-    narrow = swap(jnp.concatenate([flux, weights(variance, mask)]), "rows", 1)
-
-    own = (coadd_flux, weights(inverse_variance, source_mask))
-    wide = (2 * REACH + 8, cols)
-    to_near, to_far = call(wide_kernel, "wide", (wide, wide))(*own)
+
+    def scratch(*shape, dtype=jnp.float32):
+        return pltpu.VMEM(shape, dtype)
+
+    taken = []
+    for above, below in ((0, rows - 1), (1, rows - 2), (REACH, rows - 1 - REACH)):
+        start = (jnp.where(is_even(), above, below), 0)
+        flux, variance, mask = (
+            lax.dynamic_slice(x, start, (1, cols)) for x in (coadd_flux, inverse_variance, source_mask)
+        )
+        taken.append((flux, weights(variance, mask)))
+    products = [flux * weight for flux, weight in taken]
+    narrow = swap(jnp.concatenate([products[0], products[1], taken[0][1], products[2]]), "rows", 1)
+
+    weight, to_near, to_far = call(
+        prepare_kernel, "prepare", ((rows, cols), (2 * REACH + 8, cols), (2 * REACH, cols))
+    )(coadd_flux, inverse_variance, source_mask)
+    own = (coadd_flux, weight)
     to_near, to_far, narrow = lax.optimization_barrier((to_near, to_far, narrow))
     near = swap(to_near, "rows", 0)
     far = swap(to_far, "rows", 1)
 
-    field = ((rows + 2 * NEAR, cols + LANES), f32)
-    (parts,) = call(moments_kernel, "moments", ((1, message),), (field, field, ((rows, LANES), f32)))(*own, narrow, near)
-    parts = jnp.broadcast_to(parts[None], (nrows * ncols, 1, message))
+    field = scratch(rows + 2 * NEAR, cols + LANES)
+    (parts,) = call(
+        moments_kernel, "moments", ((nrows * ncols, 1, message),), (field, field, scratch(rows, LANES))
+    )(*own, narrow, near)
     parts = lax.all_to_all(parts, ("rows", "cols"), 0, 0, tiled=True)
 
     row_taps, col_taps = jnp.asarray(row_tables(rows)), jnp.asarray(col_tables())
-    column, reached, block = (rows + 2 * REACH, LANES), rows + 2 * REACH, (rows, LANES)
+    halos = (near, far, narrow)
+    reached, packed = rows + 2 * REACH, (rows // 2, LANES)
     numbers, left, right, first, last = call(
         functools.partial(edges_kernel, nrows, ncols),
         "edges",
-        ((16, LANES), column, column, block, block),
-        (((rows + 2 * WIDE, 4 * LANES), f32),) + (((reached, 2 * LANES), bf16),) * 2,
-    )(parts, *own, near, far, row_taps)
+        ((16, LANES), (reached, LANES), (reached, LANES), packed, packed),
+        (scratch(rows + 2 * WIDE, 4 * LANES),) + (scratch(reached, 2 * LANES, dtype=jnp.bfloat16),) * 2,
+    )(parts, *own, *halos, row_taps)
     from_left = shift(last, "cols", 1)
     from_right = shift(first, "cols", -1)
-    background, passed = call(
+    background, rms, sides = call(
         main_kernel,
         "main",
-        ((rows, cols), (rows, cols)),
-        (((rows + 2 * WIDE, cols + LANES), f32),) + (((reached, cols), bf16),) * 2,
+        ((rows, cols), (rows, cols), (rows, 4 * LANES)),
+        (scratch(rows + 2 * WIDE, cols + LANES),) + (scratch(reached, cols, dtype=jnp.bfloat16),) * 2,
         32,
-    )(numbers, left, right, *own, near, far, row_taps)
-    (rms,) = call(final_kernel, "final", ((rows, cols),))(passed, from_left, from_right, col_taps)
+    )(numbers, left, right, *own, *halos, row_taps, col_taps)
+    (rms,) = call(
+        final_kernel, "final", ((rows, cols),), (scratch(2, rows, LANES), pltpu.SemaphoreType.DMA((2,))), in_place=True
+    )(rms, sides, from_left, from_right, col_taps)
     return background, rms
 
 

time: 40.6 us -> 40.4 us (level)
  starting transfers between devices: 18.1 us -> 15.6 us
  local copies, waits for them, and re-layouts: 0.75 us -> 3.13 us
  Pallas kernels: 6.14 us -> 8.17 us
  other arithmetic: 2.11 us -> 0.96 us
  waiting for transfers between devices: 12.4 us -> 11.3 us
    unnamed x6 -> x12, local copies, waits for them, and re-layouts: 0.02 us -> 3.13 us
    pallas_call x5, Pallas kernels: 6.14 us -> 8.17 us  [run(): pl.pallas_call(kernel, out_shape=tuple((jax.ShapeDtypeStruct(shape, jnp.f...]
    all_to_all x1, starting transfers between devices: 7.96 us -> 6.55 us  [shards(): parts = lax.all_to_all(parts, ('rows', 'cols'), 0, 0, tiled=True)]
    mul x2 -> x1, other arithmetic: 2.07 us -> 0.94 us  [shards(): products = [flux * weight for flux, weight in taken]]
    ppermute x2, waiting for transfers between devices: 2.9 us -> 1.82 us  [shift(): return lax.ppermute(block, axis, pairs)]
    broadcast_in_dim x1 -> x0, local copies, waits for them, and re-layouts: 0.74 us -> none  [shards(): parts = jnp.broadcast_to(parts[None], (nrows * ncols, 1, message))]
    ppermute x3, starting transfers between devices: 6.32 us -> 5.64 us  [swap(): return lax.ppermute(block, axis, pairs + [(j, i) for i, j in pairs])]
  transfers between devices with their start and end apart: 6 -> 6, of which waited for: 3 -> 3; matrix products, arithmetic and copies ran while one was open for 5% -> 0% of each run, Pallas kernels for 10% -> 15%
where the time goes in v7:
time: 40.4 us; the launch traced here: 40 us
  starting transfers between devices  15.6 us (39%)
  waiting for transfers between devices  11.3 us (28%)
  Pallas kernels  8.17 us (20%)
  local copies, waits for them, and re-layouts  3.13 us (8%)
  other arithmetic  0.96 us (2%)
  between operations  0.74 us (2%)
    all_to_all x1, waiting for transfers between devices, shards(): parts = lax.all_to_all(parts, ('rows', 'cols'), 0, 0, tiled=True)  8.61 us
    pallas_call x5, Pallas kernels, run(): pl.pallas_call(kernel, out_shape=tuple((jax.ShapeDtypeStruct(shape, jnp.f...  8.17 us
    all_to_all x1, starting transfers between devices, shards(): parts = lax.all_to_all(parts, ('rows', 'cols'), 0, 0, tiled=True)  6.55 us
    ppermute x3, starting transfers between devices, swap(): return lax.ppermute(block, axis, pairs + [(j, i) for i, j in pairs])  5.64 us
    ppermute x2, starting transfers between devices, shift(): return lax.ppermute(block, axis, pairs)  3.43 us
    unnamed x12, local copies, waits for them, and re-layouts  3.13 us
    ppermute x2, waiting for transfers between devices, shift(): return lax.ppermute(block, axis, pairs)  1.82 us
    mul x1, other arithmetic, shards(): products = [flux * weight for flux, weight in taken]  0.94 us
  transfers between devices with their start and end apart: 6, of which 3 were waited for; matrix products, arithmetic and copies ran while one was open for 0% of the time, Pallas kernels for 15%

profile of v7, /device:TPU:0, one launch (start us, length us, event | category | flops | bytes accessed | tf_op | source)
XLA Modules:
  0.0 40.0 jit_solution(10750484529291275234)
XLA Ops:
  0.6 0.9 %dynamic-slice_multiply_fusion = (f32[1,1024]{1,0:T(1,128)S(1)}, f32[1,1024]{1,0:T(1,128)S(1)}, f32[1,1024]{1,0:T(1,128)S(1)}, f32[1,1024]{1,0:T(1,128)S(1)}) fusion(f32[128,1024]{1,0:T(8,128)} %f_ref.7, s32[]{:T(128)S(6)} %select_n.31, s32[128,1024]{1,0:T(8,128)} %mask_ref.1, f32[128,1024]{1,0:T(8,128)} %iv_ref.1, s32[]{:T(128)S(6)} %select_n.32, ...), kind=kLoop, calls=%fused_computation.4 | loop fusion | flops 12288 | bytes 53260 | tf_op jit(solution)/shard_map/mul | solution.py:449
  1.6 0.7 %collective-permute-start = (f32[4,1024]{1,0:T(4,128)S(1)}, f32[4,1024]{1,0:T(4,128)S(1)}, u32[]{:S(2)}, u32[]{:S(2)}) collective-permute-start(f32[4,1024]{1,0:T(4,128)S(1)} %pad_maximum_fusion), channel_id=1, source_target_pairs={{4,8},{12,16},{20,24},{8,4},{16,12},{24,20},{5,9},{13,17},{21,25},... | collective-permute-start | bytes 49160 | tf_op jit(solution)/shard_map/ppermute | solution.py:412
  2.3 0.0 copy-start
  2.3 1.0 %copy-done = f32[128,1024]{1,0:T(8,128)S(1)} copy-done((f32[128,1024]{1,0:T(8,128)S(1)}, f32[128,1024]{1,0:T(8,128)}, u32[]{:S(2)}) %copy-start) | copy-done | bytes 524312
  3.3 0.0 copy-start.4
  3.3 1.0 %copy-done.4 = f32[128,1024]{1,0:T(8,128)S(1)} copy-done((f32[128,1024]{1,0:T(8,128)S(1)}, f32[128,1024]{1,0:T(8,128)}, u32[]{:S(2)}) %copy-start.4) | copy-done | bytes 524312
  4.4 0.0 copy-start.5
  4.4 1.0 %copy-done.5 = s32[128,1024]{1,0:T(8,128)S(1)} copy-done((s32[128,1024]{1,0:T(8,128)S(1)}, s32[128,1024]{1,0:T(8,128)}, u32[]{:S(2)}) %copy-start.5) | copy-done | bytes 524312
  5.4 0.9 %prepare.1 = (f32[128,1024]{1,0:T(8,128)S(1)}, f32[136,1024]{1,0:T(8,128)S(1)}, f32[128,1024]{1,0:T(8,128)}) custom-call(f32[128,1024]{1,0:T(8,128)S(1)} %copy-done, f32[128,1024]{1,0:T(8,128)S(1)} %copy-done.4, s32[128,1024]{1,0:T(8,128)S(1)} %copy-done.5), custom_call_target="tpu_custom_call" | custom-call | tf_op jit(solution)/shard_map/prepare/pallas_call | solution.py:420
  6.3 0.0 collective-permute-done.narrow_ref
  6.3 4.3 %collective-permute-start.1 = (f32[136,1024]{1,0:T(8,128)S(1)}, f32[136,1024]{1,0:T(8,128)S(1)}, u32[]{:S(2)}, u32[]{:S(2)}) collective-permute-start(f32[136,1024]{1,0:T(8,128)S(1)} %get-tuple-element.20), channel_id=1, source_target_pairs={{0,4},{8,12},{16,20},{24,28},{4,0},{12,8},{20,16},{28,24},{1,5},{9... | collective-permute-start | bytes 1671176 | tf_op jit(solution)/shard_map/ppermute | solution.py:412
  10.6 0.7 %collective-permute-start.2 = (f32[128,1024]{1,0:T(8,128)}, f32[128,1024]{1,0:T(8,128)S(1)}, u32[]{:S(2)}, u32[]{:S(2)}) collective-permute-start(f32[128,1024]{1,0:T(8,128)} %get-tuple-element.21), channel_id=1, source_target_pairs={{4,8},{12,16},{20,24},{8,4},{16,12},{24,20},{5,9},{13,17},{21,25},... | collective-permute-start | bytes 1572872 | tf_op jit(solution)/shard_map/ppermute | solution.py:412
  11.3 0.9 %collective-permute-done.1.near_ref = f32[136,1024]{1,0:T(8,128)S(1)} collective-permute-done((f32[136,1024]{1,0:T(8,128)S(1)}, f32[136,1024]{1,0:T(8,128)S(1)}, u32[]{:S(2)}, u32[]{:S(2)}) %collective-permute-start.1) | collective-permute-done | bytes 557088 | tf_op jit(solution)/shard_map/ppermute | solution.py:412
  12.2 0.0 copy-start.1
  12.2 0.0 copy-start.2
  12.2 2.6 %moments.1 = f32[32,1,1152]{2,1,0:T(1,128)} custom-call(f32[128,1024]{1,0:T(8,128)S(1)} %copy-done, f32[128,1024]{1,0:T(8,128)S(1)} %get-tuple-element.16.w_ref, f32[4,1024]{1,0:T(4,128)S(1)} %collective-permute-done.narrow_ref, f32[136,1024]{1,0:T(8,128)S(1)} %collective-permute-done.1.near_ref), custom_call_target="tpu_custom_call" | custom-call | tf_op jit(solution)/shard_map/moments/pallas_call | solution.py:420
  14.8 6.5 %all-to-all-start = ((f32[32,1,1152]{2,1,0:T(1,128)}), f32[32,1,1152]{2,1,0:T(1,128)S(1)}, u32[]{:S(2)}, u32[]{:S(2)}) async-start(f32[32,1,1152]{2,1,0:T(1,128)} %moments.1), calls=%async_computation | async-start | bytes 294912 | tf_op jit(solution)/shard_map/all_to_all | solution.py:464
  21.4 0.0 copy-start.3
  21.4 0.0 collective-permute-done.2.far_ref
  21.4 8.6 %all-to-all-done.parts_ref = f32[32,1,1152]{2,1,0:T(1,128)S(1)} async-done(((f32[32,1,1152]{2,1,0:T(1,128)}), f32[32,1,1152]{2,1,0:T(1,128)S(1)}, u32[]{:S(2)}, u32[]{:S(2)}) %all-to-all-start) | async-done | bytes 147488 | tf_op jit(solution)/shard_map/all_to_all | solution.py:464
  30.0 0.0 copy-done.1
  30.0 0.0 copy-done.2
  30.0 1.0 %edges.1 = (f32[16,128]{1,0:T(8,128)S(1)}, f32[256,128]{1,0:T(8,128)S(1)}, f32[256,128]{1,0:T(8,128)S(1)}, f32[64,128]{1,0:T(8,128)S(1)}, f32[64,128]{1,0:T(8,128)S(1)}) custom-call(f32[32,1,1152]{2,1,0:T(1,128)S(1)} %all-to-all-done.parts_ref, f32[128,1024]{1,0:T(8,128)S(1)} %copy-done.1, f32[128,1024]{1,0:T(8,128)S(1)} %get-tuple-element.16.w_ref, ...), custom_call_target="tpu_custom_call" | custom-call | tf_op jit(solution)/shard_map/edges/pallas_call | solution.py:420
  31.0 2.1 %collective-permute-start.3 = (f32[64,128]{1,0:T(8,128)S(1)}, f32[64,128]{1,0:T(8,128)S(1)}, u32[]{:S(2)}, u32[]{:S(2)}) collective-permute-start(f32[64,128]{1,0:T(8,128)S(1)} %get-tuple-element.28), channel_id=1, source_target_pairs={{0,1},{1,2},{2,3},{4,5},{5,6},{6,7},{8,9},{9,10},{10,11},{12,13},{... | collective-permute-start | bytes 98312 | tf_op jit(solution)/shard_map/ppermute | solution.py:406
  33.1 1.3 %collective-permute-start.4 = (f32[64,128]{1,0:T(8,128)S(1)}, f32[64,128]{1,0:T(8,128)S(1)}, u32[]{:S(2)}, u32[]{:S(2)}) collective-permute-start(f32[64,128]{1,0:T(8,128)S(1)} %get-tuple-element.29), channel_id=1, source_target_pairs={{1,0},{2,1},{3,2},{5,4},{6,5},{7,6},{9,8},{10,9},{11,10},{13,12},{... | collective-permute-start | bytes 98312 | tf_op jit(solution)/shard_map/ppermute | solution.py:406
  34.4 0.0 copy-done.3
  34.4 2.7 %main.1 = (f32[128,1024]{1,0:T(8,128)}, f32[128,1024]{1,0:T(8,128)}, f32[128,512]{1,0:T(8,128)S(1)}) custom-call(f32[16,128]{1,0:T(8,128)S(1)} %get-tuple-element.22.coefficients_ref, f32[256,128]{1,0:T(8,128)S(1)} %get-tuple-element.23.left_ref, f32[256,128]{1,0:T(8,128)S(1)} %get-tuple-element.24.right_ref, f32[128,1024]{1,0:T(8,128)S(1)} %copy-done.1, ...), custom_call_target="tpu_custom_call" | custom-call | tf_op jit(solution)/shard_map/main/pallas_call | solution.py:420
  37.1 0.0 collective-permute-done.3.left_ref
  37.1 1.8 %collective-permute-done.4.right_ref = f32[64,128]{1,0:T(8,128)S(1)} collective-permute-done((f32[64,128]{1,0:T(8,128)S(1)}, f32[64,128]{1,0:T(8,128)S(1)}, u32[]{:S(2)}, u32[]{:S(2)}) %collective-permute-start.4) | collective-permute-done | bytes 32800 | tf_op jit(solution)/shard_map/ppermute | solution.py:406
  38.9 1.0 %final.1 = f32[128,1024]{1,0:T(8,128)} custom-call(f32[128,1024]{1,0:T(8,128)} %get-tuple-element.26.rms_in_ref, f32[128,512]{1,0:T(8,128)S(1)} %get-tuple-element.27.sides_ref, f32[64,128]{1,0:T(8,128)S(1)} %collective-permute-done.3.left_ref, f32[64,128]{1,0:T(8,128)S(1)} %collective-permute-done.4.right_ref, ...), custom_call_target="tpu_custom_call", output_to_operand_aliasing={{}: (0, {})} | custom-call | tf_op jit(solution)/shard_map/final/pallas_call | solution.py:420
  (1 shorter events, 0.0 us)
Async XLA Ops:
  1.6 4.7 %collective-permute-start = (f32[4,1024]{1,0:T(4,128)S(1)}, f32[4,1024]{1,0:T(4,128)S(1)}, u32[]{:S(2)}, u32[]{:S(2)}) collective-permute-start(f32[4,1024]{1,0:T(4,128)S(1)} %pad_maximum_fusion), channel_id=1, source_target_pairs={{4,8},{12,16},{20,24},{8,4},{16,12},{24,20},{5,9},{13,17},{21,25},... | collective-permute-start | bytes 49160 | tf_op jit(solution)/shard_map/ppermute | solution.py:412
  2.3 1.0 %copy-start = (f32[128,1024]{1,0:T(8,128)S(1)}, f32[128,1024]{1,0:T(8,128)}, u32[]{:S(2)}) copy-start(f32[128,1024]{1,0:T(8,128)} %f_ref.7) | copy-start | bytes 1572868
  3.3 1.0 %copy-start.4 = (f32[128,1024]{1,0:T(8,128)S(1)}, f32[128,1024]{1,0:T(8,128)}, u32[]{:S(2)}) copy-start(f32[128,1024]{1,0:T(8,128)} %iv_ref.1) | copy-start | bytes 1572868
  4.4 1.0 %copy-start.5 = (s32[128,1024]{1,0:T(8,128)S(1)}, s32[128,1024]{1,0:T(8,128)}, u32[]{:S(2)}) copy-start(s32[128,1024]{1,0:T(8,128)} %mask_ref.1) | copy-start | bytes 1572868
  6.3 5.9 %collective-permute-start.1 = (f32[136,1024]{1,0:T(8,128)S(1)}, f32[136,1024]{1,0:T(8,128)S(1)}, u32[]{:S(2)}, u32[]{:S(2)}) collective-permute-start(f32[136,1024]{1,0:T(8,128)S(1)} %get-tuple-element.20), channel_id=1, source_target_pairs={{0,4},{8,12},{16,20},{24,28},{4,0},{12,8},{20,16},{28,24},{1,5},{9... | collective-permute-start | bytes 1671176 | tf_op jit(solution)/shard_map/ppermute | solution.py:412
  10.6 10.8 %collective-permute-start.2 = (f32[128,1024]{1,0:T(8,128)}, f32[128,1024]{1,0:T(8,128)S(1)}, u32[]{:S(2)}, u32[]{:S(2)}) collective-permute-start(f32[128,1024]{1,0:T(8,128)} %get-tuple-element.21), channel_id=1, source_target_pairs={{4,8},{12,16},{20,24},{8,4},{16,12},{24,20},{5,9},{13,17},{21,25},... | collective-permute-start | bytes 1572872 | tf_op jit(solution)/shard_map/ppermute | solution.py:412
  12.2 17.8 %copy-start.1 = (f32[128,1024]{1,0:T(8,128)S(1)}, f32[128,1024]{1,0:T(8,128)}, u32[]{:S(2)}) copy-start(f32[128,1024]{1,0:T(8,128)} %f_ref.7) | copy-start | bytes 1572868
  12.2 17.8 %copy-start.2 = (bf16[4,256,256]{2,1,0:T(8,128)(2,1)S(1)}, bf16[4,256,256]{2,1,0:T(8,128)(2,1)}, u32[]{:S(2)}) copy-start(bf16[4,256,256]{2,1,0:T(8,128)(2,1)} %constant.43.clone.rowtaps_ref) | copy-start | bytes 1572868
  14.8 15.2 %all-to-all-start = ((f32[32,1,1152]{2,1,0:T(1,128)}), f32[32,1,1152]{2,1,0:T(1,128)S(1)}, u32[]{:S(2)}, u32[]{:S(2)}) async-start(f32[32,1,1152]{2,1,0:T(1,128)} %moments.1), calls=%async_computation | async-start | bytes 294912 | tf_op jit(solution)/shard_map/all_to_all | solution.py:464
  21.4 13.1 %copy-start.3 = (bf16[3,256,256]{2,1,0:T(8,128)(2,1)S(1)}, bf16[3,256,256]{2,1,0:T(8,128)(2,1)}, u32[]{:S(2)}) copy-start(bf16[3,256,256]{2,1,0:T(8,128)(2,1)} %constant.44.clone.coltaps_ref) | copy-start | bytes 1179652
  31.0 6.1 %collective-permute-start.3 = (f32[64,128]{1,0:T(8,128)S(1)}, f32[64,128]{1,0:T(8,128)S(1)}, u32[]{:S(2)}, u32[]{:S(2)}) collective-permute-start(f32[64,128]{1,0:T(8,128)S(1)} %get-tuple-element.28), channel_id=1, source_target_pairs={{0,1},{1,2},{2,3},{4,5},{5,6},{6,7},{8,9},{9,10},{10,11},{12,13},{... | collective-permute-start | bytes 98312 | tf_op jit(solution)/shard_map/ppermute | solution.py:406
  33.1 5.8 %collective-permute-start.4 = (f32[64,128]{1,0:T(8,128)S(1)}, f32[64,128]{1,0:T(8,128)S(1)}, u32[]{:S(2)}, u32[]{:S(2)}) collective-permute-start(f32[64,128]{1,0:T(8,128)S(1)} %get-tuple-element.29), channel_id=1, source_target_pairs={{1,0},{2,1},{3,2},{5,4},{6,5},{7,6},{9,8},{10,9},{11,10},{13,12},{... | collective-permute-start | bytes 98312 | tf_op jit(solution)/shard_map/ppermute | solution.py:406

commit v8 on v7

--- a/solution.py
+++ b/solution.py
@@ -47,8 +47,13 @@
 
 def row_tables(length):
     tables = []
-    for first, last in ((False, False), (True, False), (False, True), (True, True)):
-        tables.append(np.concatenate(split(squared_taps(length, first, last)), axis=0))
+    for first, last, odd in ((False, False, False), (True, False, False), (False, False, True), (False, True, True)):
+        table = squared_taps(length, first, last)
+        above, own, below = table[:, :REACH], table[:, REACH : REACH + length], table[:, REACH + length :]
+        near, far = (above, below) if odd else (below, above)
+        if first or last:
+            far = np.zeros_like(far)
+        tables.append(np.concatenate(split(np.concatenate([own, near, far], axis=1)), axis=0))
     return np.stack(tables)
 
 
@@ -96,9 +101,8 @@
     return alpha0 + alpha1 * grown, -alpha1 * alpha0
 
 
-def prepare_kernel(f_ref, iv_ref, mask_ref, w_ref, near_ref, far_ref):
+def wide_kernel(f_ref, w_ref, near_ref, far_ref):
     rows = f_ref.shape[0]
-    w_ref[...] = weights(iv_ref[...], mask_ref[...])
 
     def write(out_ref, begin):
         out_ref[pl.ds(0, REACH), :] = f_ref[pl.ds(begin, REACH), :]
@@ -120,7 +124,7 @@
         write(far_ref, rows - REACH)
 
 
-def moments_kernel(f_ref, w_ref, narrow_ref, near_ref, out_ref, v0_ref, v1_ref, edge_ref):
+def moments_kernel(f_ref, w_ref, narrow_ref, near_ref, out_ref, v1_out_ref, v0_ref, v1_ref, edge_ref):
     rows, cols = f_ref.shape
     width = cols + LANES
     first_row, last_row, _, _ = at_edges()
@@ -156,6 +160,7 @@
     for start in range(0, rows, 8):
         _, out = image(v0_ref, w_ref[pl.ds(start, 8), :], NEAR + start, 8)
         v1_ref[pl.ds(NEAR + start, 8), own] = out
+        v1_out_ref[pl.ds(start, 8), :] = out
 
     def edge_row(weight, at):
         _, out = image(v0_ref, weight, at, 1)
@@ -183,9 +188,10 @@
         total = jnp.sum(jnp.sum(narrow, axis=0, keepdims=True), axis=1, keepdims=True)
         result = jnp.where(lane[:1] == i, total, result)
     vectors = edge_ref[...].T
-    message = jnp.concatenate([result] + [vectors[k : k + 1, :] for k in range(VECTORS)], axis=1)
-    for k in range(out_ref.shape[0]):
-        out_ref[k] = message
+    message = [result] + [vectors[k : k + 1, :] for k in range(VECTORS)]
+    copies = jnp.concatenate(message * 8, axis=0)
+    for start in range(0, out_ref.shape[0], copies.shape[0]):
+        out_ref[pl.ds(start, copies.shape[0]), :] = copies
 
 
 def coupled(parts_ref, nrows, ncols):
@@ -223,10 +229,12 @@
 
 def neighbours(parts_ref, nrows, ncols):
     row, col = lax.axis_index("rows"), lax.axis_index("cols")
+    even = is_even()
+    towards = jnp.where(even, 1, -1)
     lane = lax.broadcasted_iota(jnp.int32, (LANES, LANES), 1)
     vectors = []
     for vector, step_col in ((1, -1), (5, 1)):
-        for step_row in (-1, 0, 1):
+        for step_row in (0, towards, -towards):
             r, c = row + step_row, col + step_col
             there = (r >= 0) & (r < nrows) & (c >= 0) & (c < ncols)
             index = jnp.where(there, r * ncols + c, 0)
@@ -236,50 +244,47 @@
     columns = jnp.concatenate(vectors, axis=0).T
     sides = []
     for begin, target in ((0, 0), (3, LANES - 1)):
-        moved = [jnp.where(lane == target, pltpu.roll(columns, (target - begin - k) % LANES, 1), 0.0) for k in range(3)]
-        sides.append(jnp.concatenate([moved[0][LANES - REACH :], moved[1], moved[2][:REACH]], axis=0))
+        own, near, far = (
+            jnp.where(lane == target, pltpu.roll(columns, (target - begin - k) % LANES, 1), 0.0) for k in range(3)
+        )
+        near = jnp.where(even, near[:REACH], near[LANES - REACH :])
+        far = jnp.where(even, far[LANES - REACH :], far[:REACH])
+        sides.append(jnp.concatenate([own, near, far], axis=0))
     return sides
 
 
-def halo(near_ref, far_ref, below, start, count, at_cols):
-    at = pl.ds(start, count)
-    one, other = (near_ref, far_ref) if below else (far_ref, near_ref)
-    return jnp.where(is_even(), one[at, at_cols], other[at, at_cols])
-
-
-def last_row(near_ref, narrow_ref, below, at_cols):
-    near = near_ref[pl.ds(2 * REACH + (0 if below else 7), 1), at_cols]
-    far = narrow_ref[pl.ds(3, 1), at_cols]
-    return jnp.where(is_even(), near, far) if below else jnp.where(is_even(), far, near)
-
-
-def pair(f_ref, w_ref, near_ref, far_ref, narrow_ref, start, count, at_cols):
-    rows = f_ref.shape[0]
-    for below, begin in ((False, WIDE - REACH), (True, WIDE + rows)):
-        if begin <= start < begin + REACH:
-            return tuple(halo(near_ref, far_ref, below, start - begin + k, count, at_cols) for k in (0, REACH))
-    at = pl.ds(start - WIDE, count)
-    return f_ref[at, at_cols], w_ref[at, at_cols]
-
-
-def product(refs, v0_ref, at_cols, target):
-    rows = refs[0].shape[0]
-    v0_ref[pl.ds(7, 1), target] = last_row(refs[2], refs[4], False, at_cols)
-    v0_ref[pl.ds(rows + 2 * WIDE - 8, 1), target] = last_row(refs[2], refs[4], True, at_cols)
-    for start in range(8, rows + 2 * WIDE - 8, 8):
-        flux, weight = pair(*refs, start, 8, at_cols)
-        v0_ref[pl.ds(start, 8), target] = flux * weight
-
-
-def clear_outside(refs, rows):
-    first_row, last_row, _, _ = at_edges()
-
-    def clear(start):
-        for ref in refs:
-            ref[pl.ds(start, REACH), :] = jnp.zeros((REACH, ref.shape[1]), jnp.bfloat16)
-
-    pl.when(first_row)(lambda: clear(0))
-    pl.when(last_row)(lambda: clear(REACH + rows))
+def fields_kernel(f_ref, w_ref, narrow_ref, near_ref, far_ref, near_v1_ref, far_v1_ref, v0_ref):
+    rows, cols = f_ref.shape
+    own, pad = pl.ds(0, cols), pl.ds(cols, LANES)
+    even = is_even()
+    top = f_ref[pl.ds(0, 1), :] * w_ref[pl.ds(0, 1), :]
+    bottom = f_ref[pl.ds(rows - 1, 1), :] * w_ref[pl.ds(rows - 1, 1), :]
+    beyond_near = jnp.where(even, near_ref[pl.ds(2 * REACH, 1), :], near_ref[pl.ds(2 * REACH + 7, 1), :])
+    beyond_far = narrow_ref[pl.ds(3, 1), :]
+    v0_ref[:, pad] = jnp.zeros((REACH + 2 * NEAR, LANES), jnp.float32)
+    guards = (
+        (near_ref, near_v1_ref, jnp.where(even, bottom, beyond_near), jnp.where(even, beyond_near, top)),
+        (far_ref, far_v1_ref, jnp.where(even, beyond_far, bottom), jnp.where(even, top, beyond_far)),
+    )
+    for halo_ref, v1_ref, above, below in guards:
+        v0_ref[pl.ds(NEAR - 1, 1), own] = above
+        v0_ref[pl.ds(NEAR + REACH, 1), own] = below
+        for start in range(0, REACH, 8):
+            v0_ref[pl.ds(NEAR + start, 8), own] = halo_ref[pl.ds(start, 8), :] * halo_ref[pl.ds(REACH + start, 8), :]
+        for start in range(0, REACH, 8):
+            at = NEAR + start
+            here = v0_ref[pl.ds(at, 8), :]
+            beside = v0_ref[pl.ds(at - 1, 8), own] + v0_ref[pl.ds(at + 1, 8), own] + beside_columns(here)[:, :cols]
+            here = here[:, :cols]
+            v1_ref[pl.ds(start, 8), :] = halo_ref[pl.ds(REACH + start, 8), :] * here + smooth_weight * (4.0 * here - beside)
+
+
+def regions(f_ref, w_ref, v1_ref, near_ref, near_v1_ref, far_ref, far_v1_ref, step):
+    for start in range(0, f_ref.shape[0], step):
+        yield start, (f_ref, start), (w_ref, start), (v1_ref, start)
+    for base, halo_ref, field_ref in ((f_ref.shape[0], near_ref, near_v1_ref), (f_ref.shape[0] + REACH, far_ref, far_v1_ref)):
+        for start in range(0, REACH, step):
+            yield base + start, (halo_ref, start), (halo_ref, REACH + start), (field_ref, start)
 
 
 def dot(left, right):
@@ -288,44 +293,34 @@
 
 def row_pass(rowtaps_ref, high, low, rows):
     first_row, last_row, _, _ = at_edges()
-    table = rowtaps_ref[first_row.astype(jnp.int32) + 2 * last_row.astype(jnp.int32)]
+    kind = jnp.where(is_even(), first_row.astype(jnp.int32), 2 + last_row.astype(jnp.int32))
+    table = rowtaps_ref[kind]
     both = dot(table, high)
     return both[:rows] + (both[rows:] + dot(table[:rows], low))
 
 
 def edges_kernel(
-    nrows, ncols, parts_ref, f_ref, w_ref, near_ref, far_ref, narrow_ref, rowtaps_ref,
-    coefficients_ref, left_ref, right_ref, first_ref, last_ref, v0_ref, high_ref, low_ref,
+    nrows, ncols, parts_ref, f_ref, w_ref, v1_ref, near_ref, near_v1_ref, far_ref, far_v1_ref, rowtaps_ref,
+    coefficients_ref, left_ref, right_ref, first_ref, last_ref, high_ref, low_ref,
 ):
     rows, cols = f_ref.shape
-    refs = (f_ref, w_ref, near_ref, far_ref, narrow_ref)
     c0, c1 = coefficients(*coupled(parts_ref, nrows, ncols))
     coefficients_ref[pl.ds(0, 8), :] = jnp.broadcast_to(c0, (8, LANES))
     coefficients_ref[pl.ds(8, 8), :] = jnp.broadcast_to(c1, (8, LANES))
-    left_ref[...], right_ref[...] = neighbours(parts_ref, nrows, ncols)
+    sides = neighbours(parts_ref, nrows, ncols)
+    left_ref[...], right_ref[...] = sides
 
     step = 16
-    lane = lax.broadcasted_iota(jnp.int32, (step, 2 * LANES), 1)
-    for side, begin in enumerate((0, cols - 2 * LANES)):
-        target = pl.ds(side * 2 * LANES, 2 * LANES)
-        product(refs, v0_ref, pl.ds(begin, 2 * LANES), target)
-        at_cols = pl.ds(side * (cols - LANES), LANES)
-        here_at = slice(side * LANES, side * LANES + LANES)
-        wrapped = lane == side * (2 * LANES - 1)
-        for start in range(8, rows + 2 * WIDE - 8, step):
-            flux, weight = pair(*refs, start, step, at_cols)
-            field = v0_ref[pl.ds(start, step), target]
-            inner = pltpu.roll(field, 2 * LANES - 1 if side == 0 else 1, 1)
-            outer = jnp.where(wrapped, 0.0, pltpu.roll(field, 1 if side == 0 else 2 * LANES - 1, 1))
-            beside = v0_ref[pl.ds(start - 1, step), target] + v0_ref[pl.ds(start + 1, step), target] + inner + outer
-            v0 = field[:, here_at]
-            beside = beside[:, here_at] + (left_ref, right_ref)[side][pl.ds(start - 8, step), :]
-            v1 = weight * v0 + smooth_weight * (4.0 * v0 - beside)
-            scatter = flux - (c0 * v0 + c1 * v1)
+    fields = (f_ref, w_ref, v1_ref, near_ref, near_v1_ref, far_ref, far_v1_ref)
+    for side, begin in enumerate((0, cols - LANES)):
+        at_cols = pl.ds(begin, LANES)
+        for start, *sources in regions(*fields, step):
+            flux, weight, v1 = (ref[pl.ds(row, step), at_cols] for ref, row in sources)
+            v1 = v1 - smooth_weight * sides[side][start : start + step]
+            scatter = flux - (c0 * (flux * weight) + c1 * v1)
             high, low = split_values(scatter * scatter)
-            high_ref[pl.ds(start - 8, step), pl.ds(side * LANES, LANES)] = high
-            low_ref[pl.ds(start - 8, step), pl.ds(side * LANES, LANES)] = low
-    clear_outside((high_ref, low_ref), rows)
+            high_ref[pl.ds(start, step), pl.ds(side * LANES, LANES)] = high
+            low_ref[pl.ds(start, step), pl.ds(side * LANES, LANES)] = low
     passed = row_pass(rowtaps_ref, high_ref[...], low_ref[...], rows)
     upper, lower = slice(0, rows // 2), slice(rows // 2, rows)
     first, last = passed[:, :LANES], passed[:, LANES:]
@@ -335,33 +330,29 @@
 
 
 def main_kernel(
-    coefficients_ref, left_ref, right_ref, f_ref, w_ref, near_ref, far_ref, narrow_ref, rowtaps_ref, coltaps_ref,
-    background_ref, rms_ref, sides_ref, v0_ref, high_ref, low_ref,
+    coefficients_ref, left_ref, right_ref, f_ref, w_ref, v1_ref, near_ref, near_v1_ref, far_ref, far_v1_ref, rowtaps_ref, coltaps_ref,
+    background_ref, rms_ref, sides_ref, high_ref, low_ref,
 ):
     rows, cols = f_ref.shape
-    refs = (f_ref, w_ref, near_ref, far_ref, narrow_ref)
-    own = pl.ds(0, cols)
     c0, c1 = coefficients_ref[pl.ds(0, 1), pl.ds(0, 1)], coefficients_ref[pl.ds(8, 1), pl.ds(0, 1)]
-    v0_ref[:, pl.ds(cols, LANES)] = jnp.zeros((rows + 2 * WIDE, LANES), jnp.float32)
-    product(refs, v0_ref, own, own)
     step = 16
-    for start in range(8, rows + 2 * WIDE - 8, step):
-        flux, weight = pair(*refs, start, step, own)
-        field = v0_ref[pl.ds(start, step), :]
-        beside = v0_ref[pl.ds(start - 1, step), own] + v0_ref[pl.ds(start + 1, step), own] + beside_columns(field)[:, :cols]
-        at = pl.ds(start - 8, step)
-        beside = jnp.concatenate(
-            [beside[:, :LANES] + left_ref[at, :], beside[:, LANES : cols - LANES], beside[:, cols - LANES :] + right_ref[at, :]],
+    fields = (f_ref, w_ref, v1_ref, near_ref, near_v1_ref, far_ref, far_v1_ref)
+    for start, *sources in regions(*fields, step):
+        flux, weight, v1 = (ref[pl.ds(row, step), :] for ref, row in sources)
+        at = pl.ds(start, step)
+        v1 = jnp.concatenate(
+            [
+                v1[:, :LANES] - smooth_weight * left_ref[at, :],
+                v1[:, LANES : cols - LANES],
+                v1[:, cols - LANES :] - smooth_weight * right_ref[at, :],
+            ],
             axis=1,
         )
-        v0 = field[:, :cols]
-        v1 = weight * v0 + smooth_weight * (4.0 * v0 - beside)
-        background = c0 * v0 + c1 * v1
-        if WIDE <= start < WIDE + rows:
-            background_ref[pl.ds(start - WIDE, step), :] = background
+        background = c0 * (flux * weight) + c1 * v1
+        if start < rows:
+            background_ref[at, :] = background
         scatter = flux - background
         high_ref[at, :], low_ref[at, :] = split_values(scatter * scatter)
-    clear_outside((high_ref, low_ref), rows)
     passed = row_pass(rowtaps_ref, high_ref[...], low_ref[...], rows)
     sides_ref[:, pl.ds(0, 2 * LANES)] = passed[:, : 2 * LANES]
     sides_ref[:, pl.ds(2 * LANES, 2 * LANES)] = passed[:, cols - 2 * LANES :]
@@ -449,38 +440,43 @@
     products = [flux * weight for flux, weight in taken]
     narrow = swap(jnp.concatenate([products[0], products[1], taken[0][1], products[2]]), "rows", 1)
 
-    weight, to_near, to_far = call(
-        prepare_kernel, "prepare", ((rows, cols), (2 * REACH + 8, cols), (2 * REACH, cols))
-    )(coadd_flux, inverse_variance, source_mask)
-    own = (coadd_flux, weight)
+    own = (coadd_flux, weights(inverse_variance, source_mask))
+    to_near, to_far = call(wide_kernel, "wide", ((2 * REACH + 8, cols), (2 * REACH, cols)))(*own)
     to_near, to_far, narrow = lax.optimization_barrier((to_near, to_far, narrow))
     near = swap(to_near, "rows", 0)
     far = swap(to_far, "rows", 1)
 
     field = scratch(rows + 2 * NEAR, cols + LANES)
-    (parts,) = call(
-        moments_kernel, "moments", ((nrows * ncols, 1, message),), (field, field, scratch(rows, LANES))
+    devices = nrows * ncols
+    parts, own_v1 = call(
+        moments_kernel,
+        "moments",
+        ((devices * (VECTORS + 1), LANES), (rows, cols)),
+        (field, field, scratch(rows, LANES)),
     )(*own, narrow, near)
-    parts = lax.all_to_all(parts, ("rows", "cols"), 0, 0, tiled=True)
+    parts = lax.all_to_all(parts.reshape(devices, 1, message), ("rows", "cols"), 0, 0, tiled=True)
+    near_v1, far_v1 = call(
+        fields_kernel, "fields", ((REACH, cols), (REACH, cols)), (scratch(REACH + 2 * NEAR, cols + LANES),)
+    )(*own, narrow, near, far)
 
     row_taps, col_taps = jnp.asarray(row_tables(rows)), jnp.asarray(col_tables())
-    halos = (near, far, narrow)
+    fields = (*own, own_v1, near, near_v1, far, far_v1)
     reached, packed = rows + 2 * REACH, (rows // 2, LANES)
     numbers, left, right, first, last = call(
         functools.partial(edges_kernel, nrows, ncols),
         "edges",
         ((16, LANES), (reached, LANES), (reached, LANES), packed, packed),
-        (scratch(rows + 2 * WIDE, 4 * LANES),) + (scratch(reached, 2 * LANES, dtype=jnp.bfloat16),) * 2,
-    )(parts, *own, *halos, row_taps)
+        (scratch(reached, 2 * LANES, dtype=jnp.bfloat16),) * 2,
+    )(parts, *fields, row_taps)
     from_left = shift(last, "cols", 1)
     from_right = shift(first, "cols", -1)
     background, rms, sides = call(
         main_kernel,
         "main",
         ((rows, cols), (rows, cols), (rows, 4 * LANES)),
-        (scratch(rows + 2 * WIDE, cols + LANES),) + (scratch(reached, cols, dtype=jnp.bfloat16),) * 2,
+        (scratch(reached, cols, dtype=jnp.bfloat16),) * 2,
         32,
-    )(numbers, left, right, *own, *halos, row_taps, col_taps)
+    )(numbers, left, right, *fields, row_taps, col_taps)
     (rms,) = call(
         final_kernel, "final", ((rows, cols),), (scratch(2, rows, LANES), pltpu.SemaphoreType.DMA((2,))), in_place=True
     )(rms, sides, from_left, from_right, col_taps)

time: 40.4 us -> 40.5 us (level)
  local copies, waits for them, and re-layouts: 3.13 us -> 1.67 us
  other arithmetic: 0.96 us -> 2.23 us
    unnamed x12, local copies, waits for them, and re-layouts: 3.13 us -> 1.67 us
    mul x0 -> x1, other arithmetic: none -> 1.27 us  [weights(): return inverse_variance * (1.0 - source_mask.astype(jnp.float32))]
    all_to_all x1, waiting for transfers between devices: 8.61 us -> 7.47 us  [shards(): lax.all_to_all(parts.reshape(devices, 1, message), ('rows', 'cols'), 0, 0...]
    ppermute x2, waiting for transfers between devices: 1.82 us -> 2.72 us  [shift(): return lax.ppermute(block, axis, pairs)]
    all_to_all x1, starting transfers between devices: 6.55 us -> 7.3 us  [shards(): lax.all_to_all(parts.reshape(devices, 1, message), ('rows', 'cols'), 0, 0...]
    ppermute x2, starting transfers between devices: 3.43 us -> 2.91 us  [shift(): return lax.ppermute(block, axis, pairs)]
    pallas_call x5 -> x6, Pallas kernels: 8.17 us -> 8.36 us  [run(): pl.pallas_call(kernel, out_shape=tuple((jax.ShapeDtypeStruct(shape, jnp.f...]
  transfers between devices with their start and end apart: 6 -> 6, of which waited for: 3 -> 3; matrix products, arithmetic and copies ran while one was open for 0% -> 3% of each run, Pallas kernels for 15% -> 14%
where the time goes in v8:
time: 40.5 us; the launch traced here: 40.1 us
  starting transfers between devices  16 us (40%)
  waiting for transfers between devices  11.1 us (27%)
  Pallas kernels  8.36 us (21%)
  other arithmetic  2.23 us (6%)
  local copies, waits for them, and re-layouts  1.67 us (4%)
  between operations  0.78 us (2%)
    pallas_call x6, Pallas kernels, run(): pl.pallas_call(kernel, out_shape=tuple((jax.ShapeDtypeStruct(shape, jnp.f...  8.36 us
    all_to_all x1, waiting for transfers between devices, shards(): lax.all_to_all(parts.reshape(devices, 1, message), ('rows', 'cols'), 0, 0...  7.47 us
    all_to_all x1, starting transfers between devices, shards(): lax.all_to_all(parts.reshape(devices, 1, message), ('rows', 'cols'), 0, 0...  7.3 us
    ppermute x3, starting transfers between devices, swap(): return lax.ppermute(block, axis, pairs + [(j, i) for i, j in pairs])  5.78 us
    ppermute x2, starting transfers between devices, shift(): return lax.ppermute(block, axis, pairs)  2.91 us
    ppermute x2, waiting for transfers between devices, shift(): return lax.ppermute(block, axis, pairs)  2.72 us
    unnamed x12, local copies, waits for them, and re-layouts  1.67 us
    mul x1, other arithmetic, weights(): return inverse_variance * (1.0 - source_mask.astype(jnp.float32))  1.27 us
  transfers between devices with their start and end apart: 6, of which 3 were waited for; matrix products, arithmetic and copies ran while one was open for 3% of the time, Pallas kernels for 14%

profile of v8, /device:TPU:0, one launch (start us, length us, event | category | flops | bytes accessed | tf_op | source)
XLA Modules:
  0.0 40.1 jit_solution(10630305483373078093)
XLA Ops:
  0.6 0.9 %dynamic-slice_multiply_fusion = (f32[1,1024]{1,0:T(1,128)S(1)}, f32[1,1024]{1,0:T(1,128)S(1)}, f32[1,1024]{1,0:T(1,128)S(1)}, f32[1,1024]{1,0:T(1,128)S(1)}) fusion(f32[128,1024]{1,0:T(8,128)} %f_ref.9, s32[]{:T(128)S(6)} %select_n.31, s32[128,1024]{1,0:T(8,128)} %param.7, f32[128,1024]{1,0:T(8,128)} %param.6, s32[]{:T(128)S(6)} %select_n.32, s32[]{:T(128)S(6)} %select_n.33), kind=kLoop, calls=%fused_computation.5 | loop fusion | flops 12288 | bytes 53260 | tf_op jit(solution)/shard_map/mul | solution.py:440
  1.6 0.0 copy-start
  1.6 0.8 %collective-permute-start = (f32[4,1024]{1,0:T(4,128)S(1)}, f32[4,1024]{1,0:T(4,128)S(1)}, u32[]{:S(2)}, u32[]{:S(2)}) collective-permute-start(f32[4,1024]{1,0:T(4,128)S(1)} %pad_maximum_fusion), channel_id=1, source_target_pairs={{4,8},{12,16},{20,24},{8,4},{16,12},{24,20},{5,9},{13,17},{21,25},... | collective-permute-start | bytes 49160 | tf_op jit(solution)/shard_map/ppermute | solution.py:403
  2.4 1.3 %subtract_multiply_fusion.w_ref = f32[128,1024]{1,0:T(8,128)S(1)} fusion(f32[128,1024]{1,0:T(8,128)} %param.6, s32[128,1024]{1,0:T(8,128)} %param.7), kind=kLoop, calls=%fused_computation | loop fusion | flops 393216 | bytes 1572864 | tf_op jit(solution)/shard_map/mul | solution.py:92
  3.7 0.0 copy-done
  3.7 0.9 %wide.1 = (f32[136,1024]{1,0:T(8,128)S(1)}, f32[128,1024]{1,0:T(8,128)}) custom-call(f32[128,1024]{1,0:T(8,128)S(1)} %copy-done, f32[128,1024]{1,0:T(8,128)S(1)} %subtract_multiply_fusion.w_ref), custom_call_target="tpu_custom_call" | custom-call | tf_op jit(solution)/shard_map/wide/pallas_call | solution.py:411
  4.6 0.0 collective-permute-done.narrow_ref
  4.6 4.3 %collective-permute-start.1 = (f32[136,1024]{1,0:T(8,128)S(1)}, f32[136,1024]{1,0:T(8,128)S(1)}, u32[]{:S(2)}, u32[]{:S(2)}) collective-permute-start(f32[136,1024]{1,0:T(8,128)S(1)} %get-tuple-element.22), channel_id=1, source_target_pairs={{0,4},{8,12},{16,20},{24,28},{4,0},{12,8},{20,16},{28,24},{1,5},{9... | collective-permute-start | bytes 1671176 | tf_op jit(solution)/shard_map/ppermute | solution.py:403
  8.9 0.7 %collective-permute-start.2 = (f32[128,1024]{1,0:T(8,128)}, f32[128,1024]{1,0:T(8,128)S(1)}, u32[]{:S(2)}, u32[]{:S(2)}) collective-permute-start(f32[128,1024]{1,0:T(8,128)} %get-tuple-element.25), channel_id=1, source_target_pairs={{4,8},{12,16},{20,24},{8,4},{16,12},{24,20},{5,9},{13,17},{21,25},... | collective-permute-start | bytes 1572872 | tf_op jit(solution)/shard_map/ppermute | solution.py:403
  9.6 0.9 %collective-permute-done.1.near_ref = f32[136,1024]{1,0:T(8,128)S(1)} collective-permute-done((f32[136,1024]{1,0:T(8,128)S(1)}, f32[136,1024]{1,0:T(8,128)S(1)}, u32[]{:S(2)}, u32[]{:S(2)}) %collective-permute-start.1) | collective-permute-done | bytes 557088 | tf_op jit(solution)/shard_map/ppermute | solution.py:403
  10.5 2.6 %moments.1 = (f32[288,128]{1,0:T(8,128)}, f32[128,1024]{1,0:T(8,128)S(1)}) custom-call(f32[128,1024]{1,0:T(8,128)S(1)} %copy-done, f32[128,1024]{1,0:T(8,128)S(1)} %subtract_multiply_fusion.w_ref, f32[4,1024]{1,0:T(4,128)S(1)} %collective-permute-done.narrow_ref, f32[136,1024]{1,0:T(8,128)S(1)} %collective-permute-done.1.near_ref), custom_call_target="tpu_custom_call" | custom-call | tf_op jit(solution)/shard_map/moments/pallas_call | solution.py:411
  13.1 7.3 %all-to-all-start = ((f32[32,1,1152]{2,1,0:T(1,128)}), f32[32,1,1152]{2,1,0:T(1,128)}, u32[]{:S(2)}, u32[]{:S(2)}) async-start(f32[32,1,1152]{2,1,0:T(1,128)} %bitcast), calls=%async_computation | async-start | bytes 294912 | tf_op jit(solution)/shard_map/all_to_all | solution.py:457
  20.4 0.0 copy-start.1
  20.4 0.0 collective-permute-done.2.far_ref
  20.4 0.4 %fields.1 = (f32[64,1024]{1,0:T(8,128)S(1)}, f32[64,1024]{1,0:T(8,128)S(1)}) custom-call(f32[128,1024]{1,0:T(8,128)S(1)} %copy-done, f32[128,1024]{1,0:T(8,128)S(1)} %subtract_multiply_fusion.w_ref, f32[4,1024]{1,0:T(4,128)S(1)} %collective-permute-done.narrow_ref, f32[136,1024]{1,0:T(8,128)S(1)} %collective-permute-done.1.near_ref, ...), custom_call_target="tpu_custom_call" | custom-call | tf_op jit(solution)/shard_map/fields/pallas_call | solution.py:411
  20.8 0.0 copy-start.3
  20.8 0.7 %copy-done.3 = f32[64,1024]{1,0:T(8,128)} copy-done((f32[64,1024]{1,0:T(8,128)}, f32[64,1024]{1,0:T(8,128)S(1)}, u32[]{:S(2)}) %copy-start.3) | copy-done | bytes 262168
  21.5 7.5 %all-to-all-done.parts_ref = f32[32,1,1152]{2,1,0:T(1,128)} async-done(((f32[32,1,1152]{2,1,0:T(1,128)}), f32[32,1,1152]{2,1,0:T(1,128)}, u32[]{:S(2)}, u32[]{:S(2)}) %all-to-all-start) | async-done | bytes 147488 | tf_op jit(solution)/shard_map/all_to_all | solution.py:457
  29.0 0.0 copy-done.1
  29.0 0.0 copy-start.4
  29.0 0.9 %copy-done.4 = f32[64,1024]{1,0:T(8,128)S(1)} copy-done((f32[64,1024]{1,0:T(8,128)S(1)}, f32[64,1024]{1,0:T(8,128)}, u32[]{:S(2)}) %copy-start.4) | copy-done | bytes 262168
  30.0 0.0 copy-start.2
  30.0 0.0 copy-start.5
  30.0 1.7 %edges.1 = (f32[16,128]{1,0:T(8,128)S(1)}, f32[256,128]{1,0:T(8,128)S(1)}, f32[256,128]{1,0:T(8,128)S(1)}, f32[64,128]{1,0:T(8,128)S(1)}, f32[64,128]{1,0:T(8,128)S(1)}) custom-call(f32[32,1,1152]{2,1,0:T(1,128)} %all-to-all-done.parts_ref, f32[128,1024]{1,0:T(8,128)S(1)} %copy-done, f32[128,1024]{1,0:T(8,128)S(1)} %subtract_multiply_fusion.w_ref, ...), custom_call_target="tpu_custom_call" | custom-call | tf_op jit(solution)/shard_map/edges/pallas_call | solution.py:411
  31.6 1.6 %collective-permute-start.3 = (f32[64,128]{1,0:T(8,128)S(1)}, f32[64,128]{1,0:T(8,128)S(1)}, u32[]{:S(2)}, u32[]{:S(2)}) collective-permute-start(f32[64,128]{1,0:T(8,128)S(1)} %get-tuple-element.34), channel_id=1, source_target_pairs={{0,1},{1,2},{2,3},{4,5},{5,6},{6,7},{8,9},{9,10},{10,11},{12,13},{... | collective-permute-start | bytes 98312 | tf_op jit(solution)/shard_map/ppermute | solution.py:397
  33.3 1.3 %collective-permute-start.4 = (f32[64,128]{1,0:T(8,128)S(1)}, f32[64,128]{1,0:T(8,128)S(1)}, u32[]{:S(2)}, u32[]{:S(2)}) collective-permute-start(f32[64,128]{1,0:T(8,128)S(1)} %get-tuple-element.35), channel_id=1, source_target_pairs={{1,0},{2,1},{3,2},{5,4},{6,5},{7,6},{9,8},{10,9},{11,10},{13,12},{... | collective-permute-start | bytes 98312 | tf_op jit(solution)/shard_map/ppermute | solution.py:397
  34.6 0.0 copy-done.2
  34.6 0.0 copy-done.5
  34.6 1.8 %main.1 = (f32[128,1024]{1,0:T(8,128)}, f32[128,1024]{1,0:T(8,128)}, f32[128,512]{1,0:T(8,128)S(1)}) custom-call(f32[16,128]{1,0:T(8,128)S(1)} %get-tuple-element.28.coefficients_ref, f32[256,128]{1,0:T(8,128)S(1)} %get-tuple-element.29.left_ref, f32[256,128]{1,0:T(8,128)S(1)} %get-tuple-element.30.right_ref, f32[128,1024]{1,0:T(8,128)S(1)} %copy-done, ...), custom_call_target="tpu_custom_call" | custom-call | tf_op jit(solution)/shard_map/main/pallas_call | solution.py:411
  36.4 0.0 collective-permute-done.3.left_ref
  36.4 2.7 %collective-permute-done.4.right_ref = f32[64,128]{1,0:T(8,128)S(1)} collective-permute-done((f32[64,128]{1,0:T(8,128)S(1)}, f32[64,128]{1,0:T(8,128)S(1)}, u32[]{:S(2)}, u32[]{:S(2)}) %collective-permute-start.4) | collective-permute-done | bytes 32800 | tf_op jit(solution)/shard_map/ppermute | solution.py:397
  39.1 1.0 %final.1 = f32[128,1024]{1,0:T(8,128)} custom-call(f32[128,1024]{1,0:T(8,128)} %get-tuple-element.32.rms_in_ref, f32[128,512]{1,0:T(8,128)S(1)} %get-tuple-element.33.sides_ref, f32[64,128]{1,0:T(8,128)S(1)} %collective-permute-done.3.left_ref, f32[64,128]{1,0:T(8,128)S(1)} %collective-permute-done.4.right_ref, ...), custom_call_target="tpu_custom_call", output_to_operand_aliasing={{}: (0, {})} | custom-call | tf_op jit(solution)/shard_map/final/pallas_call | solution.py:411
  (1 shorter events, 0.0 us)
Async XLA Ops:
  1.6 2.1 %copy-start = (f32[128,1024]{1,0:T(8,128)S(1)}, f32[128,1024]{1,0:T(8,128)}, u32[]{:S(2)}) copy-start(f32[128,1024]{1,0:T(8,128)} %f_ref.9) | copy-start | bytes 1572868
  1.6 3.0 %collective-permute-start = (f32[4,1024]{1,0:T(4,128)S(1)}, f32[4,1024]{1,0:T(4,128)S(1)}, u32[]{:S(2)}, u32[]{:S(2)}) collective-permute-start(f32[4,1024]{1,0:T(4,128)S(1)} %pad_maximum_fusion), channel_id=1, source_target_pairs={{4,8},{12,16},{20,24},{8,4},{16,12},{24,20},{5,9},{13,17},{21,25},... | collective-permute-start | bytes 49160 | tf_op jit(solution)/shard_map/ppermute | solution.py:403
  4.6 5.9 %collective-permute-start.1 = (f32[136,1024]{1,0:T(8,128)S(1)}, f32[136,1024]{1,0:T(8,128)S(1)}, u32[]{:S(2)}, u32[]{:S(2)}) collective-permute-start(f32[136,1024]{1,0:T(8,128)S(1)} %get-tuple-element.22), channel_id=1, source_target_pairs={{0,4},{8,12},{16,20},{24,28},{4,0},{12,8},{20,16},{28,24},{1,5},{9... | collective-permute-start | bytes 1671176 | tf_op jit(solution)/shard_map/ppermute | solution.py:403
  8.9 11.5 %collective-permute-start.2 = (f32[128,1024]{1,0:T(8,128)}, f32[128,1024]{1,0:T(8,128)S(1)}, u32[]{:S(2)}, u32[]{:S(2)}) collective-permute-start(f32[128,1024]{1,0:T(8,128)} %get-tuple-element.25), channel_id=1, source_target_pairs={{4,8},{12,16},{20,24},{8,4},{16,12},{24,20},{5,9},{13,17},{21,25},... | collective-permute-start | bytes 1572872 | tf_op jit(solution)/shard_map/ppermute | solution.py:403
  13.1 15.9 %all-to-all-start = ((f32[32,1,1152]{2,1,0:T(1,128)}), f32[32,1,1152]{2,1,0:T(1,128)}, u32[]{:S(2)}, u32[]{:S(2)}) async-start(f32[32,1,1152]{2,1,0:T(1,128)} %bitcast), calls=%async_computation | async-start | bytes 294912 | tf_op jit(solution)/shard_map/all_to_all | solution.py:457
  20.4 8.6 %copy-start.1 = (bf16[4,256,256]{2,1,0:T(8,128)(2,1)S(1)}, bf16[4,256,256]{2,1,0:T(8,128)(2,1)}, u32[]{:S(2)}) copy-start(bf16[4,256,256]{2,1,0:T(8,128)(2,1)} %constant.44.clone.rowtaps_ref) | copy-start | bytes 1572868
  20.8 0.7 %copy-start.3 = (f32[64,1024]{1,0:T(8,128)}, f32[64,1024]{1,0:T(8,128)S(1)}, u32[]{:S(2)}) copy-start(f32[64,1024]{1,0:T(8,128)S(1)} %get-tuple-element.27.far_v1_ref) | copy-start | bytes 786436
  29.0 1.0 %copy-start.4 = (f32[64,1024]{1,0:T(8,128)S(1)}, f32[64,1024]{1,0:T(8,128)}, u32[]{:S(2)}) copy-start(f32[64,1024]{1,0:T(8,128)} %copy-done.3) | copy-start | bytes 786436
  30.0 4.6 %copy-start.2 = (bf16[3,256,256]{2,1,0:T(8,128)(2,1)S(1)}, bf16[3,256,256]{2,1,0:T(8,128)(2,1)}, u32[]{:S(2)}) copy-start(bf16[3,256,256]{2,1,0:T(8,128)(2,1)} %constant.45.clone.coltaps_ref) | copy-start | bytes 1179652
  30.0 4.6 %copy-start.5 = (f32[64,1024]{1,0:T(8,128)S(1)}, f32[64,1024]{1,0:T(8,128)}, u32[]{:S(2)}) copy-start(f32[64,1024]{1,0:T(8,128)} %copy-done.3) | copy-start | bytes 786436
  31.6 4.7 %collective-permute-start.3 = (f32[64,128]{1,0:T(8,128)S(1)}, f32[64,128]{1,0:T(8,128)S(1)}, u32[]{:S(2)}, u32[]{:S(2)}) collective-permute-start(f32[64,128]{1,0:T(8,128)S(1)} %get-tuple-element.34), channel_id=1, source_target_pairs={{0,1},{1,2},{2,3},{4,5},{5,6},{6,7},{8,9},{9,10},{10,11},{12,13},{... | collective-permute-start | bytes 98312 | tf_op jit(solution)/shard_map/ppermute | solution.py:397
  33.3 5.8 %collective-permute-start.4 = (f32[64,128]{1,0:T(8,128)S(1)}, f32[64,128]{1,0:T(8,128)S(1)}, u32[]{:S(2)}, u32[]{:S(2)}) collective-permute-start(f32[64,128]{1,0:T(8,128)S(1)} %get-tuple-element.35), channel_id=1, source_target_pairs={{1,0},{2,1},{3,2},{5,4},{6,5},{7,6},{9,8},{10,9},{11,10},{13,12},{... | collective-permute-start | bytes 98312 | tf_op jit(solution)/shard_map/ppermute | solution.py:397

commit v9 on v8

--- a/solution.py
+++ b/solution.py
@@ -403,14 +403,17 @@
     return lax.ppermute(block, axis, pairs + [(j, i) for i, j in pairs])
 
 
-def call(kernel, name, outs, scratch=(), limit=16, in_place=False):
+def call(kernel, name, outs, scratch=(), limit=16, in_place=False, kept=()):
     vmem = pl.BlockSpec(memory_space=pltpu.VMEM)
     there = pl.BlockSpec(memory_space=pl.ANY)
 
     def run(*args):
         return pl.pallas_call(
             kernel,
-            out_shape=tuple(jax.ShapeDtypeStruct(shape, jnp.float32) for shape in outs),
+            out_shape=tuple(
+                pltpu.VMEM(shape, jnp.float32) if i in kept else jax.ShapeDtypeStruct(shape, jnp.float32)
+                for i, shape in enumerate(outs)
+            ),
             in_specs=[there if in_place and i == 0 else vmem for i in range(len(args))],
             out_specs=(there if in_place else vmem,) * len(outs),
             scratch_shapes=list(scratch),
@@ -441,7 +444,7 @@
     narrow = swap(jnp.concatenate([products[0], products[1], taken[0][1], products[2]]), "rows", 1)
 
     own = (coadd_flux, weights(inverse_variance, source_mask))
-    to_near, to_far = call(wide_kernel, "wide", ((2 * REACH + 8, cols), (2 * REACH, cols)))(*own)
+    to_near, to_far = call(wide_kernel, "wide", ((2 * REACH + 8, cols), (2 * REACH, cols)), kept=(0, 1))(*own)
     to_near, to_far, narrow = lax.optimization_barrier((to_near, to_far, narrow))
     near = swap(to_near, "rows", 0)
     far = swap(to_far, "rows", 1)
@@ -453,10 +456,16 @@
         "moments",
         ((devices * (VECTORS + 1), LANES), (rows, cols)),
         (field, field, scratch(rows, LANES)),
+        kept=(1,),
     )(*own, narrow, near)
     parts = lax.all_to_all(parts.reshape(devices, 1, message), ("rows", "cols"), 0, 0, tiled=True)
+    parts = pltpu.with_memory_space_constraint(parts, pltpu.VMEM)
     near_v1, far_v1 = call(
-        fields_kernel, "fields", ((REACH, cols), (REACH, cols)), (scratch(REACH + 2 * NEAR, cols + LANES),)
+        fields_kernel,
+        "fields",
+        ((REACH, cols), (REACH, cols)),
+        (scratch(REACH + 2 * NEAR, cols + LANES),),
+        kept=(0, 1),
     )(*own, narrow, near, far)
 
     row_taps, col_taps = jnp.asarray(row_tables(rows)), jnp.asarray(col_tables())
@@ -467,6 +476,7 @@
         "edges",
         ((16, LANES), (reached, LANES), (reached, LANES), packed, packed),
         (scratch(reached, 2 * LANES, dtype=jnp.bfloat16),) * 2,
+        kept=range(5),
     )(parts, *fields, row_taps)
     from_left = shift(last, "cols", 1)
     from_right = shift(first, "cols", -1)
@@ -475,7 +485,7 @@
         "main",
         ((rows, cols), (rows, cols), (rows, 4 * LANES)),
         (scratch(reached, cols, dtype=jnp.bfloat16),) * 2,
-        32,
+        kept=(2,),
     )(numbers, left, right, *fields, row_taps, col_taps)
     (rms,) = call(
         final_kernel, "final", ((rows, cols),), (scratch(2, rows, LANES), pltpu.SemaphoreType.DMA((2,))), in_place=True

time: 40.5 us -> 40.5 us (level)
    unnamed x12 -> x10, local copies, waits for them, and re-layouts: 1.67 us -> 1.66 us
where the time goes in v9:
time: 40.5 us; the launch traced here: 40.1 us
  starting transfers between devices  16 us (40%)
  waiting for transfers between devices  11.1 us (27%)
  Pallas kernels  8.34 us (21%)
  other arithmetic  2.23 us (6%)
  local copies, waits for them, and re-layouts  1.66 us (4%)
  between operations  0.77 us (2%)
    pallas_call x6, Pallas kernels, run(): pl.pallas_call(kernel, out_shape=tuple((pltpu.VMEM(shape, jnp.float32) if...  8.34 us
    all_to_all x1, waiting for transfers between devices, shards(): lax.all_to_all(parts.reshape(devices, 1, message), ('rows', 'cols'), 0, 0...  7.47 us
    all_to_all x1, starting transfers between devices, shards(): lax.all_to_all(parts.reshape(devices, 1, message), ('rows', 'cols'), 0, 0...  7.3 us
    ppermute x3, starting transfers between devices, swap(): return lax.ppermute(block, axis, pairs + [(j, i) for i, j in pairs])  5.78 us
    ppermute x2, starting transfers between devices, shift(): return lax.ppermute(block, axis, pairs)  2.91 us
    ppermute x2, waiting for transfers between devices, shift(): return lax.ppermute(block, axis, pairs)  2.73 us
    unnamed x10, local copies, waits for them, and re-layouts  1.66 us
    mul x1, other arithmetic, weights(): return inverse_variance * (1.0 - source_mask.astype(jnp.float32))  1.27 us
  transfers between devices with their start and end apart: 6, of which 3 were waited for; matrix products, arithmetic and copies ran while one was open for 3% of the time, Pallas kernels for 14%

profile of v9, /device:TPU:0, one launch (start us, length us, event | category | flops | bytes accessed | tf_op | source)
XLA Modules:
  0.0 40.1 jit_solution(1678781033142766952)
XLA Ops:
  0.6 0.9 %dynamic-slice_multiply_fusion = (f32[1,1024]{1,0:T(1,128)S(1)}, f32[1,1024]{1,0:T(1,128)S(1)}, f32[1,1024]{1,0:T(1,128)S(1)}, f32[1,1024]{1,0:T(1,128)S(1)}) fusion(f32[128,1024]{1,0:T(8,128)} %f_ref.9, s32[]{:T(128)S(6)} %select_n.31, s32[128,1024]{1,0:T(8,128)} %param.7, f32[128,1024]{1,0:T(8,128)} %param.6, s32[]{:T(128)S(6)} %select_n.32, s32[]{:T(128)S(6)} %select_n.33), kind=kLoop, calls=%fused_computation.5 | loop fusion | flops 12288 | bytes 53260 | tf_op jit(solution)/shard_map/mul | solution.py:443
  1.6 0.0 copy-start
  1.6 0.8 %collective-permute-start = (f32[4,1024]{1,0:T(4,128)S(1)}, f32[4,1024]{1,0:T(4,128)S(1)}, u32[]{:S(2)}, u32[]{:S(2)}) collective-permute-start(f32[4,1024]{1,0:T(4,128)S(1)} %pad_maximum_fusion), channel_id=1, source_target_pairs={{4,8},{12,16},{20,24},{8,4},{16,12},{24,20},{5,9},{13,17},{21,25},... | collective-permute-start | bytes 49160 | tf_op jit(solution)/shard_map/ppermute | solution.py:403
  2.4 1.3 %subtract_multiply_fusion.w_ref = f32[128,1024]{1,0:T(8,128)S(1)} fusion(f32[128,1024]{1,0:T(8,128)} %param.6, s32[128,1024]{1,0:T(8,128)} %param.7), kind=kLoop, calls=%fused_computation | loop fusion | flops 393216 | bytes 1572864 | tf_op jit(solution)/shard_map/mul | solution.py:92
  3.7 0.0 copy-done
  3.7 0.9 %wide.1 = (f32[136,1024]{1,0:T(8,128)S(1)}, f32[128,1024]{1,0:T(8,128)}) custom-call(f32[128,1024]{1,0:T(8,128)S(1)} %copy-done, f32[128,1024]{1,0:T(8,128)S(1)} %subtract_multiply_fusion.w_ref), custom_call_target="tpu_custom_call" | custom-call | tf_op jit(solution)/shard_map/wide/pallas_call | solution.py:411
  4.6 0.0 collective-permute-done.narrow_ref
  4.6 4.3 %collective-permute-start.1 = (f32[136,1024]{1,0:T(8,128)S(1)}, f32[136,1024]{1,0:T(8,128)S(1)}, u32[]{:S(2)}, u32[]{:S(2)}) collective-permute-start(f32[136,1024]{1,0:T(8,128)S(1)} %get-tuple-element.22), channel_id=1, source_target_pairs={{0,4},{8,12},{16,20},{24,28},{4,0},{12,8},{20,16},{28,24},{1,5},{9... | collective-permute-start | bytes 1671176 | tf_op jit(solution)/shard_map/ppermute | solution.py:403
  8.9 0.7 %collective-permute-start.2 = (f32[128,1024]{1,0:T(8,128)}, f32[128,1024]{1,0:T(8,128)S(1)}, u32[]{:S(2)}, u32[]{:S(2)}) collective-permute-start(f32[128,1024]{1,0:T(8,128)} %get-tuple-element.25), channel_id=1, source_target_pairs={{4,8},{12,16},{20,24},{8,4},{16,12},{24,20},{5,9},{13,17},{21,25},... | collective-permute-start | bytes 1572872 | tf_op jit(solution)/shard_map/ppermute | solution.py:403
  9.6 0.9 %collective-permute-done.1.near_ref = f32[136,1024]{1,0:T(8,128)S(1)} collective-permute-done((f32[136,1024]{1,0:T(8,128)S(1)}, f32[136,1024]{1,0:T(8,128)S(1)}, u32[]{:S(2)}, u32[]{:S(2)}) %collective-permute-start.1) | collective-permute-done | bytes 557088 | tf_op jit(solution)/shard_map/ppermute | solution.py:403
  10.5 2.6 %moments.1 = (f32[288,128]{1,0:T(8,128)}, f32[128,1024]{1,0:T(8,128)S(1)}) custom-call(f32[128,1024]{1,0:T(8,128)S(1)} %copy-done, f32[128,1024]{1,0:T(8,128)S(1)} %subtract_multiply_fusion.w_ref, f32[4,1024]{1,0:T(4,128)S(1)} %collective-permute-done.narrow_ref, f32[136,1024]{1,0:T(8,128)S(1)} %collective-permute-done.1.near_ref), custom_call_target="tpu_custom_call" | custom-call | tf_op jit(solution)/shard_map/moments/pallas_call | solution.py:411
  13.1 7.3 %all-to-all-start = ((f32[32,1,1152]{2,1,0:T(1,128)}), f32[32,1,1152]{2,1,0:T(1,128)}, u32[]{:S(2)}, u32[]{:S(2)}) async-start(f32[32,1,1152]{2,1,0:T(1,128)} %bitcast), calls=%async_computation | async-start | bytes 294912 | tf_op jit(solution)/shard_map/all_to_all | solution.py:461
  20.4 0.0 copy-start.1
  20.4 0.0 collective-permute-done.2.far_ref
  20.4 0.4 %fields.1 = (f32[64,1024]{1,0:T(8,128)S(1)}, f32[64,1024]{1,0:T(8,128)S(1)}) custom-call(f32[128,1024]{1,0:T(8,128)S(1)} %copy-done, f32[128,1024]{1,0:T(8,128)S(1)} %subtract_multiply_fusion.w_ref, f32[4,1024]{1,0:T(4,128)S(1)} %collective-permute-done.narrow_ref, f32[136,1024]{1,0:T(8,128)S(1)} %collective-permute-done.1.near_ref, ...), custom_call_target="tpu_custom_call" | custom-call | tf_op jit(solution)/shard_map/fields/pallas_call | solution.py:411
  20.8 0.0 copy-start.3
  20.8 0.7 %copy-done.3 = f32[64,1024]{1,0:T(8,128)} copy-done((f32[64,1024]{1,0:T(8,128)}, f32[64,1024]{1,0:T(8,128)S(1)}, u32[]{:S(2)}) %copy-start.3) | copy-done | bytes 262168
  21.5 7.5 %all-to-all-done.parts_ref = f32[32,1,1152]{2,1,0:T(1,128)} async-done(((f32[32,1,1152]{2,1,0:T(1,128)}), f32[32,1,1152]{2,1,0:T(1,128)}, u32[]{:S(2)}, u32[]{:S(2)}) %all-to-all-start) | async-done | bytes 147488 | tf_op jit(solution)/shard_map/all_to_all | solution.py:461
  29.0 0.0 copy-done.1
  29.0 0.0 copy-start.4
  29.0 0.9 %copy-done.4 = f32[64,1024]{1,0:T(8,128)S(1)} copy-done((f32[64,1024]{1,0:T(8,128)S(1)}, f32[64,1024]{1,0:T(8,128)}, u32[]{:S(2)}) %copy-start.4) | copy-done | bytes 262168
  30.0 0.0 copy-start.2
  30.0 1.7 %edges.1 = (f32[16,128]{1,0:T(8,128)S(1)}, f32[256,128]{1,0:T(8,128)S(1)}, f32[256,128]{1,0:T(8,128)S(1)}, f32[64,128]{1,0:T(8,128)S(1)}, f32[64,128]{1,0:T(8,128)S(1)}) custom-call(f32[32,1,1152]{2,1,0:T(1,128)} %all-to-all-done.parts_ref, f32[128,1024]{1,0:T(8,128)S(1)} %copy-done, f32[128,1024]{1,0:T(8,128)S(1)} %subtract_multiply_fusion.w_ref, ...), custom_call_target="tpu_custom_call" | custom-call | tf_op jit(solution)/shard_map/edges/pallas_call | solution.py:411
  31.6 1.6 %collective-permute-start.3 = (f32[64,128]{1,0:T(8,128)S(1)}, f32[64,128]{1,0:T(8,128)S(1)}, u32[]{:S(2)}, u32[]{:S(2)}) collective-permute-start(f32[64,128]{1,0:T(8,128)S(1)} %get-tuple-element.34), channel_id=1, source_target_pairs={{0,1},{1,2},{2,3},{4,5},{5,6},{6,7},{8,9},{9,10},{10,11},{12,13},{... | collective-permute-start | bytes 98312 | tf_op jit(solution)/shard_map/ppermute | solution.py:397
  33.3 1.3 %collective-permute-start.4 = (f32[64,128]{1,0:T(8,128)S(1)}, f32[64,128]{1,0:T(8,128)S(1)}, u32[]{:S(2)}, u32[]{:S(2)}) collective-permute-start(f32[64,128]{1,0:T(8,128)S(1)} %get-tuple-element.35), channel_id=1, source_target_pairs={{1,0},{2,1},{3,2},{5,4},{6,5},{7,6},{9,8},{10,9},{11,10},{13,12},{... | collective-permute-start | bytes 98312 | tf_op jit(solution)/shard_map/ppermute | solution.py:397
  34.6 0.0 copy-done.2
  34.6 1.8 %main.1 = (f32[128,1024]{1,0:T(8,128)}, f32[128,1024]{1,0:T(8,128)}, f32[128,512]{1,0:T(8,128)S(1)}) custom-call(f32[16,128]{1,0:T(8,128)S(1)} %get-tuple-element.28.coefficients_ref, f32[256,128]{1,0:T(8,128)S(1)} %get-tuple-element.29.left_ref, f32[256,128]{1,0:T(8,128)S(1)} %get-tuple-element.30.right_ref, f32[128,1024]{1,0:T(8,128)S(1)} %copy-done, ...), custom_call_target="tpu_custom_call" | custom-call | tf_op jit(solution)/shard_map/main/pallas_call | solution.py:411
  36.3 0.0 collective-permute-done.3.left_ref
  36.3 2.7 %collective-permute-done.4.right_ref = f32[64,128]{1,0:T(8,128)S(1)} collective-permute-done((f32[64,128]{1,0:T(8,128)S(1)}, f32[64,128]{1,0:T(8,128)S(1)}, u32[]{:S(2)}, u32[]{:S(2)}) %collective-permute-start.4) | collective-permute-done | bytes 32800 | tf_op jit(solution)/shard_map/ppermute | solution.py:397
  39.1 1.0 %final.1 = f32[128,1024]{1,0:T(8,128)} custom-call(f32[128,1024]{1,0:T(8,128)} %get-tuple-element.32.rms_in_ref, f32[128,512]{1,0:T(8,128)S(1)} %get-tuple-element.33.sides_ref, f32[64,128]{1,0:T(8,128)S(1)} %collective-permute-done.3.left_ref, f32[64,128]{1,0:T(8,128)S(1)} %collective-permute-done.4.right_ref, ...), custom_call_target="tpu_custom_call", output_to_operand_aliasing={{}: (0, {})} | custom-call | tf_op jit(solution)/shard_map/final/pallas_call | solution.py:411
  (1 shorter events, 0.0 us)
Async XLA Ops:
  1.6 2.1 %copy-start = (f32[128,1024]{1,0:T(8,128)S(1)}, f32[128,1024]{1,0:T(8,128)}, u32[]{:S(2)}) copy-start(f32[128,1024]{1,0:T(8,128)} %f_ref.9) | copy-start | bytes 1572868
  1.6 3.0 %collective-permute-start = (f32[4,1024]{1,0:T(4,128)S(1)}, f32[4,1024]{1,0:T(4,128)S(1)}, u32[]{:S(2)}, u32[]{:S(2)}) collective-permute-start(f32[4,1024]{1,0:T(4,128)S(1)} %pad_maximum_fusion), channel_id=1, source_target_pairs={{4,8},{12,16},{20,24},{8,4},{16,12},{24,20},{5,9},{13,17},{21,25},... | collective-permute-start | bytes 49160 | tf_op jit(solution)/shard_map/ppermute | solution.py:403
  4.6 5.9 %collective-permute-start.1 = (f32[136,1024]{1,0:T(8,128)S(1)}, f32[136,1024]{1,0:T(8,128)S(1)}, u32[]{:S(2)}, u32[]{:S(2)}) collective-permute-start(f32[136,1024]{1,0:T(8,128)S(1)} %get-tuple-element.22), channel_id=1, source_target_pairs={{0,4},{8,12},{16,20},{24,28},{4,0},{12,8},{20,16},{28,24},{1,5},{9... | collective-permute-start | bytes 1671176 | tf_op jit(solution)/shard_map/ppermute | solution.py:403
  8.9 11.5 %collective-permute-start.2 = (f32[128,1024]{1,0:T(8,128)}, f32[128,1024]{1,0:T(8,128)S(1)}, u32[]{:S(2)}, u32[]{:S(2)}) collective-permute-start(f32[128,1024]{1,0:T(8,128)} %get-tuple-element.25), channel_id=1, source_target_pairs={{4,8},{12,16},{20,24},{8,4},{16,12},{24,20},{5,9},{13,17},{21,25},... | collective-permute-start | bytes 1572872 | tf_op jit(solution)/shard_map/ppermute | solution.py:403
  13.1 15.9 %all-to-all-start = ((f32[32,1,1152]{2,1,0:T(1,128)}), f32[32,1,1152]{2,1,0:T(1,128)}, u32[]{:S(2)}, u32[]{:S(2)}) async-start(f32[32,1,1152]{2,1,0:T(1,128)} %bitcast), calls=%async_computation | async-start | bytes 294912 | tf_op jit(solution)/shard_map/all_to_all | solution.py:461
  20.4 8.6 %copy-start.1 = (bf16[4,256,256]{2,1,0:T(8,128)(2,1)S(1)}, bf16[4,256,256]{2,1,0:T(8,128)(2,1)}, u32[]{:S(2)}) copy-start(bf16[4,256,256]{2,1,0:T(8,128)(2,1)} %constant.44.clone.rowtaps_ref) | copy-start | bytes 1572868
  20.8 0.7 %copy-start.3 = (f32[64,1024]{1,0:T(8,128)}, f32[64,1024]{1,0:T(8,128)S(1)}, u32[]{:S(2)}) copy-start(f32[64,1024]{1,0:T(8,128)S(1)} %get-tuple-element.27.far_v1_ref) | copy-start | bytes 786436
  29.0 1.0 %copy-start.4 = (f32[64,1024]{1,0:T(8,128)S(1)}, f32[64,1024]{1,0:T(8,128)}, u32[]{:S(2)}) copy-start(f32[64,1024]{1,0:T(8,128)} %copy-done.3) | copy-start | bytes 786436
  30.0 4.6 %copy-start.2 = (bf16[3,256,256]{2,1,0:T(8,128)(2,1)S(1)}, bf16[3,256,256]{2,1,0:T(8,128)(2,1)}, u32[]{:S(2)}) copy-start(bf16[3,256,256]{2,1,0:T(8,128)(2,1)} %constant.45.clone.coltaps_ref) | copy-start | bytes 1179652
  31.6 4.7 %collective-permute-start.3 = (f32[64,128]{1,0:T(8,128)S(1)}, f32[64,128]{1,0:T(8,128)S(1)}, u32[]{:S(2)}, u32[]{:S(2)}) collective-permute-start(f32[64,128]{1,0:T(8,128)S(1)} %get-tuple-element.34), channel_id=1, source_target_pairs={{0,1},{1,2},{2,3},{4,5},{5,6},{6,7},{8,9},{9,10},{10,11},{12,13},{... | collective-permute-start | bytes 98312 | tf_op jit(solution)/shard_map/ppermute | solution.py:397
  33.3 5.8 %collective-permute-start.4 = (f32[64,128]{1,0:T(8,128)S(1)}, f32[64,128]{1,0:T(8,128)S(1)}, u32[]{:S(2)}, u32[]{:S(2)}) collective-permute-start(f32[64,128]{1,0:T(8,128)S(1)} %get-tuple-element.35), channel_id=1, source_target_pairs={{1,0},{2,1},{3,2},{5,4},{6,5},{7,6},{9,8},{10,9},{11,10},{13,12},{... | collective-permute-start | bytes 98312 | tf_op jit(solution)/shard_map/ppermute | solution.py:397

commit v10 on v8

--- a/solution.py
+++ b/solution.py
@@ -253,7 +253,7 @@
     return sides
 
 
-def fields_kernel(f_ref, w_ref, narrow_ref, near_ref, far_ref, near_v1_ref, far_v1_ref, v0_ref):
+def halo_fields(f_ref, w_ref, narrow_ref, near_ref, far_ref, near_v1_ref, far_v1_ref, v0_ref):
     rows, cols = f_ref.shape
     own, pad = pl.ds(0, cols), pl.ds(cols, LANES)
     even = is_even()
@@ -292,18 +292,17 @@
 
 
 def row_pass(rowtaps_ref, high, low, rows):
-    first_row, last_row, _, _ = at_edges()
-    kind = jnp.where(is_even(), first_row.astype(jnp.int32), 2 + last_row.astype(jnp.int32))
-    table = rowtaps_ref[kind]
+    table = rowtaps_ref[...]
     both = dot(table, high)
     return both[:rows] + (both[rows:] + dot(table[:rows], low))
 
 
 def edges_kernel(
-    nrows, ncols, parts_ref, f_ref, w_ref, v1_ref, near_ref, near_v1_ref, far_ref, far_v1_ref, rowtaps_ref,
-    coefficients_ref, left_ref, right_ref, first_ref, last_ref, high_ref, low_ref,
+    nrows, ncols, parts_ref, f_ref, w_ref, v1_ref, narrow_ref, near_ref, far_ref, rowtaps_ref,
+    near_v1_ref, far_v1_ref, coefficients_ref, left_ref, right_ref, first_ref, last_ref, v0_ref, high_ref, low_ref,
 ):
     rows, cols = f_ref.shape
+    halo_fields(f_ref, w_ref, narrow_ref, near_ref, far_ref, near_v1_ref, far_v1_ref, v0_ref)
     c0, c1 = coefficients(*coupled(parts_ref, nrows, ncols))
     coefficients_ref[pl.ds(0, 8), :] = jnp.broadcast_to(c0, (8, LANES))
     coefficients_ref[pl.ds(8, 8), :] = jnp.broadcast_to(c1, (8, LANES))
@@ -455,19 +454,18 @@
         (field, field, scratch(rows, LANES)),
     )(*own, narrow, near)
     parts = lax.all_to_all(parts.reshape(devices, 1, message), ("rows", "cols"), 0, 0, tiled=True)
-    near_v1, far_v1 = call(
-        fields_kernel, "fields", ((REACH, cols), (REACH, cols)), (scratch(REACH + 2 * NEAR, cols + LANES),)
-    )(*own, narrow, near, far)
-
-    row_taps, col_taps = jnp.asarray(row_tables(rows)), jnp.asarray(col_tables())
-    fields = (*own, own_v1, near, near_v1, far, far_v1)
+    first_row, last_row, _, _ = at_edges()
+    kind = jnp.where(is_even(), first_row.astype(jnp.int32), 2 + last_row.astype(jnp.int32))
+    row_taps = lax.dynamic_index_in_dim(jnp.asarray(row_tables(rows)), kind, keepdims=False)
+    col_taps = jnp.asarray(col_tables())
     reached, packed = rows + 2 * REACH, (rows // 2, LANES)
-    numbers, left, right, first, last = call(
+    near_v1, far_v1, numbers, left, right, first, last = call(
         functools.partial(edges_kernel, nrows, ncols),
         "edges",
-        ((16, LANES), (reached, LANES), (reached, LANES), packed, packed),
-        (scratch(reached, 2 * LANES, dtype=jnp.bfloat16),) * 2,
-    )(parts, *fields, row_taps)
+        ((REACH, cols), (REACH, cols), (16, LANES), (reached, LANES), (reached, LANES), packed, packed),
+        (scratch(REACH + 2 * NEAR, cols + LANES),) + (scratch(reached, 2 * LANES, dtype=jnp.bfloat16),) * 2,
+    )(parts, *own, own_v1, narrow, near, far, row_taps)
+    fields = (*own, own_v1, near, near_v1, far, far_v1)
     from_left = shift(last, "cols", 1)
     from_right = shift(first, "cols", -1)
     background, rms, sides = call(
@@ -475,7 +473,6 @@
         "main",
         ((rows, cols), (rows, cols), (rows, 4 * LANES)),
         (scratch(reached, cols, dtype=jnp.bfloat16),) * 2,
-        32,
     )(numbers, left, right, *fields, row_taps, col_taps)
     (rms,) = call(
         final_kernel, "final", ((rows, cols),), (scratch(2, rows, LANES), pltpu.SemaphoreType.DMA((2,))), in_place=True

time: 40.5 us -> 38.5 us (0.951)
  Pallas kernels: 8.36 us -> 6.49 us
  local copies, waits for them, and re-layouts: 1.67 us -> 0.93 us
    pallas_call x6 -> x5, Pallas kernels: 8.36 us -> 6.49 us  [run(): pl.pallas_call(kernel, out_shape=tuple((jax.ShapeDtypeStruct(shape, jnp.f...]
    unnamed x12 -> x4, local copies, waits for them, and re-layouts: 1.67 us -> 0.01 us
    squeeze x0 -> x1, local copies, waits for them, and re-layouts: none -> 0.92 us  [shards(): lax.dynamic_index_in_dim(jnp.asarray(row_tables(rows)), kind, keepdims=Fa...]
    all_to_all x1, starting transfers between devices: 7.3 us -> 7.9 us  [shards(): lax.all_to_all(parts.reshape(devices, 1, message), ('rows', 'cols'), 0, 0...]
  transfers between devices with their start and end apart: 6 -> 6, of which waited for: 3 -> 3; matrix products, arithmetic and copies ran while one was open for 3% -> 6% of each run, Pallas kernels for 14% -> 12%
where the time goes in v10:
time: 38.5 us; the launch traced here: 38.1 us
  starting transfers between devices  16.4 us (43%)
  waiting for transfers between devices  11.3 us (29%)
  Pallas kernels  6.49 us (17%)
  other arithmetic  2.23 us (6%)
  local copies, waits for them, and re-layouts  0.93 us (2%)
  between operations  0.78 us (2%)
    all_to_all x1, starting transfers between devices, shards(): lax.all_to_all(parts.reshape(devices, 1, message), ('rows', 'cols'), 0, 0...  7.9 us
    all_to_all x1, waiting for transfers between devices, shards(): lax.all_to_all(parts.reshape(devices, 1, message), ('rows', 'cols'), 0, 0...  7.69 us
    pallas_call x5, Pallas kernels, run(): pl.pallas_call(kernel, out_shape=tuple((jax.ShapeDtypeStruct(shape, jnp.f...  6.49 us
    ppermute x3, starting transfers between devices, swap(): return lax.ppermute(block, axis, pairs + [(j, i) for i, j in pairs])  5.84 us
    ppermute x2, waiting for transfers between devices, shift(): return lax.ppermute(block, axis, pairs)  2.72 us
    ppermute x2, starting transfers between devices, shift(): return lax.ppermute(block, axis, pairs)  2.65 us
    mul x1, other arithmetic, weights(): return inverse_variance * (1.0 - source_mask.astype(jnp.float32))  1.27 us
    mul x1, other arithmetic, shards(): products = [flux * weight for flux, weight in taken]  0.94 us
  transfers between devices with their start and end apart: 6, of which 3 were waited for; matrix products, arithmetic and copies ran while one was open for 6% of the time, Pallas kernels for 12%

profile of v10, /device:TPU:0, one launch (start us, length us, event | category | flops | bytes accessed | tf_op | source)
XLA Modules:
  0.0 38.1 jit_solution(14893848605225237493)
XLA Ops:
  0.6 0.9 %dynamic-slice_multiply_fusion = (f32[1,1024]{1,0:T(1,128)S(1)}, f32[1,1024]{1,0:T(1,128)S(1)}, f32[1,1024]{1,0:T(1,128)S(1)}, f32[1,1024]{1,0:T(1,128)S(1)}) fusion(f32[128,1024]{1,0:T(8,128)} %f_ref.7, s32[]{:T(128)S(6)} %select_n.40, s32[128,1024]{1,0:T(8,128)} %param.7, f32[128,1024]{1,0:T(8,128)} %param.6, s32[]{:T(128)S(6)} %select_n.41, s32[]{:T(128)S(6)} %select_n.42), kind=kLoop, calls=%fused_computation.6 | loop fusion | flops 12288 | bytes 53260 | tf_op jit(solution)/shard_map/mul | solution.py:439
  1.6 0.0 copy-start
  1.6 0.8 %collective-permute-start = (f32[4,1024]{1,0:T(4,128)S(1)}, f32[4,1024]{1,0:T(4,128)S(1)}, u32[]{:S(2)}, u32[]{:S(2)}) collective-permute-start(f32[4,1024]{1,0:T(4,128)S(1)} %pad_maximum_fusion), channel_id=1, source_target_pairs={{4,8},{12,16},{20,24},{8,4},{16,12},{24,20},{5,9},{13,17},{21,25},... | collective-permute-start | bytes 49160 | tf_op jit(solution)/shard_map/ppermute | solution.py:402
  2.4 1.3 %subtract_multiply_fusion.w_ref = f32[128,1024]{1,0:T(8,128)S(1)} fusion(f32[128,1024]{1,0:T(8,128)} %param.6, s32[128,1024]{1,0:T(8,128)} %param.7), kind=kLoop, calls=%fused_computation | loop fusion | flops 393216 | bytes 1572864 | tf_op jit(solution)/shard_map/mul | solution.py:92
  3.7 0.0 copy-done
  3.7 0.1 wide.1
  3.8 0.0 collective-permute-done.narrow_ref
  3.8 4.4 %collective-permute-start.1 = (f32[136,1024]{1,0:T(8,128)S(1)}, f32[136,1024]{1,0:T(8,128)S(1)}, u32[]{:S(2)}, u32[]{:S(2)}) collective-permute-start(f32[136,1024]{1,0:T(8,128)S(1)} %get-tuple-element.22), channel_id=1, source_target_pairs={{0,4},{8,12},{16,20},{24,28},{4,0},{12,8},{20,16},{28,24},{1,5},{9... | collective-permute-start | bytes 1671176 | tf_op jit(solution)/shard_map/ppermute | solution.py:402
  8.2 0.7 %collective-permute-start.2 = (f32[128,1024]{1,0:T(8,128)S(1)}, f32[128,1024]{1,0:T(8,128)S(1)}, u32[]{:S(2)}, u32[]{:S(2)}) collective-permute-start(f32[128,1024]{1,0:T(8,128)S(1)} %get-tuple-element.25), channel_id=1, source_target_pairs={{4,8},{12,16},{20,24},{8,4},{16,12},{24,20},{5,9},{13,17},{21,25},... | collective-permute-start | bytes 1572872 | tf_op jit(solution)/shard_map/ppermute | solution.py:402
  8.9 0.9 %collective-permute-done.1.near_ref = f32[136,1024]{1,0:T(8,128)S(1)} collective-permute-done((f32[136,1024]{1,0:T(8,128)S(1)}, f32[136,1024]{1,0:T(8,128)S(1)}, u32[]{:S(2)}, u32[]{:S(2)}) %collective-permute-start.1) | collective-permute-done | bytes 557088 | tf_op jit(solution)/shard_map/ppermute | solution.py:402
  9.8 2.6 %moments.1 = (f32[288,128]{1,0:T(8,128)}, f32[128,1024]{1,0:T(8,128)S(1)}) custom-call(f32[128,1024]{1,0:T(8,128)S(1)} %copy-done, f32[128,1024]{1,0:T(8,128)S(1)} %subtract_multiply_fusion.w_ref, f32[4,1024]{1,0:T(4,128)S(1)} %collective-permute-done.narrow_ref, f32[136,1024]{1,0:T(8,128)S(1)} %collective-permute-done.1.near_ref), custom_call_target="tpu_custom_call" | custom-call | tf_op jit(solution)/shard_map/moments/pallas_call | solution.py:410
  12.4 7.9 %all-to-all-start = ((f32[32,1,1152]{2,1,0:T(1,128)}), f32[32,1,1152]{2,1,0:T(1,128)S(1)}, u32[]{:S(2)}, u32[]{:S(2)}) async-start(f32[32,1,1152]{2,1,0:T(1,128)} %bitcast), calls=%async_computation | async-start | bytes 294912 | tf_op jit(solution)/shard_map/all_to_all | solution.py:456
  20.3 0.9 %dynamic-slice_bitcast_fusion.rowtaps_ref = bf16[256,256]{1,0:T(8,128)(2,1)S(1)} fusion(bf16[4,256,256]{2,1,0:T(8,128)(2,1)} %constant.53.clone, s32[]{:T(128)S(6)} %select_n.44), kind=kLoop, calls=%fused_computation.1 | loop fusion | bytes 262148 | tf_op jit(solution)/shard_map/jit(dynamic_index_in_dim)/squeeze | solution.py:459
  21.2 0.0 collective-permute-done.2.far_ref
  21.2 7.7 %all-to-all-done.parts_ref = f32[32,1,1152]{2,1,0:T(1,128)S(1)} async-done(((f32[32,1,1152]{2,1,0:T(1,128)}), f32[32,1,1152]{2,1,0:T(1,128)S(1)}, u32[]{:S(2)}, u32[]{:S(2)}) %all-to-all-start) | async-done | bytes 147488 | tf_op jit(solution)/shard_map/all_to_all | solution.py:456
  28.9 0.0 copy-start.1
  28.9 1.0 %edges.1 = (f32[64,1024]{1,0:T(8,128)S(1)}, f32[64,1024]{1,0:T(8,128)S(1)}, f32[16,128]{1,0:T(8,128)S(1)}, f32[256,128]{1,0:T(8,128)S(1)}, f32[256,128]{1,0:T(8,...) custom-call(f32[32,1,1152]{2,1,0:T(1,128)S(1)} %all-to-all-done.parts_ref, f32[128,1024]{1,0:T(8,128)S(1)} %copy-done, ...), custom_call_target="tpu_custom_call" | custom-call | tf_op jit(solution)/shard_map/edges/pallas_call | solution.py:410
  29.9 1.4 %collective-permute-start.3 = (f32[64,128]{1,0:T(8,128)S(1)}, f32[64,128]{1,0:T(8,128)S(1)}, u32[]{:S(2)}, u32[]{:S(2)}) collective-permute-start(f32[64,128]{1,0:T(8,128)S(1)} %get-tuple-element.34), channel_id=1, source_target_pairs={{0,1},{1,2},{2,3},{4,5},{5,6},{6,7},{8,9},{9,10},{10,11},{12,13},{... | collective-permute-start | bytes 98312 | tf_op jit(solution)/shard_map/ppermute | solution.py:396
  31.3 1.3 %collective-permute-start.4 = (f32[64,128]{1,0:T(8,128)S(1)}, f32[64,128]{1,0:T(8,128)S(1)}, u32[]{:S(2)}, u32[]{:S(2)}) collective-permute-start(f32[64,128]{1,0:T(8,128)S(1)} %get-tuple-element.35), channel_id=1, source_target_pairs={{1,0},{2,1},{3,2},{5,4},{6,5},{7,6},{9,8},{10,9},{11,10},{13,12},{... | collective-permute-start | bytes 98312 | tf_op jit(solution)/shard_map/ppermute | solution.py:396
  32.6 0.0 copy-done.1
  32.6 1.8 %main.1 = (f32[128,1024]{1,0:T(8,128)}, f32[128,1024]{1,0:T(8,128)}, f32[128,512]{1,0:T(8,128)S(1)}) custom-call(f32[16,128]{1,0:T(8,128)S(1)} %get-tuple-element.26.coefficients_ref, f32[256,128]{1,0:T(8,128)S(1)} %get-tuple-element.27.left_ref, f32[256,128]{1,0:T(8,128)S(1)} %get-tuple-element.28.right_ref, f32[128,1024]{1,0:T(8,128)S(1)} %copy-done, ...), custom_call_target="tpu_custom_call" | custom-call | tf_op jit(solution)/shard_map/main/pallas_call | solution.py:410
  34.4 0.0 collective-permute-done.3.left_ref
  34.4 2.7 %collective-permute-done.4.right_ref = f32[64,128]{1,0:T(8,128)S(1)} collective-permute-done((f32[64,128]{1,0:T(8,128)S(1)}, f32[64,128]{1,0:T(8,128)S(1)}, u32[]{:S(2)}, u32[]{:S(2)}) %collective-permute-start.4) | collective-permute-done | bytes 32800 | tf_op jit(solution)/shard_map/ppermute | solution.py:396
  37.1 1.0 %final.1 = f32[128,1024]{1,0:T(8,128)} custom-call(f32[128,1024]{1,0:T(8,128)} %get-tuple-element.32.rms_in_ref, f32[128,512]{1,0:T(8,128)S(1)} %get-tuple-element.33.sides_ref, f32[64,128]{1,0:T(8,128)S(1)} %collective-permute-done.3.left_ref, f32[64,128]{1,0:T(8,128)S(1)} %collective-permute-done.4.right_ref, ...), custom_call_target="tpu_custom_call", output_to_operand_aliasing={{}: (0, {})} | custom-call | tf_op jit(solution)/shard_map/final/pallas_call | solution.py:410
  (1 shorter events, 0.0 us)
Async XLA Ops:
  1.6 2.1 %copy-start = (f32[128,1024]{1,0:T(8,128)S(1)}, f32[128,1024]{1,0:T(8,128)}, u32[]{:S(2)}) copy-start(f32[128,1024]{1,0:T(8,128)} %f_ref.7) | copy-start | bytes 1572868
  1.6 2.2 %collective-permute-start = (f32[4,1024]{1,0:T(4,128)S(1)}, f32[4,1024]{1,0:T(4,128)S(1)}, u32[]{:S(2)}, u32[]{:S(2)}) collective-permute-start(f32[4,1024]{1,0:T(4,128)S(1)} %pad_maximum_fusion), channel_id=1, source_target_pairs={{4,8},{12,16},{20,24},{8,4},{16,12},{24,20},{5,9},{13,17},{21,25},... | collective-permute-start | bytes 49160 | tf_op jit(solution)/shard_map/ppermute | solution.py:402
  3.8 5.9 %collective-permute-start.1 = (f32[136,1024]{1,0:T(8,128)S(1)}, f32[136,1024]{1,0:T(8,128)S(1)}, u32[]{:S(2)}, u32[]{:S(2)}) collective-permute-start(f32[136,1024]{1,0:T(8,128)S(1)} %get-tuple-element.22), channel_id=1, source_target_pairs={{0,4},{8,12},{16,20},{24,28},{4,0},{12,8},{20,16},{28,24},{1,5},{9... | collective-permute-start | bytes 1671176 | tf_op jit(solution)/shard_map/ppermute | solution.py:402
  8.2 13.0 %collective-permute-start.2 = (f32[128,1024]{1,0:T(8,128)S(1)}, f32[128,1024]{1,0:T(8,128)S(1)}, u32[]{:S(2)}, u32[]{:S(2)}) collective-permute-start(f32[128,1024]{1,0:T(8,128)S(1)} %get-tuple-element.25), channel_id=1, source_target_pairs={{4,8},{12,16},{20,24},{8,4},{16,12},{24,20},{5,9},{13,17},{21,25},... | collective-permute-start | bytes 1572872 | tf_op jit(solution)/shard_map/ppermute | solution.py:402
  12.4 16.5 %all-to-all-start = ((f32[32,1,1152]{2,1,0:T(1,128)}), f32[32,1,1152]{2,1,0:T(1,128)S(1)}, u32[]{:S(2)}, u32[]{:S(2)}) async-start(f32[32,1,1152]{2,1,0:T(1,128)} %bitcast), calls=%async_computation | async-start | bytes 294912 | tf_op jit(solution)/shard_map/all_to_all | solution.py:456
  28.9 3.7 %copy-start.1 = (bf16[3,256,256]{2,1,0:T(8,128)(2,1)S(1)}, bf16[3,256,256]{2,1,0:T(8,128)(2,1)}, u32[]{:S(2)}) copy-start(bf16[3,256,256]{2,1,0:T(8,128)(2,1)} %constant.54.clone.coltaps_ref) | copy-start | bytes 1179652
  29.9 4.5 %collective-permute-start.3 = (f32[64,128]{1,0:T(8,128)S(1)}, f32[64,128]{1,0:T(8,128)S(1)}, u32[]{:S(2)}, u32[]{:S(2)}) collective-permute-start(f32[64,128]{1,0:T(8,128)S(1)} %get-tuple-element.34), channel_id=1, source_target_pairs={{0,1},{1,2},{2,3},{4,5},{5,6},{6,7},{8,9},{9,10},{10,11},{12,13},{... | collective-permute-start | bytes 98312 | tf_op jit(solution)/shard_map/ppermute | solution.py:396
  31.3 5.8 %collective-permute-start.4 = (f32[64,128]{1,0:T(8,128)S(1)}, f32[64,128]{1,0:T(8,128)S(1)}, u32[]{:S(2)}, u32[]{:S(2)}) collective-permute-start(f32[64,128]{1,0:T(8,128)S(1)} %get-tuple-element.35), channel_id=1, source_target_pairs={{1,0},{2,1},{3,2},{5,4},{6,5},{7,6},{9,8},{10,9},{11,10},{13,12},{... | collective-permute-start | bytes 98312 | tf_op jit(solution)/shard_map/ppermute | solution.py:396

commit v11 on v10

--- a/solution.py
+++ b/solution.py
@@ -79,8 +79,8 @@
     )
 
 
-def is_even():
-    return lax.axis_index("rows") % 2 == 0
+def is_even(axis="rows"):
+    return lax.axis_index(axis) % 2 == 0
 
 
 def beside_columns(field):
@@ -101,7 +101,16 @@
     return alpha0 + alpha1 * grown, -alpha1 * alpha0
 
 
-def wide_kernel(f_ref, w_ref, near_ref, far_ref):
+def image(ref, weight, start):
+    cols = weight.shape[1]
+    own = pl.ds(0, cols)
+    here = ref[pl.ds(start, 8), :]
+    beside = ref[pl.ds(start - 1, 8), own] + ref[pl.ds(start + 1, 8), own] + beside_columns(here)[:, :cols]
+    here = here[:, :cols]
+    return here, weight * here + smooth_weight * (4.0 * here - beside)
+
+
+def prepare_kernel(f_ref, w_ref, near_ref, far_ref, v1_ref, v0_ref):
     rows = f_ref.shape[0]
 
     def write(out_ref, begin):
@@ -123,58 +132,64 @@
         near_product(REACH)
         write(far_ref, rows - REACH)
 
-
-def moments_kernel(f_ref, w_ref, narrow_ref, near_ref, out_ref, v1_out_ref, v0_ref, v1_ref, edge_ref):
+    cols = f_ref.shape[1]
+    own = pl.ds(0, cols)
+    v0_ref[:, pl.ds(cols, LANES)] = jnp.zeros((rows + 2 * NEAR, LANES), jnp.float32)
+    for start in (0, NEAR + rows):
+        v0_ref[pl.ds(start, NEAR), own] = jnp.zeros((NEAR, cols), jnp.float32)
+    for start in range(0, rows, 8):
+        at = pl.ds(start, 8)
+        v0_ref[pl.ds(NEAR + start, 8), own] = f_ref[at, :] * w_ref[at, :]
+    for start in range(0, rows, 8):
+        _, v1_ref[pl.ds(start, 8), :] = image(v0_ref, w_ref[pl.ds(start, 8), :], NEAR + start)
+
+
+def moments_kernel(f_ref, w_ref, base_ref, narrow_ref, near_ref, out_ref, v1_out_ref, v1_ref, edge_ref):
     rows, cols = f_ref.shape
-    width = cols + LANES
     first_row, last_row, _, _ = at_edges()
     even = is_even()
     own, pad = pl.ds(0, cols), pl.ds(cols, LANES)
 
-    above, below = near_ref[pl.ds(2 * REACH - 8, 8), :], near_ref[pl.ds(REACH, 8), :]
-    nothing = jnp.zeros((6, cols), jnp.float32)
-    nearest, second, far_weight = (narrow_ref[pl.ds(k, 1), :] for k in range(3))
-    far_above = jnp.concatenate([nothing, second, nearest], axis=0)
-    far_below = jnp.concatenate([nearest, second, nothing], axis=0)
-    top = jnp.where(even, far_above, near_ref[pl.ds(REACH - 8, 8), :] * above)
-    bottom = jnp.where(even, near_ref[pl.ds(0, 8), :] * below, far_below)
-    top_weight = jnp.where(even, far_weight, above[7:])
-    bottom_weight = jnp.where(even, below[:1], far_weight)
-
-    for ref in (v0_ref, v1_ref):
-        ref[:, pad] = jnp.zeros((rows + 2 * NEAR, LANES), jnp.float32)
+    def near_rows(nearest, second):
+        return (
+            near_ref[pl.ds(nearest, 1), :] * near_ref[pl.ds(REACH + nearest, 1), :],
+            near_ref[pl.ds(second, 1), :] * near_ref[pl.ds(REACH + second, 1), :],
+            near_ref[pl.ds(REACH + nearest, 1), :],
+        )
+
+    far_rows = tuple(narrow_ref[pl.ds(k, 1), :] for k in range(3))
+    above = [jnp.where(even, far, near) for far, near in zip(far_rows, near_rows(REACH - 1, REACH - 2))]
+    below = [jnp.where(even, near, far) for far, near in zip(far_rows, near_rows(0, 1))]
+
+    v1_ref[:, pad] = jnp.zeros((rows + 2 * NEAR, LANES), jnp.float32)
     for start in (0, NEAR + rows):
-        v1_ref[pl.ds(start, 8), own] = jnp.zeros((8, cols), jnp.float32)
-    v0_ref[pl.ds(0, 8), own] = top
-    v0_ref[pl.ds(NEAR + rows, 8), own] = bottom
+        v1_ref[pl.ds(start, NEAR), own] = jnp.zeros((NEAR, cols), jnp.float32)
+    row = lax.broadcasted_iota(jnp.int32, (8, cols), 0)
     for start in range(0, rows, 8):
-        at = pl.ds(start, 8)
-        v0_ref[pl.ds(NEAR + start, 8), own] = f_ref[at, :] * w_ref[at, :]
-
-    def image(ref, weight, start, count):
-        here = ref[pl.ds(start, count), :]
-        beside = ref[pl.ds(start - 1, count), own] + ref[pl.ds(start + 1, count), own] + beside_columns(here)[:, :cols]
-        here = here[:, :cols]
-        return here, weight * here + smooth_weight * (4.0 * here - beside)
-
-    for start in range(0, rows, 8):
-        _, out = image(v0_ref, w_ref[pl.ds(start, 8), :], NEAR + start, 8)
-        v1_ref[pl.ds(NEAR + start, 8), own] = out
-        v1_out_ref[pl.ds(start, 8), :] = out
-
-    def edge_row(weight, at):
-        _, out = image(v0_ref, weight, at, 1)
-        v1_ref[pl.ds(at, 1), own] = out
-
-    pl.when(jnp.logical_not(first_row))(lambda: edge_row(top_weight, NEAR - 1))
-    pl.when(jnp.logical_not(last_row))(lambda: edge_row(bottom_weight, NEAR + rows))
+        v1 = base_ref[pl.ds(start, 8), :]
+        if start == 0:
+            v1 = v1 - jnp.where(row == 0, smooth_weight * above[0], 0.0)
+        if start == rows - 8:
+            v1 = v1 - jnp.where(row == 7, smooth_weight * below[0], 0.0)
+        v1_ref[pl.ds(NEAR + start, 8), own] = v1
+        v1_out_ref[pl.ds(start, 8), :] = v1
+
+    def edge_row(halo, inner, at):
+        nearest, second, weight = halo
+        inner = f_ref[pl.ds(inner, 1), :] * w_ref[pl.ds(inner, 1), :]
+        padded = jnp.concatenate([nearest, jnp.zeros((1, LANES), jnp.float32)], axis=1)
+        beside = second + inner + beside_columns(padded)[:, :cols]
+        v1_ref[pl.ds(at, 1), own] = weight * nearest + smooth_weight * (4.0 * nearest - beside)
+
+    pl.when(jnp.logical_not(first_row))(lambda: edge_row(above, 0, NEAR - 1))
+    pl.when(jnp.logical_not(last_row))(lambda: edge_row(below, rows - 1, NEAR + rows))
 
     lane = lax.broadcasted_iota(jnp.int32, (8, LANES), 1)
     sums = [jnp.zeros((8, cols), jnp.float32) for _ in range(4)]
     for start in range(0, rows, 8):
         weight = w_ref[pl.ds(start, 8), :]
-        v0 = v0_ref[pl.ds(NEAR + start, 8), own]
-        v1, v2 = image(v1_ref, weight, NEAR + start, 8)
+        v0 = f_ref[pl.ds(start, 8), :] * weight
+        v1, v2 = image(v1_ref, weight, NEAR + start)
         sums = [total + term for total, term in zip(sums, (v0 * v0, v0 * v1, v1 * v1, v1 * v2))]
         edges = jnp.zeros((8, LANES), jnp.float32)
         for k, field in enumerate((v0, v1, v2, weight)):
@@ -253,30 +268,51 @@
     return sides
 
 
+def guard_rows(f_ref, w_ref, narrow_ref, near_ref, at_cols):
+    rows = f_ref.shape[0]
+    even = is_even()
+    top = f_ref[pl.ds(0, 1), at_cols] * w_ref[pl.ds(0, 1), at_cols]
+    bottom = f_ref[pl.ds(rows - 1, 1), at_cols] * w_ref[pl.ds(rows - 1, 1), at_cols]
+    near = jnp.where(even, near_ref[pl.ds(2 * REACH, 1), at_cols], near_ref[pl.ds(2 * REACH + 7, 1), at_cols])
+    far = narrow_ref[pl.ds(3, 1), at_cols]
+    return (
+        (jnp.where(even, bottom, near), jnp.where(even, near, top)),
+        (jnp.where(even, far, bottom), jnp.where(even, top, far)),
+    )
+
+
 def halo_fields(f_ref, w_ref, narrow_ref, near_ref, far_ref, near_v1_ref, far_v1_ref, v0_ref):
     rows, cols = f_ref.shape
     own, pad = pl.ds(0, cols), pl.ds(cols, LANES)
-    even = is_even()
-    top = f_ref[pl.ds(0, 1), :] * w_ref[pl.ds(0, 1), :]
-    bottom = f_ref[pl.ds(rows - 1, 1), :] * w_ref[pl.ds(rows - 1, 1), :]
-    beyond_near = jnp.where(even, near_ref[pl.ds(2 * REACH, 1), :], near_ref[pl.ds(2 * REACH + 7, 1), :])
-    beyond_far = narrow_ref[pl.ds(3, 1), :]
     v0_ref[:, pad] = jnp.zeros((REACH + 2 * NEAR, LANES), jnp.float32)
-    guards = (
-        (near_ref, near_v1_ref, jnp.where(even, bottom, beyond_near), jnp.where(even, beyond_near, top)),
-        (far_ref, far_v1_ref, jnp.where(even, beyond_far, bottom), jnp.where(even, top, beyond_far)),
-    )
-    for halo_ref, v1_ref, above, below in guards:
+    guards = guard_rows(f_ref, w_ref, narrow_ref, near_ref, own)
+    for halo_ref, v1_ref, (above, below) in zip((near_ref, far_ref), (near_v1_ref, far_v1_ref), guards):
         v0_ref[pl.ds(NEAR - 1, 1), own] = above
         v0_ref[pl.ds(NEAR + REACH, 1), own] = below
         for start in range(0, REACH, 8):
             v0_ref[pl.ds(NEAR + start, 8), own] = halo_ref[pl.ds(start, 8), :] * halo_ref[pl.ds(REACH + start, 8), :]
         for start in range(0, REACH, 8):
-            at = NEAR + start
-            here = v0_ref[pl.ds(at, 8), :]
-            beside = v0_ref[pl.ds(at - 1, 8), own] + v0_ref[pl.ds(at + 1, 8), own] + beside_columns(here)[:, :cols]
-            here = here[:, :cols]
-            v1_ref[pl.ds(start, 8), :] = halo_ref[pl.ds(REACH + start, 8), :] * here + smooth_weight * (4.0 * here - beside)
+            _, v1_ref[pl.ds(start, 8), :] = image(v0_ref, halo_ref[pl.ds(REACH + start, 8), :], NEAR + start)
+
+
+def edge_fields(side, f_ref, w_ref, narrow_ref, near_ref, far_ref, near_v1_ref, far_v1_ref, v0_ref):
+    cols = f_ref.shape[1]
+    at_cols, there = pl.ds(side * (cols - LANES), LANES), pl.ds(side * LANES, LANES)
+    outermost = lax.broadcasted_iota(jnp.int32, (8, LANES), 1) == side * (LANES - 1)
+    guards = guard_rows(f_ref, w_ref, narrow_ref, near_ref, at_cols)
+    for halo_ref, v1_ref, (above, below) in zip((near_ref, far_ref), (near_v1_ref, far_v1_ref), guards):
+        v0_ref[pl.ds(NEAR - 1, 1), :] = above
+        v0_ref[pl.ds(NEAR + REACH, 1), :] = below
+        for start in range(0, REACH, 8):
+            at, weight_at = pl.ds(start, 8), pl.ds(REACH + start, 8)
+            v0_ref[pl.ds(NEAR + start, 8), :] = halo_ref[at, at_cols] * halo_ref[weight_at, at_cols]
+        for start in range(0, REACH, 8):
+            here = v0_ref[pl.ds(NEAR + start, 8), :]
+            inner = pltpu.roll(here, 1 if side else LANES - 1, 1)
+            outer = jnp.where(outermost, 0.0, pltpu.roll(here, LANES - 1 if side else 1, 1))
+            beside = v0_ref[pl.ds(NEAR + start - 1, 8), :] + v0_ref[pl.ds(NEAR + start + 1, 8), :] + inner + outer
+            weight = halo_ref[pl.ds(REACH + start, 8), at_cols]
+            v1_ref[pl.ds(start, 8), there] = weight * here + smooth_weight * (4.0 * here - beside)
 
 
 def regions(f_ref, w_ref, v1_ref, near_ref, near_v1_ref, far_ref, far_v1_ref, step):
@@ -299,10 +335,11 @@
 
 def edges_kernel(
     nrows, ncols, parts_ref, f_ref, w_ref, v1_ref, narrow_ref, near_ref, far_ref, rowtaps_ref,
-    near_v1_ref, far_v1_ref, coefficients_ref, left_ref, right_ref, first_ref, last_ref, v0_ref, high_ref, low_ref,
+    coefficients_ref, left_ref, right_ref, one_ref, other_ref, near_v1_ref, far_v1_ref, v0_ref, high_ref, low_ref,
 ):
     rows, cols = f_ref.shape
-    halo_fields(f_ref, w_ref, narrow_ref, near_ref, far_ref, near_v1_ref, far_v1_ref, v0_ref)
+    for side in range(2):
+        edge_fields(side, f_ref, w_ref, narrow_ref, near_ref, far_ref, near_v1_ref, far_v1_ref, v0_ref)
     c0, c1 = coefficients(*coupled(parts_ref, nrows, ncols))
     coefficients_ref[pl.ds(0, 8), :] = jnp.broadcast_to(c0, (8, LANES))
     coefficients_ref[pl.ds(8, 8), :] = jnp.broadcast_to(c1, (8, LANES))
@@ -313,8 +350,10 @@
     fields = (f_ref, w_ref, v1_ref, near_ref, near_v1_ref, far_ref, far_v1_ref)
     for side, begin in enumerate((0, cols - LANES)):
         at_cols = pl.ds(begin, LANES)
-        for start, *sources in regions(*fields, step):
-            flux, weight, v1 = (ref[pl.ds(row, step), at_cols] for ref, row in sources)
+        for start, (flux_ref, flux_row), (weight_ref, weight_row), (field_ref, field_row) in regions(*fields, step):
+            flux, weight = flux_ref[pl.ds(flux_row, step), at_cols], weight_ref[pl.ds(weight_row, step), at_cols]
+            v1_cols = at_cols if start < rows else pl.ds(side * LANES, LANES)
+            v1 = field_ref[pl.ds(field_row, step), v1_cols]
             v1 = v1 - smooth_weight * sides[side][start : start + step]
             scatter = flux - (c0 * (flux * weight) + c1 * v1)
             high, low = split_values(scatter * scatter)
@@ -324,15 +363,19 @@
     upper, lower = slice(0, rows // 2), slice(rows // 2, rows)
     first, last = passed[:, :LANES], passed[:, LANES:]
     on_left = lax.broadcasted_iota(jnp.int32, (rows // 2, LANES), 1) < REACH
-    first_ref[...] = jnp.where(on_left, first[upper], pltpu.roll(first[lower], REACH, 1))
-    last_ref[...] = jnp.where(on_left, pltpu.roll(last[upper], REACH, 1), last[lower])
+    first = jnp.where(on_left, first[upper], pltpu.roll(first[lower], REACH, 1))
+    last = jnp.where(on_left, pltpu.roll(last[upper], REACH, 1), last[lower])
+    even = is_even("cols")
+    one_ref[...] = jnp.where(even, last, first)
+    other_ref[...] = jnp.where(even, first, last)
 
 
 def main_kernel(
-    coefficients_ref, left_ref, right_ref, f_ref, w_ref, v1_ref, near_ref, near_v1_ref, far_ref, far_v1_ref, rowtaps_ref, coltaps_ref,
-    background_ref, rms_ref, sides_ref, high_ref, low_ref,
+    coefficients_ref, left_ref, right_ref, f_ref, w_ref, v1_ref, narrow_ref, near_ref, far_ref, rowtaps_ref, coltaps_ref,
+    background_ref, rms_ref, sides_ref, near_v1_ref, far_v1_ref, v0_ref, high_ref, low_ref,
 ):
     rows, cols = f_ref.shape
+    halo_fields(f_ref, w_ref, narrow_ref, near_ref, far_ref, near_v1_ref, far_v1_ref, v0_ref)
     c0, c1 = coefficients_ref[pl.ds(0, 1), pl.ds(0, 1)], coefficients_ref[pl.ds(8, 1), pl.ds(0, 1)]
     step = 16
     fields = (f_ref, w_ref, v1_ref, near_ref, near_v1_ref, far_ref, far_v1_ref)
@@ -367,11 +410,13 @@
     return jnp.sqrt(smoothed + 1e-06)
 
 
-def final_kernel(rms_in_ref, sides_ref, left_ref, right_ref, coltaps_ref, rms_ref, blocks_ref, sems):
+def final_kernel(rms_in_ref, sides_ref, one_ref, other_ref, coltaps_ref, rms_ref, blocks_ref, sems):
     rows, cols = rms_ref.shape
     del rms_in_ref
     _, _, first_col, last_col = at_edges()
-    left, right = left_ref[...], right_ref[...]
+    even = is_even("cols")
+    left = jnp.where(even, other_ref[...], one_ref[...])
+    right = jnp.where(even, one_ref[...], other_ref[...])
     left = jnp.concatenate([pltpu.roll(left, REACH, 1), left], axis=0)
     right = jnp.concatenate([right, pltpu.roll(right, REACH, 1)], axis=0)
     sides = sides_ref[...]
@@ -390,12 +435,6 @@
         copy.wait()
 
 
-def shift(block, axis, step):
-    count = lax.axis_size(axis)
-    pairs = [(i, i + step) for i in range(count) if 0 <= i + step < count]
-    return lax.ppermute(block, axis, pairs)
-
-
 def swap(block, axis, first):
     count = lax.axis_size(axis)
     pairs = [(i, i + 1) for i in range(first, count - 1, 2)]
@@ -440,43 +479,47 @@
     narrow = swap(jnp.concatenate([products[0], products[1], taken[0][1], products[2]]), "rows", 1)
 
     own = (coadd_flux, weights(inverse_variance, source_mask))
-    to_near, to_far = call(wide_kernel, "wide", ((2 * REACH + 8, cols), (2 * REACH, cols)))(*own)
+    field = scratch(rows + 2 * NEAR, cols + LANES)
+    to_near, to_far, base = call(
+        prepare_kernel, "prepare", ((2 * REACH + 8, cols), (2 * REACH, cols), (rows, cols)), (field,)
+    )(*own)
     to_near, to_far, narrow = lax.optimization_barrier((to_near, to_far, narrow))
     near = swap(to_near, "rows", 0)
     far = swap(to_far, "rows", 1)
 
-    field = scratch(rows + 2 * NEAR, cols + LANES)
     devices = nrows * ncols
     parts, own_v1 = call(
         moments_kernel,
         "moments",
         ((devices * (VECTORS + 1), LANES), (rows, cols)),
-        (field, field, scratch(rows, LANES)),
-    )(*own, narrow, near)
+        (field, scratch(rows, LANES)),
+    )(*own, base, narrow, near)
     parts = lax.all_to_all(parts.reshape(devices, 1, message), ("rows", "cols"), 0, 0, tiled=True)
     first_row, last_row, _, _ = at_edges()
     kind = jnp.where(is_even(), first_row.astype(jnp.int32), 2 + last_row.astype(jnp.int32))
     row_taps = lax.dynamic_index_in_dim(jnp.asarray(row_tables(rows)), kind, keepdims=False)
     col_taps = jnp.asarray(col_tables())
     reached, packed = rows + 2 * REACH, (rows // 2, LANES)
-    near_v1, far_v1, numbers, left, right, first, last = call(
+    fields = (*own, own_v1, narrow, near, far)
+    halves = (scratch(REACH, 2 * LANES),) * 2
+    numbers, left, right, to_one, to_other = call(
         functools.partial(edges_kernel, nrows, ncols),
         "edges",
-        ((REACH, cols), (REACH, cols), (16, LANES), (reached, LANES), (reached, LANES), packed, packed),
-        (scratch(REACH + 2 * NEAR, cols + LANES),) + (scratch(reached, 2 * LANES, dtype=jnp.bfloat16),) * 2,
-    )(parts, *own, own_v1, narrow, near, far, row_taps)
-    fields = (*own, own_v1, near, near_v1, far, far_v1)
-    from_left = shift(last, "cols", 1)
-    from_right = shift(first, "cols", -1)
+        ((16, LANES), (reached, LANES), (reached, LANES), packed, packed),
+        halves + (scratch(REACH + 2 * NEAR, LANES),) + (scratch(reached, 2 * LANES, dtype=jnp.bfloat16),) * 2,
+    )(parts, *fields, row_taps)
+    one = swap(to_one, "cols", 0)
+    other = swap(to_other, "cols", 1)
+    halves = (scratch(REACH, cols),) * 2
     background, rms, sides = call(
         main_kernel,
         "main",
         ((rows, cols), (rows, cols), (rows, 4 * LANES)),
-        (scratch(reached, cols, dtype=jnp.bfloat16),) * 2,
+        halves + (scratch(REACH + 2 * NEAR, cols + LANES),) + (scratch(reached, cols, dtype=jnp.bfloat16),) * 2,
     )(numbers, left, right, *fields, row_taps, col_taps)
     (rms,) = call(
         final_kernel, "final", ((rows, cols),), (scratch(2, rows, LANES), pltpu.SemaphoreType.DMA((2,))), in_place=True
-    )(rms, sides, from_left, from_right, col_taps)
+    )(rms, sides, one, other, col_taps)
     return background, rms
 
 

time: 38.5 us -> 35.5 us (0.922)
  the two profiles are of different devices: /device:TPU:0 before, /device:TPU:8 now
where the time goes in v11:
time: 35.5 us; the launch traced here: 35.2 us
  starting transfers between devices  17.2 us (48%)
  waiting for transfers between devices  7.41 us (21%)
  Pallas kernels  6.67 us (19%)
  other arithmetic  2.24 us (6%)
  local copies, waits for them, and re-layouts  0.93 us (3%)
  between operations  0.77 us (2%)
    ppermute x5, starting transfers between devices, swap(): return lax.ppermute(block, axis, pairs + [(j, i) for i, j in pairs])  9.51 us
    all_to_all x1, starting transfers between devices, shards(): lax.all_to_all(parts.reshape(devices, 1, message), ('rows', 'cols'), 0, 0...  7.67 us
    pallas_call x5, Pallas kernels, run(): pl.pallas_call(kernel, out_shape=tuple((jax.ShapeDtypeStruct(shape, jnp.f...  6.67 us
    all_to_all x1, waiting for transfers between devices, shards(): lax.all_to_all(parts.reshape(devices, 1, message), ('rows', 'cols'), 0, 0...  5.83 us
    ppermute x5, waiting for transfers between devices, swap(): return lax.ppermute(block, axis, pairs + [(j, i) for i, j in pairs])  1.58 us
    mul x1, other arithmetic, weights(): return inverse_variance * (1.0 - source_mask.astype(jnp.float32))  1.28 us
    mul x1, other arithmetic, shards(): products = [flux * weight for flux, weight in taken]  0.94 us
    squeeze x1, local copies, waits for them, and re-layouts, shards(): lax.dynamic_index_in_dim(jnp.asarray(row_tables(rows)), kind, keepdims=Fa...  0.92 us
  transfers between devices with their start and end apart: 6, of which 3 were waited for; matrix products, arithmetic and copies ran while one was open for 6% of the time, Pallas kernels for 14%

profile of v11, /device:TPU:8, one launch (start us, length us, event | category | flops | bytes accessed | tf_op | source)
XLA Modules:
  0.0 35.2 jit_solution(12898163971686231892)
XLA Ops:
  0.6 0.9 %dynamic-slice_multiply_fusion = (f32[1,1024]{1,0:T(1,128)S(1)}, f32[1,1024]{1,0:T(1,128)S(1)}, f32[1,1024]{1,0:T(1,128)S(1)}, f32[1,1024]{1,0:T(1,128)S(1)}) fusion(f32[128,1024]{1,0:T(8,128)} %f_ref.7, s32[]{:T(128)S(6)} %select_n.40, s32[128,1024]{1,0:T(8,128)} %param.7, f32[128,1024]{1,0:T(8,128)} %param.6, s32[]{:T(128)S(6)} %select_n.41, s32[]{:T(128)S(6)} %select_n.42), kind=kLoop, calls=%fused_computation.6 | loop fusion | flops 12288 | bytes 53260 | tf_op jit(solution)/shard_map/mul | solution.py:478
  1.6 0.0 copy-start
  1.6 0.8 %collective-permute-start = (f32[4,1024]{1,0:T(4,128)S(1)}, f32[4,1024]{1,0:T(4,128)S(1)}, u32[]{:S(2)}, u32[]{:S(2)}) collective-permute-start(f32[4,1024]{1,0:T(4,128)S(1)} %pad_maximum_fusion), channel_id=1, source_target_pairs={{4,8},{12,16},{20,24},{8,4},{16,12},{24,20},{5,9},{13,17},{21,25},... | collective-permute-start | bytes 49160 | tf_op jit(solution)/shard_map/ppermute | solution.py:441
  2.4 1.3 %subtract_multiply_fusion.w_ref = f32[128,1024]{1,0:T(8,128)S(1)} fusion(f32[128,1024]{1,0:T(8,128)} %param.6, s32[128,1024]{1,0:T(8,128)} %param.7), kind=kLoop, calls=%fused_computation | loop fusion | flops 393216 | bytes 1572864 | tf_op jit(solution)/shard_map/mul | solution.py:92
  3.7 0.0 copy-done
  3.7 0.5 %prepare.1 = (f32[136,1024]{1,0:T(8,128)S(1)}, f32[128,1024]{1,0:T(8,128)S(1)}, f32[128,1024]{1,0:T(8,128)S(1)}) custom-call(f32[128,1024]{1,0:T(8,128)S(1)} %copy-done, f32[128,1024]{1,0:T(8,128)S(1)} %subtract_multiply_fusion.w_ref), custom_call_target="tpu_custom_call" | custom-call | tf_op jit(solution)/shard_map/prepare/pallas_call | solution.py:449
  4.2 0.0 collective-permute-done.narrow_ref
  4.2 2.9 %collective-permute-start.1 = (f32[136,1024]{1,0:T(8,128)S(1)}, f32[136,1024]{1,0:T(8,128)S(1)}, u32[]{:S(2)}, u32[]{:S(2)}) collective-permute-start(f32[136,1024]{1,0:T(8,128)S(1)} %get-tuple-element.22), channel_id=1, source_target_pairs={{0,4},{8,12},{16,20},{24,28},{4,0},{12,8},{20,16},{28,24},{1,5},{9... | collective-permute-start | bytes 1671176 | tf_op jit(solution)/shard_map/ppermute | solution.py:441
  7.2 0.7 %collective-permute-start.2 = (f32[128,1024]{1,0:T(8,128)S(1)}, f32[128,1024]{1,0:T(8,128)S(1)}, u32[]{:S(2)}, u32[]{:S(2)}) collective-permute-start(f32[128,1024]{1,0:T(8,128)S(1)} %get-tuple-element.25), channel_id=1, source_target_pairs={{4,8},{12,16},{20,24},{8,4},{16,12},{24,20},{5,9},{13,17},{21,25},... | collective-permute-start | bytes 1572872 | tf_op jit(solution)/shard_map/ppermute | solution.py:441
  7.9 0.9 %collective-permute-done.1.near_ref = f32[136,1024]{1,0:T(8,128)S(1)} collective-permute-done((f32[136,1024]{1,0:T(8,128)S(1)}, f32[136,1024]{1,0:T(8,128)S(1)}, u32[]{:S(2)}, u32[]{:S(2)}) %collective-permute-start.1) | collective-permute-done | bytes 557088 | tf_op jit(solution)/shard_map/ppermute | solution.py:441
  8.7 2.2 %moments.1 = (f32[288,128]{1,0:T(8,128)}, f32[128,1024]{1,0:T(8,128)S(1)}) custom-call(f32[128,1024]{1,0:T(8,128)S(1)} %copy-done, f32[128,1024]{1,0:T(8,128)S(1)} %subtract_multiply_fusion.w_ref, f32[128,1024]{1,0:T(8,128)S(1)} %get-tuple-element.18.base_ref, f32[4,1024]{1,0:T(4,128)S(1)} %collective-permute-done.narrow_ref, ...), custom_call_target="tpu_custom_call" | custom-call | tf_op jit(solution)/shard_map/moments/pallas_call | solution.py:449
  11.0 7.7 %all-to-all-start = ((f32[32,1,1152]{2,1,0:T(1,128)}), f32[32,1,1152]{2,1,0:T(1,128)S(1)}, u32[]{:S(2)}, u32[]{:S(2)}) async-start(f32[32,1,1152]{2,1,0:T(1,128)} %bitcast), calls=%async_computation | async-start | bytes 294912 | tf_op jit(solution)/shard_map/all_to_all | solution.py:497
  18.7 0.9 %dynamic-slice_bitcast_fusion.rowtaps_ref = bf16[256,256]{1,0:T(8,128)(2,1)S(1)} fusion(bf16[4,256,256]{2,1,0:T(8,128)(2,1)} %constant.53.clone, s32[]{:T(128)S(6)} %select_n.44), kind=kLoop, calls=%fused_computation.1 | loop fusion | bytes 262148 | tf_op jit(solution)/shard_map/jit(dynamic_index_in_dim)/squeeze | solution.py:500
  19.6 0.0 collective-permute-done.2.far_ref
  19.6 5.8 %all-to-all-done.parts_ref = f32[32,1,1152]{2,1,0:T(1,128)S(1)} async-done(((f32[32,1,1152]{2,1,0:T(1,128)}), f32[32,1,1152]{2,1,0:T(1,128)S(1)}, u32[]{:S(2)}, u32[]{:S(2)}) %all-to-all-start) | async-done | bytes 147488 | tf_op jit(solution)/shard_map/all_to_all | solution.py:497
  25.4 0.0 copy-start.1
  25.4 0.7 %edges.1 = (f32[16,128]{1,0:T(8,128)S(1)}, f32[256,128]{1,0:T(8,128)S(1)}, f32[256,128]{1,0:T(8,128)S(1)}, f32[64,128]{1,0:T(8,128)S(1)}, f32[64,128]{1,0:T(8,128)S(1)}) custom-call(f32[32,1,1152]{2,1,0:T(1,128)S(1)} %all-to-all-done.parts_ref, f32[128,1024]{1,0:T(8,128)S(1)} %copy-done, f32[128,1024]{1,0:T(8,128)S(1)} %subtract_multiply_fusion.w_ref, ...), custom_call_target="tpu_custom_call" | custom-call | tf_op jit(solution)/shard_map/edges/pallas_call | solution.py:449
  26.2 2.2 %collective-permute-start.3 = (f32[64,128]{1,0:T(8,128)S(1)}, f32[64,128]{1,0:T(8,128)S(1)}, u32[]{:S(2)}, u32[]{:S(2)}) collective-permute-start(f32[64,128]{1,0:T(8,128)S(1)} %get-tuple-element.32), channel_id=1, source_target_pairs={{0,1},{2,3},{1,0},{3,2},{4,5},{6,7},{5,4},{7,6},{8,9},{10,11},{9,8... | collective-permute-start | bytes 98312 | tf_op jit(solution)/shard_map/ppermute | solution.py:441
  28.4 2.9 %collective-permute-start.4 = (f32[64,128]{1,0:T(8,128)S(1)}, f32[64,128]{1,0:T(8,128)S(1)}, u32[]{:S(2)}, u32[]{:S(2)}) collective-permute-start(f32[64,128]{1,0:T(8,128)S(1)} %get-tuple-element.33), channel_id=1, source_target_pairs={{1,2},{2,1},{5,6},{6,5},{9,10},{10,9},{13,14},{14,13},{17,18},{18,... | collective-permute-start | bytes 98312 | tf_op jit(solution)/shard_map/ppermute | solution.py:441
  31.3 0.0 copy-done.1
  31.3 2.2 %main.1 = (f32[128,1024]{1,0:T(8,128)}, f32[128,1024]{1,0:T(8,128)}, f32[128,512]{1,0:T(8,128)S(1)}) custom-call(f32[16,128]{1,0:T(8,128)S(1)} %get-tuple-element.26.coefficients_ref, f32[256,128]{1,0:T(8,128)S(1)} %get-tuple-element.27.left_ref, f32[256,128]{1,0:T(8,128)S(1)} %get-tuple-element.28.right_ref, f32[128,1024]{1,0:T(8,128)S(1)} %copy-done, ...), custom_call_target="tpu_custom_call" | custom-call | tf_op jit(solution)/shard_map/main/pallas_call | solution.py:449
  33.5 0.0 collective-permute-done.3.one_ref
  33.5 0.7 %collective-permute-done.4.other_ref = f32[64,128]{1,0:T(8,128)S(1)} collective-permute-done((f32[64,128]{1,0:T(8,128)S(1)}, f32[64,128]{1,0:T(8,128)S(1)}, u32[]{:S(2)}, u32[]{:S(2)}) %collective-permute-start.4) | collective-permute-done | bytes 32800 | tf_op jit(solution)/shard_map/ppermute | solution.py:441
  34.2 1.0 %final.1 = f32[128,1024]{1,0:T(8,128)} custom-call(f32[128,1024]{1,0:T(8,128)} %get-tuple-element.30.rms_in_ref, f32[128,512]{1,0:T(8,128)S(1)} %get-tuple-element.31.sides_ref, f32[64,128]{1,0:T(8,128)S(1)} %collective-permute-done.3.one_ref, f32[64,128]{1,0:T(8,128)S(1)} %collective-permute-done.4.other_ref, ...), custom_call_target="tpu_custom_call", output_to_operand_aliasing={{}: (0, {})} | custom-call | tf_op jit(solution)/shard_map/final/pallas_call | solution.py:449
  (1 shorter events, 0.0 us)
Async XLA Ops:
  1.6 2.1 %copy-start = (f32[128,1024]{1,0:T(8,128)S(1)}, f32[128,1024]{1,0:T(8,128)}, u32[]{:S(2)}) copy-start(f32[128,1024]{1,0:T(8,128)} %f_ref.7) | copy-start | bytes 1572868
  1.6 2.6 %collective-permute-start = (f32[4,1024]{1,0:T(4,128)S(1)}, f32[4,1024]{1,0:T(4,128)S(1)}, u32[]{:S(2)}, u32[]{:S(2)}) collective-permute-start(f32[4,1024]{1,0:T(4,128)S(1)} %pad_maximum_fusion), channel_id=1, source_target_pairs={{4,8},{12,16},{20,24},{8,4},{16,12},{24,20},{5,9},{13,17},{21,25},... | collective-permute-start | bytes 49160 | tf_op jit(solution)/shard_map/ppermute | solution.py:441
  4.2 4.5 %collective-permute-start.1 = (f32[136,1024]{1,0:T(8,128)S(1)}, f32[136,1024]{1,0:T(8,128)S(1)}, u32[]{:S(2)}, u32[]{:S(2)}) collective-permute-start(f32[136,1024]{1,0:T(8,128)S(1)} %get-tuple-element.22), channel_id=1, source_target_pairs={{0,4},{8,12},{16,20},{24,28},{4,0},{12,8},{20,16},{28,24},{1,5},{9... | collective-permute-start | bytes 1671176 | tf_op jit(solution)/shard_map/ppermute | solution.py:441
  7.2 12.4 %collective-permute-start.2 = (f32[128,1024]{1,0:T(8,128)S(1)}, f32[128,1024]{1,0:T(8,128)S(1)}, u32[]{:S(2)}, u32[]{:S(2)}) collective-permute-start(f32[128,1024]{1,0:T(8,128)S(1)} %get-tuple-element.25), channel_id=1, source_target_pairs={{4,8},{12,16},{20,24},{8,4},{16,12},{24,20},{5,9},{13,17},{21,25},... | collective-permute-start | bytes 1572872 | tf_op jit(solution)/shard_map/ppermute | solution.py:441
  11.0 14.5 %all-to-all-start = ((f32[32,1,1152]{2,1,0:T(1,128)}), f32[32,1,1152]{2,1,0:T(1,128)S(1)}, u32[]{:S(2)}, u32[]{:S(2)}) async-start(f32[32,1,1152]{2,1,0:T(1,128)} %bitcast), calls=%async_computation | async-start | bytes 294912 | tf_op jit(solution)/shard_map/all_to_all | solution.py:497
  25.4 5.9 %copy-start.1 = (bf16[3,256,256]{2,1,0:T(8,128)(2,1)S(1)}, bf16[3,256,256]{2,1,0:T(8,128)(2,1)}, u32[]{:S(2)}) copy-start(bf16[3,256,256]{2,1,0:T(8,128)(2,1)} %constant.54.clone.coltaps_ref) | copy-start | bytes 1179652
  26.2 7.3 %collective-permute-start.3 = (f32[64,128]{1,0:T(8,128)S(1)}, f32[64,128]{1,0:T(8,128)S(1)}, u32[]{:S(2)}, u32[]{:S(2)}) collective-permute-start(f32[64,128]{1,0:T(8,128)S(1)} %get-tuple-element.32), channel_id=1, source_target_pairs={{0,1},{2,3},{1,0},{3,2},{4,5},{6,7},{5,4},{7,6},{8,9},{10,11},{9,8... | collective-permute-start | bytes 98312 | tf_op jit(solution)/shard_map/ppermute | solution.py:441
  28.4 5.8 %collective-permute-start.4 = (f32[64,128]{1,0:T(8,128)S(1)}, f32[64,128]{1,0:T(8,128)S(1)}, u32[]{:S(2)}, u32[]{:S(2)}) collective-permute-start(f32[64,128]{1,0:T(8,128)S(1)} %get-tuple-element.33), channel_id=1, source_target_pairs={{1,2},{2,1},{5,6},{6,5},{9,10},{10,9},{13,14},{14,13},{17,18},{18,... | collective-permute-start | bytes 98312 | tf_op jit(solution)/shard_map/ppermute | solution.py:441

commit v12 on v11

--- a/solution.py
+++ b/solution.py
@@ -335,7 +335,7 @@
 
 def edges_kernel(
     nrows, ncols, parts_ref, f_ref, w_ref, v1_ref, narrow_ref, near_ref, far_ref, rowtaps_ref,
-    coefficients_ref, left_ref, right_ref, one_ref, other_ref, near_v1_ref, far_v1_ref, v0_ref, high_ref, low_ref,
+    coefficients_ref, left_ref, right_ref, other_ref, one_ref, near_v1_ref, far_v1_ref, v0_ref, high_ref, low_ref,
 ):
     rows, cols = f_ref.shape
     for side in range(2):
@@ -410,7 +410,7 @@
     return jnp.sqrt(smoothed + 1e-06)
 
 
-def final_kernel(rms_in_ref, sides_ref, one_ref, other_ref, coltaps_ref, rms_ref, blocks_ref, sems):
+def final_kernel(rms_in_ref, sides_ref, other_ref, one_ref, coltaps_ref, rms_ref, blocks_ref, sems):
     rows, cols = rms_ref.shape
     del rms_in_ref
     _, _, first_col, last_col = at_edges()
@@ -502,14 +502,14 @@
     reached, packed = rows + 2 * REACH, (rows // 2, LANES)
     fields = (*own, own_v1, narrow, near, far)
     halves = (scratch(REACH, 2 * LANES),) * 2
-    numbers, left, right, to_one, to_other = call(
+    numbers, left, right, to_other, to_one = call(
         functools.partial(edges_kernel, nrows, ncols),
         "edges",
         ((16, LANES), (reached, LANES), (reached, LANES), packed, packed),
         halves + (scratch(REACH + 2 * NEAR, LANES),) + (scratch(reached, 2 * LANES, dtype=jnp.bfloat16),) * 2,
     )(parts, *fields, row_taps)
+    other = swap(to_other, "cols", 1)
     one = swap(to_one, "cols", 0)
-    other = swap(to_other, "cols", 1)
     halves = (scratch(REACH, cols),) * 2
     background, rms, sides = call(
         main_kernel,
@@ -519,7 +519,7 @@
     )(numbers, left, right, *fields, row_taps, col_taps)
     (rms,) = call(
         final_kernel, "final", ((rows, cols),), (scratch(2, rows, LANES), pltpu.SemaphoreType.DMA((2,))), in_place=True
-    )(rms, sides, one, other, col_taps)
+    )(rms, sides, other, one, col_taps)
     return background, rms
 
 

time: 35.5 us -> 36.3 us (1.023)
  the two profiles are of different devices: /device:TPU:8 before, /device:TPU:0 now
where the time goes in v12:
time: 36.3 us; the launch traced here: 36 us
  starting transfers between devices  16.8 us (46%)
  waiting for transfers between devices  8.59 us (24%)
  Pallas kernels  6.66 us (18%)
  other arithmetic  2.24 us (6%)
  local copies, waits for them, and re-layouts  0.93 us (3%)
  between operations  0.77 us (2%)
    ppermute x5, starting transfers between devices, swap(): return lax.ppermute(block, axis, pairs + [(j, i) for i, j in pairs])  9.31 us
    all_to_all x1, waiting for transfers between devices, shards(): lax.all_to_all(parts.reshape(devices, 1, message), ('rows', 'cols'), 0, 0...  7.69 us
    all_to_all x1, starting transfers between devices, shards(): lax.all_to_all(parts.reshape(devices, 1, message), ('rows', 'cols'), 0, 0...  7.48 us
    pallas_call x5, Pallas kernels, run(): pl.pallas_call(kernel, out_shape=tuple((jax.ShapeDtypeStruct(shape, jnp.f...  6.66 us
    mul x1, other arithmetic, weights(): return inverse_variance * (1.0 - source_mask.astype(jnp.float32))  1.28 us
    mul x1, other arithmetic, shards(): products = [flux * weight for flux, weight in taken]  0.94 us
    squeeze x1, local copies, waits for them, and re-layouts, shards(): lax.dynamic_index_in_dim(jnp.asarray(row_tables(rows)), kind, keepdims=Fa...  0.92 us
    ppermute x5, waiting for transfers between devices, swap(): return lax.ppermute(block, axis, pairs + [(j, i) for i, j in pairs])  0.9 us
  transfers between devices with their start and end apart: 6, of which 2 were waited for; matrix products, arithmetic and copies ran while one was open for 6% of the time, Pallas kernels for 14%

profile of v12, /device:TPU:0, one launch (start us, length us, event | category | flops | bytes accessed | tf_op | source)
XLA Modules:
  0.0 36.0 jit_solution(802197097205024628)
XLA Ops:
  0.6 0.9 %dynamic-slice_multiply_fusion = (f32[1,1024]{1,0:T(1,128)S(1)}, f32[1,1024]{1,0:T(1,128)S(1)}, f32[1,1024]{1,0:T(1,128)S(1)}, f32[1,1024]{1,0:T(1,128)S(1)}) fusion(f32[128,1024]{1,0:T(8,128)} %f_ref.7, s32[]{:T(128)S(6)} %select_n.40, s32[128,1024]{1,0:T(8,128)} %param.7, f32[128,1024]{1,0:T(8,128)} %param.6, s32[]{:T(128)S(6)} %select_n.41, s32[]{:T(128)S(6)} %select_n.42), kind=kLoop, calls=%fused_computation.6 | loop fusion | flops 12288 | bytes 53260 | tf_op jit(solution)/shard_map/mul | solution.py:478
  1.6 0.0 copy-start
  1.6 0.8 %collective-permute-start = (f32[4,1024]{1,0:T(4,128)S(1)}, f32[4,1024]{1,0:T(4,128)S(1)}, u32[]{:S(2)}, u32[]{:S(2)}) collective-permute-start(f32[4,1024]{1,0:T(4,128)S(1)} %pad_maximum_fusion), channel_id=1, source_target_pairs={{4,8},{12,16},{20,24},{8,4},{16,12},{24,20},{5,9},{13,17},{21,25},... | collective-permute-start | bytes 49160 | tf_op jit(solution)/shard_map/ppermute | solution.py:441
  2.4 1.3 %subtract_multiply_fusion.w_ref = f32[128,1024]{1,0:T(8,128)S(1)} fusion(f32[128,1024]{1,0:T(8,128)} %param.6, s32[128,1024]{1,0:T(8,128)} %param.7), kind=kLoop, calls=%fused_computation | loop fusion | flops 393216 | bytes 1572864 | tf_op jit(solution)/shard_map/mul | solution.py:92
  3.7 0.0 copy-done
  3.7 0.5 %prepare.1 = (f32[136,1024]{1,0:T(8,128)S(1)}, f32[128,1024]{1,0:T(8,128)S(1)}, f32[128,1024]{1,0:T(8,128)S(1)}) custom-call(f32[128,1024]{1,0:T(8,128)S(1)} %copy-done, f32[128,1024]{1,0:T(8,128)S(1)} %subtract_multiply_fusion.w_ref), custom_call_target="tpu_custom_call" | custom-call | tf_op jit(solution)/shard_map/prepare/pallas_call | solution.py:449
  4.2 0.0 collective-permute-done.narrow_ref
  4.2 4.4 %collective-permute-start.1 = (f32[136,1024]{1,0:T(8,128)S(1)}, f32[136,1024]{1,0:T(8,128)S(1)}, u32[]{:S(2)}, u32[]{:S(2)}) collective-permute-start(f32[136,1024]{1,0:T(8,128)S(1)} %get-tuple-element.22), channel_id=1, source_target_pairs={{0,4},{8,12},{16,20},{24,28},{4,0},{12,8},{20,16},{28,24},{1,5},{9... | collective-permute-start | bytes 1671176 | tf_op jit(solution)/shard_map/ppermute | solution.py:441
  8.6 0.7 %collective-permute-start.2 = (f32[128,1024]{1,0:T(8,128)S(1)}, f32[128,1024]{1,0:T(8,128)S(1)}, u32[]{:S(2)}, u32[]{:S(2)}) collective-permute-start(f32[128,1024]{1,0:T(8,128)S(1)} %get-tuple-element.25), channel_id=1, source_target_pairs={{4,8},{12,16},{20,24},{8,4},{16,12},{24,20},{5,9},{13,17},{21,25},... | collective-permute-start | bytes 1572872 | tf_op jit(solution)/shard_map/ppermute | solution.py:441
  9.3 0.9 %collective-permute-done.1.near_ref = f32[136,1024]{1,0:T(8,128)S(1)} collective-permute-done((f32[136,1024]{1,0:T(8,128)S(1)}, f32[136,1024]{1,0:T(8,128)S(1)}, u32[]{:S(2)}, u32[]{:S(2)}) %collective-permute-start.1) | collective-permute-done | bytes 557088 | tf_op jit(solution)/shard_map/ppermute | solution.py:441
  10.2 2.2 %moments.1 = (f32[288,128]{1,0:T(8,128)}, f32[128,1024]{1,0:T(8,128)S(1)}) custom-call(f32[128,1024]{1,0:T(8,128)S(1)} %copy-done, f32[128,1024]{1,0:T(8,128)S(1)} %subtract_multiply_fusion.w_ref, f32[128,1024]{1,0:T(8,128)S(1)} %get-tuple-element.18.base_ref, f32[4,1024]{1,0:T(4,128)S(1)} %collective-permute-done.narrow_ref, ...), custom_call_target="tpu_custom_call" | custom-call | tf_op jit(solution)/shard_map/moments/pallas_call | solution.py:449
  12.4 7.5 %all-to-all-start = ((f32[32,1,1152]{2,1,0:T(1,128)}), f32[32,1,1152]{2,1,0:T(1,128)S(1)}, u32[]{:S(2)}, u32[]{:S(2)}) async-start(f32[32,1,1152]{2,1,0:T(1,128)} %bitcast), calls=%async_computation | async-start | bytes 294912 | tf_op jit(solution)/shard_map/all_to_all | solution.py:497
  19.9 0.9 %dynamic-slice_bitcast_fusion.rowtaps_ref = bf16[256,256]{1,0:T(8,128)(2,1)S(1)} fusion(bf16[4,256,256]{2,1,0:T(8,128)(2,1)} %constant.53.clone, s32[]{:T(128)S(6)} %select_n.44), kind=kLoop, calls=%fused_computation.1 | loop fusion | bytes 262148 | tf_op jit(solution)/shard_map/jit(dynamic_index_in_dim)/squeeze | solution.py:500
  20.8 0.0 collective-permute-done.2.far_ref
  20.9 7.7 %all-to-all-done.parts_ref = f32[32,1,1152]{2,1,0:T(1,128)S(1)} async-done(((f32[32,1,1152]{2,1,0:T(1,128)}), f32[32,1,1152]{2,1,0:T(1,128)S(1)}, u32[]{:S(2)}, u32[]{:S(2)}) %all-to-all-start) | async-done | bytes 147488 | tf_op jit(solution)/shard_map/all_to_all | solution.py:497
  28.5 0.0 copy-start.1
  28.5 0.7 %edges.1 = (f32[16,128]{1,0:T(8,128)S(1)}, f32[256,128]{1,0:T(8,128)S(1)}, f32[256,128]{1,0:T(8,128)S(1)}, f32[64,128]{1,0:T(8,128)S(1)}, f32[64,128]{1,0:T(8,128)S(1)}) custom-call(f32[32,1,1152]{2,1,0:T(1,128)S(1)} %all-to-all-done.parts_ref, f32[128,1024]{1,0:T(8,128)S(1)} %copy-done, f32[128,1024]{1,0:T(8,128)S(1)} %subtract_multiply_fusion.w_ref, ...), custom_call_target="tpu_custom_call" | custom-call | tf_op jit(solution)/shard_map/edges/pallas_call | solution.py:449
  29.3 0.7 %collective-permute-start.3 = (f32[64,128]{1,0:T(8,128)S(1)}, f32[64,128]{1,0:T(8,128)S(1)}, u32[]{:S(2)}, u32[]{:S(2)}) collective-permute-start(f32[64,128]{1,0:T(8,128)S(1)} %get-tuple-element.32), channel_id=1, source_target_pairs={{1,2},{2,1},{5,6},{6,5},{9,10},{10,9},{13,14},{14,13},{17,18},{18,... | collective-permute-start | bytes 98312 | tf_op jit(solution)/shard_map/ppermute | solution.py:441
  30.0 2.8 %collective-permute-start.4 = (f32[64,128]{1,0:T(8,128)S(1)}, f32[64,128]{1,0:T(8,128)S(1)}, u32[]{:S(2)}, u32[]{:S(2)}) collective-permute-start(f32[64,128]{1,0:T(8,128)S(1)} %get-tuple-element.33), channel_id=1, source_target_pairs={{0,1},{2,3},{1,0},{3,2},{4,5},{6,7},{5,4},{7,6},{8,9},{10,11},{9,8... | collective-permute-start | bytes 98312 | tf_op jit(solution)/shard_map/ppermute | solution.py:441
  32.8 0.0 copy-done.1
  32.8 2.2 %main.1 = (f32[128,1024]{1,0:T(8,128)}, f32[128,1024]{1,0:T(8,128)}, f32[128,512]{1,0:T(8,128)S(1)}) custom-call(f32[16,128]{1,0:T(8,128)S(1)} %get-tuple-element.26.coefficients_ref, f32[256,128]{1,0:T(8,128)S(1)} %get-tuple-element.27.left_ref, f32[256,128]{1,0:T(8,128)S(1)} %get-tuple-element.28.right_ref, f32[128,1024]{1,0:T(8,128)S(1)} %copy-done, ...), custom_call_target="tpu_custom_call" | custom-call | tf_op jit(solution)/shard_map/main/pallas_call | solution.py:449
  34.9 0.0 collective-permute-done.3.other_ref
  34.9 0.0 collective-permute-done.4.one_ref
  34.9 1.0 %final.1 = f32[128,1024]{1,0:T(8,128)} custom-call(f32[128,1024]{1,0:T(8,128)} %get-tuple-element.30.rms_in_ref, f32[128,512]{1,0:T(8,128)S(1)} %get-tuple-element.31.sides_ref, f32[64,128]{1,0:T(8,128)S(1)} %collective-permute-done.3.other_ref, f32[64,128]{1,0:T(8,128)S(1)} %collective-permute-done.4.one_ref, ...), custom_call_target="tpu_custom_call", output_to_operand_aliasing={{}: (0, {})} | custom-call | tf_op jit(solution)/shard_map/final/pallas_call | solution.py:449
  (1 shorter events, 0.0 us)
Async XLA Ops:
  1.6 2.1 %copy-start = (f32[128,1024]{1,0:T(8,128)S(1)}, f32[128,1024]{1,0:T(8,128)}, u32[]{:S(2)}) copy-start(f32[128,1024]{1,0:T(8,128)} %f_ref.7) | copy-start | bytes 1572868
  1.6 2.6 %collective-permute-start = (f32[4,1024]{1,0:T(4,128)S(1)}, f32[4,1024]{1,0:T(4,128)S(1)}, u32[]{:S(2)}, u32[]{:S(2)}) collective-permute-start(f32[4,1024]{1,0:T(4,128)S(1)} %pad_maximum_fusion), channel_id=1, source_target_pairs={{4,8},{12,16},{20,24},{8,4},{16,12},{24,20},{5,9},{13,17},{21,25},... | collective-permute-start | bytes 49160 | tf_op jit(solution)/shard_map/ppermute | solution.py:441
  4.2 5.9 %collective-permute-start.1 = (f32[136,1024]{1,0:T(8,128)S(1)}, f32[136,1024]{1,0:T(8,128)S(1)}, u32[]{:S(2)}, u32[]{:S(2)}) collective-permute-start(f32[136,1024]{1,0:T(8,128)S(1)} %get-tuple-element.22), channel_id=1, source_target_pairs={{0,4},{8,12},{16,20},{24,28},{4,0},{12,8},{20,16},{28,24},{1,5},{9... | collective-permute-start | bytes 1671176 | tf_op jit(solution)/shard_map/ppermute | solution.py:441
  8.6 12.2 %collective-permute-start.2 = (f32[128,1024]{1,0:T(8,128)S(1)}, f32[128,1024]{1,0:T(8,128)S(1)}, u32[]{:S(2)}, u32[]{:S(2)}) collective-permute-start(f32[128,1024]{1,0:T(8,128)S(1)} %get-tuple-element.25), channel_id=1, source_target_pairs={{4,8},{12,16},{20,24},{8,4},{16,12},{24,20},{5,9},{13,17},{21,25},... | collective-permute-start | bytes 1572872 | tf_op jit(solution)/shard_map/ppermute | solution.py:441
  12.4 16.1 %all-to-all-start = ((f32[32,1,1152]{2,1,0:T(1,128)}), f32[32,1,1152]{2,1,0:T(1,128)S(1)}, u32[]{:S(2)}, u32[]{:S(2)}) async-start(f32[32,1,1152]{2,1,0:T(1,128)} %bitcast), calls=%async_computation | async-start | bytes 294912 | tf_op jit(solution)/shard_map/all_to_all | solution.py:497
  28.5 4.2 %copy-start.1 = (bf16[3,256,256]{2,1,0:T(8,128)(2,1)S(1)}, bf16[3,256,256]{2,1,0:T(8,128)(2,1)}, u32[]{:S(2)}) copy-start(bf16[3,256,256]{2,1,0:T(8,128)(2,1)} %constant.54.clone.coltaps_ref) | copy-start | bytes 1179652
  29.3 5.6 %collective-permute-start.3 = (f32[64,128]{1,0:T(8,128)S(1)}, f32[64,128]{1,0:T(8,128)S(1)}, u32[]{:S(2)}, u32[]{:S(2)}) collective-permute-start(f32[64,128]{1,0:T(8,128)S(1)} %get-tuple-element.32), channel_id=1, source_target_pairs={{1,2},{2,1},{5,6},{6,5},{9,10},{10,9},{13,14},{14,13},{17,18},{18,... | collective-permute-start | bytes 98312 | tf_op jit(solution)/shard_map/ppermute | solution.py:441
  30.0 5.0 %collective-permute-start.4 = (f32[64,128]{1,0:T(8,128)S(1)}, f32[64,128]{1,0:T(8,128)S(1)}, u32[]{:S(2)}, u32[]{:S(2)}) collective-permute-start(f32[64,128]{1,0:T(8,128)S(1)} %get-tuple-element.33), channel_id=1, source_target_pairs={{0,1},{2,3},{1,0},{3,2},{4,5},{6,7},{5,4},{7,6},{8,9},{10,11},{9,8... | collective-permute-start | bytes 98312 | tf_op jit(solution)/shard_map/ppermute | solution.py:441

commit v13 on v11

--- a/solution.py
+++ b/solution.py
@@ -60,7 +60,12 @@
 def col_tables():
     tables = []
     for first, last in ((False, False), (True, False), (False, True)):
-        tables.append(np.concatenate(split(squared_taps(LANES, first, last).T), axis=1))
+        table = squared_taps(LANES, first, last)
+        if first:
+            table[:, :REACH] = 0.0
+        if last:
+            table[:, REACH + LANES :] = 0.0
+        tables.append(np.concatenate(split(table.T), axis=1))
     return np.stack(tables)
 
 
@@ -157,7 +162,8 @@
             near_ref[pl.ds(REACH + nearest, 1), :],
         )
 
-    far_rows = tuple(narrow_ref[pl.ds(k, 1), :] for k in range(3))
+    outermost = first_row | last_row
+    far_rows = tuple(jnp.where(outermost, 0.0, narrow_ref[pl.ds(k, 1), :]) for k in range(3))
     above = [jnp.where(even, far, near) for far, near in zip(far_rows, near_rows(REACH - 1, REACH - 2))]
     below = [jnp.where(even, near, far) for far, near in zip(far_rows, near_rows(0, 1))]
 
@@ -437,8 +443,10 @@
 
 def swap(block, axis, first):
     count = lax.axis_size(axis)
-    pairs = [(i, i + 1) for i in range(first, count - 1, 2)]
-    return lax.ppermute(block, axis, pairs + [(j, i) for i, j in pairs])
+    partner = list(range(count))
+    for i in range(first, count - 1, 2):
+        partner[i], partner[i + 1] = i + 1, i
+    return lax.ppermute(block, axis, list(enumerate(partner)))
 
 
 def call(kernel, name, outs, scratch=(), limit=16, in_place=False):

time: 35.5 us -> 35.5 us (level)
  no operation moved by 1% of the time
where the time goes in v13:
time: 35.5 us; the launch traced here: 35.2 us
  starting transfers between devices  17.2 us (48%)
  waiting for transfers between devices  7.41 us (21%)
  Pallas kernels  6.67 us (19%)
  other arithmetic  2.24 us (6%)
  local copies, waits for them, and re-layouts  0.93 us (3%)
  between operations  0.77 us (2%)
    ppermute x5, starting transfers between devices, swap(): return lax.ppermute(block, axis, list(enumerate(partner)))  9.51 us
    all_to_all x1, starting transfers between devices, shards(): lax.all_to_all(parts.reshape(devices, 1, message), ('rows', 'cols'), 0, 0...  7.67 us
    pallas_call x5, Pallas kernels, run(): pl.pallas_call(kernel, out_shape=tuple((jax.ShapeDtypeStruct(shape, jnp.f...  6.67 us
    all_to_all x1, waiting for transfers between devices, shards(): lax.all_to_all(parts.reshape(devices, 1, message), ('rows', 'cols'), 0, 0...  5.83 us
    ppermute x5, waiting for transfers between devices, swap(): return lax.ppermute(block, axis, list(enumerate(partner)))  1.57 us
    mul x1, other arithmetic, weights(): return inverse_variance * (1.0 - source_mask.astype(jnp.float32))  1.28 us
    mul x1, other arithmetic, shards(): products = [flux * weight for flux, weight in taken]  0.94 us
    squeeze x1, local copies, waits for them, and re-layouts, shards(): lax.dynamic_index_in_dim(jnp.asarray(row_tables(rows)), kind, keepdims=Fa...  0.92 us
  transfers between devices with their start and end apart: 6, of which 3 were waited for; matrix products, arithmetic and copies ran while one was open for 6% of the time, Pallas kernels for 14%

profile of v13, /device:TPU:8, one launch (start us, length us, event | category | flops | bytes accessed | tf_op | source)
XLA Modules:
  0.0 35.2 jit_solution(14870761013566138334)
XLA Ops:
  0.6 0.9 %dynamic-slice_multiply_fusion = (f32[1,1024]{1,0:T(1,128)S(1)}, f32[1,1024]{1,0:T(1,128)S(1)}, f32[1,1024]{1,0:T(1,128)S(1)}, f32[1,1024]{1,0:T(1,128)S(1)}) fusion(f32[128,1024]{1,0:T(8,128)} %f_ref.7, s32[]{:T(128)S(6)} %select_n.40, s32[128,1024]{1,0:T(8,128)} %param.7, f32[128,1024]{1,0:T(8,128)} %param.6, s32[]{:T(128)S(6)} %select_n.41, s32[]{:T(128)S(6)} %select_n.42), kind=kLoop, calls=%fused_computation.6 | loop fusion | flops 12288 | bytes 53260 | tf_op jit(solution)/shard_map/mul | solution.py:486
  1.6 0.0 copy-start
  1.6 0.8 %collective-permute-start = (f32[4,1024]{1,0:T(4,128)S(1)}, f32[4,1024]{1,0:T(4,128)S(1)}, u32[]{:S(2)}, u32[]{:S(2)}) collective-permute-start(f32[4,1024]{1,0:T(4,128)S(1)} %pad_maximum_fusion), channel_id=1, source_target_pairs={{0,0},{4,8},{8,4},{12,16},{16,12},{20,24},{24,20},{28,28},{1,1},{5... | collective-permute-start | bytes 49160 | tf_op jit(solution)/shard_map/ppermute | solution.py:449
  2.4 1.3 %subtract_multiply_fusion.w_ref = f32[128,1024]{1,0:T(8,128)S(1)} fusion(f32[128,1024]{1,0:T(8,128)} %param.6, s32[128,1024]{1,0:T(8,128)} %param.7), kind=kLoop, calls=%fused_computation | loop fusion | flops 393216 | bytes 1572864 | tf_op jit(solution)/shard_map/mul | solution.py:97
  3.7 0.0 copy-done
  3.7 0.5 %prepare.1 = (f32[136,1024]{1,0:T(8,128)S(1)}, f32[128,1024]{1,0:T(8,128)S(1)}, f32[128,1024]{1,0:T(8,128)S(1)}) custom-call(f32[128,1024]{1,0:T(8,128)S(1)} %copy-done, f32[128,1024]{1,0:T(8,128)S(1)} %subtract_multiply_fusion.w_ref), custom_call_target="tpu_custom_call" | custom-call | tf_op jit(solution)/shard_map/prepare/pallas_call | solution.py:457
  4.2 0.0 collective-permute-done.narrow_ref
  4.2 2.9 %collective-permute-start.1 = (f32[136,1024]{1,0:T(8,128)S(1)}, f32[136,1024]{1,0:T(8,128)S(1)}, u32[]{:S(2)}, u32[]{:S(2)}) collective-permute-start(f32[136,1024]{1,0:T(8,128)S(1)} %get-tuple-element.22), channel_id=1, source_target_pairs={{0,4},{4,0},{8,12},{12,8},{16,20},{20,16},{24,28},{28,24},{1,5},{5... | collective-permute-start | bytes 1671176 | tf_op jit(solution)/shard_map/ppermute | solution.py:449
  7.2 0.7 %collective-permute-start.2 = (f32[128,1024]{1,0:T(8,128)S(1)}, f32[128,1024]{1,0:T(8,128)S(1)}, u32[]{:S(2)}, u32[]{:S(2)}) collective-permute-start(f32[128,1024]{1,0:T(8,128)S(1)} %get-tuple-element.25), channel_id=1, source_target_pairs={{0,0},{4,8},{8,4},{12,16},{16,12},{20,24},{24,20},{28,28},{1,1},{5... | collective-permute-start | bytes 1572872 | tf_op jit(solution)/shard_map/ppermute | solution.py:449
  7.9 0.9 %collective-permute-done.1.near_ref = f32[136,1024]{1,0:T(8,128)S(1)} collective-permute-done((f32[136,1024]{1,0:T(8,128)S(1)}, f32[136,1024]{1,0:T(8,128)S(1)}, u32[]{:S(2)}, u32[]{:S(2)}) %collective-permute-start.1) | collective-permute-done | bytes 557088 | tf_op jit(solution)/shard_map/ppermute | solution.py:449
  8.7 2.2 %moments.1 = (f32[288,128]{1,0:T(8,128)}, f32[128,1024]{1,0:T(8,128)S(1)}) custom-call(f32[128,1024]{1,0:T(8,128)S(1)} %copy-done, f32[128,1024]{1,0:T(8,128)S(1)} %subtract_multiply_fusion.w_ref, f32[128,1024]{1,0:T(8,128)S(1)} %get-tuple-element.18.base_ref, f32[4,1024]{1,0:T(4,128)S(1)} %collective-permute-done.narrow_ref, ...), custom_call_target="tpu_custom_call" | custom-call | tf_op jit(solution)/shard_map/moments/pallas_call | solution.py:457
  11.0 7.7 %all-to-all-start = ((f32[32,1,1152]{2,1,0:T(1,128)}), f32[32,1,1152]{2,1,0:T(1,128)S(1)}, u32[]{:S(2)}, u32[]{:S(2)}) async-start(f32[32,1,1152]{2,1,0:T(1,128)} %bitcast), calls=%async_computation | async-start | bytes 294912 | tf_op jit(solution)/shard_map/all_to_all | solution.py:505
  18.7 0.9 %dynamic-slice_bitcast_fusion.rowtaps_ref = bf16[256,256]{1,0:T(8,128)(2,1)S(1)} fusion(bf16[4,256,256]{2,1,0:T(8,128)(2,1)} %constant.53.clone, s32[]{:T(128)S(6)} %select_n.44), kind=kLoop, calls=%fused_computation.1 | loop fusion | bytes 262148 | tf_op jit(solution)/shard_map/jit(dynamic_index_in_dim)/squeeze | solution.py:508
  19.6 0.0 collective-permute-done.2.far_ref
  19.6 5.8 %all-to-all-done.parts_ref = f32[32,1,1152]{2,1,0:T(1,128)S(1)} async-done(((f32[32,1,1152]{2,1,0:T(1,128)}), f32[32,1,1152]{2,1,0:T(1,128)S(1)}, u32[]{:S(2)}, u32[]{:S(2)}) %all-to-all-start) | async-done | bytes 147488 | tf_op jit(solution)/shard_map/all_to_all | solution.py:505
  25.4 0.0 copy-start.1
  25.4 0.7 %edges.1 = (f32[16,128]{1,0:T(8,128)S(1)}, f32[256,128]{1,0:T(8,128)S(1)}, f32[256,128]{1,0:T(8,128)S(1)}, f32[64,128]{1,0:T(8,128)S(1)}, f32[64,128]{1,0:T(8,128)S(1)}) custom-call(f32[32,1,1152]{2,1,0:T(1,128)S(1)} %all-to-all-done.parts_ref, f32[128,1024]{1,0:T(8,128)S(1)} %copy-done, f32[128,1024]{1,0:T(8,128)S(1)} %subtract_multiply_fusion.w_ref, ...), custom_call_target="tpu_custom_call" | custom-call | tf_op jit(solution)/shard_map/edges/pallas_call | solution.py:457
  26.2 2.2 %collective-permute-start.3 = (f32[64,128]{1,0:T(8,128)S(1)}, f32[64,128]{1,0:T(8,128)S(1)}, u32[]{:S(2)}, u32[]{:S(2)}) collective-permute-start(f32[64,128]{1,0:T(8,128)S(1)} %get-tuple-element.32), channel_id=1, source_target_pairs={{0,1},{1,0},{2,3},{3,2},{4,5},{5,4},{6,7},{7,6},{8,9},{9,8},{10,11... | collective-permute-start | bytes 98312 | tf_op jit(solution)/shard_map/ppermute | solution.py:449
  28.4 2.9 %collective-permute-start.4 = (f32[64,128]{1,0:T(8,128)S(1)}, f32[64,128]{1,0:T(8,128)S(1)}, u32[]{:S(2)}, u32[]{:S(2)}) collective-permute-start(f32[64,128]{1,0:T(8,128)S(1)} %get-tuple-element.33), channel_id=1, source_target_pairs={{0,0},{1,2},{2,1},{3,3},{4,4},{5,6},{6,5},{7,7},{8,8},{9,10},{10,9... | collective-permute-start | bytes 98312 | tf_op jit(solution)/shard_map/ppermute | solution.py:449
  31.3 0.0 copy-done.1
  31.3 2.2 %main.1 = (f32[128,1024]{1,0:T(8,128)}, f32[128,1024]{1,0:T(8,128)}, f32[128,512]{1,0:T(8,128)S(1)}) custom-call(f32[16,128]{1,0:T(8,128)S(1)} %get-tuple-element.26.coefficients_ref, f32[256,128]{1,0:T(8,128)S(1)} %get-tuple-element.27.left_ref, f32[256,128]{1,0:T(8,128)S(1)} %get-tuple-element.28.right_ref, f32[128,1024]{1,0:T(8,128)S(1)} %copy-done, ...), custom_call_target="tpu_custom_call" | custom-call | tf_op jit(solution)/shard_map/main/pallas_call | solution.py:457
  33.5 0.0 collective-permute-done.3.one_ref
  33.5 0.7 %collective-permute-done.4.other_ref = f32[64,128]{1,0:T(8,128)S(1)} collective-permute-done((f32[64,128]{1,0:T(8,128)S(1)}, f32[64,128]{1,0:T(8,128)S(1)}, u32[]{:S(2)}, u32[]{:S(2)}) %collective-permute-start.4) | collective-permute-done | bytes 32800 | tf_op jit(solution)/shard_map/ppermute | solution.py:449
  34.2 1.0 %final.1 = f32[128,1024]{1,0:T(8,128)} custom-call(f32[128,1024]{1,0:T(8,128)} %get-tuple-element.30.rms_in_ref, f32[128,512]{1,0:T(8,128)S(1)} %get-tuple-element.31.sides_ref, f32[64,128]{1,0:T(8,128)S(1)} %collective-permute-done.3.one_ref, f32[64,128]{1,0:T(8,128)S(1)} %collective-permute-done.4.other_ref, ...), custom_call_target="tpu_custom_call", output_to_operand_aliasing={{}: (0, {})} | custom-call | tf_op jit(solution)/shard_map/final/pallas_call | solution.py:457
  (1 shorter events, 0.0 us)
Async XLA Ops:
  1.6 2.1 %copy-start = (f32[128,1024]{1,0:T(8,128)S(1)}, f32[128,1024]{1,0:T(8,128)}, u32[]{:S(2)}) copy-start(f32[128,1024]{1,0:T(8,128)} %f_ref.7) | copy-start | bytes 1572868
  1.6 2.6 %collective-permute-start = (f32[4,1024]{1,0:T(4,128)S(1)}, f32[4,1024]{1,0:T(4,128)S(1)}, u32[]{:S(2)}, u32[]{:S(2)}) collective-permute-start(f32[4,1024]{1,0:T(4,128)S(1)} %pad_maximum_fusion), channel_id=1, source_target_pairs={{0,0},{4,8},{8,4},{12,16},{16,12},{20,24},{24,20},{28,28},{1,1},{5... | collective-permute-start | bytes 49160 | tf_op jit(solution)/shard_map/ppermute | solution.py:449
  4.2 4.5 %collective-permute-start.1 = (f32[136,1024]{1,0:T(8,128)S(1)}, f32[136,1024]{1,0:T(8,128)S(1)}, u32[]{:S(2)}, u32[]{:S(2)}) collective-permute-start(f32[136,1024]{1,0:T(8,128)S(1)} %get-tuple-element.22), channel_id=1, source_target_pairs={{0,4},{4,0},{8,12},{12,8},{16,20},{20,16},{24,28},{28,24},{1,5},{5... | collective-permute-start | bytes 1671176 | tf_op jit(solution)/shard_map/ppermute | solution.py:449
  7.2 12.4 %collective-permute-start.2 = (f32[128,1024]{1,0:T(8,128)S(1)}, f32[128,1024]{1,0:T(8,128)S(1)}, u32[]{:S(2)}, u32[]{:S(2)}) collective-permute-start(f32[128,1024]{1,0:T(8,128)S(1)} %get-tuple-element.25), channel_id=1, source_target_pairs={{0,0},{4,8},{8,4},{12,16},{16,12},{20,24},{24,20},{28,28},{1,1},{5... | collective-permute-start | bytes 1572872 | tf_op jit(solution)/shard_map/ppermute | solution.py:449
  11.0 14.5 %all-to-all-start = ((f32[32,1,1152]{2,1,0:T(1,128)}), f32[32,1,1152]{2,1,0:T(1,128)S(1)}, u32[]{:S(2)}, u32[]{:S(2)}) async-start(f32[32,1,1152]{2,1,0:T(1,128)} %bitcast), calls=%async_computation | async-start | bytes 294912 | tf_op jit(solution)/shard_map/all_to_all | solution.py:505
  25.4 5.9 %copy-start.1 = (bf16[3,256,256]{2,1,0:T(8,128)(2,1)S(1)}, bf16[3,256,256]{2,1,0:T(8,128)(2,1)}, u32[]{:S(2)}) copy-start(bf16[3,256,256]{2,1,0:T(8,128)(2,1)} %constant.54.clone.coltaps_ref) | copy-start | bytes 1179652
  26.2 7.3 %collective-permute-start.3 = (f32[64,128]{1,0:T(8,128)S(1)}, f32[64,128]{1,0:T(8,128)S(1)}, u32[]{:S(2)}, u32[]{:S(2)}) collective-permute-start(f32[64,128]{1,0:T(8,128)S(1)} %get-tuple-element.32), channel_id=1, source_target_pairs={{0,1},{1,0},{2,3},{3,2},{4,5},{5,4},{6,7},{7,6},{8,9},{9,8},{10,11... | collective-permute-start | bytes 98312 | tf_op jit(solution)/shard_map/ppermute | solution.py:449
  28.4 5.8 %collective-permute-start.4 = (f32[64,128]{1,0:T(8,128)S(1)}, f32[64,128]{1,0:T(8,128)S(1)}, u32[]{:S(2)}, u32[]{:S(2)}) collective-permute-start(f32[64,128]{1,0:T(8,128)S(1)} %get-tuple-element.33), channel_id=1, source_target_pairs={{0,0},{1,2},{2,1},{3,3},{4,4},{5,6},{6,5},{7,7},{8,8},{9,10},{10,9... | collective-permute-start | bytes 98312 | tf_op jit(solution)/shard_map/ppermute | solution.py:449

commit v14 on v13

--- a/solution.py
+++ b/solution.py
@@ -443,10 +443,8 @@
 
 def swap(block, axis, first):
     count = lax.axis_size(axis)
-    partner = list(range(count))
-    for i in range(first, count - 1, 2):
-        partner[i], partner[i + 1] = i + 1, i
-    return lax.ppermute(block, axis, list(enumerate(partner)))
+    pairs = [(i, (i + 1) % count) for i in range(first, count, 2)]
+    return lax.ppermute(block, axis, pairs + [(j, i) for i, j in pairs])
 
 
 def call(kernel, name, outs, scratch=(), limit=16, in_place=False):

time: 35.5 us -> 33.4 us (0.941)
  the two profiles are of different devices: /device:TPU:8 before, /device:TPU:0 now
where the time goes in v14:
time: 33.4 us; the launch traced here: 33.1 us
  starting transfers between devices  13.8 us (41%)
  waiting for transfers between devices  8.75 us (26%)
  Pallas kernels  6.67 us (20%)
  other arithmetic  2.23 us (7%)
  local copies, waits for them, and re-layouts  0.93 us (3%)
  between operations  0.75 us (2%)
    ppermute x5, starting transfers between devices, swap(): return lax.ppermute(block, axis, pairs + [(j, i) for i, j in pairs])  8.31 us
    pallas_call x5, Pallas kernels, run(): pl.pallas_call(kernel, out_shape=tuple((jax.ShapeDtypeStruct(shape, jnp.f...  6.67 us
    all_to_all x1, starting transfers between devices, shards(): lax.all_to_all(parts.reshape(devices, 1, message), ('rows', 'cols'), 0, 0...  5.46 us
    ppermute x5, waiting for transfers between devices, swap(): return lax.ppermute(block, axis, pairs + [(j, i) for i, j in pairs])  4.78 us
    all_to_all x1, waiting for transfers between devices, shards(): lax.all_to_all(parts.reshape(devices, 1, message), ('rows', 'cols'), 0, 0...  3.97 us
    mul x1, other arithmetic, weights(): return inverse_variance * (1.0 - source_mask.astype(jnp.float32))  1.27 us
    mul x1, other arithmetic, shards(): products = [flux * weight for flux, weight in taken]  0.94 us
    squeeze x1, local copies, waits for them, and re-layouts, shards(): lax.dynamic_index_in_dim(jnp.asarray(row_tables(rows)), kind, keepdims=Fa...  0.92 us
  transfers between devices with their start and end apart: 6, of which 3 were waited for; matrix products, arithmetic and copies ran while one was open for 7% of the time, Pallas kernels for 15%

profile of v14, /device:TPU:0, one launch (start us, length us, event | category | flops | bytes accessed | tf_op | source)
XLA Modules:
  0.0 33.1 jit_solution(14313776619901835249)
XLA Ops:
  0.6 0.9 %dynamic-slice_multiply_fusion = (f32[1,1024]{1,0:T(1,128)S(1)}, f32[1,1024]{1,0:T(1,128)S(1)}, f32[1,1024]{1,0:T(1,128)S(1)}, f32[1,1024]{1,0:T(1,128)S(1)}) fusion(f32[128,1024]{1,0:T(8,128)} %f_ref.7, s32[]{:T(128)S(6)} %select_n.40, s32[128,1024]{1,0:T(8,128)} %param.7, f32[128,1024]{1,0:T(8,128)} %param.6, s32[]{:T(128)S(6)} %select_n.41, s32[]{:T(128)S(6)} %select_n.42), kind=kLoop, calls=%fused_computation.6 | loop fusion | flops 12288 | bytes 53260 | tf_op jit(solution)/shard_map/mul | solution.py:484
  1.6 0.0 copy-start
  1.6 3.4 %collective-permute-start = (f32[4,1024]{1,0:T(4,128)S(1)}, f32[4,1024]{1,0:T(4,128)S(1)}, u32[]{:S(2)}, u32[]{:S(2)}) collective-permute-start(f32[4,1024]{1,0:T(4,128)S(1)} %pad_maximum_fusion), channel_id=1, source_target_pairs={{4,8},{12,16},{20,24},{28,0},{8,4},{16,12},{24,20},{0,28},{5,9},{1... | collective-permute-start | bytes 49160 | tf_op jit(solution)/shard_map/ppermute | solution.py:447
  5.1 1.3 %subtract_multiply_fusion.w_ref = f32[128,1024]{1,0:T(8,128)S(1)} fusion(f32[128,1024]{1,0:T(8,128)} %param.6, s32[128,1024]{1,0:T(8,128)} %param.7), kind=kLoop, calls=%fused_computation | loop fusion | flops 393216 | bytes 1572864 | tf_op jit(solution)/shard_map/mul | solution.py:97
  6.3 0.0 copy-done
  6.3 0.5 %prepare.1 = (f32[136,1024]{1,0:T(8,128)S(1)}, f32[128,1024]{1,0:T(8,128)S(1)}, f32[128,1024]{1,0:T(8,128)S(1)}) custom-call(f32[128,1024]{1,0:T(8,128)S(1)} %copy-done, f32[128,1024]{1,0:T(8,128)S(1)} %subtract_multiply_fusion.w_ref), custom_call_target="tpu_custom_call" | custom-call | tf_op jit(solution)/shard_map/prepare/pallas_call | solution.py:455
  6.9 0.0 collective-permute-done.narrow_ref
  6.9 0.1 collective-permute-start.1
  6.9 2.2 %collective-permute-start.2 = (f32[128,1024]{1,0:T(8,128)S(1)}, f32[128,1024]{1,0:T(8,128)S(1)}, u32[]{:S(2)}, u32[]{:S(2)}) collective-permute-start(f32[128,1024]{1,0:T(8,128)S(1)} %get-tuple-element.25), channel_id=1, source_target_pairs={{4,8},{12,16},{20,24},{28,0},{8,4},{16,12},{24,20},{0,28},{5,9},{1... | collective-permute-start | bytes 1572872 | tf_op jit(solution)/shard_map/ppermute | solution.py:447
  9.1 0.0 collective-permute-done.1.near_ref
  9.1 2.2 %moments.1 = (f32[288,128]{1,0:T(8,128)}, f32[128,1024]{1,0:T(8,128)S(1)}) custom-call(f32[128,1024]{1,0:T(8,128)S(1)} %copy-done, f32[128,1024]{1,0:T(8,128)S(1)} %subtract_multiply_fusion.w_ref, f32[128,1024]{1,0:T(8,128)S(1)} %get-tuple-element.18.base_ref, f32[4,1024]{1,0:T(4,128)S(1)} %collective-permute-done.narrow_ref, ...), custom_call_target="tpu_custom_call" | custom-call | tf_op jit(solution)/shard_map/moments/pallas_call | solution.py:455
  11.4 5.5 %all-to-all-start = ((f32[32,1,1152]{2,1,0:T(1,128)}), f32[32,1,1152]{2,1,0:T(1,128)S(1)}, u32[]{:S(2)}, u32[]{:S(2)}) async-start(f32[32,1,1152]{2,1,0:T(1,128)} %bitcast), calls=%async_computation | async-start | bytes 294912 | tf_op jit(solution)/shard_map/all_to_all | solution.py:503
  16.8 0.9 %dynamic-slice_bitcast_fusion.rowtaps_ref = bf16[256,256]{1,0:T(8,128)(2,1)S(1)} fusion(bf16[4,256,256]{2,1,0:T(8,128)(2,1)} %constant.53.clone, s32[]{:T(128)S(6)} %select_n.44), kind=kLoop, calls=%fused_computation.1 | loop fusion | bytes 262148 | tf_op jit(solution)/shard_map/jit(dynamic_index_in_dim)/squeeze | solution.py:506
  17.8 3.7 %collective-permute-done.2.far_ref = f32[128,1024]{1,0:T(8,128)S(1)} collective-permute-done((f32[128,1024]{1,0:T(8,128)S(1)}, f32[128,1024]{1,0:T(8,128)S(1)}, u32[]{:S(2)}, u32[]{:S(2)}) %collective-permute-start.2) | collective-permute-done | bytes 524320 | tf_op jit(solution)/shard_map/ppermute | solution.py:447
  21.5 4.0 %all-to-all-done.parts_ref = f32[32,1,1152]{2,1,0:T(1,128)S(1)} async-done(((f32[32,1,1152]{2,1,0:T(1,128)}), f32[32,1,1152]{2,1,0:T(1,128)S(1)}, u32[]{:S(2)}, u32[]{:S(2)}) %all-to-all-start) | async-done | bytes 147488 | tf_op jit(solution)/shard_map/all_to_all | solution.py:503
  25.5 0.0 copy-start.1
  25.5 0.7 %edges.1 = (f32[16,128]{1,0:T(8,128)S(1)}, f32[256,128]{1,0:T(8,128)S(1)}, f32[256,128]{1,0:T(8,128)S(1)}, f32[64,128]{1,0:T(8,128)S(1)}, f32[64,128]{1,0:T(8,128)S(1)}) custom-call(f32[32,1,1152]{2,1,0:T(1,128)S(1)} %all-to-all-done.parts_ref, f32[128,1024]{1,0:T(8,128)S(1)} %copy-done, f32[128,1024]{1,0:T(8,128)S(1)} %subtract_multiply_fusion.w_ref, ...), custom_call_target="tpu_custom_call" | custom-call | tf_op jit(solution)/shard_map/edges/pallas_call | solution.py:455
  26.2 0.1 collective-permute-start.3
  26.3 2.6 %collective-permute-start.4 = (f32[64,128]{1,0:T(8,128)S(1)}, f32[64,128]{1,0:T(8,128)S(1)}, u32[]{:S(2)}, u32[]{:S(2)}) collective-permute-start(f32[64,128]{1,0:T(8,128)S(1)} %get-tuple-element.33), channel_id=1, source_target_pairs={{1,2},{3,0},{2,1},{0,3},{5,6},{7,4},{6,5},{4,7},{9,10},{11,8},{10,... | collective-permute-start | bytes 98312 | tf_op jit(solution)/shard_map/ppermute | solution.py:447
  28.9 0.0 copy-done.1
  28.9 2.2 %main.1 = (f32[128,1024]{1,0:T(8,128)}, f32[128,1024]{1,0:T(8,128)}, f32[128,512]{1,0:T(8,128)S(1)}) custom-call(f32[16,128]{1,0:T(8,128)S(1)} %get-tuple-element.26.coefficients_ref, f32[256,128]{1,0:T(8,128)S(1)} %get-tuple-element.27.left_ref, f32[256,128]{1,0:T(8,128)S(1)} %get-tuple-element.28.right_ref, f32[128,1024]{1,0:T(8,128)S(1)} %copy-done, ...), custom_call_target="tpu_custom_call" | custom-call | tf_op jit(solution)/shard_map/main/pallas_call | solution.py:455
  31.0 0.0 collective-permute-done.3.one_ref
  31.0 1.0 %collective-permute-done.4.other_ref = f32[64,128]{1,0:T(8,128)S(1)} collective-permute-done((f32[64,128]{1,0:T(8,128)S(1)}, f32[64,128]{1,0:T(8,128)S(1)}, u32[]{:S(2)}, u32[]{:S(2)}) %collective-permute-start.4) | collective-permute-done | bytes 32800 | tf_op jit(solution)/shard_map/ppermute | solution.py:447
  32.1 1.0 %final.1 = f32[128,1024]{1,0:T(8,128)} custom-call(f32[128,1024]{1,0:T(8,128)} %get-tuple-element.30.rms_in_ref, f32[128,512]{1,0:T(8,128)S(1)} %get-tuple-element.31.sides_ref, f32[64,128]{1,0:T(8,128)S(1)} %collective-permute-done.3.one_ref, f32[64,128]{1,0:T(8,128)S(1)} %collective-permute-done.4.other_ref, ...), custom_call_target="tpu_custom_call", output_to_operand_aliasing={{}: (0, {})} | custom-call | tf_op jit(solution)/shard_map/final/pallas_call | solution.py:455
  (1 shorter events, 0.0 us)
Async XLA Ops:
  1.6 4.7 %copy-start = (f32[128,1024]{1,0:T(8,128)S(1)}, f32[128,1024]{1,0:T(8,128)}, u32[]{:S(2)}) copy-start(f32[128,1024]{1,0:T(8,128)} %f_ref.7) | copy-start | bytes 1572868
  1.6 5.2 %collective-permute-start = (f32[4,1024]{1,0:T(4,128)S(1)}, f32[4,1024]{1,0:T(4,128)S(1)}, u32[]{:S(2)}, u32[]{:S(2)}) collective-permute-start(f32[4,1024]{1,0:T(4,128)S(1)} %pad_maximum_fusion), channel_id=1, source_target_pairs={{4,8},{12,16},{20,24},{28,0},{8,4},{16,12},{24,20},{0,28},{5,9},{1... | collective-permute-start | bytes 49160 | tf_op jit(solution)/shard_map/ppermute | solution.py:447
  6.9 2.3 %collective-permute-start.1 = (f32[136,1024]{1,0:T(8,128)S(1)}, f32[136,1024]{1,0:T(8,128)S(1)}, u32[]{:S(2)}, u32[]{:S(2)}) collective-permute-start(f32[136,1024]{1,0:T(8,128)S(1)} %get-tuple-element.22), channel_id=1, source_target_pairs={{0,4},{8,12},{16,20},{24,28},{4,0},{12,8},{20,16},{28,24},{1,5},{9... | collective-permute-start | bytes 1671176 | tf_op jit(solution)/shard_map/ppermute | solution.py:447
  6.9 14.5 %collective-permute-start.2 = (f32[128,1024]{1,0:T(8,128)S(1)}, f32[128,1024]{1,0:T(8,128)S(1)}, u32[]{:S(2)}, u32[]{:S(2)}) collective-permute-start(f32[128,1024]{1,0:T(8,128)S(1)} %get-tuple-element.25), channel_id=1, source_target_pairs={{4,8},{12,16},{20,24},{28,0},{8,4},{16,12},{24,20},{0,28},{5,9},{1... | collective-permute-start | bytes 1572872 | tf_op jit(solution)/shard_map/ppermute | solution.py:447
  11.4 14.1 %all-to-all-start = ((f32[32,1,1152]{2,1,0:T(1,128)}), f32[32,1,1152]{2,1,0:T(1,128)S(1)}, u32[]{:S(2)}, u32[]{:S(2)}) async-start(f32[32,1,1152]{2,1,0:T(1,128)} %bitcast), calls=%async_computation | async-start | bytes 294912 | tf_op jit(solution)/shard_map/all_to_all | solution.py:503
  25.5 3.4 %copy-start.1 = (bf16[3,256,256]{2,1,0:T(8,128)(2,1)S(1)}, bf16[3,256,256]{2,1,0:T(8,128)(2,1)}, u32[]{:S(2)}) copy-start(bf16[3,256,256]{2,1,0:T(8,128)(2,1)} %constant.54.clone.coltaps_ref) | copy-start | bytes 1179652
  26.2 4.8 %collective-permute-start.3 = (f32[64,128]{1,0:T(8,128)S(1)}, f32[64,128]{1,0:T(8,128)S(1)}, u32[]{:S(2)}, u32[]{:S(2)}) collective-permute-start(f32[64,128]{1,0:T(8,128)S(1)} %get-tuple-element.32), channel_id=1, source_target_pairs={{0,1},{2,3},{1,0},{3,2},{4,5},{6,7},{5,4},{7,6},{8,9},{10,11},{9,8... | collective-permute-start | bytes 98312 | tf_op jit(solution)/shard_map/ppermute | solution.py:447
  26.3 5.8 %collective-permute-start.4 = (f32[64,128]{1,0:T(8,128)S(1)}, f32[64,128]{1,0:T(8,128)S(1)}, u32[]{:S(2)}, u32[]{:S(2)}) collective-permute-start(f32[64,128]{1,0:T(8,128)S(1)} %get-tuple-element.33), channel_id=1, source_target_pairs={{1,2},{3,0},{2,1},{0,3},{5,6},{7,4},{6,5},{4,7},{9,10},{11,8},{10,... | collective-permute-start | bytes 98312 | tf_op jit(solution)/shard_map/ppermute | solution.py:447

commit v15 on v14

--- a/solution.py
+++ b/solution.py
@@ -442,9 +442,19 @@
 
 
 def swap(block, axis, first):
+    nrows, ncols = lax.axis_size("rows"), lax.axis_size("cols")
     count = lax.axis_size(axis)
-    pairs = [(i, (i + 1) % count) for i in range(first, count, 2)]
-    return lax.ppermute(block, axis, pairs + [(j, i) for i, j in pairs])
+    pairs = []
+    for r in range(nrows):
+        for c in range(ncols):
+            along = r if axis == "rows" else c
+            other = along + 1 if (along - first) % 2 == 0 else along - 1
+            if 0 <= other < count:
+                partner = (other, c) if axis == "rows" else (r, other)
+            else:
+                partner = (r, c ^ 1) if axis == "rows" else (r ^ 1, c)
+            pairs.append((r * ncols + c, partner[0] * ncols + partner[1]))
+    return lax.ppermute(block, ("rows", "cols"), pairs)
 
 
 def call(kernel, name, outs, scratch=(), limit=16, in_place=False):

time: 33.4 us -> 31.3 us (0.937)
  starting transfers between devices: 13.8 us -> 11 us
  waiting for transfers between devices: 8.75 us -> 9.36 us
    all_to_all x1, waiting for transfers between devices: 3.97 us -> 7.69 us  [shards(): lax.all_to_all(parts.reshape(devices, 1, message), ('rows', 'cols'), 0, 0...]
    ppermute x5, starting transfers between devices: 8.31 us -> 5.16 us  [swap(): return lax.ppermute(block, ('rows', 'cols'), pairs)]
    ppermute x5, waiting for transfers between devices: 4.78 us -> 1.67 us  [swap(): return lax.ppermute(block, ('rows', 'cols'), pairs)]
    all_to_all x1, starting transfers between devices: 5.46 us -> 5.81 us  [shards(): lax.all_to_all(parts.reshape(devices, 1, message), ('rows', 'cols'), 0, 0...]
  transfers between devices with their start and end apart: 6 -> 6, of which waited for: 3 -> 3; matrix products, arithmetic and copies ran while one was open for 7% -> 7% of each run, Pallas kernels for 15% -> 16%
where the time goes in v15:
time: 31.3 us; the launch traced here: 31 us
  starting transfers between devices  11 us (35%)
  waiting for transfers between devices  9.36 us (30%)
  Pallas kernels  6.67 us (21%)
  other arithmetic  2.23 us (7%)
  local copies, waits for them, and re-layouts  1.01 us (3%)
  between operations  0.76 us (2%)
    all_to_all x1, waiting for transfers between devices, shards(): lax.all_to_all(parts.reshape(devices, 1, message), ('rows', 'cols'), 0, 0...  7.69 us
    pallas_call x5, Pallas kernels, run(): pl.pallas_call(kernel, out_shape=tuple((jax.ShapeDtypeStruct(shape, jnp.f...  6.67 us
    all_to_all x1, starting transfers between devices, shards(): lax.all_to_all(parts.reshape(devices, 1, message), ('rows', 'cols'), 0, 0...  5.81 us
    ppermute x5, starting transfers between devices, swap(): return lax.ppermute(block, ('rows', 'cols'), pairs)  5.16 us
    ppermute x5, waiting for transfers between devices, swap(): return lax.ppermute(block, ('rows', 'cols'), pairs)  1.67 us
    mul x1, other arithmetic, weights(): return inverse_variance * (1.0 - source_mask.astype(jnp.float32))  1.27 us
    mul x1, other arithmetic, shards(): products = [flux * weight for flux, weight in taken]  0.94 us
    squeeze x1, local copies, waits for them, and re-layouts, shards(): lax.dynamic_index_in_dim(jnp.asarray(row_tables(rows)), kind, keepdims=Fa...  0.92 us
  transfers between devices with their start and end apart: 6, of which 3 were waited for; matrix products, arithmetic and copies ran while one was open for 7% of the time, Pallas kernels for 16%

profile of v15, /device:TPU:0, one launch (start us, length us, event | category | flops | bytes accessed | tf_op | source)
XLA Modules:
  0.0 31.0 jit_solution(14542991663620132375)
XLA Ops:
  0.6 0.9 %dynamic-slice_multiply_fusion = (f32[1,1024]{1,0:T(1,128)S(1)}, f32[1,1024]{1,0:T(1,128)S(1)}, f32[1,1024]{1,0:T(1,128)S(1)}, f32[1,1024]{1,0:T(1,128)S(1)}) fusion(f32[128,1024]{1,0:T(8,128)} %f_ref.7, s32[]{:T(128)S(6)} %select_n.40, s32[128,1024]{1,0:T(8,128)} %param.7, f32[128,1024]{1,0:T(8,128)} %param.6, s32[]{:T(128)S(6)} %select_n.41, s32[]{:T(128)S(6)} %select_n.42), kind=kLoop, calls=%fused_computation.6 | loop fusion | flops 12288 | bytes 53260 | tf_op jit(solution)/shard_map/mul | solution.py:494
  1.6 0.0 copy-start
  1.6 3.1 %collective-permute-start = (f32[4,1024]{1,0:T(4,128)S(1)}, f32[4,1024]{1,0:T(4,128)S(1)}, u32[]{:S(2)}, u32[]{:S(2)}) collective-permute-start(f32[4,1024]{1,0:T(4,128)S(1)} %pad_maximum_fusion), channel_id=1, source_target_pairs={{0,1},{1,0},{2,3},{3,2},{4,8},{5,9},{6,10},{7,11},{8,4},{9,5},{10,... | collective-permute-start | bytes 49160 | tf_op jit(solution)/shard_map/ppermute | solution.py:457
  4.7 1.3 %subtract_multiply_fusion.w_ref = f32[128,1024]{1,0:T(8,128)S(1)} fusion(f32[128,1024]{1,0:T(8,128)} %param.6, s32[128,1024]{1,0:T(8,128)} %param.7), kind=kLoop, calls=%fused_computation | loop fusion | flops 393216 | bytes 1572864 | tf_op jit(solution)/shard_map/mul | solution.py:97
  6.0 0.0 copy-done
  6.0 0.5 %prepare.1 = (f32[136,1024]{1,0:T(8,128)S(1)}, f32[128,1024]{1,0:T(8,128)S(1)}, f32[128,1024]{1,0:T(8,128)S(1)}) custom-call(f32[128,1024]{1,0:T(8,128)S(1)} %copy-done, f32[128,1024]{1,0:T(8,128)S(1)} %subtract_multiply_fusion.w_ref), custom_call_target="tpu_custom_call" | custom-call | tf_op jit(solution)/shard_map/prepare/pallas_call | solution.py:465
  6.5 0.0 collective-permute-done.narrow_ref
  6.5 0.1 collective-permute-start.1
  6.6 1.8 %collective-permute-start.2 = (f32[128,1024]{1,0:T(8,128)S(1)}, f32[128,1024]{1,0:T(8,128)S(1)}, u32[]{:S(2)}, u32[]{:S(2)}) collective-permute-start(f32[128,1024]{1,0:T(8,128)S(1)} %get-tuple-element.25), channel_id=1, source_target_pairs={{0,1},{1,0},{2,3},{3,2},{4,8},{5,9},{6,10},{7,11},{8,4},{9,5},{10,... | collective-permute-start | bytes 1572872 | tf_op jit(solution)/shard_map/ppermute | solution.py:457
  8.5 0.1 collective-permute-done.1.near_ref
  8.6 2.2 %moments.1 = (f32[288,128]{1,0:T(8,128)}, f32[128,1024]{1,0:T(8,128)S(1)}) custom-call(f32[128,1024]{1,0:T(8,128)S(1)} %copy-done, f32[128,1024]{1,0:T(8,128)S(1)} %subtract_multiply_fusion.w_ref, f32[128,1024]{1,0:T(8,128)S(1)} %get-tuple-element.18.base_ref, f32[4,1024]{1,0:T(4,128)S(1)} %collective-permute-done.narrow_ref, ...), custom_call_target="tpu_custom_call" | custom-call | tf_op jit(solution)/shard_map/moments/pallas_call | solution.py:465
  10.8 5.8 %all-to-all-start = ((f32[32,1,1152]{2,1,0:T(1,128)}), f32[32,1,1152]{2,1,0:T(1,128)S(1)}, u32[]{:S(2)}, u32[]{:S(2)}) async-start(f32[32,1,1152]{2,1,0:T(1,128)} %bitcast), calls=%async_computation | async-start | bytes 294912 | tf_op jit(solution)/shard_map/all_to_all | solution.py:513
  16.6 0.9 %dynamic-slice_bitcast_fusion.rowtaps_ref = bf16[256,256]{1,0:T(8,128)(2,1)S(1)} fusion(bf16[4,256,256]{2,1,0:T(8,128)(2,1)} %constant.53.clone, s32[]{:T(128)S(6)} %select_n.44), kind=kLoop, calls=%fused_computation.1 | loop fusion | bytes 262148 | tf_op jit(solution)/shard_map/jit(dynamic_index_in_dim)/squeeze | solution.py:516
  17.5 0.0 collective-permute-done.2.far_ref
  17.5 7.7 %all-to-all-done.parts_ref = f32[32,1,1152]{2,1,0:T(1,128)S(1)} async-done(((f32[32,1,1152]{2,1,0:T(1,128)}), f32[32,1,1152]{2,1,0:T(1,128)S(1)}, u32[]{:S(2)}, u32[]{:S(2)}) %all-to-all-start) | async-done | bytes 147488 | tf_op jit(solution)/shard_map/all_to_all | solution.py:513
  25.2 0.0 copy-start.1
  25.2 0.7 %edges.1 = (f32[16,128]{1,0:T(8,128)S(1)}, f32[256,128]{1,0:T(8,128)S(1)}, f32[256,128]{1,0:T(8,128)S(1)}, f32[64,128]{1,0:T(8,128)S(1)}, f32[64,128]{1,0:T(8,128)S(1)}) custom-call(f32[32,1,1152]{2,1,0:T(1,128)S(1)} %all-to-all-done.parts_ref, f32[128,1024]{1,0:T(8,128)S(1)} %copy-done, f32[128,1024]{1,0:T(8,128)S(1)} %subtract_multiply_fusion.w_ref, ...), custom_call_target="tpu_custom_call" | custom-call | tf_op jit(solution)/shard_map/edges/pallas_call | solution.py:465
  26.0 0.1 collective-permute-start.3
  26.1 0.1 collective-permute-start.4
  26.1 0.1 copy-done.1
  26.2 2.2 %main.1 = (f32[128,1024]{1,0:T(8,128)}, f32[128,1024]{1,0:T(8,128)}, f32[128,512]{1,0:T(8,128)S(1)}) custom-call(f32[16,128]{1,0:T(8,128)S(1)} %get-tuple-element.26.coefficients_ref, f32[256,128]{1,0:T(8,128)S(1)} %get-tuple-element.27.left_ref, f32[256,128]{1,0:T(8,128)S(1)} %get-tuple-element.28.right_ref, f32[128,1024]{1,0:T(8,128)S(1)} %copy-done, ...), custom_call_target="tpu_custom_call" | custom-call | tf_op jit(solution)/shard_map/main/pallas_call | solution.py:465
  28.4 1.6 %collective-permute-done.3.one_ref = f32[64,128]{1,0:T(8,128)S(1)} collective-permute-done((f32[64,128]{1,0:T(8,128)S(1)}, f32[64,128]{1,0:T(8,128)S(1)}, u32[]{:S(2)}, u32[]{:S(2)}) %collective-permute-start.3) | collective-permute-done | bytes 32800 | tf_op jit(solution)/shard_map/ppermute | solution.py:457
  30.0 0.0 collective-permute-done.4.other_ref
  30.0 1.0 %final.1 = f32[128,1024]{1,0:T(8,128)} custom-call(f32[128,1024]{1,0:T(8,128)} %get-tuple-element.30.rms_in_ref, f32[128,512]{1,0:T(8,128)S(1)} %get-tuple-element.31.sides_ref, f32[64,128]{1,0:T(8,128)S(1)} %collective-permute-done.3.one_ref, f32[64,128]{1,0:T(8,128)S(1)} %collective-permute-done.4.other_ref, ...), custom_call_target="tpu_custom_call", output_to_operand_aliasing={{}: (0, {})} | custom-call | tf_op jit(solution)/shard_map/final/pallas_call | solution.py:465
  (1 shorter events, 0.0 us)
Async XLA Ops:
  1.6 4.4 %copy-start = (f32[128,1024]{1,0:T(8,128)S(1)}, f32[128,1024]{1,0:T(8,128)}, u32[]{:S(2)}) copy-start(f32[128,1024]{1,0:T(8,128)} %f_ref.7) | copy-start | bytes 1572868
  1.6 4.9 %collective-permute-start = (f32[4,1024]{1,0:T(4,128)S(1)}, f32[4,1024]{1,0:T(4,128)S(1)}, u32[]{:S(2)}, u32[]{:S(2)}) collective-permute-start(f32[4,1024]{1,0:T(4,128)S(1)} %pad_maximum_fusion), channel_id=1, source_target_pairs={{0,1},{1,0},{2,3},{3,2},{4,8},{5,9},{6,10},{7,11},{8,4},{9,5},{10,... | collective-permute-start | bytes 49160 | tf_op jit(solution)/shard_map/ppermute | solution.py:457
  6.5 2.0 %collective-permute-start.1 = (f32[136,1024]{1,0:T(8,128)S(1)}, f32[136,1024]{1,0:T(8,128)S(1)}, u32[]{:S(2)}, u32[]{:S(2)}) collective-permute-start(f32[136,1024]{1,0:T(8,128)S(1)} %get-tuple-element.22), channel_id=1, source_target_pairs={{0,4},{1,5},{2,6},{3,7},{4,0},{5,1},{6,2},{7,3},{8,12},{9,13},{10,... | collective-permute-start | bytes 1671176 | tf_op jit(solution)/shard_map/ppermute | solution.py:457
  6.6 10.9 %collective-permute-start.2 = (f32[128,1024]{1,0:T(8,128)S(1)}, f32[128,1024]{1,0:T(8,128)S(1)}, u32[]{:S(2)}, u32[]{:S(2)}) collective-permute-start(f32[128,1024]{1,0:T(8,128)S(1)} %get-tuple-element.25), channel_id=1, source_target_pairs={{0,1},{1,0},{2,3},{3,2},{4,8},{5,9},{6,10},{7,11},{8,4},{9,5},{10,... | collective-permute-start | bytes 1572872 | tf_op jit(solution)/shard_map/ppermute | solution.py:457
  10.8 14.5 %all-to-all-start = ((f32[32,1,1152]{2,1,0:T(1,128)}), f32[32,1,1152]{2,1,0:T(1,128)S(1)}, u32[]{:S(2)}, u32[]{:S(2)}) async-start(f32[32,1,1152]{2,1,0:T(1,128)} %bitcast), calls=%async_computation | async-start | bytes 294912 | tf_op jit(solution)/shard_map/all_to_all | solution.py:513
  25.2 1.0 %copy-start.1 = (bf16[3,256,256]{2,1,0:T(8,128)(2,1)S(1)}, bf16[3,256,256]{2,1,0:T(8,128)(2,1)}, u32[]{:S(2)}) copy-start(bf16[3,256,256]{2,1,0:T(8,128)(2,1)} %constant.54.clone.coltaps_ref) | copy-start | bytes 1179652
  26.0 4.0 %collective-permute-start.3 = (f32[64,128]{1,0:T(8,128)S(1)}, f32[64,128]{1,0:T(8,128)S(1)}, u32[]{:S(2)}, u32[]{:S(2)}) collective-permute-start(f32[64,128]{1,0:T(8,128)S(1)} %get-tuple-element.32), channel_id=1, source_target_pairs={{0,1},{1,0},{2,3},{3,2},{4,5},{5,4},{6,7},{7,6},{8,9},{9,8},{10,11... | collective-permute-start | bytes 98312 | tf_op jit(solution)/shard_map/ppermute | solution.py:457
  26.1 3.9 %collective-permute-start.4 = (f32[64,128]{1,0:T(8,128)S(1)}, f32[64,128]{1,0:T(8,128)S(1)}, u32[]{:S(2)}, u32[]{:S(2)}) collective-permute-start(f32[64,128]{1,0:T(8,128)S(1)} %get-tuple-element.33), channel_id=1, source_target_pairs={{0,4},{1,2},{2,1},{3,7},{4,0},{5,6},{6,5},{7,3},{8,12},{9,10},{10,... | collective-permute-start | bytes 98312 | tf_op jit(solution)/shard_map/ppermute | solution.py:457

commit v16 on v15

--- a/solution.py
+++ b/solution.py
@@ -69,6 +69,15 @@
     return np.stack(tables)
 
 
+def side_tables():
+    table = squared_taps(LANES, False, False).T
+    tables = []
+    for part in (table[:REACH], table[REACH + LANES :]):
+        nothing = np.zeros_like(part)
+        tables.append(np.concatenate(split(np.block([[part, nothing], [nothing, part]])), axis=1))
+    return np.stack(tables)
+
+
 def split_values(values):
     high = values.astype(jnp.bfloat16)
     return high, (values - high.astype(jnp.float32)).astype(jnp.bfloat16)
@@ -115,7 +124,14 @@
     return here, weight * here + smooth_weight * (4.0 * here - beside)
 
 
-def prepare_kernel(f_ref, w_ref, near_ref, far_ref, v1_ref, v0_ref):
+def columns_to_lanes(fields, edges, lane):
+    for k, field in fields:
+        edges = jnp.where(lane == k, pltpu.roll(field[:, field.shape[1] - LANES :], k + 1, 1), edges)
+        edges = jnp.where(lane == 4 + k, pltpu.roll(field[:, :LANES], 4 + k, 1), edges)
+    return edges
+
+
+def prepare_kernel(f_ref, w_ref, near_ref, far_ref, v1_ref, sums_ref, edge_ref, v0_ref):
     rows = f_ref.shape[0]
 
     def write(out_ref, begin):
@@ -145,11 +161,20 @@
     for start in range(0, rows, 8):
         at = pl.ds(start, 8)
         v0_ref[pl.ds(NEAR + start, 8), own] = f_ref[at, :] * w_ref[at, :]
+    lane = lax.broadcasted_iota(jnp.int32, (8, LANES), 1)
+    sums = [jnp.zeros((8, cols), jnp.float32) for _ in range(3)]
     for start in range(0, rows, 8):
-        _, v1_ref[pl.ds(start, 8), :] = image(v0_ref, w_ref[pl.ds(start, 8), :], NEAR + start)
-
-
-def moments_kernel(f_ref, w_ref, base_ref, narrow_ref, near_ref, out_ref, v1_out_ref, v1_ref, edge_ref):
+        at = pl.ds(start, 8)
+        weight = w_ref[at, :]
+        v0, v1 = image(v0_ref, weight, NEAR + start)
+        v1_ref[at, :] = v1
+        sums = [total + term for total, term in zip(sums, (v0 * v0, v0 * v1, v1 * v1))]
+        edge_ref[at, :] = columns_to_lanes(((0, v0), (3, weight)), jnp.zeros((8, LANES), jnp.float32), lane)
+    for i, total in enumerate(sums):
+        sums_ref[pl.ds(8 * i, 8), :] = sum(total[:, k : k + LANES] for k in range(0, cols, LANES))
+
+
+def moments_kernel(f_ref, w_ref, base_ref, sums_ref, edge_in_ref, narrow_ref, near_ref, out_ref, v1_out_ref, v1_ref, edge_ref):
     rows, cols = f_ref.shape
     first_row, last_row, _, _ = at_edges()
     even = is_even()
@@ -191,23 +216,28 @@
     pl.when(jnp.logical_not(last_row))(lambda: edge_row(below, rows - 1, NEAR + rows))
 
     lane = lax.broadcasted_iota(jnp.int32, (8, LANES), 1)
-    sums = [jnp.zeros((8, cols), jnp.float32) for _ in range(4)]
+    last_sum = jnp.zeros((8, cols), jnp.float32)
     for start in range(0, rows, 8):
-        weight = w_ref[pl.ds(start, 8), :]
-        v0 = f_ref[pl.ds(start, 8), :] * weight
-        v1, v2 = image(v1_ref, weight, NEAR + start)
-        sums = [total + term for total, term in zip(sums, (v0 * v0, v0 * v1, v1 * v1, v1 * v2))]
-        edges = jnp.zeros((8, LANES), jnp.float32)
-        for k, field in enumerate((v0, v1, v2, weight)):
-            edges = jnp.where(lane == k, pltpu.roll(field[:, cols - LANES :], k + 1, 1), edges)
-            edges = jnp.where(lane == 4 + k, pltpu.roll(field[:, :LANES], 4 + k, 1), edges)
-        edge_ref[pl.ds(start, 8), :] = edges
-
+        at = pl.ds(start, 8)
+        v1, v2 = image(v1_ref, w_ref[at, :], NEAR + start)
+        last_sum = last_sum + v1 * v2
+        edge_ref[at, :] = columns_to_lanes(((1, v1), (2, v2)), edge_in_ref[at, :], lane)
+
+    def narrowed(total):
+        return sum(total[:, k : k + LANES] for k in range(0, cols, LANES))
+
+    first_sum = [jnp.zeros((1, cols), jnp.float32) for _ in range(2)]
+    for halo, inner in ((above, 0), (below, rows - 1)):
+        at = pl.ds(inner, 1)
+        added = -smooth_weight * halo[0]
+        first_sum[0] = first_sum[0] + f_ref[at, :] * w_ref[at, :] * added
+        first_sum[1] = first_sum[1] + (2.0 * base_ref[at, :] + added) * added
+    totals = [jnp.sum(sums_ref[pl.ds(8 * i, 8), :], axis=0, keepdims=True) for i in range(3)]
+    totals = [totals[0], totals[1] + narrowed(first_sum[0]), totals[2] + narrowed(first_sum[1])]
+    totals.append(jnp.sum(narrowed(last_sum), axis=0, keepdims=True))
     result = jnp.zeros((1, LANES), jnp.float32)
-    for i, total in enumerate(sums):
-        narrow = sum(total[:, k : k + LANES] for k in range(0, cols, LANES))
-        total = jnp.sum(jnp.sum(narrow, axis=0, keepdims=True), axis=1, keepdims=True)
-        result = jnp.where(lane[:1] == i, total, result)
+    for i, total in enumerate(totals):
+        result = jnp.where(lane[:1] == i, jnp.sum(total, axis=1, keepdims=True), result)
     vectors = edge_ref[...].T
     message = [result] + [vectors[k : k + 1, :] for k in range(VECTORS)]
     copies = jnp.concatenate(message * 8, axis=0)
@@ -402,38 +432,40 @@
         scatter = flux - background
         high_ref[at, :], low_ref[at, :] = split_values(scatter * scatter)
     passed = row_pass(rowtaps_ref, high_ref[...], low_ref[...], rows)
-    sides_ref[:, pl.ds(0, 2 * LANES)] = passed[:, : 2 * LANES]
-    sides_ref[:, pl.ds(2 * LANES, 2 * LANES)] = passed[:, cols - 2 * LANES :]
-    high, low = split_values(pltpu.roll(passed, REACH, 1))
-    for j in range(1, cols // LANES - 1):
+    _, _, first_col, last_col = at_edges()
+    nothing = jnp.zeros((rows, LANES), jnp.float32)
+    passed = jnp.concatenate([nothing, passed, nothing], axis=1)
+    high, low = split_values(pltpu.roll(passed, passed.shape[1] - (LANES - REACH), 1))
+    blocks = cols // LANES
+    kinds = {0: first_col.astype(jnp.int32), blocks - 1: 2 * last_col.astype(jnp.int32)}
+    for j in range(blocks):
         at = slice(j * LANES, j * LANES + 2 * LANES)
-        rms_ref[:, pl.ds(j * LANES, LANES)] = column_pass(coltaps_ref[0], high[:, at], low[:, at])
-
-
-def column_pass(table, high, low):
+        smoothed = product_of_pairs(high[:, at], low[:, at], coltaps_ref[kinds.get(j, 0)])
+        if j in kinds:
+            sides_ref[:, pl.ds(LANES * (j > 0), LANES)] = smoothed
+        else:
+            rms_ref[:, pl.ds(j * LANES, LANES)] = jnp.sqrt(smoothed + 1e-06)
+
+
+def product_of_pairs(high, low, table):
+    count = table.shape[1] // 2
     both = dot(high, table)
-    smoothed = both[:, :LANES] + (both[:, LANES:] + dot(low, table[:, :LANES]))
-    return jnp.sqrt(smoothed + 1e-06)
-
-
-def final_kernel(rms_in_ref, sides_ref, one_ref, other_ref, coltaps_ref, rms_ref, blocks_ref, sems):
+    return both[:, :count] + (both[:, count:] + dot(low, table[:, :count]))
+
+
+def final_kernel(rms_in_ref, sides_ref, one_ref, other_ref, sidetaps_ref, rms_ref, blocks_ref, sems):
     rows, cols = rms_ref.shape
     del rms_in_ref
     _, _, first_col, last_col = at_edges()
     even = is_even("cols")
     left = jnp.where(even, other_ref[...], one_ref[...])
     right = jnp.where(even, one_ref[...], other_ref[...])
-    left = jnp.concatenate([pltpu.roll(left, REACH, 1), left], axis=0)
-    right = jnp.concatenate([right, pltpu.roll(right, REACH, 1)], axis=0)
-    sides = sides_ref[...]
-    windows = (
-        pltpu.roll(jnp.concatenate([left, sides[:, : 2 * LANES]], axis=1), 3 * LANES - REACH, 1)[:, : 2 * LANES],
-        pltpu.roll(jnp.concatenate([sides[:, 2 * LANES :], right], axis=1), 3 * LANES - REACH, 1)[:, : 2 * LANES],
-    )
     copies = []
-    for side, which in enumerate((first_col.astype(jnp.int32), 2 * last_col.astype(jnp.int32))):
-        high, low = split_values(windows[side])
-        blocks_ref[side] = column_pass(coltaps_ref[which], high, low)
+    for side, (halo, outside) in enumerate(((left, first_col), (right, last_col))):
+        high, low = split_values(halo)
+        added = product_of_pairs(high, low, sidetaps_ref[side])
+        added = jnp.where(outside, 0.0, jnp.concatenate([added[:, :LANES], added[:, LANES:]], axis=0))
+        blocks_ref[side] = jnp.sqrt(sides_ref[:, pl.ds(side * LANES, LANES)] + added + 1e-06)
         target = rms_ref.at[:, pl.ds(side * (cols - LANES), LANES)]
         copies.append(pltpu.make_async_copy(blocks_ref.at[side], target, sems.at[side]))
         copies[-1].start()
@@ -496,8 +528,11 @@
 
     own = (coadd_flux, weights(inverse_variance, source_mask))
     field = scratch(rows + 2 * NEAR, cols + LANES)
-    to_near, to_far, base = call(
-        prepare_kernel, "prepare", ((2 * REACH + 8, cols), (2 * REACH, cols), (rows, cols)), (field,)
+    to_near, to_far, *base = call(
+        prepare_kernel,
+        "prepare",
+        ((2 * REACH + 8, cols), (2 * REACH, cols), (rows, cols), (3 * 8, LANES), (rows, LANES)),
+        (field,),
     )(*own)
     to_near, to_far, narrow = lax.optimization_barrier((to_near, to_far, narrow))
     near = swap(to_near, "rows", 0)
@@ -509,7 +544,7 @@
         "moments",
         ((devices * (VECTORS + 1), LANES), (rows, cols)),
         (field, scratch(rows, LANES)),
-    )(*own, base, narrow, near)
+    )(*own, *base, narrow, near)
     parts = lax.all_to_all(parts.reshape(devices, 1, message), ("rows", "cols"), 0, 0, tiled=True)
     first_row, last_row, _, _ = at_edges()
     kind = jnp.where(is_even(), first_row.astype(jnp.int32), 2 + last_row.astype(jnp.int32))
@@ -530,12 +565,12 @@
     background, rms, sides = call(
         main_kernel,
         "main",
-        ((rows, cols), (rows, cols), (rows, 4 * LANES)),
+        ((rows, cols), (rows, cols), (rows, 2 * LANES)),
         halves + (scratch(REACH + 2 * NEAR, cols + LANES),) + (scratch(reached, cols, dtype=jnp.bfloat16),) * 2,
     )(numbers, left, right, *fields, row_taps, col_taps)
     (rms,) = call(
         final_kernel, "final", ((rows, cols),), (scratch(2, rows, LANES), pltpu.SemaphoreType.DMA((2,))), in_place=True
-    )(rms, sides, one, other, col_taps)
+    )(rms, sides, one, other, jnp.asarray(side_tables()))
     return background, rms
 
 

time: 31.3 us -> 31.1 us (level)
  no operation moved by 1% of the time
where the time goes in v16:
time: 31.1 us; the launch traced here: 30.8 us
  starting transfers between devices  10.8 us (35%)
  waiting for transfers between devices  9.35 us (30%)
  Pallas kernels  6.66 us (21%)
  other arithmetic  2.23 us (7%)
  local copies, waits for them, and re-layouts  1.02 us (3%)
  between operations  0.76 us (2%)
    all_to_all x1, waiting for transfers between devices, shards(): lax.all_to_all(parts.reshape(devices, 1, message), ('rows', 'cols'), 0, 0...  7.69 us
    pallas_call x5, Pallas kernels, run(): pl.pallas_call(kernel, out_shape=tuple((jax.ShapeDtypeStruct(shape, jnp.f...  6.66 us
    all_to_all x1, starting transfers between devices, shards(): lax.all_to_all(parts.reshape(devices, 1, message), ('rows', 'cols'), 0, 0...  5.71 us
    ppermute x5, starting transfers between devices, swap(): return lax.ppermute(block, ('rows', 'cols'), pairs)  5.07 us
    ppermute x5, waiting for transfers between devices, swap(): return lax.ppermute(block, ('rows', 'cols'), pairs)  1.66 us
    mul x1, other arithmetic, weights(): return inverse_variance * (1.0 - source_mask.astype(jnp.float32))  1.27 us
    mul x1, other arithmetic, shards(): products = [flux * weight for flux, weight in taken]  0.94 us
    squeeze x1, local copies, waits for them, and re-layouts, shards(): lax.dynamic_index_in_dim(jnp.asarray(row_tables(rows)), kind, keepdims=Fa...  0.92 us
  transfers between devices with their start and end apart: 6, of which 3 were waited for; matrix products, arithmetic and copies ran while one was open for 7% of the time, Pallas kernels for 16%

profile of v16, /device:TPU:0, one launch (start us, length us, event | category | flops | bytes accessed | tf_op | source)
XLA Modules:
  0.0 30.8 jit_solution(2883236066397118635)
XLA Ops:
  0.6 0.9 %dynamic-slice_multiply_fusion = (f32[1,1024]{1,0:T(1,128)S(1)}, f32[1,1024]{1,0:T(1,128)S(1)}, f32[1,1024]{1,0:T(1,128)S(1)}, f32[1,1024]{1,0:T(1,128)S(1)}) fusion(f32[128,1024]{1,0:T(8,128)} %f_ref.7, s32[]{:T(128)S(6)} %select_n.40, s32[128,1024]{1,0:T(8,128)} %param.8, f32[128,1024]{1,0:T(8,128)} %param.7, s32[]{:T(128)S(6)} %select_n.41, s32[]{:T(128)S(6)} %select_n.42), kind=kLoop, calls=%fused_computation.6 | loop fusion | flops 12288 | bytes 53260 | tf_op jit(solution)/shard_map/mul | solution.py:526
  1.6 0.0 copy-start
  1.6 3.1 %collective-permute-start = (f32[4,1024]{1,0:T(4,128)S(1)}, f32[4,1024]{1,0:T(4,128)S(1)}, u32[]{:S(2)}, u32[]{:S(2)}) collective-permute-start(f32[4,1024]{1,0:T(4,128)S(1)} %pad_maximum_fusion), channel_id=1, source_target_pairs={{0,1},{1,0},{2,3},{3,2},{4,8},{5,9},{6,10},{7,11},{8,4},{9,5},{10,... | collective-permute-start | bytes 49160 | tf_op jit(solution)/shard_map/ppermute | solution.py:489
  4.7 1.3 %subtract_multiply_fusion.w_ref = f32[128,1024]{1,0:T(8,128)S(1)} fusion(f32[128,1024]{1,0:T(8,128)} %param.7, s32[128,1024]{1,0:T(8,128)} %param.8), kind=kLoop, calls=%fused_computation | loop fusion | flops 393216 | bytes 1572864 | tf_op jit(solution)/shard_map/mul | solution.py:106
  6.0 0.0 copy-done
  6.0 0.6 %prepare.1 = (f32[136,1024]{1,0:T(8,128)S(1)}, f32[128,1024]{1,0:T(8,128)S(1)}, f32[128,1024]{1,0:T(8,128)S(1)}, f32[24,128]{1,0:T(8,128)S(1)}, f32[128,128]{1,0:T(8,128)S(1)}) custom-call(f32[128,1024]{1,0:T(8,128)S(1)} %copy-done, f32[128,1024]{1,0:T(8,128)S(1)} %subtract_multiply_fusion.w_ref), custom_call_target="tpu_custom_call" | custom-call | tf_op jit(solution)/shard_map/prepare/pallas_call | solution.py:497
  6.6 0.0 collective-permute-done.narrow_ref
  6.6 0.1 collective-permute-start.1
  6.7 1.7 %collective-permute-start.2 = (f32[128,1024]{1,0:T(8,128)S(1)}, f32[128,1024]{1,0:T(8,128)S(1)}, u32[]{:S(2)}, u32[]{:S(2)}) collective-permute-start(f32[128,1024]{1,0:T(8,128)S(1)} %get-tuple-element.29), channel_id=1, source_target_pairs={{0,1},{1,0},{2,3},{3,2},{4,8},{5,9},{6,10},{7,11},{8,4},{9,5},{10,... | collective-permute-start | bytes 1572872 | tf_op jit(solution)/shard_map/ppermute | solution.py:489
  8.5 0.2 collective-permute-done.1.near_ref
  8.6 2.2 %moments.1 = (f32[288,128]{1,0:T(8,128)}, f32[128,1024]{1,0:T(8,128)S(1)}) custom-call(f32[128,1024]{1,0:T(8,128)S(1)} %copy-done, f32[128,1024]{1,0:T(8,128)S(1)} %subtract_multiply_fusion.w_ref, f32[128,1024]{1,0:T(8,128)S(1)} %get-tuple-element.20.base_ref, f32[24,128]{1,0:T(8,128)S(1)} %get-tuple-element.21.sums_ref, ...), custom_call_target="tpu_custom_call" | custom-call | tf_op jit(solution)/shard_map/moments/pallas_call | solution.py:497
  10.8 5.7 %all-to-all-start = ((f32[32,1,1152]{2,1,0:T(1,128)}), f32[32,1,1152]{2,1,0:T(1,128)S(1)}, u32[]{:S(2)}, u32[]{:S(2)}) async-start(f32[32,1,1152]{2,1,0:T(1,128)} %bitcast), calls=%async_computation | async-start | bytes 294912 | tf_op jit(solution)/shard_map/all_to_all | solution.py:548
  16.5 0.9 %dynamic-slice_bitcast_fusion.rowtaps_ref = bf16[256,256]{1,0:T(8,128)(2,1)S(1)} fusion(bf16[4,256,256]{2,1,0:T(8,128)(2,1)} %constant.55.clone, s32[]{:T(128)S(6)} %select_n.44), kind=kLoop, calls=%fused_computation.1 | loop fusion | bytes 262148 | tf_op jit(solution)/shard_map/jit(dynamic_index_in_dim)/squeeze | solution.py:551
  17.5 0.0 collective-permute-done.2.far_ref
  17.5 7.7 %all-to-all-done.parts_ref = f32[32,1,1152]{2,1,0:T(1,128)S(1)} async-done(((f32[32,1,1152]{2,1,0:T(1,128)}), f32[32,1,1152]{2,1,0:T(1,128)S(1)}, u32[]{:S(2)}, u32[]{:S(2)}) %all-to-all-start) | async-done | bytes 147488 | tf_op jit(solution)/shard_map/all_to_all | solution.py:548
  25.2 0.0 copy-start.1
  25.2 0.7 %edges.1 = (f32[16,128]{1,0:T(8,128)S(1)}, f32[256,128]{1,0:T(8,128)S(1)}, f32[256,128]{1,0:T(8,128)S(1)}, f32[64,128]{1,0:T(8,128)S(1)}, f32[64,128]{1,0:T(8,128)S(1)}) custom-call(f32[32,1,1152]{2,1,0:T(1,128)S(1)} %all-to-all-done.parts_ref, f32[128,1024]{1,0:T(8,128)S(1)} %copy-done, f32[128,1024]{1,0:T(8,128)S(1)} %subtract_multiply_fusion.w_ref, ...), custom_call_target="tpu_custom_call" | custom-call | tf_op jit(solution)/shard_map/edges/pallas_call | solution.py:497
  25.9 0.1 collective-permute-start.3
  26.0 0.1 collective-permute-start.4
  26.1 0.1 copy-done.1
  26.2 0.0 copy-start.2
  26.2 2.3 %main.1 = (f32[128,1024]{1,0:T(8,128)}, f32[128,1024]{1,0:T(8,128)}, f32[128,256]{1,0:T(8,128)S(1)}) custom-call(f32[16,128]{1,0:T(8,128)S(1)} %get-tuple-element.30.coefficients_ref, f32[256,128]{1,0:T(8,128)S(1)} %get-tuple-element.31.left_ref, f32[256,128]{1,0:T(8,128)S(1)} %get-tuple-element.32.right_ref, f32[128,1024]{1,0:T(8,128)S(1)} %copy-done, ...), custom_call_target="tpu_custom_call" | custom-call | tf_op jit(solution)/shard_map/main/pallas_call | solution.py:497
  28.4 1.5 %collective-permute-done.3.one_ref = f32[64,128]{1,0:T(8,128)S(1)} collective-permute-done((f32[64,128]{1,0:T(8,128)S(1)}, f32[64,128]{1,0:T(8,128)S(1)}, u32[]{:S(2)}, u32[]{:S(2)}) %collective-permute-start.3) | collective-permute-done | bytes 32800 | tf_op jit(solution)/shard_map/ppermute | solution.py:489
  29.9 0.0 collective-permute-done.4.other_ref
  29.9 0.0 copy-done.2
  29.9 0.9 %final.1 = f32[128,1024]{1,0:T(8,128)} custom-call(f32[128,1024]{1,0:T(8,128)} %get-tuple-element.34.rms_in_ref, f32[128,256]{1,0:T(8,128)S(1)} %get-tuple-element.35.sides_ref, f32[64,128]{1,0:T(8,128)S(1)} %collective-permute-done.3.one_ref, f32[64,128]{1,0:T(8,128)S(1)} %collective-permute-done.4.other_ref, ...), custom_call_target="tpu_custom_call", output_to_operand_aliasing={{}: (0, {})} | custom-call | tf_op jit(solution)/shard_map/final/pallas_call | solution.py:497
  (1 shorter events, 0.0 us)
Async XLA Ops:
  1.6 4.4 %copy-start = (f32[128,1024]{1,0:T(8,128)S(1)}, f32[128,1024]{1,0:T(8,128)}, u32[]{:S(2)}) copy-start(f32[128,1024]{1,0:T(8,128)} %f_ref.7) | copy-start | bytes 1572868
  1.6 5.0 %collective-permute-start = (f32[4,1024]{1,0:T(4,128)S(1)}, f32[4,1024]{1,0:T(4,128)S(1)}, u32[]{:S(2)}, u32[]{:S(2)}) collective-permute-start(f32[4,1024]{1,0:T(4,128)S(1)} %pad_maximum_fusion), channel_id=1, source_target_pairs={{0,1},{1,0},{2,3},{3,2},{4,8},{5,9},{6,10},{7,11},{8,4},{9,5},{10,... | collective-permute-start | bytes 49160 | tf_op jit(solution)/shard_map/ppermute | solution.py:489
  6.6 2.0 %collective-permute-start.1 = (f32[136,1024]{1,0:T(8,128)S(1)}, f32[136,1024]{1,0:T(8,128)S(1)}, u32[]{:S(2)}, u32[]{:S(2)}) collective-permute-start(f32[136,1024]{1,0:T(8,128)S(1)} %get-tuple-element.26), channel_id=1, source_target_pairs={{0,4},{1,5},{2,6},{3,7},{4,0},{5,1},{6,2},{7,3},{8,12},{9,13},{10,... | collective-permute-start | bytes 1671176 | tf_op jit(solution)/shard_map/ppermute | solution.py:489
  6.7 10.7 %collective-permute-start.2 = (f32[128,1024]{1,0:T(8,128)S(1)}, f32[128,1024]{1,0:T(8,128)S(1)}, u32[]{:S(2)}, u32[]{:S(2)}) collective-permute-start(f32[128,1024]{1,0:T(8,128)S(1)} %get-tuple-element.29), channel_id=1, source_target_pairs={{0,1},{1,0},{2,3},{3,2},{4,8},{5,9},{6,10},{7,11},{8,4},{9,5},{10,... | collective-permute-start | bytes 1572872 | tf_op jit(solution)/shard_map/ppermute | solution.py:489
  10.8 14.4 %all-to-all-start = ((f32[32,1,1152]{2,1,0:T(1,128)}), f32[32,1,1152]{2,1,0:T(1,128)S(1)}, u32[]{:S(2)}, u32[]{:S(2)}) async-start(f32[32,1,1152]{2,1,0:T(1,128)} %bitcast), calls=%async_computation | async-start | bytes 294912 | tf_op jit(solution)/shard_map/all_to_all | solution.py:548
  25.2 1.0 %copy-start.1 = (bf16[3,256,256]{2,1,0:T(8,128)(2,1)S(1)}, bf16[3,256,256]{2,1,0:T(8,128)(2,1)}, u32[]{:S(2)}) copy-start(bf16[3,256,256]{2,1,0:T(8,128)(2,1)} %constant.56.clone.coltaps_ref) | copy-start | bytes 1179652
  25.9 4.0 %collective-permute-start.3 = (f32[64,128]{1,0:T(8,128)S(1)}, f32[64,128]{1,0:T(8,128)S(1)}, u32[]{:S(2)}, u32[]{:S(2)}) collective-permute-start(f32[64,128]{1,0:T(8,128)S(1)} %get-tuple-element.36), channel_id=1, source_target_pairs={{0,1},{1,0},{2,3},{3,2},{4,5},{5,4},{6,7},{7,6},{8,9},{9,8},{10,11... | collective-permute-start | bytes 98312 | tf_op jit(solution)/shard_map/ppermute | solution.py:489
  26.0 3.9 %collective-permute-start.4 = (f32[64,128]{1,0:T(8,128)S(1)}, f32[64,128]{1,0:T(8,128)S(1)}, u32[]{:S(2)}, u32[]{:S(2)}) collective-permute-start(f32[64,128]{1,0:T(8,128)S(1)} %get-tuple-element.37), channel_id=1, source_target_pairs={{0,4},{1,2},{2,1},{3,7},{4,0},{5,6},{6,5},{7,3},{8,12},{9,10},{10,... | collective-permute-start | bytes 98312 | tf_op jit(solution)/shard_map/ppermute | solution.py:489
  26.2 3.7 %copy-start.2 = (bf16[2,128,512]{2,1,0:T(8,128)(2,1)S(1)}, bf16[2,128,512]{2,1,0:T(8,128)(2,1)}, u32[]{:S(2)}) copy-start(bf16[2,128,512]{2,1,0:T(8,128)(2,1)} %constant.57.clone.sidetaps_ref) | copy-start | bytes 786436

commit v17 on v16

--- a/solution.py
+++ b/solution.py
@@ -174,7 +174,7 @@
         sums_ref[pl.ds(8 * i, 8), :] = sum(total[:, k : k + LANES] for k in range(0, cols, LANES))
 
 
-def moments_kernel(f_ref, w_ref, base_ref, sums_ref, edge_in_ref, narrow_ref, near_ref, out_ref, v1_out_ref, v1_ref, edge_ref):
+def moments_kernel(f_ref, w_ref, base_ref, sums_ref, edge_in_ref, narrow_ref, near_ref, out_ref, v1_ref, edge_ref):
     rows, cols = f_ref.shape
     first_row, last_row, _, _ = at_edges()
     even = is_even()
@@ -203,7 +203,6 @@
         if start == rows - 8:
             v1 = v1 - jnp.where(row == 7, smooth_weight * below[0], 0.0)
         v1_ref[pl.ds(NEAR + start, 8), own] = v1
-        v1_out_ref[pl.ds(start, 8), :] = v1
 
     def edge_row(halo, inner, at):
         nearest, second, weight = halo
@@ -306,57 +305,75 @@
 
 def guard_rows(f_ref, w_ref, narrow_ref, near_ref, at_cols):
     rows = f_ref.shape[0]
+    first_row, last_row, _, _ = at_edges()
     even = is_even()
     top = f_ref[pl.ds(0, 1), at_cols] * w_ref[pl.ds(0, 1), at_cols]
     bottom = f_ref[pl.ds(rows - 1, 1), at_cols] * w_ref[pl.ds(rows - 1, 1), at_cols]
+    near_last = near_ref[pl.ds(REACH - 1, 1), at_cols] * near_ref[pl.ds(2 * REACH - 1, 1), at_cols]
+    near_first = near_ref[pl.ds(0, 1), at_cols] * near_ref[pl.ds(REACH, 1), at_cols]
+    far_nearest = jnp.where(first_row | last_row, 0.0, narrow_ref[pl.ds(0, 1), at_cols])
     near = jnp.where(even, near_ref[pl.ds(2 * REACH, 1), at_cols], near_ref[pl.ds(2 * REACH + 7, 1), at_cols])
     far = narrow_ref[pl.ds(3, 1), at_cols]
     return (
+        (jnp.where(even, far_nearest, near_last), jnp.where(even, near_first, far_nearest)),
         (jnp.where(even, bottom, near), jnp.where(even, near, top)),
         (jnp.where(even, far, bottom), jnp.where(even, top, far)),
     )
 
 
-def halo_fields(f_ref, w_ref, narrow_ref, near_ref, far_ref, near_v1_ref, far_v1_ref, v0_ref):
+def sources(f_ref, w_ref, near_ref, far_ref, v1_refs):
+    rows = f_ref.shape[0]
+    return (
+        (rows, f_ref, w_ref, 0, v1_refs[0]),
+        (REACH, near_ref, near_ref, REACH, v1_refs[1]),
+        (REACH, far_ref, far_ref, REACH, v1_refs[2]),
+    )
+
+
+def all_fields(f_ref, w_ref, narrow_ref, near_ref, far_ref, v1_refs, v0_ref):
     rows, cols = f_ref.shape
     own, pad = pl.ds(0, cols), pl.ds(cols, LANES)
-    v0_ref[:, pad] = jnp.zeros((REACH + 2 * NEAR, LANES), jnp.float32)
+    v0_ref[:, pad] = jnp.zeros((rows + 2 * NEAR, LANES), jnp.float32)
     guards = guard_rows(f_ref, w_ref, narrow_ref, near_ref, own)
-    for halo_ref, v1_ref, (above, below) in zip((near_ref, far_ref), (near_v1_ref, far_v1_ref), guards):
+    for (count, flux_ref, weight_ref, weight_row, v1_ref), (above, below) in zip(
+        sources(f_ref, w_ref, near_ref, far_ref, v1_refs), guards
+    ):
         v0_ref[pl.ds(NEAR - 1, 1), own] = above
-        v0_ref[pl.ds(NEAR + REACH, 1), own] = below
-        for start in range(0, REACH, 8):
-            v0_ref[pl.ds(NEAR + start, 8), own] = halo_ref[pl.ds(start, 8), :] * halo_ref[pl.ds(REACH + start, 8), :]
-        for start in range(0, REACH, 8):
-            _, v1_ref[pl.ds(start, 8), :] = image(v0_ref, halo_ref[pl.ds(REACH + start, 8), :], NEAR + start)
-
-
-def edge_fields(side, f_ref, w_ref, narrow_ref, near_ref, far_ref, near_v1_ref, far_v1_ref, v0_ref):
+        v0_ref[pl.ds(NEAR + count, 1), own] = below
+        for start in range(0, count, 8):
+            v0_ref[pl.ds(NEAR + start, 8), own] = flux_ref[pl.ds(start, 8), :] * weight_ref[pl.ds(weight_row + start, 8), :]
+        for start in range(0, count, 8):
+            _, v1_ref[pl.ds(start, 8), :] = image(v0_ref, weight_ref[pl.ds(weight_row + start, 8), :], NEAR + start)
+
+
+def edge_fields(side, f_ref, w_ref, narrow_ref, near_ref, far_ref, v1_refs, v0_ref):
     cols = f_ref.shape[1]
     at_cols, there = pl.ds(side * (cols - LANES), LANES), pl.ds(side * LANES, LANES)
     outermost = lax.broadcasted_iota(jnp.int32, (8, LANES), 1) == side * (LANES - 1)
     guards = guard_rows(f_ref, w_ref, narrow_ref, near_ref, at_cols)
-    for halo_ref, v1_ref, (above, below) in zip((near_ref, far_ref), (near_v1_ref, far_v1_ref), guards):
+    for (count, flux_ref, weight_ref, weight_row, v1_ref), (above, below) in zip(
+        sources(f_ref, w_ref, near_ref, far_ref, v1_refs), guards
+    ):
         v0_ref[pl.ds(NEAR - 1, 1), :] = above
-        v0_ref[pl.ds(NEAR + REACH, 1), :] = below
-        for start in range(0, REACH, 8):
-            at, weight_at = pl.ds(start, 8), pl.ds(REACH + start, 8)
-            v0_ref[pl.ds(NEAR + start, 8), :] = halo_ref[at, at_cols] * halo_ref[weight_at, at_cols]
-        for start in range(0, REACH, 8):
+        v0_ref[pl.ds(NEAR + count, 1), :] = below
+        for start in range(0, count, 8):
+            weight = weight_ref[pl.ds(weight_row + start, 8), at_cols]
+            v0_ref[pl.ds(NEAR + start, 8), :] = flux_ref[pl.ds(start, 8), at_cols] * weight
+        for start in range(0, count, 8):
             here = v0_ref[pl.ds(NEAR + start, 8), :]
             inner = pltpu.roll(here, 1 if side else LANES - 1, 1)
             outer = jnp.where(outermost, 0.0, pltpu.roll(here, LANES - 1 if side else 1, 1))
             beside = v0_ref[pl.ds(NEAR + start - 1, 8), :] + v0_ref[pl.ds(NEAR + start + 1, 8), :] + inner + outer
-            weight = halo_ref[pl.ds(REACH + start, 8), at_cols]
+            weight = weight_ref[pl.ds(weight_row + start, 8), at_cols]
             v1_ref[pl.ds(start, 8), there] = weight * here + smooth_weight * (4.0 * here - beside)
 
 
-def regions(f_ref, w_ref, v1_ref, near_ref, near_v1_ref, far_ref, far_v1_ref, step):
-    for start in range(0, f_ref.shape[0], step):
-        yield start, (f_ref, start), (w_ref, start), (v1_ref, start)
-    for base, halo_ref, field_ref in ((f_ref.shape[0], near_ref, near_v1_ref), (f_ref.shape[0] + REACH, far_ref, far_v1_ref)):
-        for start in range(0, REACH, step):
-            yield base + start, (halo_ref, start), (halo_ref, REACH + start), (field_ref, start)
+def regions(f_ref, w_ref, near_ref, far_ref, v1_refs, step):
+    base = 0
+    for count, flux_ref, weight_ref, weight_row, v1_ref in sources(f_ref, w_ref, near_ref, far_ref, v1_refs):
+        for start in range(0, count, step):
+            yield base + start, (flux_ref, start), (weight_ref, weight_row + start), (v1_ref, start)
+        base += count
 
 
 def dot(left, right):
@@ -370,12 +387,13 @@
 
 
 def edges_kernel(
-    nrows, ncols, parts_ref, f_ref, w_ref, v1_ref, narrow_ref, near_ref, far_ref, rowtaps_ref,
-    coefficients_ref, left_ref, right_ref, one_ref, other_ref, near_v1_ref, far_v1_ref, v0_ref, high_ref, low_ref,
+    nrows, ncols, parts_ref, f_ref, w_ref, narrow_ref, near_ref, far_ref, rowtaps_ref,
+    coefficients_ref, left_ref, right_ref, one_ref, other_ref, own_v1_ref, near_v1_ref, far_v1_ref, v0_ref, high_ref, low_ref,
 ):
     rows, cols = f_ref.shape
+    v1_refs = (own_v1_ref, near_v1_ref, far_v1_ref)
     for side in range(2):
-        edge_fields(side, f_ref, w_ref, narrow_ref, near_ref, far_ref, near_v1_ref, far_v1_ref, v0_ref)
+        edge_fields(side, f_ref, w_ref, narrow_ref, near_ref, far_ref, v1_refs, v0_ref)
     c0, c1 = coefficients(*coupled(parts_ref, nrows, ncols))
     coefficients_ref[pl.ds(0, 8), :] = jnp.broadcast_to(c0, (8, LANES))
     coefficients_ref[pl.ds(8, 8), :] = jnp.broadcast_to(c1, (8, LANES))
@@ -383,13 +401,12 @@
     left_ref[...], right_ref[...] = sides
 
     step = 16
-    fields = (f_ref, w_ref, v1_ref, near_ref, near_v1_ref, far_ref, far_v1_ref)
+    fields = (f_ref, w_ref, near_ref, far_ref, v1_refs)
     for side, begin in enumerate((0, cols - LANES)):
         at_cols = pl.ds(begin, LANES)
         for start, (flux_ref, flux_row), (weight_ref, weight_row), (field_ref, field_row) in regions(*fields, step):
             flux, weight = flux_ref[pl.ds(flux_row, step), at_cols], weight_ref[pl.ds(weight_row, step), at_cols]
-            v1_cols = at_cols if start < rows else pl.ds(side * LANES, LANES)
-            v1 = field_ref[pl.ds(field_row, step), v1_cols]
+            v1 = field_ref[pl.ds(field_row, step), pl.ds(side * LANES, LANES)]
             v1 = v1 - smooth_weight * sides[side][start : start + step]
             scatter = flux - (c0 * (flux * weight) + c1 * v1)
             high, low = split_values(scatter * scatter)
@@ -407,16 +424,17 @@
 
 
 def main_kernel(
-    coefficients_ref, left_ref, right_ref, f_ref, w_ref, v1_ref, narrow_ref, near_ref, far_ref, rowtaps_ref, coltaps_ref,
-    background_ref, rms_ref, sides_ref, near_v1_ref, far_v1_ref, v0_ref, high_ref, low_ref,
+    coefficients_ref, left_ref, right_ref, f_ref, w_ref, narrow_ref, near_ref, far_ref, rowtaps_ref, coltaps_ref,
+    background_ref, rms_ref, sides_ref, own_v1_ref, near_v1_ref, far_v1_ref, v0_ref, high_ref, low_ref,
 ):
     rows, cols = f_ref.shape
-    halo_fields(f_ref, w_ref, narrow_ref, near_ref, far_ref, near_v1_ref, far_v1_ref, v0_ref)
+    v1_refs = (own_v1_ref, near_v1_ref, far_v1_ref)
+    all_fields(f_ref, w_ref, narrow_ref, near_ref, far_ref, v1_refs, v0_ref)
     c0, c1 = coefficients_ref[pl.ds(0, 1), pl.ds(0, 1)], coefficients_ref[pl.ds(8, 1), pl.ds(0, 1)]
     step = 16
-    fields = (f_ref, w_ref, v1_ref, near_ref, near_v1_ref, far_ref, far_v1_ref)
-    for start, *sources in regions(*fields, step):
-        flux, weight, v1 = (ref[pl.ds(row, step), :] for ref, row in sources)
+    fields = (f_ref, w_ref, near_ref, far_ref, v1_refs)
+    for start, *here in regions(*fields, step):
+        flux, weight, v1 = (ref[pl.ds(row, step), :] for ref, row in here)
         at = pl.ds(start, step)
         v1 = jnp.concatenate(
             [
@@ -539,10 +557,10 @@
     far = swap(to_far, "rows", 1)
 
     devices = nrows * ncols
-    parts, own_v1 = call(
+    (parts,) = call(
         moments_kernel,
         "moments",
-        ((devices * (VECTORS + 1), LANES), (rows, cols)),
+        ((devices * (VECTORS + 1), LANES),),
         (field, scratch(rows, LANES)),
     )(*own, *base, narrow, near)
     parts = lax.all_to_all(parts.reshape(devices, 1, message), ("rows", "cols"), 0, 0, tiled=True)
@@ -551,22 +569,22 @@
     row_taps = lax.dynamic_index_in_dim(jnp.asarray(row_tables(rows)), kind, keepdims=False)
     col_taps = jnp.asarray(col_tables())
     reached, packed = rows + 2 * REACH, (rows // 2, LANES)
-    fields = (*own, own_v1, narrow, near, far)
-    halves = (scratch(REACH, 2 * LANES),) * 2
+    fields = (*own, narrow, near, far)
+    v1_parts = [scratch(count, 2 * LANES) for count in (rows, REACH, REACH)]
     numbers, left, right, to_one, to_other = call(
         functools.partial(edges_kernel, nrows, ncols),
         "edges",
         ((16, LANES), (reached, LANES), (reached, LANES), packed, packed),
-        halves + (scratch(REACH + 2 * NEAR, LANES),) + (scratch(reached, 2 * LANES, dtype=jnp.bfloat16),) * 2,
+        [*v1_parts, scratch(rows + 2 * NEAR, LANES)] + [scratch(reached, 2 * LANES, dtype=jnp.bfloat16)] * 2,
     )(parts, *fields, row_taps)
     one = swap(to_one, "cols", 0)
     other = swap(to_other, "cols", 1)
-    halves = (scratch(REACH, cols),) * 2
+    v1_parts = [scratch(count, cols) for count in (rows, REACH, REACH)]
     background, rms, sides = call(
         main_kernel,
         "main",
         ((rows, cols), (rows, cols), (rows, 2 * LANES)),
-        halves + (scratch(REACH + 2 * NEAR, cols + LANES),) + (scratch(reached, cols, dtype=jnp.bfloat16),) * 2,
+        [*v1_parts, field] + [scratch(reached, cols, dtype=jnp.bfloat16)] * 2,
     )(numbers, left, right, *fields, row_taps, col_taps)
     (rms,) = call(
         final_kernel, "final", ((rows, cols),), (scratch(2, rows, LANES), pltpu.SemaphoreType.DMA((2,))), in_place=True

time: 31.1 us -> 31.1 us (level)
  Pallas kernels: 6.66 us -> 7.07 us
  waiting for transfers between devices: 9.35 us -> 9 us
    pallas_call x5, Pallas kernels: 6.66 us -> 7.07 us  [run(): pl.pallas_call(kernel, out_shape=tuple((jax.ShapeDtypeStruct(shape, jnp.f...]
    ppermute x5, waiting for transfers between devices: 1.66 us -> 1.33 us  [swap(): return lax.ppermute(block, ('rows', 'cols'), pairs)]
  transfers between devices with their start and end apart: 6 -> 6, of which waited for: 3 -> 3; matrix products, arithmetic and copies ran while one was open for 7% -> 7% of each run, Pallas kernels for 16% -> 18%
where the time goes in v17:
time: 31.1 us; the launch traced here: 30.8 us
  starting transfers between devices  10.8 us (35%)
  waiting for transfers between devices  9 us (29%)
  Pallas kernels  7.07 us (23%)
  other arithmetic  2.23 us (7%)
  local copies, waits for them, and re-layouts  0.94 us (3%)
  between operations  0.78 us (3%)
    all_to_all x1, waiting for transfers between devices, shards(): lax.all_to_all(parts.reshape(devices, 1, message), ('rows', 'cols'), 0, 0...  7.67 us
    pallas_call x5, Pallas kernels, run(): pl.pallas_call(kernel, out_shape=tuple((jax.ShapeDtypeStruct(shape, jnp.f...  7.07 us
    all_to_all x1, starting transfers between devices, shards(): lax.all_to_all(parts.reshape(devices, 1, message), ('rows', 'cols'), 0, 0...  5.71 us
    ppermute x5, starting transfers between devices, swap(): return lax.ppermute(block, ('rows', 'cols'), pairs)  5.07 us
    ppermute x5, waiting for transfers between devices, swap(): return lax.ppermute(block, ('rows', 'cols'), pairs)  1.33 us
    mul x1, other arithmetic, weights(): return inverse_variance * (1.0 - source_mask.astype(jnp.float32))  1.27 us
    mul x1, other arithmetic, shards(): products = [flux * weight for flux, weight in taken]  0.94 us
    squeeze x1, local copies, waits for them, and re-layouts, shards(): lax.dynamic_index_in_dim(jnp.asarray(row_tables(rows)), kind, keepdims=Fa...  0.92 us
  transfers between devices with their start and end apart: 6, of which 3 were waited for; matrix products, arithmetic and copies ran while one was open for 7% of the time, Pallas kernels for 18%

profile of v17, /device:TPU:0, one launch (start us, length us, event | category | flops | bytes accessed | tf_op | source)
XLA Modules:
  0.0 30.8 jit_solution(6386736756951842674)
XLA Ops:
  0.6 0.9 %dynamic-slice_multiply_fusion = (f32[1,1024]{1,0:T(1,128)S(1)}, f32[1,1024]{1,0:T(1,128)S(1)}, f32[1,1024]{1,0:T(1,128)S(1)}, f32[1,1024]{1,0:T(1,128)S(1)}) fusion(f32[128,1024]{1,0:T(8,128)} %f_ref.7, s32[]{:T(128)S(6)} %select_n.40, s32[128,1024]{1,0:T(8,128)} %param.8, f32[128,1024]{1,0:T(8,128)} %param.7, s32[]{:T(128)S(6)} %select_n.41, s32[]{:T(128)S(6)} %select_n.42), kind=kLoop, calls=%fused_computation.6 | loop fusion | flops 12288 | bytes 53260 | tf_op jit(solution)/shard_map/mul | solution.py:544
  1.6 0.0 copy-start
  1.6 3.1 %collective-permute-start = (f32[4,1024]{1,0:T(4,128)S(1)}, f32[4,1024]{1,0:T(4,128)S(1)}, u32[]{:S(2)}, u32[]{:S(2)}) collective-permute-start(f32[4,1024]{1,0:T(4,128)S(1)} %pad_maximum_fusion), channel_id=1, source_target_pairs={{0,1},{1,0},{2,3},{3,2},{4,8},{5,9},{6,10},{7,11},{8,4},{9,5},{10,... | collective-permute-start | bytes 49160 | tf_op jit(solution)/shard_map/ppermute | solution.py:507
  4.7 1.3 %subtract_multiply_fusion.w_ref = f32[128,1024]{1,0:T(8,128)S(1)} fusion(f32[128,1024]{1,0:T(8,128)} %param.7, s32[128,1024]{1,0:T(8,128)} %param.8), kind=kLoop, calls=%fused_computation | loop fusion | flops 393216 | bytes 1572864 | tf_op jit(solution)/shard_map/mul | solution.py:106
  6.0 0.0 copy-done
  6.0 0.6 %prepare.1 = (f32[136,1024]{1,0:T(8,128)S(1)}, f32[128,1024]{1,0:T(8,128)S(1)}, f32[128,1024]{1,0:T(8,128)S(1)}, f32[24,128]{1,0:T(8,128)S(1)}, f32[128,128]{1,0:T(8,128)S(1)}) custom-call(f32[128,1024]{1,0:T(8,128)S(1)} %copy-done, f32[128,1024]{1,0:T(8,128)S(1)} %subtract_multiply_fusion.w_ref), custom_call_target="tpu_custom_call" | custom-call | tf_op jit(solution)/shard_map/prepare/pallas_call | solution.py:515
  6.6 0.0 collective-permute-done.narrow_ref
  6.6 0.1 collective-permute-start.1
  6.7 1.7 %collective-permute-start.2 = (f32[128,1024]{1,0:T(8,128)S(1)}, f32[128,1024]{1,0:T(8,128)S(1)}, u32[]{:S(2)}, u32[]{:S(2)}) collective-permute-start(f32[128,1024]{1,0:T(8,128)S(1)} %get-tuple-element.25), channel_id=1, source_target_pairs={{0,1},{1,0},{2,3},{3,2},{4,8},{5,9},{6,10},{7,11},{8,4},{9,5},{10,... | collective-permute-start | bytes 1572872 | tf_op jit(solution)/shard_map/ppermute | solution.py:507
  8.5 0.2 collective-permute-done.1.near_ref
  8.6 2.1 %moments.1 = f32[288,128]{1,0:T(8,128)} custom-call(f32[128,1024]{1,0:T(8,128)S(1)} %copy-done, f32[128,1024]{1,0:T(8,128)S(1)} %subtract_multiply_fusion.w_ref, f32[128,1024]{1,0:T(8,128)S(1)} %get-tuple-element.18.base_ref, f32[24,128]{1,0:T(8,128)S(1)} %get-tuple-element.19.sums_ref, f32[128,128]{1,0:T(8,128)S(1)} %get-tuple-element.20.edge_in_ref, ...), custom_call_target="tpu_custom_call" | custom-call | tf_op jit(solution)/shard_map/moments/pallas_call | solution.py:515
  10.8 5.7 %all-to-all-start = ((f32[32,1,1152]{2,1,0:T(1,128)}), f32[32,1,1152]{2,1,0:T(1,128)S(1)}, u32[]{:S(2)}, u32[]{:S(2)}) async-start(f32[32,1,1152]{2,1,0:T(1,128)} %bitcast), calls=%async_computation | async-start | bytes 294912 | tf_op jit(solution)/shard_map/all_to_all | solution.py:566
  16.5 0.9 %dynamic-slice_bitcast_fusion.rowtaps_ref = bf16[256,256]{1,0:T(8,128)(2,1)S(1)} fusion(bf16[4,256,256]{2,1,0:T(8,128)(2,1)} %constant.55.clone, s32[]{:T(128)S(6)} %select_n.44), kind=kLoop, calls=%fused_computation.1 | loop fusion | bytes 262148 | tf_op jit(solution)/shard_map/jit(dynamic_index_in_dim)/squeeze | solution.py:569
  17.4 0.0 copy-start.1
  17.5 0.0 collective-permute-done.2.far_ref
  17.5 7.7 %all-to-all-done.parts_ref = f32[32,1,1152]{2,1,0:T(1,128)S(1)} async-done(((f32[32,1,1152]{2,1,0:T(1,128)}), f32[32,1,1152]{2,1,0:T(1,128)S(1)}, u32[]{:S(2)}, u32[]{:S(2)}) %all-to-all-start) | async-done | bytes 147488 | tf_op jit(solution)/shard_map/all_to_all | solution.py:566
  25.1 0.8 %edges.1 = (f32[16,128]{1,0:T(8,128)S(1)}, f32[256,128]{1,0:T(8,128)S(1)}, f32[256,128]{1,0:T(8,128)S(1)}, f32[64,128]{1,0:T(8,128)S(1)}, f32[64,128]{1,0:T(8,128)S(1)}) custom-call(f32[32,1,1152]{2,1,0:T(1,128)S(1)} %all-to-all-done.parts_ref, f32[128,1024]{1,0:T(8,128)S(1)} %copy-done, f32[128,1024]{1,0:T(8,128)S(1)} %subtract_multiply_fusion.w_ref, ...), custom_call_target="tpu_custom_call" | custom-call | tf_op jit(solution)/shard_map/edges/pallas_call | solution.py:515
  25.9 0.1 collective-permute-start.3
  26.0 0.1 collective-permute-start.4
  26.1 0.0 copy-done.1
  26.1 0.0 copy-start.2
  26.1 2.7 %main.1 = (f32[128,1024]{1,0:T(8,128)}, f32[128,1024]{1,0:T(8,128)}, f32[128,256]{1,0:T(8,128)S(1)}) custom-call(f32[16,128]{1,0:T(8,128)S(1)} %get-tuple-element.26.coefficients_ref, f32[256,128]{1,0:T(8,128)S(1)} %get-tuple-element.27.left_ref, f32[256,128]{1,0:T(8,128)S(1)} %get-tuple-element.28.right_ref, f32[128,1024]{1,0:T(8,128)S(1)} %copy-done, ...), custom_call_target="tpu_custom_call" | custom-call | tf_op jit(solution)/shard_map/main/pallas_call | solution.py:515
  28.8 1.1 %collective-permute-done.3.one_ref = f32[64,128]{1,0:T(8,128)S(1)} collective-permute-done((f32[64,128]{1,0:T(8,128)S(1)}, f32[64,128]{1,0:T(8,128)S(1)}, u32[]{:S(2)}, u32[]{:S(2)}) %collective-permute-start.3) | collective-permute-done | bytes 32800 | tf_op jit(solution)/shard_map/ppermute | solution.py:507
  29.9 0.0 collective-permute-done.4.other_ref
  29.9 0.0 copy-done.2
  29.9 0.9 %final.1 = f32[128,1024]{1,0:T(8,128)} custom-call(f32[128,1024]{1,0:T(8,128)} %get-tuple-element.30.rms_in_ref, f32[128,256]{1,0:T(8,128)S(1)} %get-tuple-element.31.sides_ref, f32[64,128]{1,0:T(8,128)S(1)} %collective-permute-done.3.one_ref, f32[64,128]{1,0:T(8,128)S(1)} %collective-permute-done.4.other_ref, ...), custom_call_target="tpu_custom_call", output_to_operand_aliasing={{}: (0, {})} | custom-call | tf_op jit(solution)/shard_map/final/pallas_call | solution.py:515
  (1 shorter events, 0.0 us)
Async XLA Ops:
  1.6 4.4 %copy-start = (f32[128,1024]{1,0:T(8,128)S(1)}, f32[128,1024]{1,0:T(8,128)}, u32[]{:S(2)}) copy-start(f32[128,1024]{1,0:T(8,128)} %f_ref.7) | copy-start | bytes 1572868
  1.6 5.0 %collective-permute-start = (f32[4,1024]{1,0:T(4,128)S(1)}, f32[4,1024]{1,0:T(4,128)S(1)}, u32[]{:S(2)}, u32[]{:S(2)}) collective-permute-start(f32[4,1024]{1,0:T(4,128)S(1)} %pad_maximum_fusion), channel_id=1, source_target_pairs={{0,1},{1,0},{2,3},{3,2},{4,8},{5,9},{6,10},{7,11},{8,4},{9,5},{10,... | collective-permute-start | bytes 49160 | tf_op jit(solution)/shard_map/ppermute | solution.py:507
  6.6 2.0 %collective-permute-start.1 = (f32[136,1024]{1,0:T(8,128)S(1)}, f32[136,1024]{1,0:T(8,128)S(1)}, u32[]{:S(2)}, u32[]{:S(2)}) collective-permute-start(f32[136,1024]{1,0:T(8,128)S(1)} %get-tuple-element.24), channel_id=1, source_target_pairs={{0,4},{1,5},{2,6},{3,7},{4,0},{5,1},{6,2},{7,3},{8,12},{9,13},{10,... | collective-permute-start | bytes 1671176 | tf_op jit(solution)/shard_map/ppermute | solution.py:507
  6.7 10.7 %collective-permute-start.2 = (f32[128,1024]{1,0:T(8,128)S(1)}, f32[128,1024]{1,0:T(8,128)S(1)}, u32[]{:S(2)}, u32[]{:S(2)}) collective-permute-start(f32[128,1024]{1,0:T(8,128)S(1)} %get-tuple-element.25), channel_id=1, source_target_pairs={{0,1},{1,0},{2,3},{3,2},{4,8},{5,9},{6,10},{7,11},{8,4},{9,5},{10,... | collective-permute-start | bytes 1572872 | tf_op jit(solution)/shard_map/ppermute | solution.py:507
  10.8 14.4 %all-to-all-start = ((f32[32,1,1152]{2,1,0:T(1,128)}), f32[32,1,1152]{2,1,0:T(1,128)S(1)}, u32[]{:S(2)}, u32[]{:S(2)}) async-start(f32[32,1,1152]{2,1,0:T(1,128)} %bitcast), calls=%async_computation | async-start | bytes 294912 | tf_op jit(solution)/shard_map/all_to_all | solution.py:566
  17.4 8.6 %copy-start.1 = (bf16[3,256,256]{2,1,0:T(8,128)(2,1)S(1)}, bf16[3,256,256]{2,1,0:T(8,128)(2,1)}, u32[]{:S(2)}) copy-start(bf16[3,256,256]{2,1,0:T(8,128)(2,1)} %constant.56.clone.coltaps_ref) | copy-start | bytes 1179652
  25.9 4.0 %collective-permute-start.3 = (f32[64,128]{1,0:T(8,128)S(1)}, f32[64,128]{1,0:T(8,128)S(1)}, u32[]{:S(2)}, u32[]{:S(2)}) collective-permute-start(f32[64,128]{1,0:T(8,128)S(1)} %get-tuple-element.32), channel_id=1, source_target_pairs={{0,1},{1,0},{2,3},{3,2},{4,5},{5,4},{6,7},{7,6},{8,9},{9,8},{10,11... | collective-permute-start | bytes 98312 | tf_op jit(solution)/shard_map/ppermute | solution.py:507
  26.0 3.9 %collective-permute-start.4 = (f32[64,128]{1,0:T(8,128)S(1)}, f32[64,128]{1,0:T(8,128)S(1)}, u32[]{:S(2)}, u32[]{:S(2)}) collective-permute-start(f32[64,128]{1,0:T(8,128)S(1)} %get-tuple-element.33), channel_id=1, source_target_pairs={{0,4},{1,2},{2,1},{3,7},{4,0},{5,6},{6,5},{7,3},{8,12},{9,10},{10,... | collective-permute-start | bytes 98312 | tf_op jit(solution)/shard_map/ppermute | solution.py:507
  26.1 3.8 %copy-start.2 = (bf16[2,128,512]{2,1,0:T(8,128)(2,1)S(1)}, bf16[2,128,512]{2,1,0:T(8,128)(2,1)}, u32[]{:S(2)}) copy-start(bf16[2,128,512]{2,1,0:T(8,128)(2,1)} %constant.57.clone.sidetaps_ref) | copy-start | bytes 786436

commit v18 on v17

--- a/solution.py
+++ b/solution.py
@@ -174,7 +174,7 @@
         sums_ref[pl.ds(8 * i, 8), :] = sum(total[:, k : k + LANES] for k in range(0, cols, LANES))
 
 
-def moments_kernel(f_ref, w_ref, base_ref, sums_ref, edge_in_ref, narrow_ref, near_ref, out_ref, v1_ref, edge_ref):
+def moments_kernel(f_ref, w_ref, base_ref, sums_ref, edge_in_ref, narrow_ref, near_ref, out_ref, v1_ref, edge_ref, copies_ref, sems):
     rows, cols = f_ref.shape
     first_row, last_row, _, _ = at_edges()
     even = is_even()
@@ -239,9 +239,14 @@
         result = jnp.where(lane[:1] == i, jnp.sum(total, axis=1, keepdims=True), result)
     vectors = edge_ref[...].T
     message = [result] + [vectors[k : k + 1, :] for k in range(VECTORS)]
-    copies = jnp.concatenate(message * 8, axis=0)
-    for start in range(0, out_ref.shape[0], copies.shape[0]):
-        out_ref[pl.ds(start, copies.shape[0]), :] = copies
+    copies_ref[...] = jnp.concatenate(message * 8, axis=0)
+    count = copies_ref.shape[0]
+    sent = []
+    for i in range(out_ref.shape[0] // count):
+        sent.append(pltpu.make_async_copy(copies_ref, out_ref.at[pl.ds(i * count, count), :], sems.at[i]))
+        sent[-1].start()
+    for copy in sent:
+        copy.wait()
 
 
 def coupled(parts_ref, nrows, ncols):
@@ -507,7 +512,7 @@
     return lax.ppermute(block, ("rows", "cols"), pairs)
 
 
-def call(kernel, name, outs, scratch=(), limit=16, in_place=False):
+def call(kernel, name, outs, scratch=(), limit=16, in_place=False, out_there=False):
     vmem = pl.BlockSpec(memory_space=pltpu.VMEM)
     there = pl.BlockSpec(memory_space=pl.ANY)
 
@@ -516,7 +521,7 @@
             kernel,
             out_shape=tuple(jax.ShapeDtypeStruct(shape, jnp.float32) for shape in outs),
             in_specs=[there if in_place and i == 0 else vmem for i in range(len(args))],
-            out_specs=(there if in_place else vmem,) * len(outs),
+            out_specs=(there if in_place or out_there else vmem,) * len(outs),
             scratch_shapes=list(scratch),
             input_output_aliases={0: 0} if in_place else {},
             compiler_params=pltpu.CompilerParams(vmem_limit_bytes=limit << 20),
@@ -557,11 +562,13 @@
     far = swap(to_far, "rows", 1)
 
     devices = nrows * ncols
+    rows_sent = 8 * (VECTORS + 1)
     (parts,) = call(
         moments_kernel,
         "moments",
         ((devices * (VECTORS + 1), LANES),),
-        (field, scratch(rows, LANES)),
+        (field, scratch(rows, LANES), scratch(rows_sent, LANES), pltpu.SemaphoreType.DMA((devices // 8,))),
+        out_there=True,
     )(*own, *base, narrow, near)
     parts = lax.all_to_all(parts.reshape(devices, 1, message), ("rows", "cols"), 0, 0, tiled=True)
     first_row, last_row, _, _ = at_edges()

time: 31.1 us -> 31.1 us (level)
  no operation moved by 1% of the time
where the time goes in v18:
time: 31.1 us; the launch traced here: 30.8 us
  starting transfers between devices  10.8 us (35%)
  waiting for transfers between devices  9 us (29%)
  Pallas kernels  7.09 us (23%)
  other arithmetic  2.23 us (7%)
  local copies, waits for them, and re-layouts  0.94 us (3%)
  between operations  0.79 us (3%)
    all_to_all x1, waiting for transfers between devices, shards(): lax.all_to_all(parts.reshape(devices, 1, message), ('rows', 'cols'), 0, 0...  7.67 us
    pallas_call x5, Pallas kernels, run(): pl.pallas_call(kernel, out_shape=tuple((jax.ShapeDtypeStruct(shape, jnp.f...  7.09 us
    all_to_all x1, starting transfers between devices, shards(): lax.all_to_all(parts.reshape(devices, 1, message), ('rows', 'cols'), 0, 0...  5.72 us
    ppermute x5, starting transfers between devices, swap(): return lax.ppermute(block, ('rows', 'cols'), pairs)  5.07 us
    ppermute x5, waiting for transfers between devices, swap(): return lax.ppermute(block, ('rows', 'cols'), pairs)  1.33 us
    mul x1, other arithmetic, weights(): return inverse_variance * (1.0 - source_mask.astype(jnp.float32))  1.27 us
    mul x1, other arithmetic, shards(): products = [flux * weight for flux, weight in taken]  0.94 us
    squeeze x1, local copies, waits for them, and re-layouts, shards(): lax.dynamic_index_in_dim(jnp.asarray(row_tables(rows)), kind, keepdims=Fa...  0.92 us
  transfers between devices with their start and end apart: 6, of which 3 were waited for; matrix products, arithmetic and copies ran while one was open for 7% of the time, Pallas kernels for 18%

profile of v18, /device:TPU:0, one launch (start us, length us, event | category | flops | bytes accessed | tf_op | source)
XLA Modules:
  0.0 30.8 jit_solution(15705990496593811033)
XLA Ops:
  0.6 0.9 %dynamic-slice_multiply_fusion = (f32[1,1024]{1,0:T(1,128)S(1)}, f32[1,1024]{1,0:T(1,128)S(1)}, f32[1,1024]{1,0:T(1,128)S(1)}, f32[1,1024]{1,0:T(1,128)S(1)}) fusion(f32[128,1024]{1,0:T(8,128)} %f_ref.7, s32[]{:T(128)S(6)} %select_n.40, s32[128,1024]{1,0:T(8,128)} %param.8, f32[128,1024]{1,0:T(8,128)} %param.7, s32[]{:T(128)S(6)} %select_n.41, s32[]{:T(128)S(6)} %select_n.42), kind=kLoop, calls=%fused_computation.6 | loop fusion | flops 12288 | bytes 53260 | tf_op jit(solution)/shard_map/mul | solution.py:549
  1.6 0.0 copy-start
  1.6 3.1 %collective-permute-start = (f32[4,1024]{1,0:T(4,128)S(1)}, f32[4,1024]{1,0:T(4,128)S(1)}, u32[]{:S(2)}, u32[]{:S(2)}) collective-permute-start(f32[4,1024]{1,0:T(4,128)S(1)} %pad_maximum_fusion), channel_id=1, source_target_pairs={{0,1},{1,0},{2,3},{3,2},{4,8},{5,9},{6,10},{7,11},{8,4},{9,5},{10,... | collective-permute-start | bytes 49160 | tf_op jit(solution)/shard_map/ppermute | solution.py:512
  4.7 1.3 %subtract_multiply_fusion.w_ref = f32[128,1024]{1,0:T(8,128)S(1)} fusion(f32[128,1024]{1,0:T(8,128)} %param.7, s32[128,1024]{1,0:T(8,128)} %param.8), kind=kLoop, calls=%fused_computation | loop fusion | flops 393216 | bytes 1572864 | tf_op jit(solution)/shard_map/mul | solution.py:106
  6.0 0.0 copy-done
  6.0 0.6 %prepare.1 = (f32[136,1024]{1,0:T(8,128)S(1)}, f32[128,1024]{1,0:T(8,128)S(1)}, f32[128,1024]{1,0:T(8,128)S(1)}, f32[24,128]{1,0:T(8,128)S(1)}, f32[128,128]{1,0:T(8,128)S(1)}) custom-call(f32[128,1024]{1,0:T(8,128)S(1)} %copy-done, f32[128,1024]{1,0:T(8,128)S(1)} %subtract_multiply_fusion.w_ref), custom_call_target="tpu_custom_call" | custom-call | tf_op jit(solution)/shard_map/prepare/pallas_call | solution.py:520
  6.6 0.0 collective-permute-done.narrow_ref
  6.6 0.1 collective-permute-start.1
  6.7 1.7 %collective-permute-start.2 = (f32[128,1024]{1,0:T(8,128)S(1)}, f32[128,1024]{1,0:T(8,128)S(1)}, u32[]{:S(2)}, u32[]{:S(2)}) collective-permute-start(f32[128,1024]{1,0:T(8,128)S(1)} %get-tuple-element.25), channel_id=1, source_target_pairs={{0,1},{1,0},{2,3},{3,2},{4,8},{5,9},{6,10},{7,11},{8,4},{9,5},{10,... | collective-permute-start | bytes 1572872 | tf_op jit(solution)/shard_map/ppermute | solution.py:512
  8.5 0.2 collective-permute-done.1.near_ref
  8.6 2.2 %moments.1 = f32[288,128]{1,0:T(8,128)} custom-call(f32[128,1024]{1,0:T(8,128)S(1)} %copy-done, f32[128,1024]{1,0:T(8,128)S(1)} %subtract_multiply_fusion.w_ref, f32[128,1024]{1,0:T(8,128)S(1)} %get-tuple-element.18.base_ref, f32[24,128]{1,0:T(8,128)S(1)} %get-tuple-element.19.sums_ref, f32[128,128]{1,0:T(8,128)S(1)} %get-tuple-element.20.edge_in_ref, ...), custom_call_target="tpu_custom_call" | custom-call | tf_op jit(solution)/shard_map/moments/pallas_call | solution.py:520
  10.8 5.7 %all-to-all-start = ((f32[32,1,1152]{2,1,0:T(1,128)}), f32[32,1,1152]{2,1,0:T(1,128)S(1)}, u32[]{:S(2)}, u32[]{:S(2)}) async-start(f32[32,1,1152]{2,1,0:T(1,128)} %bitcast), calls=%async_computation | async-start | bytes 294912 | tf_op jit(solution)/shard_map/all_to_all | solution.py:573
  16.5 0.9 %dynamic-slice_bitcast_fusion.rowtaps_ref = bf16[256,256]{1,0:T(8,128)(2,1)S(1)} fusion(bf16[4,256,256]{2,1,0:T(8,128)(2,1)} %constant.55.clone, s32[]{:T(128)S(6)} %select_n.44), kind=kLoop, calls=%fused_computation.1 | loop fusion | bytes 262148 | tf_op jit(solution)/shard_map/jit(dynamic_index_in_dim)/squeeze | solution.py:576
  17.5 0.0 copy-start.1
  17.5 0.0 collective-permute-done.2.far_ref
  17.5 7.7 %all-to-all-done.parts_ref = f32[32,1,1152]{2,1,0:T(1,128)S(1)} async-done(((f32[32,1,1152]{2,1,0:T(1,128)}), f32[32,1,1152]{2,1,0:T(1,128)S(1)}, u32[]{:S(2)}, u32[]{:S(2)}) %all-to-all-start) | async-done | bytes 147488 | tf_op jit(solution)/shard_map/all_to_all | solution.py:573
  25.2 0.8 %edges.1 = (f32[16,128]{1,0:T(8,128)S(1)}, f32[256,128]{1,0:T(8,128)S(1)}, f32[256,128]{1,0:T(8,128)S(1)}, f32[64,128]{1,0:T(8,128)S(1)}, f32[64,128]{1,0:T(8,128)S(1)}) custom-call(f32[32,1,1152]{2,1,0:T(1,128)S(1)} %all-to-all-done.parts_ref, f32[128,1024]{1,0:T(8,128)S(1)} %copy-done, f32[128,1024]{1,0:T(8,128)S(1)} %subtract_multiply_fusion.w_ref, ...), custom_call_target="tpu_custom_call" | custom-call | tf_op jit(solution)/shard_map/edges/pallas_call | solution.py:520
  26.0 0.1 collective-permute-start.3
  26.0 0.1 collective-permute-start.4
  26.1 0.0 copy-done.1
  26.1 0.0 copy-start.2
  26.1 2.7 %main.1 = (f32[128,1024]{1,0:T(8,128)}, f32[128,1024]{1,0:T(8,128)}, f32[128,256]{1,0:T(8,128)S(1)}) custom-call(f32[16,128]{1,0:T(8,128)S(1)} %get-tuple-element.26.coefficients_ref, f32[256,128]{1,0:T(8,128)S(1)} %get-tuple-element.27.left_ref, f32[256,128]{1,0:T(8,128)S(1)} %get-tuple-element.28.right_ref, f32[128,1024]{1,0:T(8,128)S(1)} %copy-done, ...), custom_call_target="tpu_custom_call" | custom-call | tf_op jit(solution)/shard_map/main/pallas_call | solution.py:520
  28.8 1.1 %collective-permute-done.3.one_ref = f32[64,128]{1,0:T(8,128)S(1)} collective-permute-done((f32[64,128]{1,0:T(8,128)S(1)}, f32[64,128]{1,0:T(8,128)S(1)}, u32[]{:S(2)}, u32[]{:S(2)}) %collective-permute-start.3) | collective-permute-done | bytes 32800 | tf_op jit(solution)/shard_map/ppermute | solution.py:512
  29.9 0.0 collective-permute-done.4.other_ref
  29.9 0.0 copy-done.2
  29.9 0.9 %final.1 = f32[128,1024]{1,0:T(8,128)} custom-call(f32[128,1024]{1,0:T(8,128)} %get-tuple-element.30.rms_in_ref, f32[128,256]{1,0:T(8,128)S(1)} %get-tuple-element.31.sides_ref, f32[64,128]{1,0:T(8,128)S(1)} %collective-permute-done.3.one_ref, f32[64,128]{1,0:T(8,128)S(1)} %collective-permute-done.4.other_ref, ...), custom_call_target="tpu_custom_call", output_to_operand_aliasing={{}: (0, {})} | custom-call | tf_op jit(solution)/shard_map/final/pallas_call | solution.py:520
  (1 shorter events, 0.0 us)
Async XLA Ops:
  1.6 4.4 %copy-start = (f32[128,1024]{1,0:T(8,128)S(1)}, f32[128,1024]{1,0:T(8,128)}, u32[]{:S(2)}) copy-start(f32[128,1024]{1,0:T(8,128)} %f_ref.7) | copy-start | bytes 1572868
  1.6 5.0 %collective-permute-start = (f32[4,1024]{1,0:T(4,128)S(1)}, f32[4,1024]{1,0:T(4,128)S(1)}, u32[]{:S(2)}, u32[]{:S(2)}) collective-permute-start(f32[4,1024]{1,0:T(4,128)S(1)} %pad_maximum_fusion), channel_id=1, source_target_pairs={{0,1},{1,0},{2,3},{3,2},{4,8},{5,9},{6,10},{7,11},{8,4},{9,5},{10,... | collective-permute-start | bytes 49160 | tf_op jit(solution)/shard_map/ppermute | solution.py:512
  6.6 2.0 %collective-permute-start.1 = (f32[136,1024]{1,0:T(8,128)S(1)}, f32[136,1024]{1,0:T(8,128)S(1)}, u32[]{:S(2)}, u32[]{:S(2)}) collective-permute-start(f32[136,1024]{1,0:T(8,128)S(1)} %get-tuple-element.24), channel_id=1, source_target_pairs={{0,4},{1,5},{2,6},{3,7},{4,0},{5,1},{6,2},{7,3},{8,12},{9,13},{10,... | collective-permute-start | bytes 1671176 | tf_op jit(solution)/shard_map/ppermute | solution.py:512
  6.7 10.8 %collective-permute-start.2 = (f32[128,1024]{1,0:T(8,128)S(1)}, f32[128,1024]{1,0:T(8,128)S(1)}, u32[]{:S(2)}, u32[]{:S(2)}) collective-permute-start(f32[128,1024]{1,0:T(8,128)S(1)} %get-tuple-element.25), channel_id=1, source_target_pairs={{0,1},{1,0},{2,3},{3,2},{4,8},{5,9},{6,10},{7,11},{8,4},{9,5},{10,... | collective-permute-start | bytes 1572872 | tf_op jit(solution)/shard_map/ppermute | solution.py:512
  10.8 14.4 %all-to-all-start = ((f32[32,1,1152]{2,1,0:T(1,128)}), f32[32,1,1152]{2,1,0:T(1,128)S(1)}, u32[]{:S(2)}, u32[]{:S(2)}) async-start(f32[32,1,1152]{2,1,0:T(1,128)} %bitcast), calls=%async_computation | async-start | bytes 294912 | tf_op jit(solution)/shard_map/all_to_all | solution.py:573
  17.5 8.6 %copy-start.1 = (bf16[3,256,256]{2,1,0:T(8,128)(2,1)S(1)}, bf16[3,256,256]{2,1,0:T(8,128)(2,1)}, u32[]{:S(2)}) copy-start(bf16[3,256,256]{2,1,0:T(8,128)(2,1)} %constant.56.clone.coltaps_ref) | copy-start | bytes 1179652
  26.0 4.0 %collective-permute-start.3 = (f32[64,128]{1,0:T(8,128)S(1)}, f32[64,128]{1,0:T(8,128)S(1)}, u32[]{:S(2)}, u32[]{:S(2)}) collective-permute-start(f32[64,128]{1,0:T(8,128)S(1)} %get-tuple-element.32), channel_id=1, source_target_pairs={{0,1},{1,0},{2,3},{3,2},{4,5},{5,4},{6,7},{7,6},{8,9},{9,8},{10,11... | collective-permute-start | bytes 98312 | tf_op jit(solution)/shard_map/ppermute | solution.py:512
  26.0 3.9 %collective-permute-start.4 = (f32[64,128]{1,0:T(8,128)S(1)}, f32[64,128]{1,0:T(8,128)S(1)}, u32[]{:S(2)}, u32[]{:S(2)}) collective-permute-start(f32[64,128]{1,0:T(8,128)S(1)} %get-tuple-element.33), channel_id=1, source_target_pairs={{0,4},{1,2},{2,1},{3,7},{4,0},{5,6},{6,5},{7,3},{8,12},{9,10},{10,... | collective-permute-start | bytes 98312 | tf_op jit(solution)/shard_map/ppermute | solution.py:512
  26.1 3.8 %copy-start.2 = (bf16[2,128,512]{2,1,0:T(8,128)(2,1)S(1)}, bf16[2,128,512]{2,1,0:T(8,128)(2,1)}, u32[]{:S(2)}) copy-start(bf16[2,128,512]{2,1,0:T(8,128)(2,1)} %constant.57.clone.sidetaps_ref) | copy-start | bytes 786436

commit v19 on v17

--- a/solution.py
+++ b/solution.py
@@ -536,9 +536,9 @@
 
     taken = []
     for above, below in ((0, rows - 1), (1, rows - 2), (REACH, rows - 1 - REACH)):
-        start = (jnp.where(is_even(), above, below), 0)
         flux, variance, mask = (
-            lax.dynamic_slice(x, start, (1, cols)) for x in (coadd_flux, inverse_variance, source_mask)
+            jnp.where(is_even(), x[above : above + 1], x[below : below + 1])
+            for x in (coadd_flux, inverse_variance, source_mask)
         )
         taken.append((flux, weights(variance, mask)))
     products = [flux * weight for flux, weight in taken]

time: 31.1 us -> 31.2 us (level)
  transfers between devices with their start and end apart: 6 -> 6, of which waited for: 3 -> 3; matrix products, arithmetic and copies ran while one was open for 7% -> 7% of each run, Pallas kernels for 18% -> 17%
where the time goes in v19:
time: 31.2 us; the launch traced here: 30.9 us
  starting transfers between devices  10.8 us (35%)
  waiting for transfers between devices  9 us (29%)
  Pallas kernels  7.07 us (23%)
  other arithmetic  2.38 us (8%)
  local copies, waits for them, and re-layouts  0.94 us (3%)
  between operations  0.77 us (2%)
    all_to_all x1, waiting for transfers between devices, shards(): lax.all_to_all(parts.reshape(devices, 1, message), ('rows', 'cols'), 0, 0...  7.67 us
    pallas_call x5, Pallas kernels, run(): pl.pallas_call(kernel, out_shape=tuple((jax.ShapeDtypeStruct(shape, jnp.f...  7.07 us
    all_to_all x1, starting transfers between devices, shards(): lax.all_to_all(parts.reshape(devices, 1, message), ('rows', 'cols'), 0, 0...  5.69 us
    ppermute x5, starting transfers between devices, swap(): return lax.ppermute(block, ('rows', 'cols'), pairs)  5.07 us
    ppermute x5, waiting for transfers between devices, swap(): return lax.ppermute(block, ('rows', 'cols'), pairs)  1.33 us
    mul x1, other arithmetic, weights(): return inverse_variance * (1.0 - source_mask.astype(jnp.float32))  1.27 us
    mul x1, other arithmetic, shards(): products = [flux * weight for flux, weight in taken]  1.09 us
    squeeze x1, local copies, waits for them, and re-layouts, shards(): lax.dynamic_index_in_dim(jnp.asarray(row_tables(rows)), kind, keepdims=Fa...  0.92 us
  transfers between devices with their start and end apart: 6, of which 3 were waited for; matrix products, arithmetic and copies ran while one was open for 7% of the time, Pallas kernels for 17%

profile of v19, /device:TPU:0, one launch (start us, length us, event | category | flops | bytes accessed | tf_op | source)
XLA Modules:
  0.0 30.9 jit_solution(5120630530734140436)
XLA Ops:
  0.6 1.1 %fusion.4 = (f32[1,1024]{1,0:T(1,128)S(1)}, f32[1,1024]{1,0:T(1,128)S(1)}, f32[1,1024]{1,0:T(1,128)S(1)}, f32[1,1024]{1,0:T(1,128)S(1)}) fusion(pred[]{:T(512)S(6)} %eq.29, s32[128,1024]{1,0:T(8,128)} %param.8, f32[128,1024]{1,0:T(8,128)} %param.7, f32[128,1024]{1,0:T(8,128)} %f_ref.7), kind=kLoop, calls=%fused_computation.16 | loop fusion | flops 21504 | bytes 90113 | tf_op jit(solution)/shard_map/mul | solution.py:544
  1.8 0.0 copy-start
  1.8 3.1 %collective-permute-start = (f32[4,1024]{1,0:T(4,128)S(1)}, f32[4,1024]{1,0:T(4,128)S(1)}, u32[]{:S(2)}, u32[]{:S(2)}) collective-permute-start(f32[4,1024]{1,0:T(4,128)S(1)} %pad_maximum_fusion), channel_id=1, source_target_pairs={{0,1},{1,0},{2,3},{3,2},{4,8},{5,9},{6,10},{7,11},{8,4},{9,5},{10,... | collective-permute-start | bytes 49160 | tf_op jit(solution)/shard_map/ppermute | solution.py:507
  4.9 1.3 %subtract_multiply_fusion.w_ref = f32[128,1024]{1,0:T(8,128)S(1)} fusion(f32[128,1024]{1,0:T(8,128)} %param.7, s32[128,1024]{1,0:T(8,128)} %param.8), kind=kLoop, calls=%fused_computation | loop fusion | flops 393216 | bytes 1572864 | tf_op jit(solution)/shard_map/mul | solution.py:106
  6.1 0.0 copy-done
  6.2 0.6 %prepare.1 = (f32[136,1024]{1,0:T(8,128)S(1)}, f32[128,1024]{1,0:T(8,128)S(1)}, f32[128,1024]{1,0:T(8,128)S(1)}, f32[24,128]{1,0:T(8,128)S(1)}, f32[128,128]{1,0:T(8,128)S(1)}) custom-call(f32[128,1024]{1,0:T(8,128)S(1)} %copy-done, f32[128,1024]{1,0:T(8,128)S(1)} %subtract_multiply_fusion.w_ref), custom_call_target="tpu_custom_call" | custom-call | tf_op jit(solution)/shard_map/prepare/pallas_call | solution.py:515
  6.8 0.0 collective-permute-done.narrow_ref
  6.8 0.1 collective-permute-start.1
  6.9 1.7 %collective-permute-start.2 = (f32[128,1024]{1,0:T(8,128)S(1)}, f32[128,1024]{1,0:T(8,128)S(1)}, u32[]{:S(2)}, u32[]{:S(2)}) collective-permute-start(f32[128,1024]{1,0:T(8,128)S(1)} %get-tuple-element.25), channel_id=1, source_target_pairs={{0,1},{1,0},{2,3},{3,2},{4,8},{5,9},{6,10},{7,11},{8,4},{9,5},{10,... | collective-permute-start | bytes 1572872 | tf_op jit(solution)/shard_map/ppermute | solution.py:507
  8.6 0.2 collective-permute-done.1.near_ref
  8.8 2.1 %moments.1 = f32[288,128]{1,0:T(8,128)} custom-call(f32[128,1024]{1,0:T(8,128)S(1)} %copy-done, f32[128,1024]{1,0:T(8,128)S(1)} %subtract_multiply_fusion.w_ref, f32[128,1024]{1,0:T(8,128)S(1)} %get-tuple-element.18.base_ref, f32[24,128]{1,0:T(8,128)S(1)} %get-tuple-element.19.sums_ref, f32[128,128]{1,0:T(8,128)S(1)} %get-tuple-element.20.edge_in_ref, ...), custom_call_target="tpu_custom_call" | custom-call | tf_op jit(solution)/shard_map/moments/pallas_call | solution.py:515
  10.9 5.7 %all-to-all-start = ((f32[32,1,1152]{2,1,0:T(1,128)}), f32[32,1,1152]{2,1,0:T(1,128)S(1)}, u32[]{:S(2)}, u32[]{:S(2)}) async-start(f32[32,1,1152]{2,1,0:T(1,128)} %bitcast), calls=%async_computation | async-start | bytes 294912 | tf_op jit(solution)/shard_map/all_to_all | solution.py:566
  16.6 0.9 %dynamic-slice_bitcast_fusion.rowtaps_ref = bf16[256,256]{1,0:T(8,128)(2,1)S(1)} fusion(bf16[4,256,256]{2,1,0:T(8,128)(2,1)} %constant.54.clone, s32[]{:T(128)S(6)} %select_n.86), kind=kLoop, calls=%fused_computation.1 | loop fusion | bytes 262148 | tf_op jit(solution)/shard_map/jit(dynamic_index_in_dim)/squeeze | solution.py:569
  17.6 0.0 copy-start.1
  17.6 0.0 collective-permute-done.2.far_ref
  17.6 7.7 %all-to-all-done.parts_ref = f32[32,1,1152]{2,1,0:T(1,128)S(1)} async-done(((f32[32,1,1152]{2,1,0:T(1,128)}), f32[32,1,1152]{2,1,0:T(1,128)S(1)}, u32[]{:S(2)}, u32[]{:S(2)}) %all-to-all-start) | async-done | bytes 147488 | tf_op jit(solution)/shard_map/all_to_all | solution.py:566
  25.3 0.8 %edges.1 = (f32[16,128]{1,0:T(8,128)S(1)}, f32[256,128]{1,0:T(8,128)S(1)}, f32[256,128]{1,0:T(8,128)S(1)}, f32[64,128]{1,0:T(8,128)S(1)}, f32[64,128]{1,0:T(8,128)S(1)}) custom-call(f32[32,1,1152]{2,1,0:T(1,128)S(1)} %all-to-all-done.parts_ref, f32[128,1024]{1,0:T(8,128)S(1)} %copy-done, f32[128,1024]{1,0:T(8,128)S(1)} %subtract_multiply_fusion.w_ref, ...), custom_call_target="tpu_custom_call" | custom-call | tf_op jit(solution)/shard_map/edges/pallas_call | solution.py:515
  26.0 0.1 collective-permute-start.3
  26.1 0.1 collective-permute-start.4
  26.2 0.0 copy-done.1
  26.2 0.0 copy-start.2
  26.2 2.7 %main.1 = (f32[128,1024]{1,0:T(8,128)}, f32[128,1024]{1,0:T(8,128)}, f32[128,256]{1,0:T(8,128)S(1)}) custom-call(f32[16,128]{1,0:T(8,128)S(1)} %get-tuple-element.26.coefficients_ref, f32[256,128]{1,0:T(8,128)S(1)} %get-tuple-element.27.left_ref, f32[256,128]{1,0:T(8,128)S(1)} %get-tuple-element.28.right_ref, f32[128,1024]{1,0:T(8,128)S(1)} %copy-done, ...), custom_call_target="tpu_custom_call" | custom-call | tf_op jit(solution)/shard_map/main/pallas_call | solution.py:515
  28.9 1.1 %collective-permute-done.3.one_ref = f32[64,128]{1,0:T(8,128)S(1)} collective-permute-done((f32[64,128]{1,0:T(8,128)S(1)}, f32[64,128]{1,0:T(8,128)S(1)}, u32[]{:S(2)}, u32[]{:S(2)}) %collective-permute-start.3) | collective-permute-done | bytes 32800 | tf_op jit(solution)/shard_map/ppermute | solution.py:507
  30.0 0.0 collective-permute-done.4.other_ref
  30.0 0.0 copy-done.2
  30.0 0.9 %final.1 = f32[128,1024]{1,0:T(8,128)} custom-call(f32[128,1024]{1,0:T(8,128)} %get-tuple-element.30.rms_in_ref, f32[128,256]{1,0:T(8,128)S(1)} %get-tuple-element.31.sides_ref, f32[64,128]{1,0:T(8,128)S(1)} %collective-permute-done.3.one_ref, f32[64,128]{1,0:T(8,128)S(1)} %collective-permute-done.4.other_ref, ...), custom_call_target="tpu_custom_call", output_to_operand_aliasing={{}: (0, {})} | custom-call | tf_op jit(solution)/shard_map/final/pallas_call | solution.py:515
  (1 shorter events, 0.0 us)
Async XLA Ops:
  1.8 4.4 %copy-start = (f32[128,1024]{1,0:T(8,128)S(1)}, f32[128,1024]{1,0:T(8,128)}, u32[]{:S(2)}) copy-start(f32[128,1024]{1,0:T(8,128)} %f_ref.7) | copy-start | bytes 1572868
  1.8 5.0 %collective-permute-start = (f32[4,1024]{1,0:T(4,128)S(1)}, f32[4,1024]{1,0:T(4,128)S(1)}, u32[]{:S(2)}, u32[]{:S(2)}) collective-permute-start(f32[4,1024]{1,0:T(4,128)S(1)} %pad_maximum_fusion), channel_id=1, source_target_pairs={{0,1},{1,0},{2,3},{3,2},{4,8},{5,9},{6,10},{7,11},{8,4},{9,5},{10,... | collective-permute-start | bytes 49160 | tf_op jit(solution)/shard_map/ppermute | solution.py:507
  6.8 2.0 %collective-permute-start.1 = (f32[136,1024]{1,0:T(8,128)S(1)}, f32[136,1024]{1,0:T(8,128)S(1)}, u32[]{:S(2)}, u32[]{:S(2)}) collective-permute-start(f32[136,1024]{1,0:T(8,128)S(1)} %get-tuple-element.24), channel_id=1, source_target_pairs={{0,4},{1,5},{2,6},{3,7},{4,0},{5,1},{6,2},{7,3},{8,12},{9,13},{10,... | collective-permute-start | bytes 1671176 | tf_op jit(solution)/shard_map/ppermute | solution.py:507
  6.9 10.7 %collective-permute-start.2 = (f32[128,1024]{1,0:T(8,128)S(1)}, f32[128,1024]{1,0:T(8,128)S(1)}, u32[]{:S(2)}, u32[]{:S(2)}) collective-permute-start(f32[128,1024]{1,0:T(8,128)S(1)} %get-tuple-element.25), channel_id=1, source_target_pairs={{0,1},{1,0},{2,3},{3,2},{4,8},{5,9},{6,10},{7,11},{8,4},{9,5},{10,... | collective-permute-start | bytes 1572872 | tf_op jit(solution)/shard_map/ppermute | solution.py:507
  10.9 14.3 %all-to-all-start = ((f32[32,1,1152]{2,1,0:T(1,128)}), f32[32,1,1152]{2,1,0:T(1,128)S(1)}, u32[]{:S(2)}, u32[]{:S(2)}) async-start(f32[32,1,1152]{2,1,0:T(1,128)} %bitcast), calls=%async_computation | async-start | bytes 294912 | tf_op jit(solution)/shard_map/all_to_all | solution.py:566
  17.6 8.6 %copy-start.1 = (bf16[3,256,256]{2,1,0:T(8,128)(2,1)S(1)}, bf16[3,256,256]{2,1,0:T(8,128)(2,1)}, u32[]{:S(2)}) copy-start(bf16[3,256,256]{2,1,0:T(8,128)(2,1)} %constant.55.clone.coltaps_ref) | copy-start | bytes 1179652
  26.0 4.0 %collective-permute-start.3 = (f32[64,128]{1,0:T(8,128)S(1)}, f32[64,128]{1,0:T(8,128)S(1)}, u32[]{:S(2)}, u32[]{:S(2)}) collective-permute-start(f32[64,128]{1,0:T(8,128)S(1)} %get-tuple-element.32), channel_id=1, source_target_pairs={{0,1},{1,0},{2,3},{3,2},{4,5},{5,4},{6,7},{7,6},{8,9},{9,8},{10,11... | collective-permute-start | bytes 98312 | tf_op jit(solution)/shard_map/ppermute | solution.py:507
  26.1 3.9 %collective-permute-start.4 = (f32[64,128]{1,0:T(8,128)S(1)}, f32[64,128]{1,0:T(8,128)S(1)}, u32[]{:S(2)}, u32[]{:S(2)}) collective-permute-start(f32[64,128]{1,0:T(8,128)S(1)} %get-tuple-element.33), channel_id=1, source_target_pairs={{0,4},{1,2},{2,1},{3,7},{4,0},{5,6},{6,5},{7,3},{8,12},{9,10},{10,... | collective-permute-start | bytes 98312 | tf_op jit(solution)/shard_map/ppermute | solution.py:507
  26.2 3.8 %copy-start.2 = (bf16[2,128,512]{2,1,0:T(8,128)(2,1)S(1)}, bf16[2,128,512]{2,1,0:T(8,128)(2,1)}, u32[]{:S(2)}) copy-start(bf16[2,128,512]{2,1,0:T(8,128)(2,1)} %constant.56.clone.sidetaps_ref) | copy-start | bytes 786436
